TPU v7x, 32 devices: a whole 2x2x4 slice. The times are simulated.
32 devices in a mesh: dp: 4 (over z), expert: 4 (over y, x), tensor: 2 (over core).
Axes of the slice: x: 2, y: 2, z: 4, core: 2. Of those that a mesh axis runs over, the one named last changes fastest.
Arguments:
- tokens: bfloat16 [8192, 1536], P(('dp', 'expert')), may hold values from -6 to 6
- teacher: bfloat16 [8192, 1536], P(('dp', 'expert')), may hold values from -6 to 6
- routes: int32 [8192, 8], P(('dp', 'expert')), may hold values from 0 to 39, all different within a row; in each aligned block of 512 rows (0 to 511, 512 to 1023, ...) at most 128 rows name the same one
- valid: int32 [8192], P(('dp', 'expert')), may hold values from 0 to 1
- teacher_rows: int32 [16, 512], P(('dp', 'expert')), may hold values from 0 to 511, each once within a row
- norm_attn: float32 [1536], replicated, may hold values from 0.5 to 1.5
- norm_moe: float32 [1536], replicated, may hold values from 0.5 to 1.5
- w_query: bfloat16 [1536, 1536], P(None, 'tensor'), may hold values from -0.15625 to 0.15625
- key_projection_weight: bfloat16 [1536, 512], P(None, 'tensor'), may hold values from -0.15625 to 0.15625
- value_projection_weight: bfloat16 [1536, 512], P(None, 'tensor'), may hold values from -0.15625 to 0.15625
- w_out: bfloat16 [1536, 1536], P('tensor'), may hold values from -0.625 to 0.625
- w_router: bfloat16 [1536, 40], replicated, may hold values from -0.078125 to 0.078125
- w_gate: bfloat16 [40, 1536, 512], P('expert', None, 'tensor'), may hold values from -0.15625 to 0.15625
- w_up: bfloat16 [40, 1536, 512], P('expert', None, 'tensor'), may hold values from -0.15625 to 0.15625
- w_down: bfloat16 [40, 512, 1536], P('expert', 'tensor'), may hold values from -1 to 1
Outputs:
- block_out: bfloat16 [8192, 1536], P(('dp', 'expert'))
- grad_tokens: float32 [8192, 1536], P(('dp', 'expert'))
- grad_norm_attn: float32 [1536], P(('dp', 'expert'))
- grad_norm_moe: float32 [1536], P(('dp', 'expert'))
- grad_query: float32 [1536, 1536], P(('dp', 'expert'), 'tensor')
- grad_key: float32 [1536, 512], P(('dp', 'expert'), 'tensor')
- grad_value: float32 [1536, 512], P(('dp', 'expert'), 'tensor')
- grad_out: float32 [1536, 1536], P('tensor', ('dp', 'expert'))
- grad_router: float32 [1536, 40], P(('dp', 'expert'))
- grad_gate: float32 [40, 1536, 512], P('expert', 'dp', 'tensor')
- grad_up: float32 [40, 1536, 512], P('expert', 'dp', 'tensor')
- grad_down: float32 [40, 512, 1536], P('expert', 'tensor', 'dp')
Inputs may be any that keep to these rules, and one draw needn't show every extreme that they name: `routes`: no expert is named by more than 128 of the 512 rows of one index of dp+expert, a bound that some block reaches of them. `teacher_rows`: each row is a permutation of 0 to 511.
All inputs are finite; a program needn't handle non-finite values.
Results may differ from a plain program's by a relative error of at most 0.017.
Values may be sent and summed in bfloat16 or wider, within the bound.
No kernel may reach another device: no remote copies, remote signals or barrier semaphores. Data moves between devices by JAX's collectives and lax.ppermute only.
A program may use at most 256 MiB of HBM per device.

v0:
```python
import jax
import jax.numpy as jnp
from jax import lax
from jax.sharding import PartitionSpec as P

HEAD_DIMENSION = 64
SEQUENCE_LENGTH = 512
ABLK = 256


EPS = 1e-06
THETA = 10000.0


def rope_tables(length, head_size):
    half_size = head_size // 2
    frequency = THETA ** (-jnp.arange(half_size, dtype=jnp.float32) * 2.0 / head_size)
    angles = jnp.arange(length, dtype=jnp.float32)[:, None] * frequency[None, :]
    return (jnp.cos(angles), jnp.sin(angles))


def apply_rotary(value_matrix, cosine_table, sine_table):
    half_size = value_matrix.shape[-1] // 2
    first_half = value_matrix[..., :half_size]
    second_half = value_matrix[..., half_size:]
    cosine_rows = cosine_table[:, None, :]
    sine_rows = sine_table[:, None, :]
    return jnp.concatenate(
        [
            first_half * cosine_rows - second_half * sine_rows,
            second_half * cosine_rows + first_half * sine_rows,
        ],
        axis=-1,
    )


def rotate_back(grads, cosine_table, sine_table):
    half_size = grads.shape[-1] // 2
    first_half = grads[..., :half_size]
    second_half = grads[..., half_size:]
    cosine_rows = cosine_table[:, None, :]
    sine_rows = sine_table[:, None, :]
    return jnp.concatenate(
        [
            first_half * cosine_rows + second_half * sine_rows,
            second_half * cosine_rows - first_half * sine_rows,
        ],
        axis=-1,
    )


def rms_forward(value_matrix, gain):
    inverse = lax.rsqrt(jnp.mean(value_matrix * value_matrix, axis=-1, keepdims=True) + EPS)
    return (value_matrix * inverse * gain, inverse)


def rms_backward(value_matrix, inverse, gain, grad_normed):
    scaled = grad_normed * gain
    grad_gain = jnp.sum(grad_normed * value_matrix * inverse, axis=0)
    grad_values = inverse * scaled - value_matrix * inverse**3 * jnp.mean(
        scaled * value_matrix, axis=-1, keepdims=True
    )
    return (grad_values, grad_gain)


def masked_scores(query_part, key_matrix, row_begin, length):
    scores = jnp.einsum(
        "qkge,tke->kgqt", query_part, key_matrix, preferred_element_type=jnp.float32
    )
    query_block = (row_begin + jnp.arange(query_part.shape[0], dtype=jnp.int32)) // ABLK
    key_block = jnp.arange(length, dtype=jnp.int32) // ABLK
    allowed = query_block[:, None] >= key_block[None, :]
    return jnp.where(allowed, scores, -1e30)


def attend_forward(args):
    queries, key_matrix, value_matrix = args
    length, kv_heads, head_size = key_matrix.shape
    group_size = queries.shape[1] // kv_heads
    rows_block = min(512, length)
    grouped = queries.reshape(length, kv_heads, group_size, head_size)

    def one_block(row_begin):
        scores = masked_scores(grouped, key_matrix, row_begin, length)
        row_peak = jnp.max(scores, axis=-1, keepdims=True)
        weights = jnp.exp(scores - row_peak)
        totals = jnp.sum(weights, axis=-1, keepdims=True)
        weights_low = (weights / totals).astype(jnp.bfloat16)
        outputs = jnp.einsum(
            "kgqt,tke->qkge", weights_low, value_matrix, preferred_element_type=jnp.float32
        )
        return (
            outputs.reshape(rows_block, kv_heads * group_size * head_size),
            (row_peak + jnp.log(totals))[..., 0],
        )

    outputs, log_sums = lax.map(one_block, jnp.arange(0, length, rows_block, dtype=jnp.int32))
    return (outputs.reshape(length, kv_heads * group_size * head_size), log_sums)


def attend_backward(args):
    queries, key_matrix, value_matrix, log_sums, grad_mixed = args
    length, kv_heads, head_size = key_matrix.shape
    group_size = queries.shape[1] // kv_heads
    rows_block = min(512, length)
    grouped = queries.reshape(length, kv_heads, group_size, head_size)
    grad_grouped = grad_mixed.reshape(length, kv_heads, group_size, head_size)

    def one_block(running, inputs):
        row_begin, block_sums = inputs
        scores = masked_scores(grouped, key_matrix, row_begin, length)
        probs = jnp.exp(scores - block_sums[..., None])
        grad_probs = jnp.einsum(
            "qkge,tke->kgqt", grad_grouped, value_matrix, preferred_element_type=jnp.float32
        )
        row_inner = jnp.sum(probs * grad_probs, axis=-1, keepdims=True)
        grad_scores = (probs * (grad_probs - row_inner)).astype(jnp.bfloat16)
        grad_query = jnp.einsum(
            "kgqt,tke->qkge", grad_scores, key_matrix, preferred_element_type=jnp.float32
        )
        grad_key = running[0] + jnp.einsum(
            "kgqt,qkge->tke", grad_scores, grouped, preferred_element_type=jnp.float32
        )
        grad_value = running[1] + jnp.einsum(
            "kgqt,qkge->tke",
            probs.astype(jnp.bfloat16),
            grad_grouped,
            preferred_element_type=jnp.float32,
        )
        return (
            (grad_key, grad_value),
            grad_query.reshape(rows_block, kv_heads * group_size, head_size),
        )

    zero_keys = jnp.zeros(key_matrix.shape, jnp.float32)
    starts = jnp.arange(0, length, rows_block, dtype=jnp.int32)
    (grad_key, grad_value), grad_query = lax.scan(
        one_block, (zero_keys, zero_keys), (starts, log_sums)
    )
    return (grad_query.reshape(length, kv_heads * group_size, head_size), grad_key, grad_value)


def on_device(
    tokens,
    teacher,
    routes,
    valid,
    teacher_rows,
    norm_attn,
    norm_moe,
    w_query,
    key_projection_weight,
    value_projection_weight,
    w_out,
    w_router,
    w_gate,
    w_up,
    w_down,
):
    rows_dev, model_width = tokens.shape
    seq_count = rows_dev // SEQUENCE_LENGTH
    heads_local = w_query.shape[1] // HEAD_DIMENSION
    kv_local = key_projection_weight.shape[1] // HEAD_DIMENSION
    experts_local = w_gate.shape[0]
    owners = lax.axis_size("expert")
    groups = lax.axis_size("dp") * owners
    all_experts = experts_local * owners
    top_count = routes.shape[1]
    capacity = rows_dev * top_count * 5 // (4 * all_experts)
    bfloat = jnp.bfloat16
    single = jnp.float32
    valid_rows = valid.astype(single)
    valid_count = lax.psum(jnp.sum(valid_rows), ("dp", "expert"))
    loss_scale = rows_dev * groups / valid_count
    inputs = tokens.astype(single)
    normed_first, inverse_first = rms_forward(inputs, norm_attn)
    attention_input = normed_first.astype(bfloat)
    cosine_table, sine_table = rope_tables(SEQUENCE_LENGTH, HEAD_DIMENSION)
    factor = HEAD_DIMENSION ** (-0.5)
    query_raw = jnp.dot(attention_input, w_query, preferred_element_type=single).reshape(
        seq_count, SEQUENCE_LENGTH, heads_local, HEAD_DIMENSION
    )
    key_unrotated = jnp.dot(
        attention_input, key_projection_weight, preferred_element_type=single
    ).reshape(seq_count, SEQUENCE_LENGTH, kv_local, HEAD_DIMENSION)
    value_unprojected = jnp.dot(
        attention_input, value_projection_weight, preferred_element_type=single
    ).reshape(seq_count, SEQUENCE_LENGTH, kv_local, HEAD_DIMENSION)
    queries = (apply_rotary(query_raw, cosine_table, sine_table) * factor).astype(bfloat)
    key_matrix = apply_rotary(key_unrotated, cosine_table, sine_table).astype(bfloat)
    value_matrix = value_unprojected.astype(bfloat)
    outputs, log_sums = lax.map(attend_forward, (queries, key_matrix, value_matrix))
    attn_low = outputs.reshape(rows_dev, heads_local * HEAD_DIMENSION).astype(bfloat)
    attn_part = jnp.dot(attn_low, w_out, preferred_element_type=single)
    attn_full = lax.psum(attn_part, "tensor")
    hidden_first = inputs + attn_full
    normed_second, inverse_second = rms_forward(hidden_first, norm_moe)
    moe_in = normed_second.astype(bfloat)
    logits = jnp.dot(moe_in, w_router, preferred_element_type=single)
    picked_mask = routes[:, :, None] == jnp.arange(all_experts, dtype=jnp.int32)[None, None, :]
    chosen = jnp.sum(jnp.where(picked_mask, logits[:, None, :], 0.0), axis=-1)
    chosen = chosen - jnp.max(chosen, axis=1, keepdims=True)
    exponent = jnp.exp(chosen)
    gates = exponent / jnp.sum(exponent, axis=1, keepdims=True)
    expert_loads = jnp.sum(picked_mask.astype(jnp.int32), axis=1)
    before = jnp.cumsum(expert_loads, axis=0) - expert_loads
    slot_index = jnp.sum(jnp.where(picked_mask, before[:, None, :], 0), axis=-1)
    places = (routes * capacity + slot_index).reshape(-1)
    token_ids = jnp.repeat(jnp.arange(rows_dev, dtype=jnp.int32), top_count) + 1
    owner_row = jnp.zeros((all_experts * capacity,), jnp.int32).at[places].set(token_ids)
    live_slot = (owner_row > 0)[:, None]
    source = jnp.maximum(owner_row - 1, 0)
    send_rows = jnp.where(live_slot, moe_in[source], jnp.zeros((), bfloat))
    send_rows = send_rows.reshape(owners, experts_local, 1, capacity, model_width)
    arrived = lax.all_to_all(send_rows, "expert", split_axis=0, concat_axis=2, tiled=True)
    expert_rows = arrived.reshape(experts_local, owners * capacity, model_width)
    gate_pre = jnp.einsum("erd,edf->erf", expert_rows, w_gate, preferred_element_type=single)
    up_pre = jnp.einsum("erd,edf->erf", expert_rows, w_up, preferred_element_type=single)
    expert_hidden = (jax.nn.silu(gate_pre) * up_pre).astype(bfloat)
    expert_out = jnp.einsum(
        "erf,efd->erd", expert_hidden, w_down, preferred_element_type=single
    ).astype(bfloat)
    returned = lax.all_to_all(
        expert_out.reshape(1, experts_local, owners, capacity, model_width),
        "expert",
        split_axis=2,
        concat_axis=0,
        tiled=True,
    )
    returned = returned.reshape(all_experts * capacity, model_width)
    picked = returned[places].reshape(rows_dev, top_count, model_width)
    moe_part = jnp.sum(gates[:, :, None] * picked, axis=1)
    moe_full = lax.psum(moe_part, "tensor")
    layer_out = hidden_first + moe_full
    target = teacher[teacher_rows[0]].astype(single)
    grad_layer = loss_scale * valid_rows[:, None] * (layer_out - target)
    gate_slot = jnp.zeros((all_experts * capacity,), single).at[places].set(gates.reshape(-1))
    grad_send = (gate_slot[:, None] * grad_layer[source]).astype(bfloat)
    grad_send = grad_send.reshape(owners, experts_local, 1, capacity, model_width)
    grad_rows = lax.all_to_all(grad_send, "expert", split_axis=0, concat_axis=2, tiled=True)
    grad_rows = grad_rows.reshape(experts_local, owners * capacity, model_width)
    grad_gates_part = jnp.sum(grad_layer[:, None, :] * picked, axis=-1)
    sigmoid_gate = jax.nn.sigmoid(gate_pre)
    grad_hidden = jnp.einsum("erd,efd->erf", grad_rows, w_down, preferred_element_type=single)
    grad_gate_pre = (
        grad_hidden * up_pre * sigmoid_gate * (1.0 + gate_pre * (1.0 - sigmoid_gate))
    ).astype(bfloat)
    grad_up_pre = (grad_hidden * gate_pre * sigmoid_gate).astype(bfloat)
    grad_down_local = jnp.einsum(
        "erf,erd->efd", expert_hidden, grad_rows, preferred_element_type=single
    )
    grad_gate_local = jnp.einsum(
        "erd,erf->edf", expert_rows, grad_gate_pre, preferred_element_type=single
    )
    grad_up_local = jnp.einsum(
        "erd,erf->edf", expert_rows, grad_up_pre, preferred_element_type=single
    )
    grad_expert_rows = (
        jnp.einsum("erf,edf->erd", grad_gate_pre, w_gate, preferred_element_type=single)
        + jnp.einsum("erf,edf->erd", grad_up_pre, w_up, preferred_element_type=single)
    ).astype(bfloat)
    grad_returned = lax.all_to_all(
        grad_expert_rows.reshape(1, experts_local, owners, capacity, model_width),
        "expert",
        split_axis=2,
        concat_axis=0,
        tiled=True,
    )
    grad_returned = grad_returned.reshape(all_experts * capacity, model_width)
    grad_moe_part = jnp.sum(
        grad_returned[places].reshape(rows_dev, top_count, model_width).astype(single), axis=1
    )
    grad_moe_in, grad_gates = lax.psum((grad_moe_part, grad_gates_part), "tensor")
    grad_chosen = gates * (grad_gates - jnp.sum(gates * grad_gates, axis=1, keepdims=True))
    grad_logits = jnp.sum(jnp.where(picked_mask, grad_chosen[:, :, None], 0.0), axis=1).astype(
        bfloat
    )
    grad_moe_in = grad_moe_in + jnp.dot(grad_logits, w_router.T, preferred_element_type=single)
    grad_router_local = jnp.dot(moe_in.T, grad_logits, preferred_element_type=single)
    grad_second, grad_norm_moe_local = rms_backward(
        hidden_first, inverse_second, norm_moe, grad_moe_in
    )
    grad_hidden_first = grad_layer + grad_second
    grad_attn = grad_hidden_first.astype(bfloat)
    grad_out_local = jnp.dot(attn_low.T, grad_attn, preferred_element_type=single)
    grad_mixed = jnp.dot(grad_attn, w_out.T, preferred_element_type=single).astype(bfloat)
    grad_mixed = grad_mixed.reshape(seq_count, SEQUENCE_LENGTH, heads_local * HEAD_DIMENSION)
    grad_queries, grad_keys, grad_values = lax.map(
        attend_backward, (queries, key_matrix, value_matrix, log_sums, grad_mixed)
    )
    grad_query_raw = (
        rotate_back(grad_queries * factor, cosine_table, sine_table)
        .astype(bfloat)
        .reshape(rows_dev, heads_local * HEAD_DIMENSION)
    )
    grad_key_raw = (
        rotate_back(grad_keys, cosine_table, sine_table)
        .astype(bfloat)
        .reshape(rows_dev, kv_local * HEAD_DIMENSION)
    )
    grad_value_raw = grad_values.astype(bfloat).reshape(rows_dev, kv_local * HEAD_DIMENSION)
    grad_attn_in = (
        jnp.dot(grad_query_raw, w_query.T, preferred_element_type=single)
        + jnp.dot(grad_key_raw, key_projection_weight.T, preferred_element_type=single)
        + jnp.dot(grad_value_raw, value_projection_weight.T, preferred_element_type=single)
    )
    grad_attn_in = lax.psum(grad_attn_in.astype(jnp.bfloat16), "tensor").astype(jnp.float32)
    grad_first, grad_norm_attn_local = rms_backward(inputs, inverse_first, norm_attn, grad_attn_in)
    grad_tokens = grad_hidden_first + grad_first
    grad_query_local = jnp.dot(attention_input.T, grad_query_raw, preferred_element_type=single)
    grad_key_local = jnp.dot(attention_input.T, grad_key_raw, preferred_element_type=single)
    grad_value_local = jnp.dot(attention_input.T, grad_value_raw, preferred_element_type=single)
    dense_sums = (
        lax.psum_scatter(grad_query_local, ("dp", "expert"), scatter_dimension=0, tiled=True),
        lax.psum_scatter(grad_key_local, ("dp", "expert"), scatter_dimension=0, tiled=True),
        lax.psum_scatter(grad_value_local, ("dp", "expert"), scatter_dimension=0, tiled=True),
        lax.psum_scatter(grad_out_local, ("dp", "expert"), scatter_dimension=1, tiled=True),
        lax.psum_scatter(grad_router_local, ("dp", "expert"), scatter_dimension=0, tiled=True),
        lax.psum_scatter(grad_norm_attn_local, ("dp", "expert"), scatter_dimension=0, tiled=True),
        lax.psum_scatter(grad_norm_moe_local, ("dp", "expert"), scatter_dimension=0, tiled=True),
    )
    expert_sums = (
        lax.psum_scatter(
            grad_gate_local.astype(jnp.bfloat16), "dp", scatter_dimension=1, tiled=True
        ).astype(jnp.float32),
        lax.psum_scatter(
            grad_up_local.astype(jnp.bfloat16), "dp", scatter_dimension=1, tiled=True
        ).astype(jnp.float32),
        lax.psum_scatter(
            grad_down_local.astype(jnp.bfloat16), "dp", scatter_dimension=2, tiled=True
        ).astype(jnp.float32),
    )
    return (
        layer_out.astype(bfloat),
        grad_tokens,
        dense_sums[5],
        dense_sums[6],
        dense_sums[0],
        dense_sums[1],
        dense_sums[2],
        dense_sums[3],
        dense_sums[4],
        expert_sums[0],
        expert_sums[1],
        expert_sums[2],
    )


def solution(mesh):
    placed = (
        P(("dp", "expert"), None),
        P(("dp", "expert"), None),
        P(("dp", "expert"), None),
        P(("dp", "expert")),
        P(("dp", "expert"), None),
        P(),
        P(),
        P(None, "tensor"),
        P(None, "tensor"),
        P(None, "tensor"),
        P("tensor", None),
        P(),
        P("expert", None, "tensor"),
        P("expert", None, "tensor"),
        P("expert", "tensor", None),
    )
    return jax.shard_map(
        on_device,
        mesh=mesh,
        in_specs=placed,
        out_specs=(
            P(("dp", "expert"), None),
            P(("dp", "expert"), None),
            P(("dp", "expert")),
            P(("dp", "expert")),
            P(("dp", "expert"), "tensor"),
            P(("dp", "expert"), "tensor"),
            P(("dp", "expert"), "tensor"),
            P("tensor", ("dp", "expert")),
            P(("dp", "expert"), None),
            P("expert", "dp", "tensor"),
            P("expert", "dp", "tensor"),
            P("expert", "tensor", "dp"),
        ),
        check_vma=False,
    )
```

profile of v0, /device:TPU:0, one launch (start us, length us, event | category | flops | bytes accessed | tf_op | source)
XLA Modules:
  0.0 2271.4 jit_solution(559322296877886373)
XLA Ops:
  33.7 15.5 scatter_custom_fusion
  62.8 32.9 %gather_fusion = bf16[5120,1536]{1,0:T(8,128)(2,1)} fusion(bf16[512,1536]{1,0:T(8,128)(2,1)} %multiply_convert_fusion.4, s32[5120]{0:T(1024)S(1)} %maximum_clamp_fusion), kind=kCustom, calls=%fused_computation | custom fusion | bytes 31477760 | tf_op jit(solution)/shard_map/gather | solution.py:213
  103.8 175.8 %all_to_all.60 = bf16[4,10,1,128,1536]{4,3,1,2,0:T(8,128)(2,1)S(1)} all-to-all(bf16[4,10,1,128,1536]{4,3,1,2,0:T(8,128)(2,1)S(1)} %broadcast_select_fusion), channel_id=1, replica_groups=mesh['dp'=4,'expert'=4,'tensor'=2] {'expert'}, dimensions={0} | all-to-all | bytes 31457280 | tf_op jit(solution)/shard_map/all_to_all | solution.py:215
  286.2 14.2 fusion.75
  300.4 16.8 multiply_convert_fusion.3
  317.2 13.8 convolution_convert_fusion
  331.0 13.4 copy.118
  355.2 166.5 %all-to-all-done.1 = bf16[1,10,4,128,1536]{4,3,1,0,2:T(8,128)(2,1)} async-done(((bf16[1,10,4,128,1536]{4,3,1,0,2:T(8,128)(2,1)}), bf16[1,10,4,128,1536]{4,3,1,0,2:T(8,128)(2,1)}, u32[]{:S(2)}, u32[]{:S(2)}) %all-to-all-start.1) | async-done | bytes 15728672 | tf_op jit(solution)/shard_map/all_to_all | solution.py:223
  521.7 32.8 %gather_fusion.1 = bf16[4096,1536]{1,0:T(8,128)(2,1)} fusion(bf16[5120,1536]{1,0:T(8,128)(2,1)} %bitcast.25, s32[4096]{0:T(1024)S(1)} %broadcast_clamp_fusion), kind=kCustom, calls=%fused_computation.1 | custom fusion | bytes 25182208 | tf_op jit(solution)/shard_map/gather | solution.py:231
  554.5 12.7 fusion
  568.5 41.3 %psum.44 = f32[]{:T(128)} all-reduce(f32[]{:T(128)} %convert_reduce_fusion.2), channel_id=1, replica_groups=mesh['dp'=4,'expert'=4,'tensor'=2] {'dp','expert'}, use_global_device_ids=true, to_apply=%region_16.17 | all-reduce | flops 1 | bytes 8 | tf_op jit(solution)/shard_map/psum | solution.py:173
  616.7 15.5 scatter_custom_fusion.1
  638.3 35.5 %gather_fusion.3 = f32[5120,1536]{1,0:T(8,128)} fusion(f32[512,1536]{1,0:T(8,128)} %get-tuple-element.127, s32[5120]{0:T(1024)S(1)} %maximum_clamp_fusion), kind=kCustom, calls=%fused_computation.3 | custom fusion | bytes 62935040 | tf_op jit(solution)/shard_map/gather | solution.py:238
  685.3 166.3 %all_to_all.61 = bf16[4,10,1,128,1536]{4,3,1,2,0:T(8,128)(2,1)S(1)} all-to-all(bf16[4,10,1,128,1536]{4,3,1,2,0:T(8,128)(2,1)S(1)} %multiply_convert_fusion), channel_id=1, replica_groups=mesh['dp'=4,'expert'=4,'tensor'=2] {'expert'}, dimensions={0} | all-to-all | bytes 31457280 | tf_op jit(solution)/shard_map/all_to_all | solution.py:240
  857.9 15.0 multiply_convert_fusion.1
  872.8 18.7 fusion.76
  891.5 20.8 add_convert_fusion
  920.2 166.0 %all_to_all.62 = bf16[1,10,4,128,1536]{4,3,1,0,2:T(8,128)(2,1)} all-to-all(bf16[1,10,4,128,1536]{4,3,1,0,2:T(8,128)(2,1)S(1)} %copy.122), channel_id=1, replica_groups=mesh['dp'=4,'expert'=4,'tensor'=2] {'expert'}, dimensions={2} | all-to-all | bytes 31457280 | tf_op jit(solution)/shard_map/all_to_all | solution.py:262
  1086.2 32.8 %gather_fusion.4 = bf16[4096,1536]{1,0:T(8,128)(2,1)} fusion(bf16[5120,1536]{1,0:T(8,128)(2,1)} %bitcast.186, s32[4096]{0:T(1024)S(1)} %copy-done.41), kind=kCustom, calls=%fused_computation.4 | custom fusion | bytes 25182208 | tf_op jit(solution)/shard_map/gather | solution.py:271
  1119.0 12.7 convert_reduce_fusion
  1149.8 13.7 convolution_convert_fusion.1
  1163.6 15.7 copy.145
  1179.3 13.0 copy.149
  1282.3 136.1 %reduce-scatter.27.cloned.1.call-done = bf16[384,2560]{1,0:T(8,128)(2,1)} async-done(((bf16[1536,2560]{1,0:T(8,128)(2,1)}), bf16[384,2560]{1,0:T(8,128)(2,1)}) %reduce-scatter.27.cloned.1.call-update) | async-done | bytes 1966096
  1432.3 125.1 %reduce-scatter.23.cloned.1.call-done = bf16[10,384,256]{2,1,0:T(8,128)(2,1)} async-done(((bf16[10,1536,256]{2,1,0:T(8,128)(2,1)}), bf16[10,384,256]{2,1,0:T(8,128)(2,1)}) %reduce-scatter.23.cloned.1.call-update) | async-done | bytes 1966096 | tf_op jit(solution)/shard_map/reduce_scatter | solution.py:326
  1561.3 135.4 %reduce-scatter.21.cloned.1.call-done = bf16[10,384,256]{2,1,0:T(8,128)(2,1)} async-done(((bf16[10,1536,256]{2,1,0:T(8,128)(2,1)}), bf16[10,384,256]{2,1,0:T(8,128)(2,1)}) %reduce-scatter.21.cloned.1.call-update) | async-done | bytes 1966096 | tf_op jit(solution)/shard_map/reduce_scatter | solution.py:323
  1700.5 19.6 all-reduce.14.cloned.1.call-done
  1723.1 77.3 %all-reduce.2 = (f32[1536]{0:T(1024)S(1)}, f32[1536]{0:T(1024)S(1)}) all-reduce(f32[1536]{0:T(1024)S(1)} %get-tuple-element.110, f32[1536]{0:T(1024)S(1)} %get-tuple-element.108), channel_id=2, replica_groups=mesh['dp'=4,'expert'=4,'tensor'=2] {'dp','expert'}, use_global_device_ids=true, to_apply=%region_29.30.clone | all-reduce | flops 3072 | bytes 24576
  1807.0 44.1 %reduce-scatter.17.cloned.1.call-done = f32[96,256]{1,0:T(8,128)} async-done(((f32[1536,256]{1,0:T(8,128)}), f32[96,256]{1,0:T(8,128)}) %reduce-scatter.17.cloned.1.call-update) | async-done | bytes 98320 | tf_op jit(solution)/shard_map/reduce_scatter | solution.py:316
  1851.1 128.7 %reduce-scatter.15.cloned.1.call-done = f32[96,256]{1,0:T(8,128)} async-done(((f32[1536,256]{1,0:T(8,128)}), f32[96,256]{1,0:T(8,128)}) %reduce-scatter.15.cloned.1.call-update) | async-done | bytes 98320 | tf_op jit(solution)/shard_map/reduce_scatter | solution.py:315
  1979.8 142.0 %reduce-scatter.19.cloned.1.call-done = f32[768,96]{0,1:T(8,128)} async-done(((f32[768,1536]{0,1:T(8,128)}), f32[768,96]{0,1:T(8,128)}) %reduce-scatter.19.cloned.1.call-update) | async-done | bytes 294928 | tf_op jit(solution)/shard_map/reduce_scatter | solution.py:317
  2121.9 142.5 %reduce-scatter.13.cloned.1.call-done = f32[96,768]{1,0:T(8,128)} async-done(((f32[1536,768]{1,0:T(8,128)}), f32[96,768]{1,0:T(8,128)}) %reduce-scatter.13.cloned.1.call-update) | async-done | bytes 294928 | tf_op jit(solution)/shard_map/reduce_scatter | solution.py:314
  (260 shorter events, 242.2 us)
Async XLA Ops:
  7.2 20.5 copy-start
  7.2 6.5 copy-start.44
  7.2 49.6 %all-reduce.8.cloned.1.call-start = ((), (), s32[]{:S(2)}) async-start(), calls=%async_computation.12 | async-start | bytes 6291456 | tf_op jit(solution)/shard_map/psum | solution.py:195
  10.4 10.2 copy-start.7
  49.3 12.0 copy-start.46
  60.3 35.5 %copy-start.54 = (f32[512]{0:T(512)}, f32[512]{0:T(512)S(1)}, u32[]{:S(2)}) copy-start(f32[512]{0:T(512)S(1)} %get-tuple-element.140) | copy-start | bytes 6148
  344.5 7.2 copy-start.33
  344.5 177.2 %all-to-all-start.1 = ((bf16[1,10,4,128,1536]{4,3,1,0,2:T(8,128)(2,1)}), bf16[1,10,4,128,1536]{4,3,1,0,2:T(8,128)(2,1)}, u32[]{:S(2)}, u32[]{:S(2)}) async-start(bf16[1,10,4,128,1536]{4,3,1,0,2:T(8,128)(2,1)} %copy.118), calls=%async_computation.1 | async-start | bytes 31457280 | tf_op jit(solution)/shard_map/all_to_all | solution.py:223
  351.4 280.8 %all-reduce.10.cloned.1.call-start = ((), (), s32[]{:S(2)}) async-start(), calls=%async_computation.13 | async-start | bytes 6291456 | tf_op jit(solution)/shard_map/psum | solution.py:233
  351.7 202.8 %copy-start.40 = (s32[4096]{0:T(1024)}, s32[4096]{0:T(1024)S(1)}, u32[]{:S(2)}) copy-start(s32[4096]{0:T(1024)S(1)} %broadcast_clamp_fusion) | copy-start | bytes 49156
  567.2 43.3 %copy-start.59 = (s32[1,512]{1,0:T(1,128)S(1)}, s32[1,512]{1,0:T(1,128)}, u32[]{:S(2)}) copy-start(s32[1,512]{1,0:T(1,128)} %param.19) | copy-start | bytes 6148
  567.2 648.0 %all-reduce.12.cloned.1.call-start = ((), (), s32[]{:S(2)}) async-start(), calls=%async_computation.14 | async-start | bytes 6291456 | tf_op jit(solution)/shard_map/psum | solution.py:273
  920.2 166.0 %copy-start.41 = (s32[4096]{0:T(1024)S(1)}, s32[4096]{0:T(1024)}, u32[]{:S(2)}) copy-start(s32[4096]{0:T(1024)} %copy-done.40) | copy-start | bytes 49156
  1131.7 14.5 copy-start.32
  1131.8 14.5 copy-start.49
  1131.8 14.5 copy-start.53
  1131.8 14.6 copy-start.36
  1131.8 149.0 %reduce-scatter.25.cloned.1.call-start = ((), (), s32[]{:S(2)}) async-start(), calls=%async_computation.22 | async-start | bytes 835584
  1149.6 268.8 %reduce-scatter.27.cloned.1.call-start = ((), (), s32[]{:S(2)}) async-start(), calls=%async_computation.23 | async-start | bytes 9830400
  1192.2 365.2 %reduce-scatter.23.cloned.1.call-start = ((), (), s32[]{:S(2)}) async-start(), calls=%async_computation.21 | async-start | bytes 9830400 | tf_op jit(solution)/shard_map/reduce_scatter | solution.py:326
  1203.5 493.1 %reduce-scatter.21.cloned.1.call-start = ((), (), s32[]{:S(2)}) async-start(), calls=%async_computation.20 | async-start | bytes 9830400 | tf_op jit(solution)/shard_map/reduce_scatter | solution.py:323
  1214.5 505.6 %all-reduce.14.cloned.1.call-start = ((), (), s32[]{:S(2)}) async-start(), calls=%async_computation.15 | async-start | bytes 3145728 | tf_op jit(solution)/shard_map/psum | solution.py:307
  1226.3 11.4 slice-start
  1226.3 11.4 slice-start.1
  1226.3 12.7 slice-start.2
  1239.1 7.0 copy-start.10
  1239.1 7.0 copy-start.12
  1258.8 592.3 %reduce-scatter.17.cloned.1.call-start = ((), (), s32[]{:S(2)}) async-start(), calls=%async_computation.18 | async-start | bytes 1671168 | tf_op jit(solution)/shard_map/reduce_scatter | solution.py:316
  1262.3 717.6 %reduce-scatter.15.cloned.1.call-start = ((), (), s32[]{:S(2)}) async-start(), calls=%async_computation.17 | async-start | bytes 1671168 | tf_op jit(solution)/shard_map/reduce_scatter | solution.py:315
  1265.8 856.1 %reduce-scatter.19.cloned.1.call-start = ((), (), s32[]{:S(2)}) async-start(), calls=%async_computation.19 | async-start | bytes 5013504 | tf_op jit(solution)/shard_map/reduce_scatter | solution.py:317
  1271.5 992.9 %reduce-scatter.13.cloned.1.call-start = ((), (), s32[]{:S(2)}) async-start(), calls=%async_computation.16 | async-start | bytes 5013504 | tf_op jit(solution)/shard_map/reduce_scatter | solution.py:314
  1561.3 240.3 %copy-start.57 = (f32[512]{0:T(512)S(1)}, f32[512]{0:T(512)}, u32[]{:S(2)}) copy-start(f32[512]{0:T(512)} %get-tuple-element.137) | copy-start | bytes 6148
  (47 other events, 127.2 us)
Sparse Core Ops, SparseCore 0:
  30.9 25.9 all-reduce.7
  567.3 23.1 all-reduce.9
  1131.9 19.9 all-reduce.11
  1157.1 123.6 reduce-scatter.24
  1283.0 135.3 reduce-scatter.26
  1420.7 136.7 reduce-scatter.22
  1559.8 136.7 reduce-scatter.20
  1699.1 20.8 all-reduce.13
  1725.4 125.6 reduce-scatter.16
  1856.3 123.4 reduce-scatter.14
  1985.6 136.2 reduce-scatter.18
  2128.3 136.0 reduce-scatter.12
where the time goes:
time: 2280 us; the launch traced here: 2270 us
  waiting for transfers between devices  1050 us (46%)
  blocking collectives  630 us (28%)
  local copies, waits for them, and re-layouts  265 us (12%)
  matrix products  199 us (9%)
  other arithmetic  103 us (5%)
    all_to_all x1, blocking collectives, on_device(): lax.all_to_all(send_rows, 'expert', split_axis=0, concat_axis=2, tiled=True)  176 us
    all_to_all x1, waiting for transfers between devices, on_device(): lax.all_to_all(expert_out.reshape(1, experts_local, owners, capacity, mod...  167 us
    all_to_all x1, blocking collectives, on_device(): lax.all_to_all(grad_send, 'expert', split_axis=0, concat_axis=2, tiled=True)  166 us
    all_to_all x1, blocking collectives, on_device(): lax.all_to_all(grad_expert_rows.reshape(1, experts_local, owners, capacit...  166 us
    reduce_scatter x1, waiting for transfers between devices, on_device(): lax.psum_scatter(grad_query_local, ('dp', 'expert'), scatter_dimension=0,...  143 us
    reduce_scatter x1, waiting for transfers between devices, on_device(): lax.psum_scatter(grad_out_local, ('dp', 'expert'), scatter_dimension=1, t...  142 us
    unnamed x14, waiting for transfers between devices  137 us
    reduce_scatter x1, waiting for transfers between devices, on_device(): lax.psum_scatter(grad_gate_local.astype(jnp.bfloat16), 'dp', scatter_dime...  135 us
  transfers between devices with their start and end apart: 13, of which 11 were waited for; matrix products, arithmetic and copies ran while one was open for 9% of the time, Pallas kernels for 0%

commit v1 on v0

v1 whole, which is shorter than its diff:
```python
import functools

import jax
import jax.numpy as jnp
from jax import lax
from jax.experimental import pallas as pl
from jax.experimental.pallas import tpu as pltpu
from jax.sharding import PartitionSpec as P

HEAD_DIMENSION = 64
SEQUENCE_LENGTH = 512
ABLK = 256


EPS = 1e-06
THETA = 10000.0
VMEM_LIMIT = 60 * 1024 * 1024
bfloat = jnp.bfloat16
single = jnp.float32


def swap(value):
    return lax.ppermute(value, "tensor", [(0, 1), (1, 0)])


def to_peer(value, axis, step):
    return lax.ppermute(value, axis, [(i, i ^ step) for i in range(lax.axis_size(axis))])


def to_mirror(value):
    count = lax.axis_size("dp")
    return lax.ppermute(value, "dp", [(i, count - 1 - i) for i in range(count)])


def gather_groups(value):
    return [value] + [to_peer(value, "expert", s) for s in range(1, lax.axis_size("expert"))]


def sum_all(value, axes):
    for axis in axes:
        step = 1
        while step < lax.axis_size(axis):
            value = value + to_peer(value, axis, step)
            step *= 2
    return value


def scatter_dense(packed):
    count_dp, count_ex = lax.axis_size("dp"), lax.axis_size("expert")
    at_dp, at_ex = lax.axis_index("dp"), lax.axis_index("expert")
    rows, columns = packed.shape
    block = rows // (count_dp * count_ex)
    cut = packed.reshape(count_dp, count_ex, block, columns)

    def part(step):
        return lax.dynamic_index_in_dim(cut, at_ex ^ step, 1, keepdims=False)

    total = part(0).astype(single)
    for step in range(1, count_ex):
        total = total + to_peer(part(step).astype(bfloat), "expert", step).astype(single)

    def row(step):
        return lax.dynamic_index_in_dim(total, at_dp ^ step, 0, keepdims=False)

    result = row(0)
    for step in range(1, count_dp):
        result = result + to_peer(row(step).astype(bfloat), "dp", step).astype(single)
    return result


def dot(left, right):
    return lax.dot_general(left, right, (((1,), (0,)), ((), ())), preferred_element_type=single)


def dot_nt(left, right):
    return lax.dot_general(left, right, (((1,), (1,)), ((), ())), preferred_element_type=single)


def dot_tn(left, right):
    return lax.dot_general(left, right, (((0,), (0,)), ((), ())), preferred_element_type=single)


def picks(slots_ref, group, capacity):
    slot = slots_ref[0, group : group + 1, :]
    return slot == lax.broadcasted_iota(jnp.int32, (capacity, slot.shape[1]), 0)


def gather_rows(picked, mine, other, to_ref, group, capacity):
    span = mine.shape[0]
    low = picked.astype(bfloat)
    rows = dot(low[:, :span], mine[...]) + dot(low[:, span:], other[...])
    to_ref[group * capacity : (group + 1) * capacity, :] = rows.astype(bfloat)


def slot_gates(picked, gates_ref, group):
    return jnp.sum(jnp.where(picked, gates_ref[0, group : group + 1, :], 0.0), axis=1, keepdims=True)


def add_back(step, picked, rows, acc_mine, acc_other, group):
    back = dot_tn(picked.astype(bfloat), rows)
    span = acc_mine.shape[1]

    @pl.when(step == 0)
    def _():
        acc_mine[group] = back[:span]
        acc_other[group] = back[span:]

    @pl.when(step > 0)
    def _():
        acc_mine[group] += back[:span]
        acc_other[group] += back[span:]


def half_columns(half_ref, width):
    return pl.ds(pl.multiple_of(half_ref[0] * width, 128), width)


def forward_kernel(groups, with_out, half_ref, slots_ref, gates_ref, gate_w, up_w, *refs):
    step = pl.program_id(0)
    if with_out:
        down_w, refs = refs[0], refs[1:]
    x_refs, refs = refs[: 2 * groups], refs[2 * groups :]
    if with_out:
        half_rows, gate_ref, up_ref, out_mine, out_other, rows_ref, acc_mine, acc_other = refs
    else:
        half_rows, gate_ref, up_ref, rows_ref = refs
    capacity = rows_ref.shape[0] // groups
    picked = [picks(slots_ref, g, capacity) for g in range(groups)]
    for g in range(groups):
        gather_rows(picked[g], x_refs[2 * g], x_refs[2 * g + 1], rows_ref, g, capacity)
    rows = rows_ref[...]
    half_rows[0] = rows_ref[:, half_columns(half_ref, half_rows.shape[2])]
    gate_pre = dot(rows, gate_w[0])
    up_pre = dot(rows, up_w[0])
    gate_ref[0] = gate_pre
    up_ref[0] = up_pre
    if not with_out:
        return
    gates = jnp.concatenate([slot_gates(picked[g], gates_ref, g) for g in range(groups)], axis=0)
    hidden = (gate_pre * jax.nn.sigmoid(gate_pre) * up_pre * gates).astype(bfloat)
    out = dot(hidden, down_w[0]).astype(bfloat)
    for g in range(groups):
        add_back(step, picked[g], out[g * capacity : (g + 1) * capacity], acc_mine, acc_other, g)

    @pl.when(step == pl.num_programs(0) - 1)
    def _():
        out_mine[...] = acc_mine[...].astype(out_mine.dtype)
        out_other[...] = acc_other[...].astype(out_other.dtype)


def hidden_grads(gate_pre, up_pre, gates, grad_hidden):
    sig = jax.nn.sigmoid(gate_pre)
    silu = gate_pre * sig
    hidden = silu * up_pre
    grad_gates = jnp.sum(hidden * grad_hidden, axis=1, keepdims=True)
    scaled = grad_hidden * gates
    grad_gate_pre = (scaled * up_pre * sig * (1.0 + gate_pre * (1.0 - sig))).astype(bfloat)
    grad_up_pre = (scaled * silu).astype(bfloat)
    return (hidden * gates).astype(bfloat), grad_gate_pre, grad_up_pre, grad_gates


def backward_kernel(groups, half_ref, slots_ref, gates_ref, gate_w, up_w, down_w, *refs):
    step = pl.program_id(0)
    g_refs, refs = refs[: 2 * groups], refs[2 * groups :]
    gate_ref, up_ref = refs[:2]
    half_grad, hidden_ref, grad_gate_ref, grad_up_ref, gg_ref, out_mine, out_other = refs[2:9]
    rows_ref, acc_mine, acc_other = refs[9:]
    capacity = rows_ref.shape[0] // groups
    picked = [picks(slots_ref, g, capacity) for g in range(groups)]
    for g in range(groups):
        gather_rows(picked[g], g_refs[2 * g], g_refs[2 * g + 1], rows_ref, g, capacity)
    half_grad[0] = rows_ref[:, half_columns(half_ref, half_grad.shape[2])]
    gates = jnp.concatenate([slot_gates(picked[g], gates_ref, g) for g in range(groups)], axis=0)
    grad_hidden = dot_nt(rows_ref[...], down_w[0])
    hidden, grad_gate_pre, grad_up_pre, grad_gates = hidden_grads(
        gate_ref[0], up_ref[0], gates, grad_hidden
    )
    hidden_ref[0] = hidden
    grad_gate_ref[0] = grad_gate_pre
    grad_up_ref[0] = grad_up_pre
    for g in range(groups):
        own = grad_gates[g * capacity : (g + 1) * capacity]
        gg_ref[0, g : g + 1, :] = jnp.sum(jnp.where(picked[g], own, 0.0), axis=0, keepdims=True)
    back = (dot_nt(grad_gate_pre, gate_w[0]) + dot_nt(grad_up_pre, up_w[0])).astype(bfloat)
    for g in range(groups):
        add_back(step, picked[g], back[g * capacity : (g + 1) * capacity], acc_mine, acc_other, g)

    @pl.when(step == pl.num_programs(0) - 1)
    def _():
        out_mine[...] = acc_mine[...].astype(out_mine.dtype)
        out_other[...] = acc_other[...].astype(out_other.dtype)


def weights_kernel(groups, half_ref, slots_ref, gates_ref, down_w, *refs):
    g_refs, refs = refs[: 2 * groups], refs[2 * groups :]
    gate_ref, up_ref, rows_far, rows_near, grad_near, hidden_near, gate_near, up_near = refs[:8]
    d_gate, d_up, d_down, rows_ref = refs[8:]
    capacity = rows_ref.shape[0] // groups
    picked = [picks(slots_ref, g, capacity) for g in range(groups)]
    for g in range(groups):
        gather_rows(picked[g], g_refs[2 * g], g_refs[2 * g + 1], rows_ref, g, capacity)
    gates = jnp.concatenate([slot_gates(picked[g], gates_ref, g) for g in range(groups)], axis=0)
    grad_hidden = dot_nt(rows_ref[...], down_w[0])
    hidden, grad_gate_pre, grad_up_pre, _ = hidden_grads(gate_ref[0], up_ref[0], gates, grad_hidden)
    grad_far = rows_ref[:, half_columns(half_ref, d_gate.shape[1])]
    d_down[0] = (dot_tn(hidden, grad_far) + dot_tn(hidden_near[0], grad_near[0])).astype(bfloat)
    far, near = rows_far[0], rows_near[0]
    d_gate[0] = (dot_tn(far, grad_gate_pre) + dot_tn(near, gate_near[0])).astype(bfloat)
    d_up[0] = (dot_tn(far, grad_up_pre) + dot_tn(near, up_near[0])).astype(bfloat)


def per_expert(*shape):
    return pl.BlockSpec((1,) + shape, lambda e, half: (e,) + (0,) * len(shape))


def resident(*shape):
    return pl.BlockSpec(shape, lambda e, half: (0,) * len(shape))


def expert_call(kernel, name, experts, in_specs, out_specs, out_shape, scratch, flops, moved, args):
    return pl.pallas_call(
        kernel,
        name=name,
        grid_spec=pltpu.PrefetchScalarGridSpec(
            num_scalar_prefetch=1,
            grid=(experts,),
            in_specs=in_specs,
            out_specs=out_specs,
            scratch_shapes=scratch,
        ),
        out_shape=out_shape,
        compiler_params=pltpu.CompilerParams(
            dimension_semantics=("arbitrary",), vmem_limit_bytes=VMEM_LIMIT
        ),
        cost_estimate=pl.CostEstimate(flops=flops, bytes_accessed=moved, transcendentals=0),
    )(*args)


def expert_forward(half, slots, gates, weights, x_parts, capacity):
    experts, groups, tokens = slots.shape
    span, width = x_parts[0].shape
    with_out = len(weights) == 3
    rows = groups * capacity
    hidden = weights[0].shape[2]
    specs = [per_expert(groups, tokens)] * 2 + [per_expert(width, hidden)] * 2
    outs = [per_expert(rows, width // 2), per_expert(rows, hidden), per_expert(rows, hidden)]
    shapes = [
        jax.ShapeDtypeStruct((experts, rows, width // 2), bfloat),
        jax.ShapeDtypeStruct((experts, rows, hidden), single),
        jax.ShapeDtypeStruct((experts, rows, hidden), single),
    ]
    scratch = [pltpu.VMEM((rows, width), bfloat)]
    if with_out:
        specs += [per_expert(hidden, width)]
        outs += [resident(groups, span, width)] * 2
        shapes += [jax.ShapeDtypeStruct((groups, span, width), bfloat)] * 2
        scratch += [pltpu.VMEM((groups, span, width), single)] * 2
    specs += [resident(span, width)] * (2 * groups)
    once = 2 * experts * rows * width
    flops = once * (tokens + 2 * hidden) + (once * (tokens + hidden) if with_out else 0)
    moved = 2 * experts * (len(weights) * width * hidden + rows * width // 2 + 4 * rows * hidden)
    return expert_call(
        functools.partial(forward_kernel, groups, with_out),
        "expert_forward" if with_out else "expert_forward_far",
        experts, specs, outs, shapes, scratch, flops, moved,
        (half, slots, gates) + tuple(weights) + tuple(x_parts),
    )


def expert_backward(half, slots, gates, weights, g_parts, gate_pre, up_pre, capacity):
    experts, groups, tokens = slots.shape
    span, width = g_parts[0].shape
    rows = groups * capacity
    hidden = weights[0].shape[2]
    specs = [per_expert(groups, tokens)] * 2 + [per_expert(width, hidden)] * 2
    specs += [per_expert(hidden, width)] + [resident(span, width)] * (2 * groups)
    specs += [per_expert(rows, hidden)] * 2
    outs = [per_expert(rows, width // 2)] + [per_expert(rows, hidden)] * 3
    outs += [per_expert(groups, tokens)] + [resident(groups, span, width)] * 2
    shapes = [jax.ShapeDtypeStruct((experts, rows, width // 2), bfloat)]
    shapes += [jax.ShapeDtypeStruct((experts, rows, hidden), bfloat)] * 3
    shapes += [jax.ShapeDtypeStruct((experts, groups, tokens), single)]
    shapes += [jax.ShapeDtypeStruct((groups, span, width), bfloat)] * 2
    scratch = [pltpu.VMEM((rows, width), bfloat)]
    scratch += [pltpu.VMEM((groups, span, width), single)] * 2
    flops = 2 * experts * rows * width * (2 * tokens + 3 * hidden)
    moved = 2 * experts * (3 * width * hidden + rows * width // 2 + 7 * rows * hidden)
    return expert_call(
        functools.partial(backward_kernel, groups),
        "expert_backward",
        experts, specs, outs, shapes, scratch, flops, moved,
        (half, slots, gates) + tuple(weights) + tuple(g_parts) + (gate_pre, up_pre),
    )


def expert_weights(half, slots, gates, down_w, g_parts, far, near, capacity):
    experts, groups, tokens = slots.shape
    span, width = g_parts[0].shape
    rows = groups * capacity
    hidden = down_w.shape[1]
    wide, thin = per_expert(rows, width // 2), per_expert(rows, hidden)
    specs = [per_expert(groups, tokens)] * 2 + [per_expert(hidden, width)]
    specs += [resident(span, width)] * (2 * groups)
    specs += [thin, thin, wide, wide, wide, thin, thin, thin]
    outs = [per_expert(width // 2, hidden)] * 2 + [per_expert(hidden, width // 2)]
    shapes = [jax.ShapeDtypeStruct((experts, width // 2, hidden), bfloat)] * 2
    shapes += [jax.ShapeDtypeStruct((experts, hidden, width // 2), bfloat)]
    scratch = [pltpu.VMEM((rows, width), bfloat)]
    flops = 2 * experts * rows * width * (tokens + 4 * hidden)
    moved = 2 * experts * (3 * width * hidden + 3 * rows * width // 2 + 7 * rows * hidden)
    return expert_call(
        functools.partial(weights_kernel, groups),
        "expert_weights",
        experts, specs, outs, shapes, scratch, flops, moved,
        (half, slots, gates, down_w) + tuple(g_parts) + tuple(far) + tuple(near),
    )


def rope_tables(length, head_size):
    half_size = head_size // 2
    frequency = THETA ** (-jnp.arange(half_size, dtype=jnp.float32) * 2.0 / head_size)
    angles = jnp.arange(length, dtype=jnp.float32)[:, None] * frequency[None, :]
    return (jnp.cos(angles), jnp.sin(angles))


def apply_rotary(value_matrix, cosine_table, sine_table):
    half_size = value_matrix.shape[-1] // 2
    first_half = value_matrix[..., :half_size]
    second_half = value_matrix[..., half_size:]
    cosine_rows = cosine_table[:, None, :]
    sine_rows = sine_table[:, None, :]
    return jnp.concatenate(
        [
            first_half * cosine_rows - second_half * sine_rows,
            second_half * cosine_rows + first_half * sine_rows,
        ],
        axis=-1,
    )


def rotate_back(grads, cosine_table, sine_table):
    half_size = grads.shape[-1] // 2
    first_half = grads[..., :half_size]
    second_half = grads[..., half_size:]
    cosine_rows = cosine_table[:, None, :]
    sine_rows = sine_table[:, None, :]
    return jnp.concatenate(
        [
            first_half * cosine_rows + second_half * sine_rows,
            second_half * cosine_rows - first_half * sine_rows,
        ],
        axis=-1,
    )


def rms_forward(value_matrix, gain):
    inverse = lax.rsqrt(jnp.mean(value_matrix * value_matrix, axis=-1, keepdims=True) + EPS)
    return (value_matrix * inverse * gain, inverse)


def rms_backward(value_matrix, inverse, gain, grad_normed):
    scaled = grad_normed * gain
    grad_gain = jnp.sum(grad_normed * value_matrix * inverse, axis=0)
    grad_values = inverse * scaled - value_matrix * inverse**3 * jnp.mean(
        scaled * value_matrix, axis=-1, keepdims=True
    )
    return (grad_values, grad_gain)


def masked_scores(query_part, key_matrix, row_begin, length):
    scores = jnp.einsum(
        "qkge,tke->kgqt", query_part, key_matrix, preferred_element_type=jnp.float32
    )
    query_block = (row_begin + jnp.arange(query_part.shape[0], dtype=jnp.int32)) // ABLK
    key_block = jnp.arange(length, dtype=jnp.int32) // ABLK
    allowed = query_block[:, None] >= key_block[None, :]
    return jnp.where(allowed, scores, -1e30)


def attend_forward(args):
    queries, key_matrix, value_matrix = args
    length, kv_heads, head_size = key_matrix.shape
    group_size = queries.shape[1] // kv_heads
    rows_block = min(512, length)
    grouped = queries.reshape(length, kv_heads, group_size, head_size)

    def one_block(row_begin):
        scores = masked_scores(grouped, key_matrix, row_begin, length)
        row_peak = jnp.max(scores, axis=-1, keepdims=True)
        weights = jnp.exp(scores - row_peak)
        totals = jnp.sum(weights, axis=-1, keepdims=True)
        weights_low = (weights / totals).astype(jnp.bfloat16)
        outputs = jnp.einsum(
            "kgqt,tke->qkge", weights_low, value_matrix, preferred_element_type=jnp.float32
        )
        return (
            outputs.reshape(rows_block, kv_heads * group_size * head_size),
            (row_peak + jnp.log(totals))[..., 0],
        )

    outputs, log_sums = lax.map(one_block, jnp.arange(0, length, rows_block, dtype=jnp.int32))
    return (outputs.reshape(length, kv_heads * group_size * head_size), log_sums)


def attend_backward(args):
    queries, key_matrix, value_matrix, log_sums, grad_mixed = args
    length, kv_heads, head_size = key_matrix.shape
    group_size = queries.shape[1] // kv_heads
    rows_block = min(512, length)
    grouped = queries.reshape(length, kv_heads, group_size, head_size)
    grad_grouped = grad_mixed.reshape(length, kv_heads, group_size, head_size)

    def one_block(running, inputs):
        row_begin, block_sums = inputs
        scores = masked_scores(grouped, key_matrix, row_begin, length)
        probs = jnp.exp(scores - block_sums[..., None])
        grad_probs = jnp.einsum(
            "qkge,tke->kgqt", grad_grouped, value_matrix, preferred_element_type=jnp.float32
        )
        row_inner = jnp.sum(probs * grad_probs, axis=-1, keepdims=True)
        grad_scores = (probs * (grad_probs - row_inner)).astype(jnp.bfloat16)
        grad_query = jnp.einsum(
            "kgqt,tke->qkge", grad_scores, key_matrix, preferred_element_type=jnp.float32
        )
        grad_key = running[0] + jnp.einsum(
            "kgqt,qkge->tke", grad_scores, grouped, preferred_element_type=jnp.float32
        )
        grad_value = running[1] + jnp.einsum(
            "kgqt,qkge->tke",
            probs.astype(jnp.bfloat16),
            grad_grouped,
            preferred_element_type=jnp.float32,
        )
        return (
            (grad_key, grad_value),
            grad_query.reshape(rows_block, kv_heads * group_size, head_size),
        )

    zero_keys = jnp.zeros(key_matrix.shape, jnp.float32)
    starts = jnp.arange(0, length, rows_block, dtype=jnp.int32)
    (grad_key, grad_value), grad_query = lax.scan(
        one_block, (zero_keys, zero_keys), (starts, log_sums)
    )
    return (grad_query.reshape(length, kv_heads * group_size, head_size), grad_key, grad_value)


def assemble(mine, other):
    first = lax.axis_index("tensor") == 0
    return jnp.concatenate([jnp.where(first, mine, other), jnp.where(first, other, mine)], axis=0)


def both_halves(mine_groups):
    parts = []
    for mine in mine_groups:
        parts += [mine, swap(mine)]
    return parts


def combine_groups(mine, other):
    total = None
    for group in range(mine.shape[0]):
        part = mine[group].astype(single) + swap(other[group]).astype(single)
        if group:
            part = to_peer(part.astype(bfloat), "expert", group).astype(single)
        total = part if total is None else total + part
    return total


def on_device(
    tokens,
    teacher,
    routes,
    valid,
    teacher_rows,
    norm_attn,
    norm_moe,
    w_query,
    key_projection_weight,
    value_projection_weight,
    w_out,
    w_router,
    w_gate,
    w_up,
    w_down,
):
    rows_dev, model_width = tokens.shape
    seq_count = rows_dev // SEQUENCE_LENGTH
    heads_local = w_query.shape[1] // HEAD_DIMENSION
    kv_local = key_projection_weight.shape[1] // HEAD_DIMENSION
    query_width = w_query.shape[1]
    key_width = key_projection_weight.shape[1]
    experts_local = w_gate.shape[0]
    owners = lax.axis_size("expert")
    count_dp = lax.axis_size("dp")
    groups = count_dp * owners
    all_experts = experts_local * owners
    top_count = routes.shape[1]
    capacity = rows_dev * top_count * 5 // (4 * all_experts)
    at_dp, at_ex, core = lax.axis_index("dp"), lax.axis_index("expert"), lax.axis_index("tensor")
    span = rows_dev // 2
    shards = count_dp // 2
    half = (at_dp // shards).astype(jnp.int32).reshape(1)

    def mine_of(value, axis=0):
        return lax.dynamic_slice_in_dim(value, core * span, span, axis)

    def other_of(value, axis=0):
        return lax.dynamic_slice_in_dim(value, (1 - core) * span, span, axis)

    routes_t = routes.T
    routes_t = jnp.concatenate([mine_of(routes_t, 1), other_of(routes_t, 1)], axis=1)
    routes_two = jnp.stack([routes_t, to_mirror(routes_t)])
    all_routes = jnp.stack(gather_groups(routes_two), axis=1)
    expert_ids = jnp.arange(all_experts, dtype=jnp.int32)
    local_ids = at_ex * experts_local + jnp.arange(experts_local, dtype=jnp.int32)
    local_mask = jnp.any(all_routes[:, :, None] == local_ids[:, None, None], axis=3)
    earlier = jnp.triu(jnp.ones((rows_dev, rows_dev), bfloat), 1)
    before = jnp.dot(local_mask.astype(bfloat), earlier, preferred_element_type=single)
    slots = jnp.where(local_mask, before.astype(jnp.int32), -1).transpose(0, 2, 1, 3)
    mine_mask = jnp.any(routes_t[None, :, :span] == expert_ids[:, None, None], axis=1)

    valid_rows = valid.astype(single)
    valid_count = sum_all(jnp.full((8, 128), jnp.sum(valid_rows)), ("dp", "expert"))[0, 0]
    loss_scale = rows_dev * groups / valid_count
    inputs = tokens.astype(single)
    normed_first, inverse_first = rms_forward(inputs, norm_attn)
    attention_input = normed_first.astype(bfloat)
    cosine_table, sine_table = rope_tables(SEQUENCE_LENGTH, HEAD_DIMENSION)
    factor = HEAD_DIMENSION ** (-0.5)
    query_raw = jnp.dot(attention_input, w_query, preferred_element_type=single).reshape(
        seq_count, SEQUENCE_LENGTH, heads_local, HEAD_DIMENSION
    )
    key_unrotated = jnp.dot(
        attention_input, key_projection_weight, preferred_element_type=single
    ).reshape(seq_count, SEQUENCE_LENGTH, kv_local, HEAD_DIMENSION)
    value_unprojected = jnp.dot(
        attention_input, value_projection_weight, preferred_element_type=single
    ).reshape(seq_count, SEQUENCE_LENGTH, kv_local, HEAD_DIMENSION)
    queries = (apply_rotary(query_raw, cosine_table, sine_table) * factor).astype(bfloat)
    key_matrix = apply_rotary(key_unrotated, cosine_table, sine_table).astype(bfloat)
    value_matrix = value_unprojected.astype(bfloat)
    outputs, log_sums = lax.map(attend_forward, (queries, key_matrix, value_matrix))
    attn_low = outputs.reshape(rows_dev, heads_local * HEAD_DIMENSION).astype(bfloat)
    attn_part = jnp.dot(attn_low, w_out, preferred_element_type=single)

    hidden_first = mine_of(inputs) + mine_of(attn_part) + swap(other_of(attn_part))
    normed_second, inverse_second = rms_forward(hidden_first, norm_moe)
    moe_in = normed_second.astype(bfloat)
    logits = lax.dot_general(
        w_router, moe_in, (((0,), (1,)), ((), ())), preferred_element_type=single
    )
    peak = jnp.max(jnp.where(mine_mask, logits, -jnp.inf), axis=0, keepdims=True)
    exponent = jnp.where(mine_mask, jnp.exp(logits - peak), 0.0)
    gates = exponent / jnp.sum(exponent, axis=0, keepdims=True)

    def local_gates(gates_mine):
        stacked = jnp.stack(gather_groups(gates_mine))
        local = lax.dynamic_slice_in_dim(stacked, at_ex * experts_local, experts_local, 1)
        return jnp.concatenate([local, swap(local)], axis=2).transpose(1, 0, 2)

    near_gates = local_gates(gates)
    near_x = both_halves(gather_groups(moe_in))
    near_rows, gate_pre, up_pre, part_mine, part_other = expert_forward(
        half, slots[0], near_gates, (w_gate, w_up, w_down), near_x, capacity
    )
    far_gates = local_gates(to_mirror(gates))
    far_x = both_halves(gather_groups(to_mirror(moe_in)))
    far_rows, far_gate_pre, far_up_pre = expert_forward(
        half, slots[1], far_gates, (w_gate, w_up), far_x, capacity
    )

    layer_out = hidden_first + combine_groups(part_mine, part_other)
    rows_wanted = mine_of(teacher_rows[0])
    chooser = (rows_wanted[:, None] == jnp.arange(rows_dev, dtype=jnp.int32)).astype(bfloat)
    target = jnp.dot(chooser, teacher, preferred_element_type=single)
    grad_layer = loss_scale * mine_of(valid_rows)[:, None] * (layer_out - target)
    layer_low = layer_out.astype(bfloat)
    block_out = assemble(layer_low, swap(layer_low))

    grad_low = grad_layer.astype(bfloat)
    near_g = both_halves(gather_groups(grad_low))
    near_grad, hidden_low, grad_gate_pre, grad_up_pre, grad_gates, part_mine, part_other = (
        expert_backward(
            half, slots[0], near_gates, (w_gate, w_up, w_down), near_g, gate_pre, up_pre, capacity
        )
    )
    far_g = both_halves(gather_groups(to_mirror(grad_low)))
    d_gate, d_up, d_down = expert_weights(
        half,
        slots[1],
        far_gates,
        w_down,
        far_g,
        (far_gate_pre, far_up_pre, far_rows),
        (near_rows, near_grad, hidden_low, grad_gate_pre, grad_up_pre),
        capacity,
    )

    grad_gates = grad_gates.transpose(1, 0, 2)
    gate_parts = grad_gates[:, :, :span] + swap(grad_gates[:, :, span:])
    owner_ids = jnp.arange(owners, dtype=jnp.int32)[:, None, None]
    grad_gates = jnp.zeros((owners, experts_local, span), single)
    for step in range(owners):
        part = gate_parts[step]
        if step:
            part = to_peer(part, "expert", step)
        grad_gates = grad_gates + jnp.where(owner_ids == (at_ex ^ step), part[None], 0.0)
    grad_gates = grad_gates.reshape(all_experts, span)
    inner = jnp.sum(gates * grad_gates, axis=0, keepdims=True)
    grad_logits = (gates * (grad_gates - inner)).astype(bfloat)

    grad_moe_in = combine_groups(part_mine, part_other) + lax.dot_general(
        grad_logits, w_router, (((0,), (1,)), ((), ())), preferred_element_type=single
    )
    grad_router_part = lax.dot_general(
        moe_in, grad_logits, (((0,), (1,)), ((), ())), preferred_element_type=single
    )
    grad_second, grad_norm_moe_part = rms_backward(
        hidden_first, inverse_second, norm_moe, grad_moe_in
    )
    grad_hidden_mine = grad_layer + grad_second
    grad_attn_mine = grad_hidden_mine.astype(bfloat)
    grad_attn = assemble(grad_attn_mine, swap(grad_attn_mine))
    grad_hidden_first = assemble(grad_hidden_mine, swap(grad_hidden_mine))
    small = jnp.concatenate([grad_router_part, grad_norm_moe_part[:, None]], axis=1)
    small = small + swap(small)
    grad_out_t = lax.dot_general(
        grad_attn, attn_low, (((0,), (0,)), ((), ())), preferred_element_type=single
    )
    filler = jnp.zeros((model_width, 128 - small.shape[1]), single)
    first_pack = scatter_dense(
        jnp.concatenate([grad_out_t, small, filler], axis=1).astype(bfloat)
    )

    grad_mixed = jnp.dot(grad_attn, w_out.T, preferred_element_type=single).astype(bfloat)
    grad_mixed = grad_mixed.reshape(seq_count, SEQUENCE_LENGTH, heads_local * HEAD_DIMENSION)
    grad_queries, grad_keys, grad_values = lax.map(
        attend_backward, (queries, key_matrix, value_matrix, log_sums, grad_mixed)
    )
    grad_query_raw = (
        rotate_back(grad_queries * factor, cosine_table, sine_table)
        .astype(bfloat)
        .reshape(rows_dev, heads_local * HEAD_DIMENSION)
    )
    grad_key_raw = (
        rotate_back(grad_keys, cosine_table, sine_table)
        .astype(bfloat)
        .reshape(rows_dev, kv_local * HEAD_DIMENSION)
    )
    grad_value_raw = grad_values.astype(bfloat).reshape(rows_dev, kv_local * HEAD_DIMENSION)
    grad_attn_in = (
        jnp.dot(grad_query_raw, w_query.T, preferred_element_type=single)
        + jnp.dot(grad_key_raw, key_projection_weight.T, preferred_element_type=single)
        + jnp.dot(grad_value_raw, value_projection_weight.T, preferred_element_type=single)
    ).astype(bfloat)
    grad_raw = jnp.concatenate([grad_query_raw, grad_key_raw, grad_value_raw], axis=1)
    grad_qkv = jnp.dot(attention_input.T, grad_raw, preferred_element_type=single)
    grad_attn_in = grad_attn_in.astype(single) + swap(grad_attn_in).astype(single)
    grad_first, grad_norm_attn_part = rms_backward(inputs, inverse_first, norm_attn, grad_attn_in)
    grad_tokens = grad_hidden_first + grad_first
    tail = jnp.concatenate(
        [grad_norm_attn_part[:, None], jnp.zeros((model_width, 127), single)], axis=1
    )
    second_pack = scatter_dense(jnp.concatenate([grad_qkv, tail], axis=1).astype(bfloat))

    at_shard = at_dp % shards

    def scatter_experts(value, axis):
        size = value.shape[axis] // shards
        total = None
        for step in range(shards):
            part = lax.dynamic_slice_in_dim(value, (at_shard ^ step) * size, size, axis)
            if step:
                part = to_peer(part, "dp", step)
            part = part.astype(single)
            total = part if total is None else total + part
        return total

    return (
        block_out,
        grad_tokens,
        second_pack[:, query_width + 2 * key_width],
        first_pack[:, query_width + all_experts],
        second_pack[:, :query_width],
        second_pack[:, query_width : query_width + key_width],
        second_pack[:, query_width + key_width : query_width + 2 * key_width],
        first_pack[:, :query_width].T,
        first_pack[:, query_width : query_width + all_experts],
        scatter_experts(d_gate, 1),
        scatter_experts(d_up, 1),
        scatter_experts(d_down, 2),
    )


def solution(mesh):
    placed = (
        P(("dp", "expert"), None),
        P(("dp", "expert"), None),
        P(("dp", "expert"), None),
        P(("dp", "expert")),
        P(("dp", "expert"), None),
        P(),
        P(),
        P(None, "tensor"),
        P(None, "tensor"),
        P(None, "tensor"),
        P("tensor", None),
        P(),
        P("expert", None, "tensor"),
        P("expert", None, "tensor"),
        P("expert", "tensor", None),
    )
    return jax.shard_map(
        on_device,
        mesh=mesh,
        in_specs=placed,
        out_specs=(
            P(("dp", "expert"), None),
            P(("dp", "expert"), None),
            P(("dp", "expert")),
            P(("dp", "expert")),
            P(("dp", "expert"), "tensor"),
            P(("dp", "expert"), "tensor"),
            P(("dp", "expert"), "tensor"),
            P("tensor", ("dp", "expert")),
            P(("dp", "expert"), None),
            P("expert", "dp", "tensor"),
            P("expert", "dp", "tensor"),
            P("expert", "tensor", "dp"),
        ),
        check_vma=False,
    )
```

time: 2280 us -> 725 us (0.32)
  waiting for transfers between devices: 1050 us -> 245 us
  blocking collectives: 630 us -> 0 us
  Pallas kernels: 0 us -> 199 us
  local copies, waits for them, and re-layouts: 265 us -> 70.5 us
  matrix products: 199 us -> 49.1 us
  starting transfers between devices: 8.28 us -> 76.1 us
  other arithmetic: 103 us -> 74.8 us
    reduce_scatter x6 -> x0, waiting for transfers between devices: 718 us -> none  [the longest x1 143 us: on_device(): lax.psum_scatter(grad_query_local, ('dp', 'expert'), scatter_dimension=0,...]
    all_to_all x3 -> x0, blocking collectives: 508 us -> none  [the longest x1 176 us: on_device(): lax.all_to_all(send_rows, 'expert', split_axis=0, concat_axis=2, tiled=True)]
    ppermute x0 -> x86, waiting for transfers between devices: none -> 245 us  [the longest x49 243 us: to_peer(): lax.ppermute(value, axis, [(i, i ^ step) for i in range(lax.axis_size(axi...]
    pallas_call x0 -> x4, Pallas kernels: none -> 199 us  [expert_call(): pl.pallas_call(kernel, name=name, grid_spec=pltpu.PrefetchScalarGridSpec(...]
    all_to_all x1 -> x0, waiting for transfers between devices: 167 us -> none  [on_device(): lax.all_to_all(expert_out.reshape(1, experts_local, owners, capacity, mod...]
    dot_general x15 -> x7, matrix products: 158 us -> 10.7 us  [the longest x1 2.87 us: on_device(): lax.dot_general(grad_attn, attn_low, (((0,), (0,)), ((), ())), preferred_...]
    gather x5 -> x0, local copies, waits for them, and re-layouts: 140 us -> none  [the longest x1 35.5 us: on_device(): grad_send = (gate_slot[:, None] * grad_layer[source]).astype(bfloat)]
    unnamed x14 -> x0, waiting for transfers between devices: 137 us -> none
  transfers between devices with their start and end apart: 13 -> 86, of which waited for: 11 -> 24; matrix products, arithmetic and copies ran while one was open for 9% -> 21% of each run, Pallas kernels for 0% -> 28%
where the time goes in v1:
time: 725 us; the launch traced here: 718 us
  waiting for transfers between devices  245 us (34%)
  Pallas kernels  199 us (27%)
  starting transfers between devices  76.1 us (10%)
  other arithmetic  74.8 us (10%)
  local copies, waits for them, and re-layouts  70.5 us (10%)
  matrix products  49.1 us (7%)
    ppermute x49, waiting for transfers between devices, to_peer(): lax.ppermute(value, axis, [(i, i ^ step) for i in range(lax.axis_size(axi...  243 us
    pallas_call x4, Pallas kernels, expert_call(): pl.pallas_call(kernel, name=name, grid_spec=pltpu.PrefetchScalarGridSpec(...  199 us
    ppermute x49, starting transfers between devices, to_peer(): lax.ppermute(value, axis, [(i, i ^ step) for i in range(lax.axis_size(axi...  57.3 us
    unnamed x179, local copies, waits for them, and re-layouts  15.5 us
  transfers between devices with their start and end apart: 86, of which 24 were waited for; matrix products, arithmetic and copies ran while one was open for 21% of the time, Pallas kernels for 28%

profile of v1, /device:TPU:0, one launch (start us, length us, event | category | flops | bytes accessed | tf_op | source)
XLA Modules:
  0.0 717.6 jit_solution(787382317471006516)
XLA Ops:
  30.0 4.7 collective-permute-start.1
  48.8 31.4 %collective-permute-done.4 = s32[2,8,512]{2,1,0:T(8,128)S(1)} collective-permute-done((s32[2,8,512]{2,1,0:T(8,128)S(1)}, s32[2,8,512]{2,1,0:T(8,128)S(1)}, u32[]{:S(2)}, u32[]{:S(2)}) %collective-permute-start.4) | collective-permute-done | bytes 32800 | tf_op jit(solution)/shard_map/ppermute | solution.py:27
  97.8 64.9 %expert_forward.1 = (bf16[10,512,768]{2,1,0:T(8,128)(2,1)}, f32[10,512,256]{2,1,0:T(8,128)}, f32[10,512,256]{2,1,0:T(8,128)}, bf16[4,256,1536]{2,1,0:T(8,128)(2,1)}, bf16[4,256,1536]{2,1,0:T(8,128)(2,1)}) custom-call(s32[1]{0:T(128)} %bitcast.14.half_ref, s32[10,4,512]{2,1,0:T(4,128)} %get-tuple-element.245.slots_ref, f32[10,4,512]{2,1,0:T(4,128)} %copy.79.gates_ref, ...), custom_call_target="tpu_custom_call" | custom-call | flops 28185722880 | bytes 41943040 | tf_op jit(solution)/shard_map/expert_forward/pallas_call | solution.py:221
  167.7 3.6 collective-permute-done.24
  184.4 3.7 collective-permute-start.62
  196.2 11.2 %collective-permute-done.63 = f32[40,256]{1,0:T(8,128)S(1)} collective-permute-done((f32[40,256]{1,0:T(8,128)S(1)}, f32[40,256]{1,0:T(8,128)S(1)}, u32[]{:S(2)}, u32[]{:S(2)}) %collective-permute-start.63) | collective-permute-done | bytes 40992 | tf_op jit(solution)/shard_map/ppermute | solution.py:27
  208.1 15.3 %collective-permute-done.64 = f32[40,256]{1,0:T(8,128)S(1)} collective-permute-done((f32[40,256]{1,0:T(8,128)S(1)}, f32[40,256]{1,0:T(8,128)S(1)}, u32[]{:S(2)}, u32[]{:S(2)}) %collective-permute-start.64) | collective-permute-done | bytes 40992 | tf_op jit(solution)/shard_map/ppermute | solution.py:27
  232.3 12.7 %collective-permute-done.22 = bf16[256,1536]{1,0:T(8,128)(2,1)} collective-permute-done((bf16[256,1536]{1,0:T(8,128)(2,1)}, bf16[256,1536]{1,0:T(8,128)(2,1)}, u32[]{:S(2)}, u32[]{:S(2)}) %collective-permute-start.22) | collective-permute-done | bytes 786464 | tf_op jit(solution)/shard_map/ppermute | solution.py:27
  245.1 16.4 %collective-permute-done.20 = bf16[256,1536]{1,0:T(8,128)(2,1)} collective-permute-done((bf16[256,1536]{1,0:T(8,128)(2,1)}, bf16[256,1536]{1,0:T(8,128)(2,1)}, u32[]{:S(2)}, u32[]{:S(2)}) %collective-permute-start.20) | collective-permute-done | bytes 786464 | tf_op jit(solution)/shard_map/ppermute | solution.py:27
  281.5 3.6 collective-permute-start.67
  288.5 16.7 %collective-permute-done.31.refs_4_ = bf16[256,1536]{1,0:T(8,128)(2,1)} collective-permute-done((bf16[256,1536]{1,0:T(8,128)(2,1)}, bf16[256,1536]{1,0:T(8,128)(2,1)}, u32[]{:S(2)}, u32[]{:S(2)}) %collective-permute-start.31) | collective-permute-done | bytes 786464 | tf_op jit(solution)/shard_map/ppermute | solution.py:27
  305.8 23.3 %expert_forward_far.1 = (bf16[10,512,768]{2,1,0:T(8,128)(2,1)}, f32[10,512,256]{2,1,0:T(8,128)}, f32[10,512,256]{2,1,0:T(8,128)}) custom-call(s32[1]{0:T(128)} %bitcast.14.half_ref, s32[10,4,512]{2,1,0:T(4,128)} %get-tuple-element.244.slots_ref, f32[10,4,512]{2,1,0:T(4,128)} %maximum_bitcast_fusion.4.gates_ref, bf16[10,1536,256]{2,1,0:T(8,128)(2,1)} %gate_w.5, ...), custom_call_target="tpu_custom_call" | custom-call | flops 16106127360 | bytes 34078720 | tf_op jit(solution)/shard_map/expert_forward_far/pallas_call | solution.py:221
  330.9 76.5 %expert_backward.1 = (bf16[10,512,768]{2,1,0:T(8,128)(2,1)}, bf16[10,512,256]{2,1,0:T(8,128)(2,1)}, bf16[10,512,256]{2,1,0:T(8,128)(2,1)}, bf16[10,512,256]{2,1,...) custom-call(s32[1]{0:T(128)} %bitcast.14.half_ref, ...), custom_call_target="tpu_custom_call" | custom-call | flops 28185722880 | bytes 49807360 | tf_op jit(solution)/shard_map/expert_backward/pallas_call | solution.py:221
  426.8 8.6 %collective-permute-done.73.refs_6_ = bf16[256,1536]{1,0:T(8,128)(2,1)} collective-permute-done((bf16[256,1536]{1,0:T(8,128)(2,1)}, bf16[256,1536]{1,0:T(8,128)(2,1)}, u32[]{:S(2)}, u32[]{:S(2)}) %collective-permute-start.73) | collective-permute-done | bytes 786464 | tf_op jit(solution)/shard_map/ppermute | solution.py:27
  436.7 3.8 fusion.27
  444.0 34.5 %expert_weights.1 = (bf16[10,768,256]{2,1,0:T(8,128)(2,1)}, bf16[10,768,256]{2,1,0:T(8,128)(2,1)}, bf16[10,256,768]{2,1,0:T(8,128)(2,1)}) custom-call(s32[1]{0:T(128)} %bitcast.14.half_ref, s32[10,4,512]{2,1,0:T(4,128)} %get-tuple-element.244.slots_ref, f32[10,4,512]{2,1,0:T(4,128)} %maximum_bitcast_fusion.4.gates_ref, bf16[10,256,1536]{2,1,0:T(8,128)(2,1)} %down_w.3, ...), custom_call_target="tpu_custom_call" | custom-call | flops 24159191040 | bytes 65536000 | tf_op jit(solution)/shard_map/expert_weights/pallas_call | solution.py:221
  499.5 10.8 %fusion = (f32[4,3,512]{2,1,0:T(4,128)S(1)}, f32[4,512,512,3]{2,1,3,0:T(8,128)}) fusion(f32[4,512,512,3]{2,1,3,0:T(8,128)} %copy-done.1, f32[4,3,512]{2,1,0:T(4,128)S(1)} %copy-done.46, pred[512,512]{0,1:T(8,128)(4,1)S(1)} %broadcast_compare_fusion, bf16[512,4,64,1]{0,2,3,1:T(8,128)(2,1)} %bitcast.271, bf16[512,4,3,64]{0,3,2,1:T(8,128)(2,1)S(1)} %bitcast.258), kind=kOutput, calls=%fused_computation.2 | convolution fusion | flops 415229952 | bytes 26525696 | tf_op jit(solution)/shard_map/while/body/eval_jaxpr/while/body/eval_jaxpr/qkge,tke->kgqt/dot_general | solution.py:417
  512.2 7.0 fusion.2
  548.3 4.3 convert_add_fusion.2
  552.6 17.3 %collective-permute-done.84 = bf16[10,384,256]{2,1,0:T(8,128)(2,1)} collective-permute-done((bf16[10,384,256]{2,1,0:T(8,128)(2,1)}, bf16[10,384,256]{2,1,0:T(8,128)(2,1)}, u32[]{:S(2)}, u32[]{:S(2)}) %collective-permute-start.84) | collective-permute-done | bytes 1966112 | tf_op jit(solution)/shard_map/ppermute | solution.py:27
  571.1 4.0 convert_add_fusion.1
  575.2 35.1 %collective-permute-done.85 = bf16[10,256,384]{2,1,0:T(8,128)(2,1)} collective-permute-done((bf16[10,256,384]{2,1,0:T(8,128)(2,1)}, bf16[10,256,384]{2,1,0:T(8,128)(2,1)}, u32[]{:S(2)}, u32[]{:S(2)}) %collective-permute-start.85) | collective-permute-done | bytes 1966112 | tf_op jit(solution)/shard_map/ppermute | solution.py:27
  610.2 4.0 convert_add_fusion
  616.4 3.7 collective-permute-start.61
  624.3 7.3 %concatenate.89 = bf16[4,4,96,1408]{3,2,0,1:T(8,128)(2,1)} concatenate(bf16[4,4,96,1280]{3,2,0,1:T(8,128)(2,1)} %copy.85, bf16[4,4,96,1]{3,2,0,1:T(8,128)(2,1)S(1)} %copy.86, bf16[4,4,96,127]{3,2,0,1:T(8,128)(2,1)S(1)} %broadcast_in_dim.228), dimensions={3} | concatenate | bytes 8650752 | tf_op jit(solution)/shard_map/concatenate | solution.py:664
  631.6 3.7 dynamic-slice_bitcast_fusion.2
  638.8 3.9 broadcast_select_fusion.3
  646.0 17.3 %collective-permute-done.51 = bf16[4,96,1408]{2,1,0:T(8,128)(2,1)} collective-permute-done((bf16[4,96,1408]{2,1,0:T(8,128)(2,1)}, bf16[4,96,1408]{2,1,0:T(8,128)(2,1)}, u32[]{:S(2)}, u32[]{:S(2)}) %collective-permute-start.51) | collective-permute-done | bytes 1081376 | tf_op jit(solution)/shard_map/ppermute | solution.py:27
  663.3 22.0 %collective-permute-done.50 = bf16[4,96,1408]{2,1,0:T(8,128)(2,1)} collective-permute-done((bf16[4,96,1408]{2,1,0:T(8,128)(2,1)}, bf16[4,96,1408]{2,1,0:T(8,128)(2,1)}, u32[]{:S(2)}, u32[]{:S(2)}) %collective-permute-start.50) | collective-permute-done | bytes 1081376 | tf_op jit(solution)/shard_map/ppermute | solution.py:27
  688.3 3.6 collective-permute-start.54
  692.7 4.6 fusion.15
  699.6 15.4 %collective-permute-done.53 = bf16[96,1408]{1,0:T(8,128)(2,1)S(1)} collective-permute-done((bf16[96,1408]{1,0:T(8,128)(2,1)S(1)}, bf16[96,1408]{1,0:T(8,128)(2,1)S(1)}, u32[]{:S(2)}, u32[]{:S(2)}) %collective-permute-start.53) | collective-permute-done | bytes 270368 | tf_op jit(solution)/shard_map/ppermute | solution.py:27
  (469 shorter events, 219.8 us)
Async XLA Ops:
  41.9 43.8 %collective-permute-start.10 = (bf16[256,1536]{1,0:T(8,128)(2,1)S(1)}, bf16[256,1536]{1,0:T(8,128)(2,1)S(1)}, u32[]{:S(2)}, u32[]{:S(2)}) collective-permute-start(bf16[256,1536]{1,0:T(8,128)(2,1)S(1)} %multiply_convert_fusion.refs_1_), channel_id=1, source_target_pairs={{0,2},{2,0},{4,6},{6,4},{1,3},{3,1},{5,7},{7,5},{8,10},{10,8},{12,... | collective-permute-start | bytes 2359304 | tf_op jit(solution)/shard_map/ppermute | solution.py:27
  43.4 42.8 %collective-permute-start.12 = (bf16[256,1536]{1,0:T(8,128)(2,1)S(1)}, bf16[256,1536]{1,0:T(8,128)(2,1)S(1)}, u32[]{:S(2)}, u32[]{:S(2)}) collective-permute-start(bf16[256,1536]{1,0:T(8,128)(2,1)S(1)} %multiply_convert_fusion.refs_1_), channel_id=1, source_target_pairs={{0,4},{2,6},{4,0},{6,2},{1,5},{3,7},{5,1},{7,3},{8,12},{10,14},{12... | collective-permute-start | bytes 2359304 | tf_op jit(solution)/shard_map/ppermute | solution.py:27
  44.9 41.4 %collective-permute-start.14 = (bf16[256,1536]{1,0:T(8,128)(2,1)S(1)}, bf16[256,1536]{1,0:T(8,128)(2,1)S(1)}, u32[]{:S(2)}, u32[]{:S(2)}) collective-permute-start(bf16[256,1536]{1,0:T(8,128)(2,1)S(1)} %multiply_convert_fusion.refs_1_), channel_id=1, source_target_pairs={{0,6},{2,4},{4,2},{6,0},{1,7},{3,5},{5,3},{7,1},{8,14},{10,12},{12... | collective-permute-start | bytes 2359304 | tf_op jit(solution)/shard_map/ppermute | solution.py:27
  45.4 34.8 %collective-permute-start.4 = (s32[2,8,512]{2,1,0:T(8,128)S(1)}, s32[2,8,512]{2,1,0:T(8,128)S(1)}, u32[]{:S(2)}, u32[]{:S(2)}) collective-permute-start(s32[2,8,512]{2,1,0:T(8,128)S(1)} %get-tuple-element.251), channel_id=1, source_target_pairs={{0,6},{2,4},{4,2},{6,0},{1,7},{3,5},{5,3},{7,1},{8,14},{10,12},{12... | collective-permute-start | bytes 98312 | tf_op jit(solution)/shard_map/ppermute | solution.py:27
  95.0 93.1 %collective-permute-start.75 = (bf16[256,1536]{1,0:T(8,128)(2,1)S(1)}, bf16[256,1536]{1,0:T(8,128)(2,1)}, u32[]{:S(2)}, u32[]{:S(2)}) collective-permute-start(bf16[256,1536]{1,0:T(8,128)(2,1)S(1)} %multiply_convert_fusion.refs_1_), channel_id=1, source_target_pairs={{0,24},{8,16},{16,8},{24,0},{1,25},{9,17},{17,9},{25,1},{2,26},{10... | collective-permute-start | bytes 2359304 | tf_op jit(solution)/shard_map/ppermute | solution.py:32
  188.1 36.7 %collective-permute-start.77 = (bf16[256,1536]{1,0:T(8,128)(2,1)}, bf16[256,1536]{1,0:T(8,128)(2,1)S(1)}, u32[]{:S(2)}, u32[]{:S(2)}) collective-permute-start(bf16[256,1536]{1,0:T(8,128)(2,1)} %collective-permute-done.75.refs_0_), channel_id=1, source_target_pairs={{0,2},{2,0},{4,6},{6,4},{1,3},{3,1},{5,7},{7,5},{8,10},{10,8},{12,... | collective-permute-start | bytes 2359304 | tf_op jit(solution)/shard_map/ppermute | solution.py:27
  190.2 36.1 %collective-permute-start.79 = (bf16[256,1536]{1,0:T(8,128)(2,1)}, bf16[256,1536]{1,0:T(8,128)(2,1)S(1)}, u32[]{:S(2)}, u32[]{:S(2)}) collective-permute-start(bf16[256,1536]{1,0:T(8,128)(2,1)} %collective-permute-done.75.refs_0_), channel_id=1, source_target_pairs={{0,4},{2,6},{4,0},{6,2},{1,5},{3,7},{5,1},{7,3},{8,12},{10,14},{12... | collective-permute-start | bytes 2359304 | tf_op jit(solution)/shard_map/ppermute | solution.py:27
  224.8 36.6 %collective-permute-start.20 = (bf16[256,1536]{1,0:T(8,128)(2,1)}, bf16[256,1536]{1,0:T(8,128)(2,1)}, u32[]{:S(2)}, u32[]{:S(2)}) collective-permute-start(bf16[256,1536]{1,0:T(8,128)(2,1)} %get-tuple-element.220), channel_id=1, source_target_pairs={{0,4},{2,6},{4,0},{6,2},{1,5},{3,7},{5,1},{7,3},{8,12},{10,14},{12... | collective-permute-start | bytes 2359304 | tf_op jit(solution)/shard_map/ppermute | solution.py:27
  227.2 34.3 %collective-permute-start.18 = (bf16[256,1536]{1,0:T(8,128)(2,1)S(1)}, bf16[256,1536]{1,0:T(8,128)(2,1)}, u32[]{:S(2)}, u32[]{:S(2)}) collective-permute-start(bf16[256,1536]{1,0:T(8,128)(2,1)S(1)} %get-tuple-element.218), channel_id=1, source_target_pairs={{0,2},{2,0},{4,6},{6,4},{1,3},{3,1},{5,7},{7,5},{8,10},{10,8},{12,... | collective-permute-start | bytes 2359304 | tf_op jit(solution)/shard_map/ppermute | solution.py:27
  231.8 35.4 %collective-permute-start.66 = (f32[4,10,256]{2,0,1:T(4,128)S(1)}, f32[4,10,256]{2,0,1:T(4,128)S(1)}, u32[]{:S(2)}, u32[]{:S(2)}) collective-permute-start(f32[4,10,256]{2,0,1:T(4,128)S(1)} %fusion.84), channel_id=1, source_target_pairs={{0,1},{1,0},{2,3},{3,2},{4,5},{5,4},{6,7},{7,6},{8,9},{9,8},{10,11... | collective-permute-start | bytes 122888 | tf_op jit(solution)/shard_map/ppermute | solution.py:23
  231.8 37.1 %collective-permute-start.76 = (bf16[256,1536]{1,0:T(8,128)(2,1)}, bf16[256,1536]{1,0:T(8,128)(2,1)}, u32[]{:S(2)}, u32[]{:S(2)}) collective-permute-start(bf16[256,1536]{1,0:T(8,128)(2,1)} %collective-permute-done.75.refs_0_), channel_id=1, source_target_pairs={{0,1},{1,0},{2,3},{3,2},{4,5},{5,4},{6,7},{7,6},{8,9},{9,8},{10,11... | collective-permute-start | bytes 2359304 | tf_op jit(solution)/shard_map/ppermute | solution.py:23
  268.9 36.3 %collective-permute-start.31 = (bf16[256,1536]{1,0:T(8,128)(2,1)}, bf16[256,1536]{1,0:T(8,128)(2,1)}, u32[]{:S(2)}, u32[]{:S(2)}) collective-permute-start(bf16[256,1536]{1,0:T(8,128)(2,1)} %get-tuple-element.266.refs_0_), channel_id=1, source_target_pairs={{0,4},{2,6},{4,0},{6,2},{1,5},{3,7},{5,1},{7,3},{8,12},{10,14},{12... | collective-permute-start | bytes 2359304 | tf_op jit(solution)/shard_map/ppermute | solution.py:27
  269.8 35.5 %collective-permute-start.33 = (bf16[256,1536]{1,0:T(8,128)(2,1)}, bf16[256,1536]{1,0:T(8,128)(2,1)}, u32[]{:S(2)}, u32[]{:S(2)}) collective-permute-start(bf16[256,1536]{1,0:T(8,128)(2,1)} %get-tuple-element.266.refs_0_), channel_id=1, source_target_pairs={{0,6},{2,4},{4,2},{6,0},{1,7},{3,5},{5,3},{7,1},{8,14},{10,12},{12... | collective-permute-start | bytes 2359304 | tf_op jit(solution)/shard_map/ppermute | solution.py:27
  281.5 47.6 %collective-permute-start.28 = (bf16[256,1536]{1,0:T(8,128)(2,1)}, bf16[256,1536]{1,0:T(8,128)(2,1)}, u32[]{:S(2)}, u32[]{:S(2)}) collective-permute-start(bf16[256,1536]{1,0:T(8,128)(2,1)} %get-tuple-element.266.refs_0_), channel_id=1, source_target_pairs={{0,1},{1,0},{2,3},{3,2},{4,5},{5,4},{6,7},{7,6},{8,9},{9,8},{10,11... | collective-permute-start | bytes 2359304 | tf_op jit(solution)/shard_map/ppermute | solution.py:23
  281.5 47.6 %collective-permute-start.67 = (bf16[256,1536]{1,0:T(8,128)(2,1)}, bf16[256,1536]{1,0:T(8,128)(2,1)}, u32[]{:S(2)}, u32[]{:S(2)}) collective-permute-start(bf16[256,1536]{1,0:T(8,128)(2,1)} %get-tuple-element.266.refs_0_), channel_id=1, source_target_pairs={{0,24},{8,16},{16,8},{24,0},{1,25},{9,17},{17,9},{25,1},{2,26},{10... | collective-permute-start | bytes 2359304 | tf_op jit(solution)/shard_map/ppermute | solution.py:32
  288.5 41.6 %collective-permute-start.30 = (bf16[256,1536]{1,0:T(8,128)(2,1)}, bf16[256,1536]{1,0:T(8,128)(2,1)}, u32[]{:S(2)}, u32[]{:S(2)}) collective-permute-start(bf16[256,1536]{1,0:T(8,128)(2,1)} %collective-permute-done.29.refs_2_), channel_id=1, source_target_pairs={{0,1},{1,0},{2,3},{3,2},{4,5},{5,4},{6,7},{7,6},{8,9},{9,8},{10,11... | collective-permute-start | bytes 2359304 | tf_op jit(solution)/shard_map/ppermute | solution.py:23
  329.1 79.3 %collective-permute-start.23 = (bf16[256,1536]{1,0:T(8,128)(2,1)S(1)}, bf16[256,1536]{1,0:T(8,128)(2,1)}, u32[]{:S(2)}, u32[]{:S(2)}) collective-permute-start(bf16[256,1536]{1,0:T(8,128)(2,1)S(1)} %get-tuple-element.198), channel_id=1, source_target_pairs={{0,1},{1,0},{2,3},{3,2},{4,5},{5,4},{6,7},{7,6},{8,9},{9,8},{10,11... | collective-permute-start | bytes 2359304 | tf_op jit(solution)/shard_map/ppermute | solution.py:23
  329.1 93.6 %collective-permute-start.69 = (bf16[256,1536]{1,0:T(8,128)(2,1)}, bf16[256,1536]{1,0:T(8,128)(2,1)}, u32[]{:S(2)}, u32[]{:S(2)}) collective-permute-start(bf16[256,1536]{1,0:T(8,128)(2,1)} %collective-permute-done.67.refs_0_), channel_id=1, source_target_pairs={{0,2},{2,0},{4,6},{6,4},{1,3},{3,1},{5,7},{7,5},{8,10},{10,8},{12,... | collective-permute-start | bytes 2359304 | tf_op jit(solution)/shard_map/ppermute | solution.py:27
  330.2 96.6 %collective-permute-start.71 = (bf16[256,1536]{1,0:T(8,128)(2,1)}, bf16[256,1536]{1,0:T(8,128)(2,1)}, u32[]{:S(2)}, u32[]{:S(2)}) collective-permute-start(bf16[256,1536]{1,0:T(8,128)(2,1)} %collective-permute-done.67.refs_0_), channel_id=1, source_target_pairs={{0,4},{2,6},{4,0},{6,2},{1,5},{3,7},{5,1},{7,3},{8,12},{10,14},{12... | collective-permute-start | bytes 2359304 | tf_op jit(solution)/shard_map/ppermute | solution.py:27
  436.2 45.5 %collective-permute-start.35 = (bf16[256,1536]{1,0:T(8,128)(2,1)}, bf16[256,1536]{1,0:T(8,128)(2,1)S(1)}, u32[]{:S(2)}, u32[]{:S(2)}) collective-permute-start(bf16[256,1536]{1,0:T(8,128)(2,1)} %get-tuple-element.207), channel_id=1, source_target_pairs={{0,1},{1,0},{2,3},{3,2},{4,5},{5,4},{6,7},{7,6},{8,9},{9,8},{10,11... | collective-permute-start | bytes 2359304 | tf_op jit(solution)/shard_map/ppermute | solution.py:23
  440.5 41.2 %collective-permute-start.41 = (bf16[256,1536]{1,0:T(8,128)(2,1)}, bf16[256,1536]{1,0:T(8,128)(2,1)}, u32[]{:S(2)}, u32[]{:S(2)}) collective-permute-start(bf16[256,1536]{1,0:T(8,128)(2,1)} %get-tuple-element.212), channel_id=1, source_target_pairs={{0,6},{2,4},{4,2},{6,0},{1,7},{3,5},{5,3},{7,1},{8,14},{10,12},{12... | collective-permute-start | bytes 2359304 | tf_op jit(solution)/shard_map/ppermute | solution.py:27
  442.3 39.4 %collective-permute-start.39 = (bf16[256,1536]{1,0:T(8,128)(2,1)}, bf16[256,1536]{1,0:T(8,128)(2,1)}, u32[]{:S(2)}, u32[]{:S(2)}) collective-permute-start(bf16[256,1536]{1,0:T(8,128)(2,1)} %get-tuple-element.213), channel_id=1, source_target_pairs={{0,4},{2,6},{4,0},{6,2},{1,5},{3,7},{5,1},{7,3},{8,12},{10,14},{12... | collective-permute-start | bytes 2359304 | tf_op jit(solution)/shard_map/ppermute | solution.py:27
  443.2 38.5 %collective-permute-start.37 = (bf16[256,1536]{1,0:T(8,128)(2,1)}, bf16[256,1536]{1,0:T(8,128)(2,1)}, u32[]{:S(2)}, u32[]{:S(2)}) collective-permute-start(bf16[256,1536]{1,0:T(8,128)(2,1)} %get-tuple-element.211), channel_id=1, source_target_pairs={{0,2},{2,0},{4,6},{6,4},{1,3},{3,1},{5,7},{7,5},{8,10},{10,8},{12,... | collective-permute-start | bytes 2359304 | tf_op jit(solution)/shard_map/ppermute | solution.py:27
  481.7 65.8 %collective-permute-start.83 = (bf16[10,384,256]{2,1,0:T(8,128)(2,1)}, bf16[10,384,256]{2,1,0:T(8,128)(2,1)}, u32[]{:S(2)}, u32[]{:S(2)}) collective-permute-start(bf16[10,384,256]{2,1,0:T(8,128)(2,1)} %constant_dynamic-slice_fusion.2), channel_id=1, source_target_pairs={{0,8},{8,0},{16,24},{24,16},{1,9},{9,1},{17,25},{25,17},{2,10},{10... | collective-permute-start | bytes 5898248 | tf_op jit(solution)/shard_map/ppermute | solution.py:27
  488.8 81.1 %collective-permute-start.84 = (bf16[10,384,256]{2,1,0:T(8,128)(2,1)}, bf16[10,384,256]{2,1,0:T(8,128)(2,1)}, u32[]{:S(2)}, u32[]{:S(2)}) collective-permute-start(bf16[10,384,256]{2,1,0:T(8,128)(2,1)} %constant_dynamic-slice_fusion.1), channel_id=1, source_target_pairs={{0,8},{8,0},{16,24},{24,16},{1,9},{9,1},{17,25},{25,17},{2,10},{10... | collective-permute-start | bytes 5898248 | tf_op jit(solution)/shard_map/ppermute | solution.py:27
  492.2 118.0 %collective-permute-start.85 = (bf16[10,256,384]{2,1,0:T(8,128)(2,1)}, bf16[10,256,384]{2,1,0:T(8,128)(2,1)}, u32[]{:S(2)}, u32[]{:S(2)}) collective-permute-start(bf16[10,256,384]{2,1,0:T(8,128)(2,1)} %constant_dynamic-slice_fusion), channel_id=1, source_target_pairs={{0,8},{8,0},{16,24},{24,16},{1,9},{9,1},{17,25},{25,17},{2,10},{10... | collective-permute-start | bytes 5898248 | tf_op jit(solution)/shard_map/ppermute | solution.py:27
  531.9 88.9 %collective-permute-start.48 = (bf16[512,1536]{1,0:T(8,128)(2,1)}, bf16[512,1536]{1,0:T(8,128)(2,1)}, u32[]{:S(2)}, u32[]{:S(2)}) collective-permute-start(bf16[512,1536]{1,0:T(8,128)(2,1)} %fusion.19), channel_id=1, source_target_pairs={{0,1},{1,0},{2,3},{3,2},{4,5},{5,4},{6,7},{7,6},{8,9},{9,8},{10,11... | collective-permute-start | bytes 4718600 | tf_op jit(solution)/shard_map/ppermute | solution.py:23
  545.6 68.6 %collective-permute-start.58 = (bf16[4,96,896]{2,1,0:T(8,128)(2,1)S(1)}, bf16[4,96,896]{2,1,0:T(8,128)(2,1)S(1)}, u32[]{:S(2)}, u32[]{:S(2)}) collective-permute-start(bf16[4,96,896]{2,1,0:T(8,128)(2,1)S(1)} %get-tuple-element.222), channel_id=1, source_target_pairs={{0,6},{2,4},{4,2},{6,0},{1,7},{3,5},{5,3},{7,1},{8,14},{10,12},{12... | collective-permute-start | bytes 2064392 | tf_op jit(solution)/shard_map/ppermute | solution.py:27
  547.4 66.7 %collective-permute-start.57 = (bf16[4,96,896]{2,1,0:T(8,128)(2,1)S(1)}, bf16[4,96,896]{2,1,0:T(8,128)(2,1)S(1)}, u32[]{:S(2)}, u32[]{:S(2)}) collective-permute-start(bf16[4,96,896]{2,1,0:T(8,128)(2,1)S(1)} %get-tuple-element.223), channel_id=1, source_target_pairs={{0,4},{2,6},{4,0},{6,2},{1,5},{3,7},{5,1},{7,3},{8,12},{10,14},{12... | collective-permute-start | bytes 2064392 | tf_op jit(solution)/shard_map/ppermute | solution.py:27
  569.9 44.3 %collective-permute-start.56 = (bf16[4,96,896]{2,1,0:T(8,128)(2,1)S(1)}, bf16[4,96,896]{2,1,0:T(8,128)(2,1)S(1)}, u32[]{:S(2)}, u32[]{:S(2)}) collective-permute-start(bf16[4,96,896]{2,1,0:T(8,128)(2,1)S(1)} %get-tuple-element.221), channel_id=1, source_target_pairs={{0,2},{2,0},{4,6},{6,4},{1,3},{3,1},{5,7},{7,5},{8,10},{10,8},{12,... | collective-permute-start | bytes 2064392 | tf_op jit(solution)/shard_map/ppermute | solution.py:27
  637.1 48.2 %collective-permute-start.50 = (bf16[4,96,1408]{2,1,0:T(8,128)(2,1)}, bf16[4,96,1408]{2,1,0:T(8,128)(2,1)}, u32[]{:S(2)}, u32[]{:S(2)}) collective-permute-start(bf16[4,96,1408]{2,1,0:T(8,128)(2,1)} %get-tuple-element.204), channel_id=1, source_target_pairs={{0,4},{2,6},{4,0},{6,2},{1,5},{3,7},{5,1},{7,3},{8,12},{10,14},{12... | collective-permute-start | bytes 3244040 | tf_op jit(solution)/shard_map/ppermute | solution.py:27
  638.0 47.3 %collective-permute-start.49 = (bf16[4,96,1408]{2,1,0:T(8,128)(2,1)}, bf16[4,96,1408]{2,1,0:T(8,128)(2,1)}, u32[]{:S(2)}, u32[]{:S(2)}) collective-permute-start(bf16[4,96,1408]{2,1,0:T(8,128)(2,1)} %get-tuple-element.202), channel_id=1, source_target_pairs={{0,2},{2,0},{4,6},{6,4},{1,3},{3,1},{5,7},{7,5},{8,10},{10,8},{12,... | collective-permute-start | bytes 3244040 | tf_op jit(solution)/shard_map/ppermute | solution.py:27
  (141 other events, 1490.5 us)

commit v2 on v1

--- a/solution.py
+++ b/solution.py
@@ -14,7 +14,6 @@
 
 EPS = 1e-06
 THETA = 10000.0
-VMEM_LIMIT = 60 * 1024 * 1024
 bfloat = jnp.bfloat16
 single = jnp.float32
 
@@ -32,8 +31,21 @@
     return lax.ppermute(value, "dp", [(i, count - 1 - i) for i in range(count)])
 
 
+def after(value, *others):
+    return lax.optimization_barrier((value,) + others)[0]
+
+
 def gather_groups(value):
     return [value] + [to_peer(value, "expert", s) for s in range(1, lax.axis_size("expert"))]
+
+
+def gather_tokens(value):
+    if lax.axis_size("expert") != 4:
+        return gather_groups(value)
+    cut = value.shape[0] // 2
+    first, second = to_peer(value, "expert", 1), to_peer(value, "expert", 2)
+    low, high = to_peer(second[:cut], "expert", 1), to_peer(first[cut:], "expert", 2)
+    return [value, first, second, jnp.concatenate([low, high], axis=0)]
 
 
 def sum_all(value, axes):
@@ -45,27 +57,27 @@
     return value
 
 
-def scatter_dense(packed):
+def scatter_dense(packed, kind=bfloat):
     count_dp, count_ex = lax.axis_size("dp"), lax.axis_size("expert")
     at_dp, at_ex = lax.axis_index("dp"), lax.axis_index("expert")
-    rows, columns = packed.shape
-    block = rows // (count_dp * count_ex)
-    cut = packed.reshape(count_dp, count_ex, block, columns)
+    block = packed.shape[0] // (count_dp * count_ex)
+    cut = packed.reshape((count_dp, count_ex, block) + packed.shape[1:])
 
     def part(step):
         return lax.dynamic_index_in_dim(cut, at_ex ^ step, 1, keepdims=False)
 
+    sent = [part(step).astype(kind) for step in range(1, count_ex)]
     total = part(0).astype(single)
     for step in range(1, count_ex):
-        total = total + to_peer(part(step).astype(bfloat), "expert", step).astype(single)
+        total = total + to_peer(sent[step - 1], "expert", step).astype(single)
 
     def row(step):
         return lax.dynamic_index_in_dim(total, at_dp ^ step, 0, keepdims=False)
 
     result = row(0)
     for step in range(1, count_dp):
-        result = result + to_peer(row(step).astype(bfloat), "dp", step).astype(single)
-    return result
+        result = result + to_peer(row(step).astype(kind), "dp", step).astype(single)
+    return result, sent
 
 
 def dot(left, right):
@@ -80,72 +92,65 @@
     return lax.dot_general(left, right, (((0,), (0,)), ((), ())), preferred_element_type=single)
 
 
-def picks(slots_ref, group, capacity):
-    slot = slots_ref[0, group : group + 1, :]
+def picks(slots_ref, expert, group, capacity):
+    slot = slots_ref[expert, group : group + 1, :]
     return slot == lax.broadcasted_iota(jnp.int32, (capacity, slot.shape[1]), 0)
 
 
-def gather_rows(picked, mine, other, to_ref, group, capacity):
+def gather_kernel(group, slots_ref, mine, other, rows_ref, picked_ref):
+    experts, capacity, width = rows_ref.shape
     span = mine.shape[0]
-    low = picked.astype(bfloat)
-    rows = dot(low[:, :span], mine[...]) + dot(low[:, span:], other[...])
-    to_ref[group * capacity : (group + 1) * capacity, :] = rows.astype(bfloat)
-
-
-def slot_gates(picked, gates_ref, group):
-    return jnp.sum(jnp.where(picked, gates_ref[0, group : group + 1, :], 0.0), axis=1, keepdims=True)
-
-
-def add_back(step, picked, rows, acc_mine, acc_other, group):
-    back = dot_tn(picked.astype(bfloat), rows)
-    span = acc_mine.shape[1]
-
-    @pl.when(step == 0)
+    for e in range(experts):
+        picked_ref[e * capacity : (e + 1) * capacity, :] = picks(
+            slots_ref, e, group, capacity
+        ).astype(bfloat)
+    rows = dot(picked_ref[:, :span], mine[...]) + dot(picked_ref[:, span:], other[...])
+    rows_ref[...] = rows.astype(bfloat).reshape(experts, capacity, width)
+
+
+def return_kernel(group, slots_ref, rows_ref, mine, other, picked_ref):
+    experts, capacity, width = rows_ref.shape
+    span = mine.shape[0]
+
+    @pl.when(pl.program_id(0) == 0)
     def _():
-        acc_mine[group] = back[:span]
-        acc_other[group] = back[span:]
-
-    @pl.when(step > 0)
-    def _():
-        acc_mine[group] += back[:span]
-        acc_other[group] += back[span:]
-
-
-def half_columns(half_ref, width):
-    return pl.ds(pl.multiple_of(half_ref[0] * width, 128), width)
-
-
-def forward_kernel(groups, with_out, half_ref, slots_ref, gates_ref, gate_w, up_w, *refs):
-    step = pl.program_id(0)
+        for e in range(experts):
+            picked_ref[e * capacity : (e + 1) * capacity, :] = picks(
+                slots_ref, e, group, capacity
+            ).astype(bfloat)
+
+    back = dot_tn(picked_ref[...], rows_ref[...].reshape(experts * capacity, width)).astype(bfloat)
+    mine[...] = back[:span]
+    other[...] = back[span:]
+
+
+def slot_gates(slots_ref, gates_ref, groups, capacity):
+    parts = []
+    for g in range(groups):
+        picked = picks(slots_ref, 0, g, capacity)
+        gate = gates_ref[0, g : g + 1, :]
+        parts.append(jnp.sum(jnp.where(picked, gate, 0.0), axis=1, keepdims=True))
+    return jnp.concatenate(parts, axis=0)
+
+
+def joined(refs):
+    return jnp.concatenate([ref[0] for ref in refs], axis=0)
+
+
+def forward_kernel(groups, with_out, slots_ref, gates_ref, gate_w, up_w, *refs):
     if with_out:
         down_w, refs = refs[0], refs[1:]
-    x_refs, refs = refs[: 2 * groups], refs[2 * groups :]
-    if with_out:
-        half_rows, gate_ref, up_ref, out_mine, out_other, rows_ref, acc_mine, acc_other = refs
-    else:
-        half_rows, gate_ref, up_ref, rows_ref = refs
-    capacity = rows_ref.shape[0] // groups
-    picked = [picks(slots_ref, g, capacity) for g in range(groups)]
-    for g in range(groups):
-        gather_rows(picked[g], x_refs[2 * g], x_refs[2 * g + 1], rows_ref, g, capacity)
-    rows = rows_ref[...]
-    half_rows[0] = rows_ref[:, half_columns(half_ref, half_rows.shape[2])]
+    row_refs, refs = refs[:groups], refs[groups:]
+    gate_ref, up_ref = refs[:2]
+    rows = joined(row_refs)
     gate_pre = dot(rows, gate_w[0])
     up_pre = dot(rows, up_w[0])
     gate_ref[0] = gate_pre
     up_ref[0] = up_pre
-    if not with_out:
-        return
-    gates = jnp.concatenate([slot_gates(picked[g], gates_ref, g) for g in range(groups)], axis=0)
-    hidden = (gate_pre * jax.nn.sigmoid(gate_pre) * up_pre * gates).astype(bfloat)
-    out = dot(hidden, down_w[0]).astype(bfloat)
-    for g in range(groups):
-        add_back(step, picked[g], out[g * capacity : (g + 1) * capacity], acc_mine, acc_other, g)
-
-    @pl.when(step == pl.num_programs(0) - 1)
-    def _():
-        out_mine[...] = acc_mine[...].astype(out_mine.dtype)
-        out_other[...] = acc_other[...].astype(out_other.dtype)
+    if with_out:
+        gates = slot_gates(slots_ref, gates_ref, groups, row_refs[0].shape[1])
+        hidden = (gate_pre * jax.nn.sigmoid(gate_pre) * up_pre * gates).astype(bfloat)
+        refs[2][0] = dot(hidden, down_w[0]).astype(bfloat)
 
 
 def hidden_grads(gate_pre, up_pre, gates, grad_hidden):
@@ -159,160 +164,183 @@
     return (hidden * gates).astype(bfloat), grad_gate_pre, grad_up_pre, grad_gates
 
 
-def backward_kernel(groups, half_ref, slots_ref, gates_ref, gate_w, up_w, down_w, *refs):
-    step = pl.program_id(0)
-    g_refs, refs = refs[: 2 * groups], refs[2 * groups :]
-    gate_ref, up_ref = refs[:2]
-    half_grad, hidden_ref, grad_gate_ref, grad_up_ref, gg_ref, out_mine, out_other = refs[2:9]
-    rows_ref, acc_mine, acc_other = refs[9:]
-    capacity = rows_ref.shape[0] // groups
-    picked = [picks(slots_ref, g, capacity) for g in range(groups)]
-    for g in range(groups):
-        gather_rows(picked[g], g_refs[2 * g], g_refs[2 * g + 1], rows_ref, g, capacity)
-    half_grad[0] = rows_ref[:, half_columns(half_ref, half_grad.shape[2])]
-    gates = jnp.concatenate([slot_gates(picked[g], gates_ref, g) for g in range(groups)], axis=0)
-    grad_hidden = dot_nt(rows_ref[...], down_w[0])
+def backward_kernel(groups, slots_ref, gates_ref, gate_w, up_w, down_w, gate_ref, up_ref, *refs):
+    row_refs, refs = refs[:groups], refs[groups:]
+    hidden_ref, grad_gate_ref, grad_up_ref, gg_ref, back_ref = refs
+    capacity = row_refs[0].shape[1]
+    gates = slot_gates(slots_ref, gates_ref, groups, capacity)
+    grad_hidden = dot_nt(joined(row_refs), down_w[0])
     hidden, grad_gate_pre, grad_up_pre, grad_gates = hidden_grads(
         gate_ref[0], up_ref[0], gates, grad_hidden
     )
     hidden_ref[0] = hidden
     grad_gate_ref[0] = grad_gate_pre
     grad_up_ref[0] = grad_up_pre
+    back = dot_nt(grad_gate_pre, gate_w[0]) + dot_nt(grad_up_pre, up_w[0])
+    back_ref[0] = back.astype(bfloat)
     for g in range(groups):
         own = grad_gates[g * capacity : (g + 1) * capacity]
-        gg_ref[0, g : g + 1, :] = jnp.sum(jnp.where(picked[g], own, 0.0), axis=0, keepdims=True)
-    back = (dot_nt(grad_gate_pre, gate_w[0]) + dot_nt(grad_up_pre, up_w[0])).astype(bfloat)
+        picked = picks(slots_ref, 0, g, capacity)
+        gg_ref[0, g : g + 1, :] = jnp.sum(jnp.where(picked, own, 0.0), axis=0, keepdims=True)
+
+
+def weights_kernel(groups, half_ref, slots_ref, gates_ref, down_w, gate_ref, up_ref, *refs):
+    hidden_near, gate_near, up_near = refs[:3]
+    near_x, near_g, far_x, far_g = (refs[3 + i * groups : 3 + (i + 1) * groups] for i in range(4))
+    d_gate, d_up, d_down, rows_ref = refs[3 + 4 * groups :]
+    capacity = far_g[0].shape[1]
+    width = d_gate.shape[1]
     for g in range(groups):
-        add_back(step, picked[g], back[g * capacity : (g + 1) * capacity], acc_mine, acc_other, g)
-
-    @pl.when(step == pl.num_programs(0) - 1)
-    def _():
-        out_mine[...] = acc_mine[...].astype(out_mine.dtype)
-        out_other[...] = acc_other[...].astype(out_other.dtype)
-
-
-def weights_kernel(groups, half_ref, slots_ref, gates_ref, down_w, *refs):
-    g_refs, refs = refs[: 2 * groups], refs[2 * groups :]
-    gate_ref, up_ref, rows_far, rows_near, grad_near, hidden_near, gate_near, up_near = refs[:8]
-    d_gate, d_up, d_down, rows_ref = refs[8:]
-    capacity = rows_ref.shape[0] // groups
-    picked = [picks(slots_ref, g, capacity) for g in range(groups)]
-    for g in range(groups):
-        gather_rows(picked[g], g_refs[2 * g], g_refs[2 * g + 1], rows_ref, g, capacity)
-    gates = jnp.concatenate([slot_gates(picked[g], gates_ref, g) for g in range(groups)], axis=0)
+        rows_ref[g * capacity : (g + 1) * capacity, :] = far_g[g][0]
+    gates = slot_gates(slots_ref, gates_ref, groups, capacity)
     grad_hidden = dot_nt(rows_ref[...], down_w[0])
     hidden, grad_gate_pre, grad_up_pre, _ = hidden_grads(gate_ref[0], up_ref[0], gates, grad_hidden)
-    grad_far = rows_ref[:, half_columns(half_ref, d_gate.shape[1])]
-    d_down[0] = (dot_tn(hidden, grad_far) + dot_tn(hidden_near[0], grad_near[0])).astype(bfloat)
-    far, near = rows_far[0], rows_near[0]
+    grad_far = rows_ref[:, pl.ds(pl.multiple_of(half_ref[0] * width, 128), width)]
+    d_down[0] = (dot_tn(hidden, grad_far) + dot_tn(hidden_near[0], joined(near_g))).astype(bfloat)
+    far, near = joined(far_x), joined(near_x)
     d_gate[0] = (dot_tn(far, grad_gate_pre) + dot_tn(near, gate_near[0])).astype(bfloat)
     d_up[0] = (dot_tn(far, grad_up_pre) + dot_tn(near, up_near[0])).astype(bfloat)
 
 
-def per_expert(*shape):
-    return pl.BlockSpec((1,) + shape, lambda e, half: (e,) + (0,) * len(shape))
-
-
-def resident(*shape):
-    return pl.BlockSpec(shape, lambda e, half: (0,) * len(shape))
-
-
-def expert_call(kernel, name, experts, in_specs, out_specs, out_shape, scratch, flops, moved, args):
+def kernel_call(kernel, name, grid, in_specs, out_specs, out_shape, scratch, flops, moved, vmem, args, prefetch=0):
     return pl.pallas_call(
         kernel,
         name=name,
         grid_spec=pltpu.PrefetchScalarGridSpec(
-            num_scalar_prefetch=1,
-            grid=(experts,),
+            num_scalar_prefetch=prefetch,
+            grid=grid,
             in_specs=in_specs,
             out_specs=out_specs,
             scratch_shapes=scratch,
         ),
         out_shape=out_shape,
         compiler_params=pltpu.CompilerParams(
-            dimension_semantics=("arbitrary",), vmem_limit_bytes=VMEM_LIMIT
+            dimension_semantics=("arbitrary",), vmem_limit_bytes=vmem * 1024 * 1024
         ),
         cost_estimate=pl.CostEstimate(flops=flops, bytes_accessed=moved, transcendentals=0),
     )(*args)
 
 
-def expert_forward(half, slots, gates, weights, x_parts, capacity):
+def per_expert(*shape):
+    return pl.BlockSpec((1,) + shape, lambda e, *_: (e,) + (0,) * len(shape))
+
+
+def half_wide(rows, width):
+    return pl.BlockSpec((1, rows, width), lambda e, half: (e, 0, half[0]))
+
+
+def gather_rows(slots, group, mine, other, capacity):
     experts, groups, tokens = slots.shape
-    span, width = x_parts[0].shape
+    span, width = mine.shape
+    chunk = experts // 2 if experts % 2 == 0 else experts
+    whole = pl.BlockSpec((span, width), lambda i: (0, 0))
+    return kernel_call(
+        functools.partial(gather_kernel, group),
+        "gather_rows",
+        (experts // chunk,),
+        [pl.BlockSpec((chunk, groups, tokens), lambda i: (i, 0, 0)), whole, whole],
+        pl.BlockSpec((chunk, capacity, width), lambda i: (i, 0, 0)),
+        jax.ShapeDtypeStruct((experts, capacity, width), bfloat),
+        [pltpu.VMEM((chunk * capacity, tokens), bfloat)],
+        2 * experts * capacity * tokens * width,
+        2 * (experts * capacity + tokens) * width,
+        24,
+        (slots, mine, other),
+    )
+
+
+def return_rows(slots, group, rows, capacity, span):
+    experts, groups, tokens = slots.shape
+    width = rows.shape[2]
+    cut = width // 3
+    part = pl.BlockSpec((span, cut), lambda n: (0, n))
+    return kernel_call(
+        functools.partial(return_kernel, group),
+        "return_rows",
+        (3,),
+        [
+            pl.BlockSpec((experts, groups, tokens), lambda n: (0, 0, 0)),
+            pl.BlockSpec((experts, capacity, cut), lambda n: (0, group, n)),
+        ],
+        [part, part],
+        [jax.ShapeDtypeStruct((span, width), bfloat)] * 2,
+        [pltpu.VMEM((experts * capacity, tokens), bfloat)],
+        2 * experts * capacity * tokens * width,
+        2 * (experts * capacity + tokens) * width,
+        24,
+        (slots, rows),
+    )
+
+
+def expert_forward(slots, gates, weights, rows):
+    experts, groups, tokens = slots.shape
+    capacity, width = rows[0].shape[1:]
     with_out = len(weights) == 3
-    rows = groups * capacity
+    total = groups * capacity
     hidden = weights[0].shape[2]
     specs = [per_expert(groups, tokens)] * 2 + [per_expert(width, hidden)] * 2
-    outs = [per_expert(rows, width // 2), per_expert(rows, hidden), per_expert(rows, hidden)]
-    shapes = [
-        jax.ShapeDtypeStruct((experts, rows, width // 2), bfloat),
-        jax.ShapeDtypeStruct((experts, rows, hidden), single),
-        jax.ShapeDtypeStruct((experts, rows, hidden), single),
-    ]
-    scratch = [pltpu.VMEM((rows, width), bfloat)]
+    outs = [per_expert(total, hidden)] * 2
+    shapes = [jax.ShapeDtypeStruct((experts, total, hidden), single)] * 2
     if with_out:
         specs += [per_expert(hidden, width)]
-        outs += [resident(groups, span, width)] * 2
-        shapes += [jax.ShapeDtypeStruct((groups, span, width), bfloat)] * 2
-        scratch += [pltpu.VMEM((groups, span, width), single)] * 2
-    specs += [resident(span, width)] * (2 * groups)
-    once = 2 * experts * rows * width
-    flops = once * (tokens + 2 * hidden) + (once * (tokens + hidden) if with_out else 0)
-    moved = 2 * experts * (len(weights) * width * hidden + rows * width // 2 + 4 * rows * hidden)
-    return expert_call(
+        outs += [per_expert(total, width)]
+        shapes += [jax.ShapeDtypeStruct((experts, total, width), bfloat)]
+    specs += [per_expert(capacity, width)] * groups
+    return kernel_call(
         functools.partial(forward_kernel, groups, with_out),
         "expert_forward" if with_out else "expert_forward_far",
-        experts, specs, outs, shapes, scratch, flops, moved,
-        (half, slots, gates) + tuple(weights) + tuple(x_parts),
-    )
-
-
-def expert_backward(half, slots, gates, weights, g_parts, gate_pre, up_pre, capacity):
+        (experts,), specs, outs, shapes, [],
+        2 * experts * total * width * hidden * len(weights),
+        2 * experts * (len(weights) * (width * hidden) + (len(weights) - 1) * total * width + 4 * total * hidden),
+        32,
+        (slots, gates) + tuple(weights) + tuple(rows),
+    )
+
+
+def expert_backward(slots, gates, weights, gate_pre, up_pre, rows):
     experts, groups, tokens = slots.shape
-    span, width = g_parts[0].shape
-    rows = groups * capacity
+    capacity, width = rows[0].shape[1:]
+    total = groups * capacity
     hidden = weights[0].shape[2]
+    thin = per_expert(total, hidden)
     specs = [per_expert(groups, tokens)] * 2 + [per_expert(width, hidden)] * 2
-    specs += [per_expert(hidden, width)] + [resident(span, width)] * (2 * groups)
-    specs += [per_expert(rows, hidden)] * 2
-    outs = [per_expert(rows, width // 2)] + [per_expert(rows, hidden)] * 3
-    outs += [per_expert(groups, tokens)] + [resident(groups, span, width)] * 2
-    shapes = [jax.ShapeDtypeStruct((experts, rows, width // 2), bfloat)]
-    shapes += [jax.ShapeDtypeStruct((experts, rows, hidden), bfloat)] * 3
+    specs += [per_expert(hidden, width), thin, thin] + [per_expert(capacity, width)] * groups
+    outs = [thin] * 3 + [per_expert(groups, tokens), per_expert(total, width)]
+    shapes = [jax.ShapeDtypeStruct((experts, total, hidden), bfloat)] * 3
     shapes += [jax.ShapeDtypeStruct((experts, groups, tokens), single)]
-    shapes += [jax.ShapeDtypeStruct((groups, span, width), bfloat)] * 2
-    scratch = [pltpu.VMEM((rows, width), bfloat)]
-    scratch += [pltpu.VMEM((groups, span, width), single)] * 2
-    flops = 2 * experts * rows * width * (2 * tokens + 3 * hidden)
-    moved = 2 * experts * (3 * width * hidden + rows * width // 2 + 7 * rows * hidden)
-    return expert_call(
+    shapes += [jax.ShapeDtypeStruct((experts, total, width), bfloat)]
+    return kernel_call(
         functools.partial(backward_kernel, groups),
         "expert_backward",
-        experts, specs, outs, shapes, scratch, flops, moved,
-        (half, slots, gates) + tuple(weights) + tuple(g_parts) + (gate_pre, up_pre),
-    )
-
-
-def expert_weights(half, slots, gates, down_w, g_parts, far, near, capacity):
+        (experts,), specs, outs, shapes, [],
+        2 * experts * total * width * hidden * 3,
+        2 * experts * (3 * width * hidden + 2 * total * width + 7 * total * hidden),
+        36,
+        (slots, gates) + tuple(weights) + (gate_pre, up_pre) + tuple(rows),
+    )
+
+
+def expert_weights(half, slots, gates, down_w, far, near, near_x, near_g, far_x, far_g):
     experts, groups, tokens = slots.shape
-    span, width = g_parts[0].shape
-    rows = groups * capacity
+    capacity, width = far_g[0].shape[1:]
+    total = groups * capacity
     hidden = down_w.shape[1]
-    wide, thin = per_expert(rows, width // 2), per_expert(rows, hidden)
-    specs = [per_expert(groups, tokens)] * 2 + [per_expert(hidden, width)]
-    specs += [resident(span, width)] * (2 * groups)
-    specs += [thin, thin, wide, wide, wide, thin, thin, thin]
+    thin, wide = per_expert(total, hidden), half_wide(capacity, width // 2)
+    specs = [per_expert(groups, tokens)] * 2 + [per_expert(hidden, width)] + [thin] * 5
+    specs += [wide] * (3 * groups) + [per_expert(capacity, width)] * groups
     outs = [per_expert(width // 2, hidden)] * 2 + [per_expert(hidden, width // 2)]
     shapes = [jax.ShapeDtypeStruct((experts, width // 2, hidden), bfloat)] * 2
     shapes += [jax.ShapeDtypeStruct((experts, hidden, width // 2), bfloat)]
-    scratch = [pltpu.VMEM((rows, width), bfloat)]
-    flops = 2 * experts * rows * width * (tokens + 4 * hidden)
-    moved = 2 * experts * (3 * width * hidden + 3 * rows * width // 2 + 7 * rows * hidden)
-    return expert_call(
+    return kernel_call(
         functools.partial(weights_kernel, groups),
         "expert_weights",
-        experts, specs, outs, shapes, scratch, flops, moved,
-        (half, slots, gates, down_w) + tuple(g_parts) + tuple(far) + tuple(near),
+        (experts,), specs, outs, shapes, [pltpu.VMEM((total, width), bfloat)],
+        2 * experts * total * width * hidden * 4,
+        2 * experts * (5 * width * hidden // 2 + 5 * total * width // 2 + 7 * total * hidden),
+        40,
+        (half, slots, gates, down_w) + tuple(far) + tuple(near)
+        + tuple(near_x) + tuple(near_g) + tuple(far_x) + tuple(far_g),
+        prefetch=1,
     )
 
 
@@ -449,21 +477,31 @@
     return jnp.concatenate([jnp.where(first, mine, other), jnp.where(first, other, mine)], axis=0)
 
 
-def both_halves(mine_groups):
-    parts = []
-    for mine in mine_groups:
-        parts += [mine, swap(mine)]
-    return parts
-
-
-def combine_groups(mine, other):
-    total = None
-    for group in range(mine.shape[0]):
-        part = mine[group].astype(single) + swap(other[group]).astype(single)
-        if group:
-            part = to_peer(part.astype(bfloat), "expert", group).astype(single)
-        total = part if total is None else total + part
-    return total
+def all_rows(slots, mine_groups, capacity):
+    return [
+        gather_rows(slots, g, mine, swap(mine), capacity) for g, mine in enumerate(mine_groups)
+    ]
+
+
+def combine_groups(slots, rows, capacity, span):
+    owners = slots.shape[1]
+    parts = {}
+    for group in reversed(range(owners)):
+        mine, other = return_rows(slots, group, rows, capacity, span)
+        parts[group] = mine.astype(single) + swap(other).astype(single)
+    if owners != 4:
+        total = parts[0]
+        for step in range(1, owners):
+            total = total + to_peer(parts[step].astype(bfloat), "expert", step).astype(single)
+        return total
+    cut = span // 2
+    far = parts[3].astype(bfloat)
+    low = to_peer(far[:cut], "expert", 1).astype(single)
+    high = to_peer(far[cut:], "expert", 2).astype(single)
+    first = jnp.concatenate([parts[1][:cut], parts[1][cut:] + high], axis=0).astype(bfloat)
+    second = jnp.concatenate([parts[2][:cut] + low, parts[2][cut:]], axis=0).astype(bfloat)
+    first, second = to_peer(first, "expert", 1), to_peer(second, "expert", 2)
+    return parts[0] + first.astype(single) + second.astype(single)
 
 
 def on_device(
@@ -541,6 +579,7 @@
     value_matrix = value_unprojected.astype(bfloat)
     outputs, log_sums = lax.map(attend_forward, (queries, key_matrix, value_matrix))
     attn_low = outputs.reshape(rows_dev, heads_local * HEAD_DIMENSION).astype(bfloat)
+    attn_low = after(attn_low, slots, valid_count)
     attn_part = jnp.dot(attn_low, w_out, preferred_element_type=single)
 
     hidden_first = mine_of(inputs) + mine_of(attn_part) + swap(other_of(attn_part))
@@ -558,18 +597,19 @@
         local = lax.dynamic_slice_in_dim(stacked, at_ex * experts_local, experts_local, 1)
         return jnp.concatenate([local, swap(local)], axis=2).transpose(1, 0, 2)
 
+    near_tokens = gather_tokens(moe_in)
     near_gates = local_gates(gates)
-    near_x = both_halves(gather_groups(moe_in))
-    near_rows, gate_pre, up_pre, part_mine, part_other = expert_forward(
-        half, slots[0], near_gates, (w_gate, w_up, w_down), near_x, capacity
-    )
-    far_gates = local_gates(to_mirror(gates))
-    far_x = both_halves(gather_groups(to_mirror(moe_in)))
-    far_rows, far_gate_pre, far_up_pre = expert_forward(
-        half, slots[1], far_gates, (w_gate, w_up), far_x, capacity
-    )
-
-    layer_out = hidden_first + combine_groups(part_mine, part_other)
+    near_x = all_rows(slots[0], near_tokens, capacity)
+    gate_pre, up_pre, expert_out = expert_forward(
+        slots[0], near_gates, (w_gate, w_up, w_down), near_x
+    )
+    far_gates = local_gates(after(to_mirror(gates), near_gates))
+    far_x = all_rows(
+        slots[1], gather_tokens(after(to_mirror(moe_in), near_tokens[-1])), capacity
+    )
+    far_gate_pre, far_up_pre = expert_forward(slots[1], far_gates, (w_gate, w_up), far_x)
+
+    layer_out = hidden_first + combine_groups(slots[0], expert_out, capacity, span)
     rows_wanted = mine_of(teacher_rows[0])
     chooser = (rows_wanted[:, None] == jnp.arange(rows_dev, dtype=jnp.int32)).astype(bfloat)
     target = jnp.dot(chooser, teacher, preferred_element_type=single)
@@ -578,22 +618,25 @@
     block_out = assemble(layer_low, swap(layer_low))
 
     grad_low = grad_layer.astype(bfloat)
-    near_g = both_halves(gather_groups(grad_low))
-    near_grad, hidden_low, grad_gate_pre, grad_up_pre, grad_gates, part_mine, part_other = (
-        expert_backward(
-            half, slots[0], near_gates, (w_gate, w_up, w_down), near_g, gate_pre, up_pre, capacity
-        )
-    )
-    far_g = both_halves(gather_groups(to_mirror(grad_low)))
+    near_grads = gather_tokens(grad_low)
+    near_g = all_rows(slots[0], near_grads, capacity)
+    hidden_low, grad_gate_pre, grad_up_pre, grad_gates, grad_rows = expert_backward(
+        slots[0], near_gates, (w_gate, w_up, w_down), gate_pre, up_pre, near_g
+    )
+    far_g = all_rows(
+        slots[1], gather_tokens(after(to_mirror(grad_low), near_grads[-1])), capacity
+    )
     d_gate, d_up, d_down = expert_weights(
         half,
         slots[1],
         far_gates,
         w_down,
+        (far_gate_pre, far_up_pre),
+        (hidden_low, grad_gate_pre, grad_up_pre),
+        near_x,
+        near_g,
+        far_x,
         far_g,
-        (far_gate_pre, far_up_pre, far_rows),
-        (near_rows, near_grad, hidden_low, grad_gate_pre, grad_up_pre),
-        capacity,
     )
 
     grad_gates = grad_gates.transpose(1, 0, 2)
@@ -609,7 +652,7 @@
     inner = jnp.sum(gates * grad_gates, axis=0, keepdims=True)
     grad_logits = (gates * (grad_gates - inner)).astype(bfloat)
 
-    grad_moe_in = combine_groups(part_mine, part_other) + lax.dot_general(
+    grad_moe_in = combine_groups(slots[0], grad_rows, capacity, span) + lax.dot_general(
         grad_logits, w_router, (((0,), (1,)), ((), ())), preferred_element_type=single
     )
     grad_router_part = lax.dot_general(
@@ -628,7 +671,7 @@
         grad_attn, attn_low, (((0,), (0,)), ((), ())), preferred_element_type=single
     )
     filler = jnp.zeros((model_width, 128 - small.shape[1]), single)
-    first_pack = scatter_dense(
+    first_pack, _ = scatter_dense(
         jnp.concatenate([grad_out_t, small, filler], axis=1).astype(bfloat)
     )
 
@@ -658,10 +701,8 @@
     grad_attn_in = grad_attn_in.astype(single) + swap(grad_attn_in).astype(single)
     grad_first, grad_norm_attn_part = rms_backward(inputs, inverse_first, norm_attn, grad_attn_in)
     grad_tokens = grad_hidden_first + grad_first
-    tail = jnp.concatenate(
-        [grad_norm_attn_part[:, None], jnp.zeros((model_width, 127), single)], axis=1
-    )
-    second_pack = scatter_dense(jnp.concatenate([grad_qkv, tail], axis=1).astype(bfloat))
+    second_pack, sent = scatter_dense(grad_qkv.astype(bfloat))
+    grad_norm_attn, _ = scatter_dense(grad_norm_attn_part, single)
 
     at_shard = at_dp % shards
 
@@ -671,7 +712,7 @@
         for step in range(shards):
             part = lax.dynamic_slice_in_dim(value, (at_shard ^ step) * size, size, axis)
             if step:
-                part = to_peer(part, "dp", step)
+                part = after(to_peer(part, "dp", step), *sent)
             part = part.astype(single)
             total = part if total is None else total + part
         return total
@@ -679,11 +720,11 @@
     return (
         block_out,
         grad_tokens,
-        second_pack[:, query_width + 2 * key_width],
+        grad_norm_attn,
         first_pack[:, query_width + all_experts],
         second_pack[:, :query_width],
         second_pack[:, query_width : query_width + key_width],
-        second_pack[:, query_width + key_width : query_width + 2 * key_width],
+        second_pack[:, query_width + key_width :],
         first_pack[:, :query_width].T,
         first_pack[:, query_width : query_width + all_experts],
         scatter_experts(d_gate, 1),

time: 725 us -> 688 us (0.949)
  waiting for transfers between devices: 245 us -> 196 us
  Pallas kernels: 199 us -> 173 us
  starting transfers between devices: 76.1 us -> 99.8 us
  local copies, waits for them, and re-layouts: 70.5 us -> 92.9 us
  other arithmetic: 74.8 us -> 65.2 us
    ppermute x49 -> x61, waiting for transfers between devices: 243 us -> 189 us  [to_peer(): lax.ppermute(value, axis, [(i, i ^ step) for i in range(lax.axis_size(axi...]
    unnamed x179 -> x247, local copies, waits for them, and re-layouts: 15.5 us -> 51.5 us
    pallas_call x4 -> x28, Pallas kernels: 199 us -> 173 us  [kernel_call(): pl.pallas_call(kernel, name=name, grid_spec=pltpu.PrefetchScalarGridSpec(...]
    ppermute x49 -> x61, starting transfers between devices: 57.3 us -> 82.5 us  [to_peer(): lax.ppermute(value, axis, [(i, i ^ step) for i in range(lax.axis_size(axi...]
    convert_element_type x3 -> x2, other arithmetic: 8.82 us -> 1.56 us  [combine_groups(): far = parts[3].astype(bfloat)]
  transfers between devices with their start and end apart: 86 -> 98, of which waited for: 24 -> 29; matrix products, arithmetic and copies ran while one was open for 21% -> 22% of each run, Pallas kernels for 28% -> 26%
where the time goes in v2:
time: 688 us; the launch traced here: 679 us
  waiting for transfers between devices  196 us (28%)
  Pallas kernels  173 us (25%)
  starting transfers between devices  99.8 us (15%)
  local copies, waits for them, and re-layouts  92.9 us (14%)
  other arithmetic  65.2 us (9%)
  matrix products  47.6 us (7%)
    ppermute x61, waiting for transfers between devices, to_peer(): lax.ppermute(value, axis, [(i, i ^ step) for i in range(lax.axis_size(axi...  189 us
    pallas_call x28, Pallas kernels, kernel_call(): pl.pallas_call(kernel, name=name, grid_spec=pltpu.PrefetchScalarGridSpec(...  173 us
    ppermute x61, starting transfers between devices, to_peer(): lax.ppermute(value, axis, [(i, i ^ step) for i in range(lax.axis_size(axi...  82.5 us
    unnamed x247, local copies, waits for them, and re-layouts  51.5 us
  transfers between devices with their start and end apart: 98, of which 29 were waited for; matrix products, arithmetic and copies ran while one was open for 22% of the time, Pallas kernels for 26%

profile of v2, /device:TPU:0, one launch (start us, length us, event | category | flops | bytes accessed | tf_op | source)
XLA Modules:
  0.0 679.0 jit_solution(11137340303597650956)
XLA Ops:
  1.5 5.0 collective-permute-start
  49.0 17.1 %collective-permute-done.16.mine = bf16[256,1536]{1,0:T(8,128)(2,1)S(1)} collective-permute-done((bf16[256,1536]{1,0:T(8,128)(2,1)S(1)}, bf16[256,1536]{1,0:T(8,128)(2,1)S(1)}, u32[]{:S(2)}, u32[]{:S(2)}) %collective-permute-start.16) | collective-permute-done | bytes 786464 | tf_op jit(solution)/shard_map/ppermute | solution.py:26
  73.6 5.2 collective-permute-done.9
  96.8 22.4 %expert_forward.1 = (f32[10,512,256]{2,1,0:T(8,128)S(1)}, f32[10,512,256]{2,1,0:T(8,128)}, bf16[10,512,1536]{2,1,0:T(8,128)(2,1)}) custom-call(s32[10,4,512]{2,1,0:T(4,128)S(1)} %get-tuple-element.294.slots_ref, f32[10,4,512]{2,1,0:T(4,128)S(1)} %copy.112.gates_ref, bf16[10,1536,256]{2,1,0:T(8,128)(2,1)} %gate_w.5, bf16[10,1536,256]{2,1,0:T(8,128)(2,1)} %up_w.5, ...), custom_call_target="tpu_custom_call" | custom-call | flops 12079595520 | bytes 65536000 | tf_op jit(solution)/shard_map/expert_forward/pallas_call | solution.py:206
  119.3 7.4 %copy-done.1 = bf16[10,512,1536]{2,1,0:T(8,128)(2,1)S(1)} copy-done((bf16[10,512,1536]{2,1,0:T(8,128)(2,1)S(1)}, bf16[10,512,1536]{2,1,0:T(8,128)(2,1)}, u32[]{:S(2)}) %copy-start.1) | copy-done | bytes 15728664
  126.6 4.0 return_rows.11
  141.0 5.5 copy-done.2
  162.9 22.5 %collective-permute-done.27 = bf16[128,1536]{1,0:T(8,128)(2,1)S(1)} collective-permute-done((bf16[128,1536]{1,0:T(8,128)(2,1)S(1)}, bf16[128,1536]{1,0:T(8,128)(2,1)S(1)}, u32[]{:S(2)}, u32[]{:S(2)}) %collective-permute-start.27) | collective-permute-done | bytes 393248 | tf_op jit(solution)/shard_map/ppermute | solution.py:26
  186.9 9.2 %collective-permute-done.24 = bf16[128,1536]{1,0:T(8,128)(2,1)S(1)} collective-permute-done((bf16[128,1536]{1,0:T(8,128)(2,1)S(1)}, bf16[128,1536]{1,0:T(8,128)(2,1)S(1)}, u32[]{:S(2)}, u32[]{:S(2)}) %collective-permute-start.24) | collective-permute-done | bytes 393248 | tf_op jit(solution)/shard_map/ppermute | solution.py:26
  206.0 10.9 %collective-permute-done.81.mine = bf16[256,1536]{1,0:T(8,128)(2,1)} collective-permute-done((bf16[256,1536]{1,0:T(8,128)(2,1)}, bf16[256,1536]{1,0:T(8,128)(2,1)}, u32[]{:S(2)}, u32[]{:S(2)}) %collective-permute-start.81) | collective-permute-done | bytes 786464 | tf_op jit(solution)/shard_map/ppermute | solution.py:26
  220.2 11.3 %collective-permute-done.28 = bf16[256,1536]{1,0:T(8,128)(2,1)} collective-permute-done((bf16[256,1536]{1,0:T(8,128)(2,1)}, bf16[256,1536]{1,0:T(8,128)(2,1)}, u32[]{:S(2)}, u32[]{:S(2)}) %collective-permute-start.28) | collective-permute-done | bytes 786464 | tf_op jit(solution)/shard_map/ppermute | solution.py:26
  232.0 4.8 fusion.117
  250.1 7.2 %collective-permute-done.33.mine = bf16[256,1536]{1,0:T(8,128)(2,1)} collective-permute-done((bf16[256,1536]{1,0:T(8,128)(2,1)}, bf16[256,1536]{1,0:T(8,128)(2,1)}, u32[]{:S(2)}, u32[]{:S(2)}) %collective-permute-start.33) | collective-permute-done | bytes 786464 | tf_op jit(solution)/shard_map/ppermute | solution.py:26
  262.8 4.9 gather_rows.26.refs_2_.refs_13_
  270.5 4.2 gather_rows.27.refs_3_.refs_14_
  280.0 14.8 %expert_forward_far.1 = (f32[10,512,256]{2,1,0:T(8,128)S(1)}, f32[10,512,256]{2,1,0:T(8,128)}) custom-call(s32[10,4,512]{2,1,0:T(4,128)S(1)} %get-tuple-element.293.slots_ref, f32[10,4,512]{2,1,0:T(4,128)S(1)} %maximum_bitcast_fusion.4.gates_ref, bf16[10,1536,256]{2,1,0:T(8,128)(2,1)} %gate_w.5, bf16[10,1536,256]{2,1,0:T(8,128)(2,1)} %up_w.5, ...), custom_call_target="tpu_custom_call" | custom-call | flops 8053063680 | bytes 41943040 | tf_op jit(solution)/shard_map/expert_forward_far/pallas_call | solution.py:206
  294.7 4.1 gather_rows.20.refs_0_.refs_7_
  305.5 4.1 gather_rows.22.refs_2_.refs_9_
  315.9 28.9 %expert_backward.1 = (bf16[10,512,256]{2,1,0:T(8,128)(2,1)S(1)}, bf16[10,512,256]{2,1,0:T(8,128)(2,1)S(1)}, bf16[10,512,256]{2,1,0:T(8,128)(2,1)S(1)}, f32[10,4,512]{2,1,0:T(4,128)S(1)}, bf16[10,512,1536]{2,1,0:T(8,128)(2,1)}) custom-call(s32[10,4,512]{2,1,0:T(4,128)S(1)} %get-tuple-element.294.slots_ref, f32[10,4,512]{2,1,0:T(4,128)S(1)} %copy.112.gates_ref, ...), custom_call_target="tpu_custom_call" | custom-call | flops 12079595520 | bytes 73400320 | tf_op jit(solution)/shard_map/expert_backward/pallas_call | solution.py:206
  344.8 8.2 %copy-done.3 = bf16[10,512,1536]{2,1,0:T(8,128)(2,1)S(1)} copy-done((bf16[10,512,1536]{2,1,0:T(8,128)(2,1)S(1)}, bf16[10,512,1536]{2,1,0:T(8,128)(2,1)}, u32[]{:S(2)}) %copy-start.3) | copy-done | bytes 15728664
  427.1 27.4 %expert_weights.1 = (bf16[10,768,256]{2,1,0:T(8,128)(2,1)S(1)}, bf16[10,768,256]{2,1,0:T(8,128)(2,1)}, bf16[10,256,768]{2,1,0:T(8,128)(2,1)}) custom-call(s32[1]{0:T(128)} %bitcast.83.half_ref, s32[10,4,512]{2,1,0:T(4,128)S(1)} %get-tuple-element.293.slots_ref, f32[10,4,512]{2,1,0:T(4,128)S(1)} %maximum_bitcast_fusion.4.gates_ref, ...), custom_call_target="tpu_custom_call" | custom-call | flops 16106127360 | bytes 77332480 | tf_op jit(solution)/shard_map/expert_weights/pallas_call | solution.py:206
  455.9 10.5 %collective-permute-start.95 = (bf16[10,384,256]{2,1,0:T(8,128)(2,1)}, bf16[10,384,256]{2,1,0:T(8,128)(2,1)}, u32[]{:S(2)}, u32[]{:S(2)}) collective-permute-start(bf16[10,384,256]{2,1,0:T(8,128)(2,1)} %constant_dynamic-slice_fusion.2), channel_id=1, source_target_pairs={{0,8},{8,0},{16,24},{24,16},{1,9},{9,1},{17,25},{25,17},{2,10},{10... | collective-permute-start | bytes 5898248 | tf_op jit(solution)/shard_map/ppermute | solution.py:26
  468.1 4.0 fusion.112
  486.3 10.8 %fusion = (f32[4,3,512]{2,1,0:T(4,128)S(1)}, f32[4,512,512,3]{2,1,3,0:T(8,128)}) fusion(f32[4,512,512,3]{2,1,3,0:T(8,128)} %copy-done.55, f32[4,3,512]{2,1,0:T(4,128)S(1)} %log_add_fusion, pred[512,512]{0,1:T(8,128)(4,1)S(1)} %copy-done.63, bf16[512,4,64,1]{0,2,3,1:T(8,128)(2,1)} %bitcast.248, bf16[512,4,3,64]{0,3,2,1:T(8,128)(2,1)S(1)} %bitcast.234), kind=kOutput, calls=%fused_computation.2 | convolution fusion | flops 415229952 | bytes 26525696 | tf_op jit(solution)/shard_map/while/body/eval_jaxpr/while/body/eval_jaxpr/qkge,tke->kgqt/dot_general | solution.py:445
  499.0 6.9 %fusion.2 = bf16[4,3,512,512]{2,3,1,0:T(8,128)(2,1)S(1)} fusion(f32[4,512,512,3]{2,1,3,0:T(8,128)} %get-tuple-element.325, f32[4,512,512,3]{2,1,3,0:T(8,128)S(1)} %bitcast.228, f32[4,3,512]{2,1,0:T(4,128)S(1)} %get-tuple-element.324, f32[4,3,512]{2,1,0:T(4,128)S(1)} %log_add_fusion, pred[512,512]{0,1:T(8,128)(4,1)S(1)} %copy-done.63), kind=kLoop, calls=%fused_computation.4 | loop fusion | flops 15728640 | bytes 31768576 | tf_op jit(solution)/shard_map/while/body/eval_jaxpr/while/body/eval_jaxpr/convert_element_type | solution.py:449
  530.2 22.4 %collective-permute-done.96 = bf16[10,384,256]{2,1,0:T(8,128)(2,1)} collective-permute-done((bf16[10,384,256]{2,1,0:T(8,128)(2,1)}, bf16[10,384,256]{2,1,0:T(8,128)(2,1)}, u32[]{:S(2)}, u32[]{:S(2)}) %collective-permute-start.96) | collective-permute-done | bytes 1966112 | tf_op jit(solution)/shard_map/ppermute | solution.py:26
  553.9 39.2 %collective-permute-done.97 = bf16[10,256,384]{2,1,0:T(8,128)(2,1)} collective-permute-done((bf16[10,256,384]{2,1,0:T(8,128)(2,1)}, bf16[10,256,384]{2,1,0:T(8,128)(2,1)}, u32[]{:S(2)}, u32[]{:S(2)}) %collective-permute-start.97) | collective-permute-done | bytes 1966112 | tf_op jit(solution)/shard_map/ppermute | solution.py:26
  604.6 6.8 collective-permute-done.60
  620.9 5.2 collective-permute-start.63
  639.0 4.4 collective-permute-done.71
  643.4 12.7 %collective-permute-done.70 = bf16[96,1280]{1,0:T(8,128)(2,1)S(1)} collective-permute-done((bf16[96,1280]{1,0:T(8,128)(2,1)}, bf16[96,1280]{1,0:T(8,128)(2,1)S(1)}, u32[]{:S(2)}, u32[]{:S(2)}) %collective-permute-start.70) | collective-permute-done | bytes 245792 | tf_op jit(solution)/shard_map/ppermute | solution.py:26
  672.0 6.0 fusion.15
  (610 shorter events, 316.9 us)
Async XLA Ops:
  1.5 31.9 %collective-permute-start = (s32[8,512]{1,0:T(8,128)S(1)}, s32[8,512]{1,0:T(8,128)S(1)}, u32[]{:S(2)}, u32[]{:S(2)}) collective-permute-start(s32[8,512]{1,0:T(8,128)S(1)} %get-tuple-element.302), channel_id=1, source_target_pairs={{0,24},{8,16},{16,8},{24,0},{1,25},{9,17},{17,9},{25,1},{2,26},{10... | collective-permute-start | bytes 49160 | tf_op jit(solution)/shard_map/ppermute | solution.py:31
  84.8 56.2 %collective-permute-start.77 = (bf16[256,1536]{1,0:T(8,128)(2,1)S(1)}, bf16[256,1536]{1,0:T(8,128)(2,1)}, u32[]{:S(2)}, u32[]{:S(2)}) collective-permute-start(bf16[256,1536]{1,0:T(8,128)(2,1)S(1)} %multiply_convert_fusion.mine), channel_id=1, source_target_pairs={{0,24},{8,16},{16,8},{24,0},{1,25},{9,17},{17,9},{25,1},{2,26},{10... | collective-permute-start | bytes 2359304 | tf_op jit(solution)/shard_map/ppermute | solution.py:31
  131.5 25.3 %collective-permute-start.26 = (bf16[256,1536]{1,0:T(8,128)(2,1)}, bf16[256,1536]{1,0:T(8,128)(2,1)}, u32[]{:S(2)}, u32[]{:S(2)}) collective-permute-start(bf16[256,1536]{1,0:T(8,128)(2,1)} %get-tuple-element.162), channel_id=1, source_target_pairs={{0,1},{1,0},{2,3},{3,2},{4,5},{5,4},{6,7},{7,6},{8,9},{9,8},{10,11... | collective-permute-start | bytes 2359304 | tf_op jit(solution)/shard_map/ppermute | solution.py:22
  137.5 60.2 %collective-permute-start.73 = (f32[40,256]{1,0:T(8,128)}, f32[40,256]{1,0:T(8,128)}, u32[]{:S(2)}, u32[]{:S(2)}) collective-permute-start(f32[40,256]{1,0:T(8,128)} %collective-permute-done.72), channel_id=1, source_target_pairs={{0,2},{2,0},{4,6},{6,4},{1,3},{3,1},{5,7},{7,5},{8,10},{10,8},{12,... | collective-permute-start | bytes 122888 | tf_op jit(solution)/shard_map/ppermute | solution.py:26
  138.0 59.6 %collective-permute-start.74 = (f32[40,256]{1,0:T(8,128)}, f32[40,256]{1,0:T(8,128)}, u32[]{:S(2)}, u32[]{:S(2)}) collective-permute-start(f32[40,256]{1,0:T(8,128)} %collective-permute-done.72), channel_id=1, source_target_pairs={{0,4},{2,6},{4,0},{6,2},{1,5},{3,7},{5,1},{7,3},{8,12},{10,14},{12... | collective-permute-start | bytes 122888 | tf_op jit(solution)/shard_map/ppermute | solution.py:26
  138.5 60.7 %collective-permute-start.75 = (f32[40,256]{1,0:T(8,128)}, f32[40,256]{1,0:T(8,128)}, u32[]{:S(2)}, u32[]{:S(2)}) collective-permute-start(f32[40,256]{1,0:T(8,128)} %collective-permute-done.72), channel_id=1, source_target_pairs={{0,6},{2,4},{4,2},{6,0},{1,7},{3,5},{5,3},{7,1},{8,14},{10,12},{12... | collective-permute-start | bytes 122888 | tf_op jit(solution)/shard_map/ppermute | solution.py:26
  156.8 61.1 %collective-permute-start.79 = (bf16[256,1536]{1,0:T(8,128)(2,1)}, bf16[256,1536]{1,0:T(8,128)(2,1)}, u32[]{:S(2)}, u32[]{:S(2)}) collective-permute-start(bf16[256,1536]{1,0:T(8,128)(2,1)} %collective-permute-done.77.mine), channel_id=1, source_target_pairs={{0,2},{2,0},{4,6},{6,4},{1,3},{3,1},{5,7},{7,5},{8,10},{10,8},{12,... | collective-permute-start | bytes 2359304 | tf_op jit(solution)/shard_map/ppermute | solution.py:26
  197.6 33.9 %collective-permute-start.28 = (bf16[256,1536]{1,0:T(8,128)(2,1)}, bf16[256,1536]{1,0:T(8,128)(2,1)}, u32[]{:S(2)}, u32[]{:S(2)}) collective-permute-start(bf16[256,1536]{1,0:T(8,128)(2,1)} %pad_maximum_fusion.5), channel_id=1, source_target_pairs={{0,4},{2,6},{4,0},{6,2},{1,5},{3,7},{5,1},{7,3},{8,12},{10,14},{12... | collective-permute-start | bytes 2359304 | tf_op jit(solution)/shard_map/ppermute | solution.py:26
  199.2 32.8 %collective-permute-start.25 = (bf16[256,1536]{1,0:T(8,128)(2,1)}, bf16[256,1536]{1,0:T(8,128)(2,1)}, u32[]{:S(2)}, u32[]{:S(2)}) collective-permute-start(bf16[256,1536]{1,0:T(8,128)(2,1)} %pad_maximum_fusion.4), channel_id=1, source_target_pairs={{0,2},{2,0},{4,6},{6,4},{1,3},{3,1},{5,7},{7,5},{8,10},{10,8},{12,... | collective-permute-start | bytes 2359304 | tf_op jit(solution)/shard_map/ppermute | solution.py:26
  216.9 24.4 %collective-permute-start.76 = (f32[4,10,256]{2,0,1:T(4,128)S(1)}, f32[4,10,256]{2,0,1:T(4,128)S(1)}, u32[]{:S(2)}, u32[]{:S(2)}) collective-permute-start(f32[4,10,256]{2,0,1:T(4,128)S(1)} %fusion.73), channel_id=1, source_target_pairs={{0,1},{1,0},{2,3},{3,2},{4,5},{5,4},{6,7},{7,6},{8,9},{9,8},{10,11... | collective-permute-start | bytes 122888 | tf_op jit(solution)/shard_map/ppermute | solution.py:22
  232.0 27.0 %collective-permute-start.80 = (bf16[256,1536]{1,0:T(8,128)(2,1)}, bf16[256,1536]{1,0:T(8,128)(2,1)}, u32[]{:S(2)}, u32[]{:S(2)}) collective-permute-start(bf16[256,1536]{1,0:T(8,128)(2,1)} %collective-permute-done.79.mine), channel_id=1, source_target_pairs={{0,1},{1,0},{2,3},{3,2},{4,5},{5,4},{6,7},{7,6},{8,9},{9,8},{10,11... | collective-permute-start | bytes 2359304 | tf_op jit(solution)/shard_map/ppermute | solution.py:22
  241.3 29.1 %collective-permute-start.85 = (bf16[256,1536]{1,0:T(8,128)(2,1)}, bf16[256,1536]{1,0:T(8,128)(2,1)}, u32[]{:S(2)}, u32[]{:S(2)}) collective-permute-start(bf16[256,1536]{1,0:T(8,128)(2,1)} %constant_dynamic-update-slice_fusion.4.mine), channel_id=1, source_target_pairs={{0,1},{1,0},{2,3},{3,2},{4,5},{5,4},{6,7},{7,6},{8,9},{9,8},{10,11... | collective-permute-start | bytes 2359304 | tf_op jit(solution)/shard_map/ppermute | solution.py:22
  242.7 25.1 %collective-permute-start.31 = (bf16[256,1536]{1,0:T(8,128)(2,1)}, bf16[256,1536]{1,0:T(8,128)(2,1)}, u32[]{:S(2)}, u32[]{:S(2)}) collective-permute-start(bf16[256,1536]{1,0:T(8,128)(2,1)} %get-tuple-element.322.mine), channel_id=1, source_target_pairs={{0,2},{2,0},{4,6},{6,4},{1,3},{3,1},{5,7},{7,5},{8,10},{10,8},{12,... | collective-permute-start | bytes 2359304 | tf_op jit(solution)/shard_map/ppermute | solution.py:26
  276.7 28.9 %collective-permute-start.34 = (bf16[256,1536]{1,0:T(8,128)(2,1)}, bf16[256,1536]{1,0:T(8,128)(2,1)S(1)}, u32[]{:S(2)}, u32[]{:S(2)}) collective-permute-start(bf16[256,1536]{1,0:T(8,128)(2,1)} %collective-permute-done.33.mine), channel_id=1, source_target_pairs={{0,1},{1,0},{2,3},{3,2},{4,5},{5,4},{6,7},{7,6},{8,9},{9,8},{10,11... | collective-permute-start | bytes 2359304 | tf_op jit(solution)/shard_map/ppermute | solution.py:22
  279.8 31.7 %collective-permute-start.37 = (bf16[256,1536]{1,0:T(8,128)(2,1)S(1)}, bf16[256,1536]{1,0:T(8,128)(2,1)S(1)}, u32[]{:S(2)}, u32[]{:S(2)}) collective-permute-start(bf16[256,1536]{1,0:T(8,128)(2,1)S(1)} %constant_dynamic-update-slice_fusion.2.mine), channel_id=1, source_target_pairs={{0,1},{1,0},{2,3},{3,2},{4,5},{5,4},{6,7},{7,6},{8,9},{9,8},{10,11... | collective-permute-start | bytes 2359304 | tf_op jit(solution)/shard_map/ppermute | solution.py:22
  298.9 75.3 %collective-permute-start.87 = (bf16[256,1536]{1,0:T(8,128)(2,1)}, bf16[256,1536]{1,0:T(8,128)(2,1)}, u32[]{:S(2)}, u32[]{:S(2)}) collective-permute-start(bf16[256,1536]{1,0:T(8,128)(2,1)} %collective-permute-done.86.mine), channel_id=1, source_target_pairs={{0,1},{1,0},{2,3},{3,2},{4,5},{5,4},{6,7},{7,6},{8,9},{9,8},{10,11... | collective-permute-start | bytes 2359304 | tf_op jit(solution)/shard_map/ppermute | solution.py:22
  299.4 82.7 %collective-permute-start.88 = (bf16[256,1536]{1,0:T(8,128)(2,1)}, bf16[256,1536]{1,0:T(8,128)(2,1)S(1)}, u32[]{:S(2)}, u32[]{:S(2)}) collective-permute-start(bf16[256,1536]{1,0:T(8,128)(2,1)} %collective-permute-done.86.mine), channel_id=1, source_target_pairs={{0,2},{2,0},{4,6},{6,4},{1,3},{3,1},{5,7},{7,5},{8,10},{10,8},{12,... | collective-permute-start | bytes 2359304 | tf_op jit(solution)/shard_map/ppermute | solution.py:26
  300.9 80.5 %collective-permute-start.90 = (bf16[256,1536]{1,0:T(8,128)(2,1)}, bf16[256,1536]{1,0:T(8,128)(2,1)S(1)}, u32[]{:S(2)}, u32[]{:S(2)}) collective-permute-start(bf16[256,1536]{1,0:T(8,128)(2,1)} %collective-permute-done.86.mine), channel_id=1, source_target_pairs={{0,4},{2,6},{4,0},{6,2},{1,5},{3,7},{5,1},{7,3},{8,12},{10,14},{12... | collective-permute-start | bytes 2359304 | tf_op jit(solution)/shard_map/ppermute | solution.py:26
  400.0 66.4 %collective-permute-start.38 = (bf16[256,1536]{1,0:T(8,128)(2,1)}, bf16[256,1536]{1,0:T(8,128)(2,1)S(1)}, u32[]{:S(2)}, u32[]{:S(2)}) collective-permute-start(bf16[256,1536]{1,0:T(8,128)(2,1)} %copy-done.51), channel_id=1, source_target_pairs={{0,1},{1,0},{2,3},{3,2},{4,5},{5,4},{6,7},{7,6},{8,9},{9,8},{10,11... | collective-permute-start | bytes 2359304 | tf_op jit(solution)/shard_map/ppermute | solution.py:22
  419.3 47.1 %collective-permute-start.45 = (bf16[256,1536]{1,0:T(8,128)(2,1)S(1)}, bf16[256,1536]{1,0:T(8,128)(2,1)S(1)}, u32[]{:S(2)}, u32[]{:S(2)}) collective-permute-start(bf16[256,1536]{1,0:T(8,128)(2,1)S(1)} %pad_maximum_fusion.7), channel_id=1, source_target_pairs={{0,4},{2,6},{4,0},{6,2},{1,5},{3,7},{5,1},{7,3},{8,12},{10,14},{12... | collective-permute-start | bytes 2359304 | tf_op jit(solution)/shard_map/ppermute | solution.py:26
  422.3 44.2 %collective-permute-start.42 = (bf16[256,1536]{1,0:T(8,128)(2,1)S(1)}, bf16[256,1536]{1,0:T(8,128)(2,1)S(1)}, u32[]{:S(2)}, u32[]{:S(2)}) collective-permute-start(bf16[256,1536]{1,0:T(8,128)(2,1)S(1)} %pad_maximum_fusion.6), channel_id=1, source_target_pairs={{0,2},{2,0},{4,6},{6,4},{1,3},{3,1},{5,7},{7,5},{8,10},{10,8},{12,... | collective-permute-start | bytes 2359304 | tf_op jit(solution)/shard_map/ppermute | solution.py:26
  455.9 73.7 %collective-permute-start.95 = (bf16[10,384,256]{2,1,0:T(8,128)(2,1)}, bf16[10,384,256]{2,1,0:T(8,128)(2,1)}, u32[]{:S(2)}, u32[]{:S(2)}) collective-permute-start(bf16[10,384,256]{2,1,0:T(8,128)(2,1)} %constant_dynamic-slice_fusion.2), channel_id=1, source_target_pairs={{0,8},{8,0},{16,24},{24,16},{1,9},{9,1},{17,25},{25,17},{2,10},{10... | collective-permute-start | bytes 5898248 | tf_op jit(solution)/shard_map/ppermute | solution.py:26
  474.2 78.4 %collective-permute-start.96 = (bf16[10,384,256]{2,1,0:T(8,128)(2,1)}, bf16[10,384,256]{2,1,0:T(8,128)(2,1)}, u32[]{:S(2)}, u32[]{:S(2)}) collective-permute-start(bf16[10,384,256]{2,1,0:T(8,128)(2,1)} %constant_dynamic-slice_fusion.1), channel_id=1, source_target_pairs={{0,8},{8,0},{16,24},{24,16},{1,9},{9,1},{17,25},{25,17},{2,10},{10... | collective-permute-start | bytes 5898248 | tf_op jit(solution)/shard_map/ppermute | solution.py:26
  477.5 115.5 %collective-permute-start.97 = (bf16[10,256,384]{2,1,0:T(8,128)(2,1)}, bf16[10,256,384]{2,1,0:T(8,128)(2,1)}, u32[]{:S(2)}, u32[]{:S(2)}) collective-permute-start(bf16[10,256,384]{2,1,0:T(8,128)(2,1)} %constant_dynamic-slice_fusion), channel_id=1, source_target_pairs={{0,8},{8,0},{16,24},{24,16},{1,9},{9,1},{17,25},{25,17},{2,10},{10... | collective-permute-start | bytes 5898248 | tf_op jit(solution)/shard_map/ppermute | solution.py:26
  478.4 46.0 %collective-permute-start.29 = (bf16[256,1536]{1,0:T(8,128)(2,1)}, bf16[256,1536]{1,0:T(8,128)(2,1)}, u32[]{:S(2)}, u32[]{:S(2)}) collective-permute-start(bf16[256,1536]{1,0:T(8,128)(2,1)} %get-tuple-element.277), channel_id=1, source_target_pairs={{0,1},{1,0},{2,3},{3,2},{4,5},{5,4},{6,7},{7,6},{8,9},{9,8},{10,11... | collective-permute-start | bytes 2359304 | tf_op jit(solution)/shard_map/ppermute | solution.py:22
  479.6 139.0 %collective-permute-start.50 = (f32[256,1536]{1,0:T(8,128)}, f32[256,1536]{1,0:T(8,128)}, u32[]{:S(2)}, u32[]{:S(2)}) collective-permute-start(f32[256,1536]{1,0:T(8,128)} %get-tuple-element.254), channel_id=1, source_target_pairs={{0,1},{1,0},{2,3},{3,2},{4,5},{5,4},{6,7},{7,6},{8,9},{9,8},{10,11... | collective-permute-start | bytes 4718600 | tf_op jit(solution)/shard_map/ppermute | solution.py:22
  524.4 78.1 %collective-permute-start.62 = (bf16[4,96,896]{2,1,0:T(8,128)(2,1)S(1)}, bf16[4,96,896]{2,1,0:T(8,128)(2,1)S(1)}, u32[]{:S(2)}, u32[]{:S(2)}) collective-permute-start(bf16[4,96,896]{2,1,0:T(8,128)(2,1)S(1)} %get-tuple-element.266), channel_id=1, source_target_pairs={{0,6},{2,4},{4,2},{6,0},{1,7},{3,5},{5,3},{7,1},{8,14},{10,12},{12... | collective-permute-start | bytes 2064392 | tf_op jit(solution)/shard_map/ppermute | solution.py:26
  529.6 100.0 %collective-permute-start.68 = (bf16[4,96,1280]{2,1,0:T(8,128)(2,1)S(1)}, bf16[4,96,1280]{2,1,0:T(8,128)(2,1)S(1)}, u32[]{:S(2)}, u32[]{:S(2)}) collective-permute-start(bf16[4,96,1280]{2,1,0:T(8,128)(2,1)S(1)} %get-tuple-element.261), channel_id=1, source_target_pairs={{0,6},{2,4},{4,2},{6,0},{1,7},{3,5},{5,3},{7,1},{8,14},{10,12},{12... | collective-permute-start | bytes 2949128 | tf_op jit(solution)/shard_map/ppermute | solution.py:26
  552.6 51.2 %collective-permute-start.61 = (bf16[4,96,896]{2,1,0:T(8,128)(2,1)S(1)}, bf16[4,96,896]{2,1,0:T(8,128)(2,1)S(1)}, u32[]{:S(2)}, u32[]{:S(2)}) collective-permute-start(bf16[4,96,896]{2,1,0:T(8,128)(2,1)S(1)} %get-tuple-element.267), channel_id=1, source_target_pairs={{0,4},{2,6},{4,0},{6,2},{1,5},{3,7},{5,1},{7,3},{8,12},{10,14},{12... | collective-permute-start | bytes 2064392 | tf_op jit(solution)/shard_map/ppermute | solution.py:26
  602.5 27.1 %collective-permute-start.67 = (bf16[4,96,1280]{2,1,0:T(8,128)(2,1)S(1)}, bf16[4,96,1280]{2,1,0:T(8,128)(2,1)S(1)}, u32[]{:S(2)}, u32[]{:S(2)}) collective-permute-start(bf16[4,96,1280]{2,1,0:T(8,128)(2,1)S(1)} %get-tuple-element.262), channel_id=1, source_target_pairs={{0,4},{2,6},{4,0},{6,2},{1,5},{3,7},{5,1},{7,3},{8,12},{10,14},{12... | collective-permute-start | bytes 2949128 | tf_op jit(solution)/shard_map/ppermute | solution.py:26
  603.8 26.1 %collective-permute-start.66 = (bf16[4,96,1280]{2,1,0:T(8,128)(2,1)S(1)}, bf16[4,96,1280]{2,1,0:T(8,128)(2,1)S(1)}, u32[]{:S(2)}, u32[]{:S(2)}) collective-permute-start(bf16[4,96,1280]{2,1,0:T(8,128)(2,1)S(1)} %get-tuple-element.260), channel_id=1, source_target_pairs={{0,2},{2,0},{4,6},{6,4},{1,3},{3,1},{5,7},{7,5},{8,10},{10,8},{12,... | collective-permute-start | bytes 2949128 | tf_op jit(solution)/shard_map/ppermute | solution.py:26
  629.5 29.6 %collective-permute-start.52 = (bf16[512,1536]{1,0:T(8,128)(2,1)}, bf16[512,1536]{1,0:T(8,128)(2,1)}, u32[]{:S(2)}, u32[]{:S(2)}) collective-permute-start(bf16[512,1536]{1,0:T(8,128)(2,1)} %fusion.19), channel_id=1, source_target_pairs={{0,1},{1,0},{2,3},{3,2},{4,5},{5,4},{6,7},{7,6},{8,9},{9,8},{10,11... | collective-permute-start | bytes 4718600 | tf_op jit(solution)/shard_map/ppermute | solution.py:22
  (185 other events, 1760.3 us)

commit v3 on v0

v3 whole, which is shorter than its diff:
```python
import functools

import jax
import jax.numpy as jnp
from jax import lax
from jax.experimental import pallas as pl
from jax.experimental.pallas import tpu as pltpu
from jax.sharding import PartitionSpec as P

HEAD_DIMENSION = 64
SEQUENCE_LENGTH = 512
ABLK = 256


EPS = 1e-06
VMEM_LIMIT = 56 * 1024 * 1024
THETA = 10000.0
bfloat = jnp.bfloat16
single = jnp.float32


def pass_kernel(*refs):
    pass


def after_all(values, *others):
    anywhere = pl.BlockSpec(memory_space=pl.ANY)
    return pl.pallas_call(
        pass_kernel,
        name="after",
        in_specs=[anywhere] * (len(values) + len(others)),
        out_specs=[anywhere] * len(values),
        out_shape=[jax.ShapeDtypeStruct(value.shape, value.dtype) for value in values],
        input_output_aliases={i: i for i in range(len(values))},
        cost_estimate=pl.CostEstimate(flops=0, bytes_accessed=0, transcendentals=0),
    )(*values, *others)


def after(value, *others):
    return after_all([value], *others)[0] if others else value


def hold_kernel(value_ref, out_ref):
    out_ref[...] = jnp.zeros_like(out_ref)


def hold(value):
    return pl.pallas_call(
        hold_kernel,
        name="hold",
        in_specs=[pl.BlockSpec(memory_space=pl.ANY)],
        out_shape=jax.ShapeDtypeStruct((8, 128), single),
        cost_estimate=pl.CostEstimate(flops=10**12, bytes_accessed=10**9, transcendentals=0),
    )(value)


def swap(value):
    return lax.ppermute(value, "tensor", [(0, 1), (1, 0)])


def to_peer(value, axis, step):
    return lax.ppermute(value, axis, [(i, i ^ step) for i in range(lax.axis_size(axis))])


def to_mirror(value):
    count = lax.axis_size("dp")
    return lax.ppermute(value, "dp", [(i, count - 1 - i) for i in range(count)])


def from_peers(value):
    return [to_peer(value, "expert", s) for s in range(1, lax.axis_size("expert"))]


def halves_kernel(low_ref, high_ref, *refs):
    refs[-2][...] = low_ref[...]
    refs[-1][...] = high_ref[...]


def low_and_high(low, high, *others):
    rows, width = low.shape
    half = jax.ShapeDtypeStruct((rows // 2, width), low.dtype)
    return pl.pallas_call(
        halves_kernel,
        name="halves",
        grid=(1,),
        in_specs=[
            pl.BlockSpec((rows // 2, width), lambda i: (0, 0)),
            pl.BlockSpec((rows // 2, width), lambda i: (1, 0)),
        ]
        + [pl.BlockSpec(memory_space=pl.ANY)] * len(others),
        out_specs=[pl.BlockSpec((rows // 2, width), lambda i: (0, 0))] * 2,
        out_shape=[half, half],
        cost_estimate=pl.CostEstimate(flops=0, bytes_accessed=2**20, transcendentals=0),
    )(low, high, *others)


def spread(value, pause=()):
    own_other = swap(value)
    if lax.axis_size("expert") != 4:
        near = from_peers(value)
        near[0] = after(near[0], own_other, hold(value), *pause)
        return [value, own_other] + [part for mine in near for part in (mine, swap(mine))]
    first, second = to_peer(value, "expert", 1), to_peer(value, "expert", 2)
    for_first, for_second = low_and_high(second, first, own_other, hold(value), *pause)
    low, high = to_peer(for_first, "expert", 1), to_peer(for_second, "expert", 2)
    first_other, second_other = swap(first), swap(second)
    low = after(low, hold(for_first), first_other, second_other)
    third = jnp.concatenate([low, high], axis=0)
    third_other = after(swap(third), hold(third))
    return [value, own_other, first, first_other, second, second_other, third, third_other]


def send_farthest(far):
    cut = far.shape[0] // 2
    low, high = far[:cut], far[cut:]
    return [to_peer(low, "expert", 1), to_peer(high, "expert", 2)], (low, high)


def send_nearer(first, second, came):
    cut = came[0].shape[0]
    low, high = came[0].astype(single), came[1].astype(single)
    first = jnp.concatenate([first[:cut], first[cut:] + high], axis=0).astype(bfloat)
    second = jnp.concatenate([second[:cut] + low, second[cut:]], axis=0).astype(bfloat)
    return [to_peer(first, "expert", 1), to_peer(second, "expert", 2)], (first, second)


def sum_at_owners(parts):
    if len(parts) != 4:
        arrived = [to_peer(part.astype(bfloat), "expert", i) for i, part in enumerate(parts[1:], 1)]
        return add_up(parts[0], arrived)
    came, sent = send_farthest(parts[3].astype(bfloat))
    came[0] = after(came[0], hold(sent[0]))
    came, sent = send_nearer(parts[1], parts[2], came)
    came[0] = after(came[0], hold(sent[0]))
    return add_up(parts[0], came)


def add_up(own, arrived):
    total = own.astype(single)
    for part in arrived:
        total = total + part.astype(single)
    return total


def sum_all(value, axes):
    for axis in axes:
        step = 1
        while step < lax.axis_size(axis):
            value = value + to_peer(value, axis, step)
            step *= 2
    return value


def over_owners(packed):
    count_dp, count_ex = lax.axis_size("dp"), lax.axis_size("expert")
    at_ex = lax.axis_index("expert")
    block = packed.shape[0] // (count_dp * count_ex)
    cut = packed.reshape(count_dp, count_ex, block, packed.shape[1])
    parts = [
        lax.dynamic_index_in_dim(cut, at_ex ^ step, 1, keepdims=False).astype(single)
        for step in range(count_ex)
    ]
    return sum_at_owners(parts)


def over_dp(total):
    at_dp, count = lax.axis_index("dp"), lax.axis_size("dp")
    parts = {r: lax.dynamic_index_in_dim(total, at_dp ^ r, 0, keepdims=False) for r in range(count)}
    step = 1
    while step < count:
        leaving = [r for r in parts if r & step]
        sent = jnp.concatenate([parts[r].astype(bfloat) for r in leaving], axis=0)
        came = to_peer(sent, "dp", step).astype(single)
        rows = came.shape[0] // len(leaving)
        for i, r in enumerate(leaving):
            parts[r ^ step] = parts[r ^ step] + came[i * rows : (i + 1) * rows]
            del parts[r]
        step *= 2
    return parts[0]


def dot(left, right):
    return lax.dot_general(left, right, (((1,), (0,)), ((), ())), preferred_element_type=single)


def dot_nt(left, right):
    return lax.dot_general(left, right, (((1,), (1,)), ((), ())), preferred_element_type=single)


def dot_tn(left, right):
    return lax.dot_general(left, right, (((0,), (0,)), ((), ())), preferred_element_type=single)


def picks(slot, capacity):
    return slot == lax.broadcasted_iota(jnp.int32, (capacity, slot.shape[1]), 0)


def gather_rows(slots_ref, expert, parts, rows_ref):
    capacity = 2 * rows_ref.shape[0] // len(parts)
    width = rows_ref.shape[1]
    for group in range(len(parts) // 2):
        mine, other = parts[2 * group], parts[2 * group + 1]
        span = mine.shape[0]
        slot = slots_ref[expert, group : group + 1, :]
        picked = picks(slot, capacity).astype(bfloat)
        rows = dot(picked[:, :span], mine[:, :width]) + dot(picked[:, span:], other[:, :width])
        rows_ref[group * capacity : (group + 1) * capacity, :] = rows.astype(bfloat)


def slot_gates(expert, tails, count):
    lane = lax.broadcasted_iota(jnp.int32, tails.shape, 1)
    chosen = (lane == expert) | (lane == expert + count) | (lane == expert + 2 * count)
    return jnp.sum(jnp.where(chosen, tails.astype(single), 0.0), axis=1, keepdims=True)


def half_columns(place_ref, width):
    return pl.ds(pl.multiple_of(place_ref[1] * width, 128), width)


def return_order(groups):
    rest = list(range(1, groups)) + [0]
    return [[3], [1, 2, 0]] if groups == 4 else [rest]


def forward_kernel(count, groups, start, with_out, place_ref, slots_ref, gate_w, up_w, *refs):
    if with_out:
        down_w, refs = refs[0], refs[1:]
    parts, refs = refs[: 2 * groups], refs[2 * groups :]
    gate_ref, up_ref, half_ref, tail_ref, refs = refs[0], refs[1], refs[2], refs[3], refs[4:]
    step = pl.program_id(0)
    rows_ref = refs[-1]
    width = gate_w.shape[1]
    gather_rows(slots_ref, start + step, parts, rows_ref)
    half_ref[0] = rows_ref[:, half_columns(place_ref, half_ref.shape[2])]
    tails = rows_ref[:, width:]
    tail_ref[0] = tails
    rows = rows_ref[:, :width]
    gate_pre = dot(rows, gate_w[0])
    up_pre = dot(rows, up_w[0])
    gate_ref[0] = gate_pre.astype(bfloat)
    up_ref[0] = up_pre.astype(bfloat)
    if with_out:
        gates = slot_gates(place_ref[0] + start + step, tails, count)
        hidden = (gate_pre * jax.nn.sigmoid(gate_pre) * up_pre * gates).astype(bfloat)
        refs[0][0] = dot(hidden, down_w[0]).astype(bfloat)


def hidden_grads(gate_pre, up_pre, gates, grad_hidden):
    sig = jax.nn.sigmoid(gate_pre)
    silu = gate_pre * sig
    hidden = silu * up_pre
    scaled = grad_hidden * gates
    grad_gate_pre = (scaled * up_pre * sig * (1.0 + gate_pre * (1.0 - sig))).astype(bfloat)
    grad_up_pre = (scaled * silu).astype(bfloat)
    return hidden, (hidden * gates).astype(bfloat), grad_gate_pre, grad_up_pre


def backward_kernel(count, groups, place_ref, slots_ref, gate_w, up_w, down_w, gate_ref, up_ref, tail_ref, *refs):
    parts, refs = refs[: 2 * groups], refs[2 * groups :]
    hidden_ref, grad_gate_ref, grad_up_ref, half_ref, refs = refs[0], refs[1], refs[2], refs[3], refs[4:]
    back_ref, rows_ref = refs
    width = gate_w.shape[1]
    step = pl.program_id(0)
    expert = place_ref[0] + step
    gather_rows(slots_ref, step, parts, rows_ref)
    half_ref[0] = rows_ref[:, half_columns(place_ref, half_ref.shape[2])]
    gates = slot_gates(expert, tail_ref[0], count)
    grad_hidden = dot_nt(rows_ref[:, :width], down_w[0])
    hidden, hidden_low, grad_gate_pre, grad_up_pre = hidden_grads(
        gate_ref[0].astype(single), up_ref[0].astype(single), gates, grad_hidden
    )
    hidden_ref[0] = hidden_low
    grad_gate_ref[0] = grad_gate_pre
    grad_up_ref[0] = grad_up_pre
    back = dot_nt(grad_gate_pre, gate_w[0]) + dot_nt(grad_up_pre, up_w[0])
    back_ref[0, :, :width] = back.astype(bfloat)
    tails = rows_ref[:, width:].astype(single)
    lane = lax.broadcasted_iota(jnp.int32, tails.shape, 1)
    inner = jnp.sum(jnp.where(lane < 3, tails, 0.0), axis=1, keepdims=True)
    inner = inner * (place_ref[2] == 0).astype(single)
    grad_logit = gates * (jnp.sum(hidden * grad_hidden, axis=1, keepdims=True) - inner)
    back_ref[0, :, width:] = jnp.where(lane == expert, grad_logit, 0.0).astype(bfloat)


def weights_kernel(count, groups, start, place_ref, slots_ref, down_w, gate_ref, up_ref, tail_ref, *refs):
    hidden_near, gate_near, up_near, near_x, near_g, far_x = refs[:6]
    parts, refs = refs[6 : 6 + 2 * groups], refs[6 + 2 * groups :]
    shards, (rows_ref, full_ref) = refs[:-2], refs[-2:]
    expert = start + pl.program_id(0)
    gather_rows(slots_ref, expert, parts, rows_ref)
    gates = slot_gates(place_ref[0] + expert, tail_ref[0], count)
    grad_hidden = dot_nt(rows_ref[...], down_w[0])
    _, hidden, grad_gate_pre, grad_up_pre = hidden_grads(
        gate_ref[0].astype(single), up_ref[0].astype(single), gates, grad_hidden
    )
    far_g = rows_ref[:, half_columns(place_ref, full_ref.shape[1])]
    far, near = far_x[0], near_x[0]
    sums = (
        dot_tn(far, grad_gate_pre) + dot_tn(near, gate_near[0]),
        dot_tn(far, grad_up_pre) + dot_tn(near, up_near[0]),
        dot_tn(far_g, hidden) + dot_tn(near_g[0], hidden_near[0]),
    )
    for i, value in enumerate(sums):
        full_ref[i] = value.astype(bfloat)
    size = shards[0].shape[2]
    for step, shard in enumerate(shards):
        at = pl.multiple_of((place_ref[3] ^ step) * size, size)
        for i in range(3):
            shard[0, i] = full_ref[i, pl.ds(at, size), :]


def finish_kernel(own_ref, *refs):
    arrived, (d_gate, d_up, d_down) = refs[:-3], refs[-3:]

    def total(i):
        value = own_ref[0, i].astype(single)
        for ref in arrived:
            value = value + ref[0, i].astype(single)
        return value

    d_gate[0] = total(0)
    d_up[0] = total(1)
    d_down[0] = total(2).T


def finish_more_kernel(gate_in, up_in, down_in, own_ref, *refs):
    finish_kernel(own_ref, *refs)


def return_kernel(first, cycle, slots_ref, rows_ref, mine, other, picked_ref):
    experts, capacity, width = rows_ref.shape
    span = mine.shape[1]
    group = (pl.program_id(0) + first) % cycle

    @pl.when(pl.program_id(1) == 0)
    def _():
        for e in range(experts):
            slot = slots_ref[e, pl.ds(group, 1), :]
            picked_ref[e * capacity : (e + 1) * capacity, :] = picks(slot, capacity).astype(bfloat)

    back = dot_tn(picked_ref[...], rows_ref[...].reshape(experts * capacity, width)).astype(bfloat)
    mine[0] = back[:span]
    other[0] = back[span:]


def pack_kernel(lane_at, left, right, left_tail, right_tail, value, base, inverse, out_ref):
    columns = right.shape[1]
    out_ref[:, :columns] = dot_tn(left[...], right[...]).astype(bfloat)
    product = value[...] * base[...].astype(single) * inverse[...]
    high = product.astype(bfloat)
    low = (product - high.astype(single)).astype(bfloat)
    lane = lax.broadcasted_iota(jnp.int32, (product.shape[0], 128), 1)
    chosen = (lane == lane_at).astype(bfloat)
    tail = dot_tn(high, chosen) + dot_tn(low, chosen)
    if lane_at:
        tail = tail + dot_tn(left_tail[...], right_tail[...])
    out_ref[:, columns:] = tail.astype(bfloat)


def kernel_call(kernel, name, grid, in_specs, out_specs, out_shape, scratch, flops, moved, args, prefetch=0, aliases=None):
    return pl.pallas_call(
        kernel,
        name=name,
        grid_spec=pltpu.PrefetchScalarGridSpec(
            num_scalar_prefetch=prefetch,
            grid=grid,
            in_specs=in_specs,
            out_specs=out_specs,
            scratch_shapes=scratch,
        ),
        out_shape=out_shape,
        input_output_aliases=aliases or {},
        compiler_params=pltpu.CompilerParams(
            dimension_semantics=("arbitrary",) * len(grid), vmem_limit_bytes=VMEM_LIMIT
        ),
        cost_estimate=pl.CostEstimate(flops=flops, bytes_accessed=moved, transcendentals=0),
    )(*args)


def per_expert(*shape, start=0):
    return pl.BlockSpec((1,) + shape, lambda e, *_: (e + start,) + (0,) * len(shape))


def once(*shape):
    return pl.BlockSpec(
        shape, lambda e, *_: (0,) * len(shape), pipeline_mode=pl.Buffered(buffer_count=1)
    )


def return_rows(slots, rows, order, capacity, span):
    experts, groups, tokens = slots.shape
    width = rows.shape[2]
    amount, first = len(order), order[0]
    cycle = amount if amount > 1 else groups
    cuts = 2 if width % 256 == 0 else 1
    cut = width // cuts
    part = pl.BlockSpec((1, span, cut), lambda g, n: (g, 0, n))
    return kernel_call(
        functools.partial(return_kernel, first, cycle),
        "return_rows",
        (amount, cuts),
        [
            pl.BlockSpec((experts, groups, tokens), lambda g, n: (0, 0, 0)),
            pl.BlockSpec((experts, capacity, cut), lambda g, n: (0, (g + first) % cycle, n)),
        ],
        [part, part],
        [jax.ShapeDtypeStruct((amount, span, width), bfloat)] * 2,
        [pltpu.VMEM((experts * capacity, tokens), bfloat)],
        2 * amount * experts * capacity * tokens * width,
        2 * amount * (experts * capacity + tokens) * width,
        (slots, rows),
    )


def expert_forward(place, count, slots, weights, parts, capacity, start, experts):
    _, groups, tokens = slots.shape
    span, whole = parts[0].shape
    width, hidden = weights[0].shape[1:]
    with_out = len(weights) == 3
    total = groups * capacity
    specs = [once(*slots.shape)] + [per_expert(width, hidden, start=start)] * 2
    outs = [per_expert(total, hidden)] * 2
    outs += [per_expert(total, width // 2), per_expert(total, whole - width)]
    shapes = [jax.ShapeDtypeStruct((experts, total, hidden), bfloat)] * 2
    shapes += [jax.ShapeDtypeStruct((experts, total, width // 2), bfloat)]
    shapes += [jax.ShapeDtypeStruct((experts, total, whole - width), bfloat)]
    scratch = [pltpu.VMEM((total, whole), bfloat)]
    if with_out:
        specs += [per_expert(hidden, width, start=start)]
        outs += [per_expert(total, width)]
        shapes += [jax.ShapeDtypeStruct((experts, total, width), bfloat)]
    return kernel_call(
        functools.partial(forward_kernel, count, groups, start, with_out),
        "expert_forward" if with_out else "expert_forward_far",
        (experts,), specs + [once(*part.shape) for part in parts], outs, shapes, scratch,
        2 * experts * total * (width * hidden * len(weights) + tokens * whole),
        2 * experts * (len(weights) * width * hidden + total * width + 4 * total * hidden),
        (place, slots) + tuple(weights) + tuple(parts),
        prefetch=1,
    )


def expert_backward(place, count, slots, weights, gate_pre, up_pre, tails, parts, capacity):
    experts, groups, tokens = slots.shape
    span, whole = parts[0].shape
    width, hidden = weights[0].shape[1:]
    total = groups * capacity
    thin = per_expert(total, hidden)
    specs = [once(*slots.shape)] + [per_expert(width, hidden)] * 2
    specs += [per_expert(hidden, width), thin, thin, per_expert(total, tails.shape[2])]
    outs = [thin] * 3 + [per_expert(total, width // 2), per_expert(total, whole)]
    shapes = [jax.ShapeDtypeStruct((experts, total, hidden), bfloat)] * 3
    shapes += [jax.ShapeDtypeStruct((experts, total, width // 2), bfloat)]
    shapes += [jax.ShapeDtypeStruct((experts, total, whole), bfloat)]
    return kernel_call(
        functools.partial(backward_kernel, count, groups),
        "expert_backward",
        (experts,), specs + [once(*part.shape) for part in parts], outs, shapes,
        [pltpu.VMEM((total, whole), bfloat)],
        2 * experts * total * width * (hidden * 3 + tokens),
        2 * experts * (3 * width * hidden + 3 * total * width // 2 + 7 * total * hidden),
        (place, slots) + tuple(weights) + (gate_pre, up_pre, tails) + tuple(parts),
        prefetch=1,
    )


def expert_weights(place, count, slots, down_w, far, near, parts, capacity, start, far_start, experts, shards):
    _, groups, tokens = slots.shape
    hidden, width = down_w.shape[1:]
    total = groups * capacity
    far_pre, (far_tails, far_half) = far[:2], far[2:]
    thin = per_expert(total, hidden, start=far_start)
    wide = per_expert(total, width // 2, start=far_start)
    thin_at = per_expert(total, hidden, start=start)
    wide_at = per_expert(total, width // 2, start=start)
    specs = [once(*slots.shape), per_expert(hidden, width, start=start)]
    specs += [thin, thin, per_expert(total, far_tails.shape[2], start=far_start)] + [thin_at] * 3
    specs += [wide_at, wide_at, wide]
    size = width // (2 * shards)
    return kernel_call(
        functools.partial(weights_kernel, count, groups, start),
        "expert_weights",
        (experts,), specs + [once(*part.shape) for part in parts],
        [per_expert(3, size, hidden)] * shards,
        [jax.ShapeDtypeStruct((experts, 3, size, hidden), bfloat)] * shards,
        [pltpu.VMEM((total, width), bfloat), pltpu.VMEM((3, width // 2, hidden), bfloat)],
        2 * experts * total * width * (hidden * 4 + tokens),
        2 * experts * (5 * width * hidden // 2 + 3 * total * width // 2 + 7 * total * hidden),
        (place, slots, down_w) + tuple(far_pre) + (far_tails,) + tuple(near) + (far_half,) + tuple(parts),
        prefetch=1,
    )


def pack_sums(left, right, tail, value, base, inverse, lane_at):
    tokens, width = left.shape
    columns = right.shape[1]
    left_tail, right_tail = tail if tail else (left, right)
    block = width // 4
    tall = lambda array: pl.BlockSpec((array.shape[0], block), lambda i: (0, i))
    whole = lambda array: pl.BlockSpec(array.shape, lambda i: (0, 0))
    return kernel_call(
        functools.partial(pack_kernel, lane_at),
        "pack_sums",
        (4,),
        [tall(left), whole(right), tall(left_tail), whole(right_tail), tall(value), tall(base), whole(inverse)],
        pl.BlockSpec((block, columns + 128), lambda i: (i, 0)),
        jax.ShapeDtypeStruct((width, columns + 128), bfloat),
        [],
        2 * tokens * width * (columns + 128),
        2 * (tokens * (4 * width + columns) + width * (columns + 128)),
        (left, right, left_tail, right_tail, value, base, inverse),
    )


def finish_weights(experts, start, own, arrived, before):
    some, _, size, hidden = own.shape
    ready = [per_expert(3, size, hidden)] * (1 + len(arrived))
    kernel = finish_kernel if before is None else finish_more_kernel
    kept = [] if before is None else [pl.BlockSpec(memory_space=pl.ANY)] * 3
    return kernel_call(
        kernel,
        "finish_weights",
        (some,),
        kept + ready,
        [per_expert(size, hidden, start=start)] * 2 + [per_expert(hidden, size, start=start)],
        [jax.ShapeDtypeStruct((experts, size, hidden), single)] * 2
        + [jax.ShapeDtypeStruct((experts, hidden, size), single)],
        [],
        3 * some * size * hidden,
        12 * some * size * hidden,
        tuple(before or ()) + (own,) + tuple(arrived),
        aliases={} if before is None else {0: 0, 1: 1, 2: 2},
    )


def rope_tables(length, head_size):
    half_size = head_size // 2
    frequency = THETA ** (-jnp.arange(half_size, dtype=jnp.float32) * 2.0 / head_size)
    angles = jnp.arange(length, dtype=jnp.float32)[:, None] * frequency[None, :]
    return (jnp.cos(angles), jnp.sin(angles))


def apply_rotary(value_matrix, cosine_table, sine_table):
    half_size = value_matrix.shape[-1] // 2
    first_half = value_matrix[..., :half_size]
    second_half = value_matrix[..., half_size:]
    cosine_rows = cosine_table[:, None, :]
    sine_rows = sine_table[:, None, :]
    return jnp.concatenate(
        [
            first_half * cosine_rows - second_half * sine_rows,
            second_half * cosine_rows + first_half * sine_rows,
        ],
        axis=-1,
    )


def rotate_back(grads, cosine_table, sine_table):
    half_size = grads.shape[-1] // 2
    first_half = grads[..., :half_size]
    second_half = grads[..., half_size:]
    cosine_rows = cosine_table[:, None, :]
    sine_rows = sine_table[:, None, :]
    return jnp.concatenate(
        [
            first_half * cosine_rows + second_half * sine_rows,
            second_half * cosine_rows - first_half * sine_rows,
        ],
        axis=-1,
    )


def rms_forward(value_matrix, gain):
    inverse = lax.rsqrt(jnp.mean(value_matrix * value_matrix, axis=-1, keepdims=True) + EPS)
    return (value_matrix * inverse * gain, inverse)


def rms_backward(value_matrix, inverse, gain, grad_normed):
    scaled = grad_normed * gain
    grad_gain = jnp.sum(grad_normed * value_matrix * inverse, axis=0)
    grad_values = inverse * scaled - value_matrix * inverse**3 * jnp.mean(
        scaled * value_matrix, axis=-1, keepdims=True
    )
    return (grad_values, grad_gain)


def masked_scores(query_part, key_matrix, row_begin, length):
    scores = jnp.einsum(
        "qkge,tke->kgqt", query_part, key_matrix, preferred_element_type=jnp.float32
    )
    query_block = (row_begin + jnp.arange(query_part.shape[0], dtype=jnp.int32)) // ABLK
    key_block = jnp.arange(length, dtype=jnp.int32) // ABLK
    allowed = query_block[:, None] >= key_block[None, :]
    return jnp.where(allowed, scores, -1e30)


def attend_forward(args):
    queries, key_matrix, value_matrix = args
    length, kv_heads, head_size = key_matrix.shape
    group_size = queries.shape[1] // kv_heads
    rows_block = min(512, length)
    grouped = queries.reshape(length, kv_heads, group_size, head_size)

    def one_block(row_begin):
        scores = masked_scores(grouped, key_matrix, row_begin, length)
        row_peak = jnp.max(scores, axis=-1, keepdims=True)
        weights = jnp.exp(scores - row_peak)
        totals = jnp.sum(weights, axis=-1, keepdims=True)
        weights_low = (weights / totals).astype(jnp.bfloat16)
        outputs = jnp.einsum(
            "kgqt,tke->qkge", weights_low, value_matrix, preferred_element_type=jnp.float32
        )
        return (
            outputs.reshape(rows_block, kv_heads * group_size * head_size),
            (row_peak + jnp.log(totals))[..., 0],
        )

    outputs, log_sums = lax.map(one_block, jnp.arange(0, length, rows_block, dtype=jnp.int32))
    return (outputs.reshape(length, kv_heads * group_size * head_size), log_sums)


def attend_backward(args):
    queries, key_matrix, value_matrix, log_sums, grad_mixed = args
    length, kv_heads, head_size = key_matrix.shape
    group_size = queries.shape[1] // kv_heads
    rows_block = min(512, length)
    grouped = queries.reshape(length, kv_heads, group_size, head_size)
    grad_grouped = grad_mixed.reshape(length, kv_heads, group_size, head_size)

    def one_block(running, inputs):
        row_begin, block_sums = inputs
        scores = masked_scores(grouped, key_matrix, row_begin, length)
        probs = jnp.exp(scores - block_sums[..., None])
        grad_probs = jnp.einsum(
            "qkge,tke->kgqt", grad_grouped, value_matrix, preferred_element_type=jnp.float32
        )
        row_inner = jnp.sum(probs * grad_probs, axis=-1, keepdims=True)
        grad_scores = (probs * (grad_probs - row_inner)).astype(jnp.bfloat16)
        grad_query = jnp.einsum(
            "kgqt,tke->qkge", grad_scores, key_matrix, preferred_element_type=jnp.float32
        )
        grad_key = running[0] + jnp.einsum(
            "kgqt,qkge->tke", grad_scores, grouped, preferred_element_type=jnp.float32
        )
        grad_value = running[1] + jnp.einsum(
            "kgqt,qkge->tke",
            probs.astype(jnp.bfloat16),
            grad_grouped,
            preferred_element_type=jnp.float32,
        )
        return (
            (grad_key, grad_value),
            grad_query.reshape(rows_block, kv_heads * group_size, head_size),
        )

    zero_keys = jnp.zeros(key_matrix.shape, jnp.float32)
    starts = jnp.arange(0, length, rows_block, dtype=jnp.int32)
    (grad_key, grad_value), grad_query = lax.scan(
        one_block, (zero_keys, zero_keys), (starts, log_sums)
    )
    return (grad_query.reshape(length, kv_heads * group_size, head_size), grad_key, grad_value)


def assemble(mine, other):
    first = lax.axis_index("tensor") == 0
    return jnp.concatenate([jnp.where(first, mine, other), jnp.where(first, other, mine)], axis=0)


def in_three(value):
    parts = []
    for _ in range(3):
        low = lax.reduce_precision(value, 8, 7)
        parts.append(low.astype(bfloat))
        value = value - low
    return parts


def widen(value, columns):
    filler = jnp.zeros((value.shape[0], -sum(c.shape[1] for c in [value] + columns) % 128), bfloat)
    return jnp.concatenate([value] + columns + [filler], axis=1)


def combine_groups(slots, rows, capacity, span, between):
    owners = slots.shape[1]
    parts = {}

    def to_tokens(rows, order):
        mine, other = return_rows(slots, rows, order, capacity, span)
        return mine, swap(other), other

    def add(order, mine, other):
        for i, group in enumerate(order):
            parts[group] = mine[i].astype(single) + other[i].astype(single)

    orders = return_order(owners)
    if len(orders) == 1:
        mine, other, _ = to_tokens(after(rows, *between(())), orders[0])
        add(orders[0], mine, other)
        sent = [parts[step].astype(bfloat) for step in range(1, owners)]
        return parts[0], [to_peer(part, "expert", i) for i, part in enumerate(sent, 1)], sent
    mine, other, leaving = to_tokens(rows, orders[0])
    add(orders[0], mine, after(other, hold(leaving)))
    came, sent = send_farthest(parts[3].astype(bfloat))
    mine, other, leaving = to_tokens(after(rows, *between(sent)), orders[1])
    add(orders[1], mine, after(other, hold(leaving)))
    came, sent = send_nearer(parts[1], parts[2], came)
    return parts[0], came, sent


def on_device(
    tokens,
    teacher,
    routes,
    valid,
    teacher_rows,
    norm_attn,
    norm_moe,
    w_query,
    key_projection_weight,
    value_projection_weight,
    w_out,
    w_router,
    w_gate,
    w_up,
    w_down,
):
    rows_dev, model_width = tokens.shape
    seq_count = rows_dev // SEQUENCE_LENGTH
    heads_local = w_query.shape[1] // HEAD_DIMENSION
    kv_local = key_projection_weight.shape[1] // HEAD_DIMENSION
    query_width = w_query.shape[1]
    key_width = key_projection_weight.shape[1]
    experts_local = w_gate.shape[0]
    owners = lax.axis_size("expert")
    count_dp = lax.axis_size("dp")
    groups = count_dp * owners
    all_experts = experts_local * owners
    top_count = routes.shape[1]
    capacity = rows_dev * top_count * 5 // (4 * all_experts)
    at_dp, at_ex, core = lax.axis_index("dp"), lax.axis_index("expert"), lax.axis_index("tensor")
    span = rows_dev // 2
    shards = count_dp // 2
    place = [at_ex * experts_local, at_dp // shards, core, at_dp % shards]
    place = jnp.stack(place).astype(jnp.int32)

    def mine_of(value, axis=0):
        return lax.dynamic_slice_in_dim(value, core * span, span, axis)

    def other_of(value, axis=0):
        return lax.dynamic_slice_in_dim(value, (1 - core) * span, span, axis)

    routes_t = routes.T
    routes_t = jnp.concatenate([mine_of(routes_t, 1), other_of(routes_t, 1)], axis=1)
    routes_two = jnp.stack([routes_t, to_mirror(routes_t)])
    all_routes = jnp.stack([routes_two] + from_peers(routes_two), axis=1)
    expert_ids = jnp.arange(all_experts, dtype=jnp.int32)
    local_ids = at_ex * experts_local + jnp.arange(experts_local, dtype=jnp.int32)
    local_mask = jnp.any(all_routes[:, :, None] == local_ids[:, None, None], axis=3)
    earlier = jnp.triu(jnp.ones((rows_dev, rows_dev), bfloat), 1)
    before = jnp.dot(local_mask.astype(bfloat), earlier, preferred_element_type=single)
    slots = jnp.where(local_mask, before.astype(jnp.int32), -1).transpose(0, 2, 1, 3)
    mine_mask = jnp.any(routes_t[None, :, :span] == expert_ids[:, None, None], axis=1)

    valid_rows = valid.astype(single)
    valid_count = sum_all(jnp.full((8, 128), jnp.sum(valid_rows)), ("dp", "expert"))
    loss_scale = rows_dev * groups / valid_count[0, 0]
    inputs = tokens.astype(single)
    normed_first, inverse_first = rms_forward(inputs, norm_attn)
    attention_input = normed_first.astype(bfloat)
    cosine_table, sine_table = rope_tables(SEQUENCE_LENGTH, HEAD_DIMENSION)
    factor = HEAD_DIMENSION ** (-0.5)
    query_raw = jnp.dot(attention_input, w_query, preferred_element_type=single).reshape(
        seq_count, SEQUENCE_LENGTH, heads_local, HEAD_DIMENSION
    )
    key_unrotated = jnp.dot(
        attention_input, key_projection_weight, preferred_element_type=single
    ).reshape(seq_count, SEQUENCE_LENGTH, kv_local, HEAD_DIMENSION)
    value_unprojected = jnp.dot(
        attention_input, value_projection_weight, preferred_element_type=single
    ).reshape(seq_count, SEQUENCE_LENGTH, kv_local, HEAD_DIMENSION)
    queries = (apply_rotary(query_raw, cosine_table, sine_table) * factor).astype(bfloat)
    key_matrix = apply_rotary(key_unrotated, cosine_table, sine_table).astype(bfloat)
    value_matrix = value_unprojected.astype(bfloat)
    outputs, log_sums = lax.map(attend_forward, (queries, key_matrix, value_matrix))
    attn_low = outputs.reshape(rows_dev, heads_local * HEAD_DIMENSION).astype(bfloat)
    attn_low = after(attn_low, slots, valid_count)
    attn_part = jnp.dot(attn_low, w_out, preferred_element_type=single)

    leaving = other_of(attn_part)
    hidden_first = mine_of(inputs) + mine_of(attn_part) + after(swap(leaving), hold(leaving))
    normed_second, inverse_second = rms_forward(hidden_first, norm_moe)
    moe_in = normed_second.astype(bfloat)
    logits = lax.dot_general(
        w_router, moe_in, (((0,), (1,)), ((), ())), preferred_element_type=single
    )
    peak = jnp.max(jnp.where(mine_mask, logits, -jnp.inf), axis=0, keepdims=True)
    exponent = jnp.where(mine_mask, jnp.exp(logits - peak), 0.0)
    gates = exponent / jnp.sum(exponent, axis=0, keepdims=True)
    token = widen(moe_in, in_three(gates.T))

    some = experts_local // 2
    pieces = ((0, some), (some, experts_local - some))
    few = max(1, experts_local // 5)

    def interleave(mine, other):
        return [part for pair in zip(mine, other) for part in pair]

    def far_forward(parts, start, amount):
        return expert_forward(
            place, all_experts, slots[1], (w_gate, w_up), parts, capacity, start, amount
        )

    mirror = to_mirror(token)
    near_parts = spread(token)
    mirror = after(mirror, *near_parts)
    peers = from_peers(mirror)
    mirror_other = swap(mirror)
    near_parts[0] = after(near_parts[0], mirror)
    gate_pre, up_pre, near_half, near_tails, results = expert_forward(
        place, all_experts, slots[0], (w_gate, w_up, w_down), near_parts, capacity, 0, experts_local
    )
    results = after(results, mirror_other, *peers)
    peers_other = []

    def swap_peers(sent):
        peers[:] = after_all(peers, *sent)
        peers_other.extend(swap(peer) for peer in peers)
        return sent

    own, arrived, sent = combine_groups(slots[0], results, capacity, span, swap_peers)
    far_tokens = interleave([mirror] + peers, [mirror_other] + peers_other)
    far_tokens[0] = after(far_tokens[0], *sent)
    far = [far_forward(far_tokens, *pieces[0])]
    arrived[0] = after(arrived[0], far[0][0], hold(sent[0]))
    moe = add_up(own, arrived)

    layer_out = hidden_first + moe
    rows_wanted = mine_of(teacher_rows[0])
    chooser = (rows_wanted[:, None] == jnp.arange(rows_dev, dtype=jnp.int32)).astype(bfloat)
    target = jnp.dot(chooser, teacher, preferred_element_type=single)
    grad_layer = loss_scale * mine_of(valid_rows)[:, None] * (layer_out - target)
    layer_low = layer_out.astype(bfloat)
    inner = jnp.sum(grad_layer * moe, axis=1, keepdims=True)
    token_grad = widen(grad_layer.astype(bfloat), in_three(inner))

    far_tokens[0] = after(far_tokens[0], token_grad)
    far.append(far_forward(far_tokens, *pieces[1]))
    mirror = to_mirror(token_grad)
    near_parts = spread(token_grad, (far[1][0],))
    mirror = after(mirror, *near_parts)
    peers = from_peers(mirror)
    mirror_other = swap(mirror)
    near_parts[0] = after(near_parts[0], mirror)
    hidden_low, grad_gate_pre, grad_up_pre, near_grad_half, results = expert_backward(
        place, all_experts, slots[0], (w_gate, w_up, w_down), gate_pre, up_pre, near_tails, near_parts, capacity
    )
    results = after(results, mirror_other, *peers)
    weight_parts, far_grads = [], []

    def weights_of(start, amount):
        piece = 0 if start < some else 1
        far_gate, far_up, far_half, far_tails = far[piece]
        values = expert_weights(
            place,
            all_experts,
            slots[1],
            w_down,
            (far_gate, far_up, far_tails, far_half),
            (hidden_low, grad_gate_pre, grad_up_pre, near_half, near_grad_half),
            far_grads,
            capacity,
            start,
            start - pieces[piece][0],
            amount,
            shards,
        )
        came = [to_peer(values[step], "dp", step) for step in range(1, shards)]
        weight_parts.append((start, values[0], came))
        return values

    def first_weights(sent):
        peers[:] = after_all(peers, *sent)
        peers_other = [swap(peer) for peer in peers]
        far_grads.extend(interleave([mirror] + peers, [mirror_other] + peers_other))
        return weights_of(0, few)

    own, arrived, sent = combine_groups(slots[0], results, capacity, span, first_weights)
    layer_other = swap(after(layer_low, *sent))
    block_out = assemble(layer_low, layer_other)
    far_grads[0] = after(far_grads[0], *sent)
    values = weights_of(few, some - few)
    arrived[0] = after(arrived[0], *values, layer_other, hold(sent[0]))
    grad_wide = add_up(own, arrived)
    grad_logits = grad_wide[:, model_width : model_width + all_experts].astype(bfloat)
    grad_moe_in = grad_wide[:, :model_width] + lax.dot_general(
        grad_logits, w_router, (((1,), (1,)), ((), ())), preferred_element_type=single
    )
    grad_second, _ = rms_backward(hidden_first, inverse_second, norm_moe, grad_moe_in)
    grad_hidden_mine = grad_layer + grad_second
    grad_attn_mine = grad_hidden_mine.astype(bfloat)
    far_grads[0] = after(far_grads[0], grad_attn_mine)
    values = weights_of(some, experts_local - some)
    grad_attn = assemble(
        grad_attn_mine, after(swap(grad_attn_mine), *values, *weight_parts[0][2])
    )
    first_pack = pack_sums(
        grad_attn,
        attn_low,
        (moe_in, widen(grad_logits, [])),
        grad_moe_in,
        hidden_first,
        inverse_second,
        all_experts,
    )
    first_total = over_owners(first_pack)

    grad_mixed = jnp.dot(grad_attn, w_out.T, preferred_element_type=single).astype(bfloat)
    grad_mixed = grad_mixed.reshape(seq_count, SEQUENCE_LENGTH, heads_local * HEAD_DIMENSION)
    grad_queries, grad_keys, grad_values = lax.map(
        attend_backward, (queries, key_matrix, value_matrix, log_sums, grad_mixed)
    )
    grad_query_raw = (
        rotate_back(grad_queries * factor, cosine_table, sine_table)
        .astype(bfloat)
        .reshape(rows_dev, heads_local * HEAD_DIMENSION)
    )
    grad_key_raw = (
        rotate_back(grad_keys, cosine_table, sine_table)
        .astype(bfloat)
        .reshape(rows_dev, kv_local * HEAD_DIMENSION)
    )
    grad_value_raw = grad_values.astype(bfloat).reshape(rows_dev, kv_local * HEAD_DIMENSION)
    grad_raw = jnp.concatenate([grad_query_raw, grad_key_raw, grad_value_raw], axis=1)
    grad_attn_in = (
        jnp.dot(grad_query_raw, w_query.T, preferred_element_type=single)
        + jnp.dot(grad_key_raw, key_projection_weight.T, preferred_element_type=single)
        + jnp.dot(grad_value_raw, value_projection_weight.T, preferred_element_type=single)
    )
    second_pack = pack_sums(
        attention_input, grad_raw, None, grad_attn_in, tokens, inverse_first, 0
    )
    second_pack = after(second_pack, first_total, *weight_parts[1][2])
    first_dense = over_dp(first_total)
    second_total = over_owners(second_pack)
    grad_attn_mine = mine_of(grad_attn_in) + swap(other_of(grad_attn_in).astype(bfloat)).astype(
        single
    )
    grad_first, _ = rms_backward(
        mine_of(inputs), mine_of(inverse_first), norm_attn, grad_attn_mine
    )
    grad_tokens_mine = grad_hidden_mine + grad_first
    grad_tokens = assemble(grad_tokens_mine, swap(grad_tokens_mine))

    second_dense = over_dp(after(second_total, grad_tokens, first_dense))
    shared = jnp.concatenate([first_dense[:, query_width:], second_dense[:, -128:]], axis=1)
    shared = shared + swap(shared)

    weight_grads = None
    for start, values, came in weight_parts:
        came = [after(part, second_total) for part in came]
        weight_grads = finish_weights(experts_local, start, values, came, weight_grads)

    key_at = query_width
    return (
        block_out,
        grad_tokens,
        shared[:, -128],
        shared[:, all_experts],
        second_dense[:, :key_at],
        second_dense[:, key_at : key_at + key_width],
        second_dense[:, key_at + key_width : key_at + 2 * key_width],
        first_dense[:, :query_width].T,
        shared[:, :all_experts],
        weight_grads[0],
        weight_grads[1],
        weight_grads[2],
    )


def solution(mesh):
    placed = (
        P(("dp", "expert"), None),
        P(("dp", "expert"), None),
        P(("dp", "expert"), None),
        P(("dp", "expert")),
        P(("dp", "expert"), None),
        P(),
        P(),
        P(None, "tensor"),
        P(None, "tensor"),
        P(None, "tensor"),
        P("tensor", None),
        P(),
        P("expert", None, "tensor"),
        P("expert", None, "tensor"),
        P("expert", "tensor", None),
    )
    return jax.shard_map(
        on_device,
        mesh=mesh,
        in_specs=placed,
        out_specs=(
            P(("dp", "expert"), None),
            P(("dp", "expert"), None),
            P(("dp", "expert")),
            P(("dp", "expert")),
            P(("dp", "expert"), "tensor"),
            P(("dp", "expert"), "tensor"),
            P(("dp", "expert"), "tensor"),
            P("tensor", ("dp", "expert")),
            P(("dp", "expert"), None),
            P("expert", "dp", "tensor"),
            P("expert", "dp", "tensor"),
            P("expert", "tensor", "dp"),
        ),
        check_vma=False,
    )
```

time: 2280 us -> 619 us (0.27)
  waiting for transfers between devices: 1050 us -> 120 us
  blocking collectives: 630 us -> 0 us
  Pallas kernels: 0 us -> 233 us
  local copies, waits for them, and re-layouts: 265 us -> 54.5 us
  matrix products: 199 us -> 51.7 us
  starting transfers between devices: 8.28 us -> 63.1 us
    reduce_scatter x6 -> x0, waiting for transfers between devices: 718 us -> none  [the longest x1 143 us: on_device(): lax.psum_scatter(grad_query_local, ('dp', 'expert'), scatter_dimension=0,...]
    all_to_all x3 -> x0, blocking collectives: 508 us -> none  [the longest x1 176 us: on_device(): lax.all_to_all(send_rows, 'expert', split_axis=0, concat_axis=2, tiled=True)]
    pallas_call x0 -> x72, Pallas kernels: none -> 233 us  [the longest x16 219 us: kernel_call(): pl.pallas_call(kernel, name=name, grid_spec=pltpu.PrefetchScalarGridSpec(...]
    all_to_all x1 -> x0, waiting for transfers between devices: 167 us -> none  [on_device(): lax.all_to_all(expert_out.reshape(1, experts_local, owners, capacity, mod...]
    dot_general x15 -> x4, matrix products: 158 us -> 6.24 us  [the longest x1 5.16 us: on_device(): target = jnp.dot(chooser, teacher, preferred_element_type=single)]
    gather x5 -> x0, local copies, waits for them, and re-layouts: 140 us -> none  [the longest x1 35.5 us: on_device(): grad_send = (gate_slot[:, None] * grad_layer[source]).astype(bfloat)]
    unnamed x14 -> x0, waiting for transfers between devices: 137 us -> none
    ppermute x0 -> x73, waiting for transfers between devices: none -> 120 us  [the longest x44 106 us: to_peer(): lax.ppermute(value, axis, [(i, i ^ step) for i in range(lax.axis_size(axi...]
  transfers between devices with their start and end apart: 13 -> 73, of which waited for: 11 -> 27; matrix products, arithmetic and copies ran while one was open for 9% -> 24% of each run, Pallas kernels for 0% -> 34%
where the time goes in v3:
time: 619 us; the launch traced here: 610 us
  Pallas kernels  233 us (38%)
  waiting for transfers between devices  120 us (19%)
  other arithmetic  85 us (14%)
  starting transfers between devices  63.1 us (10%)
  local copies, waits for them, and re-layouts  54.5 us (9%)
  matrix products  51.7 us (8%)
    pallas_call x16, Pallas kernels, kernel_call(): pl.pallas_call(kernel, name=name, grid_spec=pltpu.PrefetchScalarGridSpec(...  219 us
    ppermute x44, waiting for transfers between devices, to_peer(): lax.ppermute(value, axis, [(i, i ^ step) for i in range(lax.axis_size(axi...  106 us
    ppermute x44, starting transfers between devices, to_peer(): lax.ppermute(value, axis, [(i, i ^ step) for i in range(lax.axis_size(axi...  51.8 us
    unnamed x192, local copies, waits for them, and re-layouts  23.2 us
    ppermute x26, waiting for transfers between devices, swap(): return lax.ppermute(value, 'tensor', [(0, 1), (1, 0)])  13.8 us
  transfers between devices with their start and end apart: 73, of which 27 were waited for; matrix products, arithmetic and copies ran while one was open for 24% of the time, Pallas kernels for 34%

profile of v3, /device:TPU:0, one launch (start us, length us, event | category | flops | bytes accessed | tf_op | source)
XLA Modules:
  0.0 610.3 jit_solution(4199735654848051410)
XLA Ops:
  1.6 5.0 collective-permute-start
  23.6 4.7 fusion.15
  30.3 3.9 collective-permute-done.5
  71.6 16.5 %collective-permute-done.11.high_ref.refs_3_ = bf16[256,1664]{1,0:T(8,128)(2,1)} collective-permute-done((bf16[256,1664]{1,0:T(8,128)(2,1)}, bf16[256,1664]{1,0:T(8,128)(2,1)}, u32[]{:S(2)}, u32[]{:S(2)}) %collective-permute-start.11) | collective-permute-done | bytes 852000 | tf_op jit(solution)/shard_map/ppermute | solution.py:62
  94.6 8.1 %collective-permute-done.15.refs_0_ = bf16[128,1664]{1,0:T(8,128)(2,1)} collective-permute-done((bf16[128,1664]{1,0:T(8,128)(2,1)}, bf16[128,1664]{1,0:T(8,128)(2,1)}, u32[]{:S(2)}, u32[]{:S(2)}) %collective-permute-start.15) | collective-permute-done | bytes 426016 | tf_op jit(solution)/shard_map/ppermute | solution.py:62
  111.5 30.3 %expert_forward.1 = (bf16[10,512,256]{2,1,0:T(8,128)(2,1)}, bf16[10,512,256]{2,1,0:T(8,128)(2,1)}, bf16[10,512,768]{2,1,0:T(8,128)(2,1)}, bf16[10,512,128]{2,1,0:T(8,128)(2,1)}, bf16[10,512,1536]{2,1,0:T(8,128)(2,1)}) custom-call(s32[4]{0:T(128)} %pad_add_fusion.3.place_ref, s32[10,4,512]{2,1,0:T(4,128)} %get-tuple-element.323.slots_ref, ...), custom_call_target="tpu_custom_call" | custom-call | flops 20803747840 | bytes 49807360 | tf_op jit(solution)/shard_map/expert_forward/pallas_call | solution.py:361
  142.7 6.2 %collective-permute-done.20.refs_3_.refs_1_ = bf16[256,1664]{1,0:T(8,128)(2,1)} collective-permute-done((bf16[256,1664]{1,0:T(8,128)(2,1)}, bf16[256,1664]{1,0:T(8,128)(2,1)}, u32[]{:S(2)}, u32[]{:S(2)}) %collective-permute-start.20) | collective-permute-done | bytes 852000 | tf_op jit(solution)/shard_map/ppermute | solution.py:62
  148.9 5.1 return_rows.4
  158.9 11.7 %return_rows.5 = (bf16[3,256,1536]{2,1,0:T(8,128)(2,1)}, bf16[3,256,1536]{2,1,0:T(8,128)(2,1)}) custom-call(s32[10,4,512]{2,1,0:T(4,128)} %get-tuple-element.323.slots_ref, bf16[10,512,1536]{2,1,0:T(8,128)(2,1)} %after.45.rows_ref), custom_call_target="tpu_custom_call" | custom-call | flops 6039797760 | bytes 16515072 | tf_op jit(solution)/shard_map/return_rows/pallas_call | solution.py:361
  179.1 4.1 collective-permute-done.24
  191.7 15.1 %expert_forward_far.2 = (bf16[5,512,256]{2,1,0:T(8,128)(2,1)}, bf16[5,512,256]{2,1,0:T(8,128)(2,1)}, bf16[5,512,768]{2,1,0:T(8,128)(2,1)}, bf16[5,512,128]{2,1,0:T(8,128)(2,1)}) custom-call(s32[4]{0:T(128)} %pad_add_fusion.3.place_ref, s32[10,4,512]{2,1,0:T(4,128)} %get-tuple-element.322.slots_ref, bf16[10,1536,256]{2,1,0:T(8,128)(2,1)} %gate_w.7, ...), custom_call_target="tpu_custom_call" | custom-call | flops 8388608000 | bytes 20971520 | tf_op jit(solution)/shard_map/expert_forward_far/pallas_call | solution.py:361
  209.7 5.2 multiply_reduce_fusion.3
  222.1 15.1 %expert_forward_far.3 = (bf16[5,512,256]{2,1,0:T(8,128)(2,1)}, bf16[5,512,256]{2,1,0:T(8,128)(2,1)}, bf16[5,512,768]{2,1,0:T(8,128)(2,1)}, bf16[5,512,128]{2,1,0:T(8,128)(2,1)}) custom-call(s32[4]{0:T(128)} %pad_add_fusion.3.place_ref, s32[10,4,512]{2,1,0:T(4,128)} %get-tuple-element.322.slots_ref, bf16[10,1536,256]{2,1,0:T(8,128)(2,1)} %gate_w.7, ...), custom_call_target="tpu_custom_call" | custom-call | flops 8388608000 | bytes 20971520 | tf_op jit(solution)/shard_map/expert_forward_far/pallas_call | solution.py:361
  245.3 8.2 %collective-permute-done.37.refs_0_ = bf16[128,1664]{1,0:T(8,128)(2,1)} collective-permute-done((bf16[128,1664]{1,0:T(8,128)(2,1)}, bf16[128,1664]{1,0:T(8,128)(2,1)}, u32[]{:S(2)}, u32[]{:S(2)}) %collective-permute-start.37) | collective-permute-done | bytes 426016 | tf_op jit(solution)/shard_map/ppermute | solution.py:62
  262.9 41.4 %expert_backward.1 = (bf16[10,512,256]{2,1,0:T(8,128)(2,1)}, bf16[10,512,256]{2,1,0:T(8,128)(2,1)}, bf16[10,512,256]{2,1,0:T(8,128)(2,1)}, bf16[10,512,768]{2,1,0:T(8,128)(2,1)}, bf16[10,512,1664]{2,1,0:T(8,128)(2,1)}) custom-call(s32[4]{0:T(128)} %pad_add_fusion.3.place_ref, s32[10,4,512]{2,1,0:T(4,128)} %get-tuple-element.323.slots_ref, ...), custom_call_target="tpu_custom_call" | custom-call | flops 20132659200 | bytes 65536000 | tf_op jit(solution)/shard_map/expert_backward/pallas_call | solution.py:361
  306.2 6.0 return_rows.6
  326.3 13.0 %expert_weights.3 = (bf16[2,3,384,256]{3,2,1,0:T(8,128)(2,1)}, bf16[2,3,384,256]{3,2,1,0:T(8,128)(2,1)}) custom-call(s32[4]{0:T(128)} %pad_add_fusion.3.place_ref, s32[10,4,512]{2,1,0:T(4,128)} %get-tuple-element.322.slots_ref, bf16[10,256,1536]{2,1,0:T(8,128)(2,1)} %down_w.7, bf16[5,512,256]{2,1,0:T(8,128)(2,1)} %get-tuple-element.178.refs_1_.gate_ref, ...), custom_call_target="tpu_custom_call" | custom-call | flops 4831838208 | bytes 12320768 | tf_op jit(solution)/shard_map/expert_weights/pallas_call | solution.py:361
  339.3 11.3 %return_rows.7 = (bf16[3,256,1664]{2,1,0:T(8,128)(2,1)}, bf16[3,256,1664]{2,1,0:T(8,128)(2,1)}) custom-call(s32[10,4,512]{2,1,0:T(4,128)} %get-tuple-element.323.slots_ref, bf16[10,512,1664]{2,1,0:T(8,128)(2,1)} %after.58.rows_ref), custom_call_target="tpu_custom_call" | custom-call | flops 6543114240 | bytes 17891328 | tf_op jit(solution)/shard_map/return_rows/pallas_call | solution.py:361
  364.7 16.7 %expert_weights.4 = (bf16[3,3,384,256]{3,2,1,0:T(8,128)(2,1)}, bf16[3,3,384,256]{3,2,1,0:T(8,128)(2,1)}) custom-call(s32[4]{0:T(128)} %pad_add_fusion.3.place_ref, s32[10,4,512]{2,1,0:T(4,128)} %get-tuple-element.322.slots_ref, bf16[10,256,1536]{2,1,0:T(8,128)(2,1)} %down_w.7, bf16[5,512,256]{2,1,0:T(8,128)(2,1)} %get-tuple-element.178.refs_1_.gate_ref, ...), custom_call_target="tpu_custom_call" | custom-call | flops 7247757312 | bytes 18481152 | tf_op jit(solution)/shard_map/expert_weights/pallas_call | solution.py:361
  393.9 23.1 %expert_weights.5 = (bf16[5,3,384,256]{3,2,1,0:T(8,128)(2,1)}, bf16[5,3,384,256]{3,2,1,0:T(8,128)(2,1)}) custom-call(s32[4]{0:T(128)} %pad_add_fusion.3.place_ref, s32[10,4,512]{2,1,0:T(4,128)} %get-tuple-element.322.slots_ref, bf16[10,256,1536]{2,1,0:T(8,128)(2,1)} %down_w.7, bf16[5,512,256]{2,1,0:T(8,128)(2,1)} %get-tuple-element.182.refs_2_.gate_ref, ...), custom_call_target="tpu_custom_call" | custom-call | flops 12079595520 | bytes 30801920 | tf_op jit(solution)/shard_map/expert_weights/pallas_call | solution.py:361
  423.2 6.4 %pack_sums.2 = bf16[1536,896]{1,0:T(8,128)(2,1)} custom-call(bf16[512,1536]{1,0:T(8,128)(2,1)} %pad_maximum_fusion.2.left, bf16[512,768]{1,0:T(8,128)(2,1)} %after.37.right, bf16[256,1536]{1,0:T(8,128)(2,1)} %copy-done.14, bf16[256,128]{1,0:T(8,128)(2,1)} %concatenate.124.right_tail, f32[256,1536]{1,0:T(8,128)} %copy-done.10, f32[256,1536]{1,0:T(8,128)} %copy-done.3, ...), custom_call_target="tpu_custom_call" | custom-call | flops 1409286144 | bytes 9830400 | tf_op jit(solution)/shard_map/pack_sums/pallas_call | solution.py:361
  439.3 8.2 %fusion.20 = bf16[4,64,512]{2,1,0:T(8,128)(2,1)} fusion(bf16[512,4,3,64]{0,3,2,1:T(8,128)(2,1)S(1)} %bitcast.315, f32[4,512,512,3]{2,1,3,0:T(8,128)} %copy-done.1, f32[4,3,512]{2,1,0:T(4,128)S(1)} %copy-done.65, pred[512,512]{0,1:T(8,128)(4,1)S(1)} %copy-done.13), kind=kOutput, calls=%fused_computation.58 | convolution fusion | flops 412221440 | bytes 13918208 | tf_op jit(solution)/shard_map/while/body/eval_jaxpr/while/body/eval_jaxpr/kgqt,qkge->tke/dot_general | solution.py:645
  447.5 9.2 %fusion = (f32[4,3,512]{2,1,0:T(4,128)S(1)}, f32[4,512,512,3]{2,1,3,0:T(8,128)}) fusion(f32[4,512,512,3]{2,1,3,0:T(8,128)} %copy-done.1, f32[4,3,512]{2,1,0:T(4,128)S(1)} %copy-done.65, pred[512,512]{0,1:T(8,128)(4,1)S(1)} %copy-done.13, bf16[512,4,64,1]{0,2,3,1:T(8,128)(2,1)S(1)} %bitcast.327, bf16[512,4,3,64]{0,3,2,1:T(8,128)(2,1)S(1)} %bitcast.316), kind=kOutput, calls=%fused_computation.2 | convolution fusion | flops 415229952 | bytes 26525696 | tf_op jit(solution)/shard_map/while/body/eval_jaxpr/while/body/eval_jaxpr/qkge,tke->kgqt/dot_general | solution.py:634
  456.8 7.1 %fusion.2 = bf16[4,3,512,512]{2,3,1,0:T(8,128)(2,1)S(1)} fusion(f32[4,512,512,3]{2,1,3,0:T(8,128)} %get-tuple-element.344, f32[4,512,512,3]{2,1,3,0:T(8,128)S(1)} %bitcast.303, f32[4,3,512]{2,1,0:T(4,128)S(1)} %get-tuple-element.343, f32[4,3,512]{2,1,0:T(4,128)S(1)} %copy-done.65, pred[512,512]{0,1:T(8,128)(4,1)S(1)} %copy-done.13), kind=kLoop, calls=%fused_computation.4 | loop fusion | flops 15728640 | bytes 31768576 | tf_op jit(solution)/shard_map/while/body/eval_jaxpr/while/body/eval_jaxpr/convert_element_type | solution.py:638
  469.5 4.8 fusion.95
  484.8 9.1 %pack_sums.3.refs_0_ = bf16[1536,1408]{1,0:T(8,128)(2,1)} custom-call(bf16[512,1536]{1,0:T(8,128)(2,1)} %copy-done.8, bf16[512,1280]{1,0:T(8,128)(2,1)} %pad_maximum_fusion.3.right.right_tail, bf16[512,1536]{1,0:T(8,128)(2,1)} %copy-done.8, bf16[512,1280]{1,0:T(8,128)(2,1)} %pad_maximum_fusion.3.right.right_tail, f32[512,1536]{1,0:T(8,128)} %copy-done.5, ...), custom_call_target="tpu_custom_call" | custom-call | flops 2214592512 | bytes 11927552 | tf_op jit(solution)/shard_map/pack_sums/pallas_call | solution.py:361
  502.5 11.3 %collective-permute-done.59.refs_0_ = bf16[4,96,896]{2,1,0:T(8,128)(2,1)} collective-permute-done((bf16[4,96,896]{2,1,0:T(8,128)(2,1)}, bf16[4,96,896]{2,1,0:T(8,128)(2,1)}, u32[]{:S(2)}, u32[]{:S(2)}) %collective-permute-start.59) | collective-permute-done | bytes 688160 | tf_op jit(solution)/shard_map/ppermute | solution.py:62
  532.1 8.7 %collective-permute-done.63 = bf16[96,896]{1,0:T(8,128)(2,1)} collective-permute-done((bf16[96,896]{1,0:T(8,128)(2,1)}, bf16[96,896]{1,0:T(8,128)(2,1)}, u32[]{:S(2)}, u32[]{:S(2)}) %collective-permute-start.63) | collective-permute-done | bytes 172064 | tf_op jit(solution)/shard_map/ppermute | solution.py:62
  553.7 16.9 %collective-permute-done.66.refs_0_ = bf16[4,96,1408]{2,1,0:T(8,128)(2,1)} collective-permute-done((bf16[4,96,1408]{2,1,0:T(8,128)(2,1)}, bf16[4,96,1408]{2,1,0:T(8,128)(2,1)}, u32[]{:S(2)}, u32[]{:S(2)}) %collective-permute-start.66) | collective-permute-done | bytes 1081376 | tf_op jit(solution)/shard_map/ppermute | solution.py:62
  579.4 9.7 %collective-permute-done.69 = bf16[192,1408]{1,0:T(8,128)(2,1)S(1)} collective-permute-done((bf16[192,1408]{1,0:T(8,128)(2,1)S(1)}, bf16[192,1408]{1,0:T(8,128)(2,1)S(1)}, u32[]{:S(2)}, u32[]{:S(2)}) %collective-permute-start.69) | collective-permute-done | bytes 540704 | tf_op jit(solution)/shard_map/ppermute | solution.py:62
  595.3 4.7 finish_weights.4
  600.0 7.0 %finish_weights.5 = (f32[10,384,256]{2,1,0:T(8,128)}, f32[10,384,256]{2,1,0:T(8,128)}, f32[10,256,384]{2,1,0:T(8,128)}) custom-call(f32[10,384,256]{2,1,0:T(8,128)} %get-tuple-element.213.gate_in, f32[10,384,256]{2,1,0:T(8,128)} %get-tuple-element.214.up_in, ...), custom_call_target="tpu_custom_call", output_to_operand_aliasing={{0}: (0, {}), {1}: (1, {}), {2}: (2, {})} | custom-call | flops 1474560 | bytes 5898240 | tf_op jit(solution)/shard_map/finish_weights/pallas_call | solution.py:361
  (525 shorter events, 253.3 us)
Async XLA Ops:
  1.6 42.3 %collective-permute-start = (s32[8,512]{1,0:T(8,128)S(1)}, s32[8,512]{1,0:T(8,128)S(1)}, u32[]{:S(2)}, u32[]{:S(2)}) collective-permute-start(s32[8,512]{1,0:T(8,128)S(1)} %get-tuple-element.329), channel_id=1, source_target_pairs={{0,24},{8,16},{16,8},{24,0},{1,25},{9,17},{17,9},{25,1},{2,26},{10... | collective-permute-start | bytes 49160 | tf_op jit(solution)/shard_map/ppermute | solution.py:67
  8.6 20.4 %collective-permute-start.4 = (f32[8,128]{1,0:T(8,128)S(1)}, f32[8,128]{1,0:T(8,128)S(1)}, u32[]{:S(2)}, u32[]{:S(2)}) collective-permute-start(f32[8,128]{1,0:T(8,128)S(1)} %broadcast_in_dim.121), channel_id=1, source_target_pairs={{0,8},{8,0},{16,24},{24,16},{1,9},{9,1},{17,25},{25,17},{2,10},{10... | collective-permute-start | bytes 12296 | tf_op jit(solution)/shard_map/ppermute | solution.py:62
  66.6 21.5 %collective-permute-start.11 = (bf16[256,1664]{1,0:T(8,128)(2,1)}, bf16[256,1664]{1,0:T(8,128)(2,1)}, u32[]{:S(2)}, u32[]{:S(2)}) collective-permute-start(bf16[256,1664]{1,0:T(8,128)(2,1)} %concatenate.111.value_ref.refs_1_.refs_0_), channel_id=1, source_target_pairs={{0,2},{2,0},{4,6},{6,4},{1,3},{3,1},{5,7},{7,5},{8,10},{10,8},{12,... | collective-permute-start | bytes 2555912 | tf_op jit(solution)/shard_map/ppermute | solution.py:62
  68.1 21.2 %collective-permute-start.13 = (bf16[256,1664]{1,0:T(8,128)(2,1)}, bf16[256,1664]{1,0:T(8,128)(2,1)}, u32[]{:S(2)}, u32[]{:S(2)}) collective-permute-start(bf16[256,1664]{1,0:T(8,128)(2,1)} %concatenate.111.value_ref.refs_1_.refs_0_), channel_id=1, source_target_pairs={{0,4},{2,6},{4,0},{6,2},{1,5},{3,7},{5,1},{7,3},{8,12},{10,14},{12... | collective-permute-start | bytes 2555912 | tf_op jit(solution)/shard_map/ppermute | solution.py:62
  70.2 37.6 %collective-permute-start.9 = (bf16[256,1664]{1,0:T(8,128)(2,1)}, bf16[256,1664]{1,0:T(8,128)(2,1)}, u32[]{:S(2)}, u32[]{:S(2)}) collective-permute-start(bf16[256,1664]{1,0:T(8,128)(2,1)} %concatenate.111.value_ref.refs_1_.refs_0_), channel_id=1, source_target_pairs={{0,24},{8,16},{16,8},{24,0},{1,25},{9,17},{17,9},{25,1},{2,26},{10... | collective-permute-start | bytes 2555912 | tf_op jit(solution)/shard_map/ppermute | solution.py:67
  107.8 34.0 %collective-permute-start.18 = (bf16[256,1664]{1,0:T(8,128)(2,1)}, bf16[256,1664]{1,0:T(8,128)(2,1)S(1)}, u32[]{:S(2)}, u32[]{:S(2)}) collective-permute-start(bf16[256,1664]{1,0:T(8,128)(2,1)} %after.41.refs_1_.refs_0_), channel_id=1, source_target_pairs={{0,1},{1,0},{2,3},{3,2},{4,5},{5,4},{6,7},{7,6},{8,9},{9,8},{10,11... | collective-permute-start | bytes 2555912 | tf_op jit(solution)/shard_map/ppermute | solution.py:58
  108.0 33.9 %collective-permute-start.19 = (bf16[256,1664]{1,0:T(8,128)(2,1)}, bf16[256,1664]{1,0:T(8,128)(2,1)S(1)}, u32[]{:S(2)}, u32[]{:S(2)}) collective-permute-start(bf16[256,1664]{1,0:T(8,128)(2,1)} %after.41.refs_1_.refs_0_), channel_id=1, source_target_pairs={{0,2},{2,0},{4,6},{6,4},{1,3},{3,1},{5,7},{7,5},{8,10},{10,8},{12,... | collective-permute-start | bytes 2555912 | tf_op jit(solution)/shard_map/ppermute | solution.py:62
  109.4 39.5 %collective-permute-start.20 = (bf16[256,1664]{1,0:T(8,128)(2,1)}, bf16[256,1664]{1,0:T(8,128)(2,1)}, u32[]{:S(2)}, u32[]{:S(2)}) collective-permute-start(bf16[256,1664]{1,0:T(8,128)(2,1)} %after.41.refs_1_.refs_0_), channel_id=1, source_target_pairs={{0,4},{2,6},{4,0},{6,2},{1,5},{3,7},{5,1},{7,3},{8,12},{10,14},{12... | collective-permute-start | bytes 2555912 | tf_op jit(solution)/shard_map/ppermute | solution.py:62
  110.9 38.0 %collective-permute-start.21 = (bf16[256,1664]{1,0:T(8,128)(2,1)}, bf16[256,1664]{1,0:T(8,128)(2,1)}, u32[]{:S(2)}, u32[]{:S(2)}) collective-permute-start(bf16[256,1664]{1,0:T(8,128)(2,1)} %after.41.refs_1_.refs_0_), channel_id=1, source_target_pairs={{0,6},{2,4},{4,2},{6,0},{1,7},{3,5},{5,3},{7,1},{8,14},{10,12},{12... | collective-permute-start | bytes 2555912 | tf_op jit(solution)/shard_map/ppermute | solution.py:62
  184.4 22.4 %collective-permute-start.25 = (bf16[256,1536]{1,0:T(8,128)(2,1)}, bf16[256,1536]{1,0:T(8,128)(2,1)}, u32[]{:S(2)}, u32[]{:S(2)}) collective-permute-start(bf16[256,1536]{1,0:T(8,128)(2,1)} %pad_maximum_fusion.10.refs_1_.value_ref), channel_id=1, source_target_pairs={{0,2},{2,0},{4,6},{6,4},{1,3},{3,1},{5,7},{7,5},{8,10},{10,8},{12,... | collective-permute-start | bytes 2359304 | tf_op jit(solution)/shard_map/ppermute | solution.py:62
  217.8 19.5 %collective-permute-start.32 = (bf16[256,1664]{1,0:T(8,128)(2,1)}, bf16[256,1664]{1,0:T(8,128)(2,1)}, u32[]{:S(2)}, u32[]{:S(2)}) collective-permute-start(bf16[256,1664]{1,0:T(8,128)(2,1)} %concatenate.115.value_ref.refs_1_.refs_0_), channel_id=1, source_target_pairs={{0,1},{1,0},{2,3},{3,2},{4,5},{5,4},{6,7},{7,6},{8,9},{9,8},{10,11... | collective-permute-start | bytes 2555912 | tf_op jit(solution)/shard_map/ppermute | solution.py:58
  217.8 21.7 %collective-permute-start.33 = (bf16[256,1664]{1,0:T(8,128)(2,1)}, bf16[256,1664]{1,0:T(8,128)(2,1)}, u32[]{:S(2)}, u32[]{:S(2)}) collective-permute-start(bf16[256,1664]{1,0:T(8,128)(2,1)} %concatenate.115.value_ref.refs_1_.refs_0_), channel_id=1, source_target_pairs={{0,2},{2,0},{4,6},{6,4},{1,3},{3,1},{5,7},{7,5},{8,10},{10,8},{12,... | collective-permute-start | bytes 2555912 | tf_op jit(solution)/shard_map/ppermute | solution.py:62
  218.6 21.4 %collective-permute-start.35 = (bf16[256,1664]{1,0:T(8,128)(2,1)}, bf16[256,1664]{1,0:T(8,128)(2,1)}, u32[]{:S(2)}, u32[]{:S(2)}) collective-permute-start(bf16[256,1664]{1,0:T(8,128)(2,1)} %concatenate.115.value_ref.refs_1_.refs_0_), channel_id=1, source_target_pairs={{0,4},{2,6},{4,0},{6,2},{1,5},{3,7},{5,1},{7,3},{8,12},{10,14},{12... | collective-permute-start | bytes 2555912 | tf_op jit(solution)/shard_map/ppermute | solution.py:62
  220.7 38.6 %collective-permute-start.31 = (bf16[256,1664]{1,0:T(8,128)(2,1)}, bf16[256,1664]{1,0:T(8,128)(2,1)}, u32[]{:S(2)}, u32[]{:S(2)}) collective-permute-start(bf16[256,1664]{1,0:T(8,128)(2,1)} %concatenate.115.value_ref.refs_1_.refs_0_), channel_id=1, source_target_pairs={{0,24},{8,16},{16,8},{24,0},{1,25},{9,17},{17,9},{25,1},{2,26},{10... | collective-permute-start | bytes 2555912 | tf_op jit(solution)/shard_map/ppermute | solution.py:67
  259.3 45.1 %collective-permute-start.40 = (bf16[256,1664]{1,0:T(8,128)(2,1)}, bf16[256,1664]{1,0:T(8,128)(2,1)S(1)}, u32[]{:S(2)}, u32[]{:S(2)}) collective-permute-start(bf16[256,1664]{1,0:T(8,128)(2,1)} %after.53.refs_1_.refs_6_.refs_0_), channel_id=1, source_target_pairs={{0,1},{1,0},{2,3},{3,2},{4,5},{5,4},{6,7},{7,6},{8,9},{9,8},{10,11... | collective-permute-start | bytes 2555912 | tf_op jit(solution)/shard_map/ppermute | solution.py:58
  259.4 44.9 %collective-permute-start.41 = (bf16[256,1664]{1,0:T(8,128)(2,1)}, bf16[256,1664]{1,0:T(8,128)(2,1)S(1)}, u32[]{:S(2)}, u32[]{:S(2)}) collective-permute-start(bf16[256,1664]{1,0:T(8,128)(2,1)} %after.53.refs_1_.refs_6_.refs_0_), channel_id=1, source_target_pairs={{0,2},{2,0},{4,6},{6,4},{1,3},{3,1},{5,7},{7,5},{8,10},{10,8},{12,... | collective-permute-start | bytes 2555912 | tf_op jit(solution)/shard_map/ppermute | solution.py:62
  260.2 45.1 %collective-permute-start.42 = (bf16[256,1664]{1,0:T(8,128)(2,1)}, bf16[256,1664]{1,0:T(8,128)(2,1)}, u32[]{:S(2)}, u32[]{:S(2)}) collective-permute-start(bf16[256,1664]{1,0:T(8,128)(2,1)} %after.53.refs_1_.refs_6_.refs_0_), channel_id=1, source_target_pairs={{0,4},{2,6},{4,0},{6,2},{1,5},{3,7},{5,1},{7,3},{8,12},{10,14},{12... | collective-permute-start | bytes 2555912 | tf_op jit(solution)/shard_map/ppermute | solution.py:62
  261.8 43.5 %collective-permute-start.43 = (bf16[256,1664]{1,0:T(8,128)(2,1)}, bf16[256,1664]{1,0:T(8,128)(2,1)}, u32[]{:S(2)}, u32[]{:S(2)}) collective-permute-start(bf16[256,1664]{1,0:T(8,128)(2,1)} %after.53.refs_1_.refs_6_.refs_0_), channel_id=1, source_target_pairs={{0,6},{2,4},{4,2},{6,0},{1,7},{3,5},{5,3},{7,1},{8,14},{10,12},{12... | collective-permute-start | bytes 2555912 | tf_op jit(solution)/shard_map/ppermute | solution.py:62
  323.0 37.9 %collective-permute-start.50 = (bf16[128,1664]{1,0:T(8,128)(2,1)}, bf16[128,1664]{1,0:T(8,128)(2,1)}, u32[]{:S(2)}, u32[]{:S(2)}) collective-permute-start(bf16[128,1664]{1,0:T(8,128)(2,1)} %get-tuple-element.311.refs_3_), channel_id=1, source_target_pairs={{0,2},{2,0},{4,6},{6,4},{1,3},{3,1},{5,7},{7,5},{8,10},{10,8},{12,... | collective-permute-start | bytes 1277960 | tf_op jit(solution)/shard_map/ppermute | solution.py:62
  323.8 34.3 %collective-permute-start.49 = (bf16[128,1664]{1,0:T(8,128)(2,1)}, bf16[128,1664]{1,0:T(8,128)(2,1)}, u32[]{:S(2)}, u32[]{:S(2)}) collective-permute-start(bf16[128,1664]{1,0:T(8,128)(2,1)} %get-tuple-element.310.refs_4_), channel_id=1, source_target_pairs={{0,4},{2,6},{4,0},{6,2},{1,5},{3,7},{5,1},{7,3},{8,12},{10,14},{12... | collective-permute-start | bytes 1277960 | tf_op jit(solution)/shard_map/ppermute | solution.py:62
  351.2 67.5 %collective-permute-start.55 = (bf16[2,3,384,256]{3,2,1,0:T(8,128)(2,1)}, bf16[2,3,384,256]{3,2,1,0:T(8,128)(2,1)}, u32[]{:S(2)}, u32[]{:S(2)}) collective-permute-start(bf16[2,3,384,256]{3,2,1,0:T(8,128)(2,1)} %get-tuple-element.200.refs_2_), channel_id=1, source_target_pairs={{0,8},{8,0},{16,24},{24,16},{1,9},{9,1},{17,25},{25,17},{2,10},{10... | collective-permute-start | bytes 3538952 | tf_op jit(solution)/shard_map/ppermute | solution.py:62
  360.2 24.3 %collective-permute-start.52 = (bf16[256,1664]{1,0:T(8,128)(2,1)}, bf16[256,1664]{1,0:T(8,128)(2,1)}, u32[]{:S(2)}, u32[]{:S(2)}) collective-permute-start(bf16[256,1664]{1,0:T(8,128)(2,1)} %pad_maximum_fusion.8.refs_1_.value_ref), channel_id=1, source_target_pairs={{0,2},{2,0},{4,6},{6,4},{1,3},{3,1},{5,7},{7,5},{8,10},{10,8},{12,... | collective-permute-start | bytes 2555912 | tf_op jit(solution)/shard_map/ppermute | solution.py:62
  363.0 21.6 %collective-permute-start.53 = (bf16[256,1664]{1,0:T(8,128)(2,1)}, bf16[256,1664]{1,0:T(8,128)(2,1)}, u32[]{:S(2)}, u32[]{:S(2)}) collective-permute-start(bf16[256,1664]{1,0:T(8,128)(2,1)} %pad_maximum_fusion.9.refs_2_), channel_id=1, source_target_pairs={{0,4},{2,6},{4,0},{6,2},{1,5},{3,7},{5,1},{7,3},{8,12},{10,14},{12... | collective-permute-start | bytes 2555912 | tf_op jit(solution)/shard_map/ppermute | solution.py:62
  364.1 20.4 %collective-permute-start.51 = (bf16[256,1536]{1,0:T(8,128)(2,1)}, bf16[256,1536]{1,0:T(8,128)(2,1)}, u32[]{:S(2)}, u32[]{:S(2)}) collective-permute-start(bf16[256,1536]{1,0:T(8,128)(2,1)} %after.60), channel_id=1, source_target_pairs={{0,1},{1,0},{2,3},{3,2},{4,5},{5,4},{6,7},{7,6},{8,9},{9,8},{10,11... | collective-permute-start | bytes 2359304 | tf_op jit(solution)/shard_map/ppermute | solution.py:58
  381.4 141.0 %collective-permute-start.64 = (bf16[3,3,384,256]{3,2,1,0:T(8,128)(2,1)}, bf16[3,3,384,256]{3,2,1,0:T(8,128)(2,1)}, u32[]{:S(2)}, u32[]{:S(2)}) collective-permute-start(bf16[3,3,384,256]{3,2,1,0:T(8,128)(2,1)} %get-tuple-element.204.refs_2_), channel_id=1, source_target_pairs={{0,8},{8,0},{16,24},{24,16},{1,9},{9,1},{17,25},{25,17},{2,10},{10... | collective-permute-start | bytes 5308424 | tf_op jit(solution)/shard_map/ppermute | solution.py:62
  392.1 26.6 %collective-permute-start.54 = (bf16[256,1536]{1,0:T(8,128)(2,1)S(1)}, bf16[256,1536]{1,0:T(8,128)(2,1)S(1)}, u32[]{:S(2)}, u32[]{:S(2)}) collective-permute-start(bf16[256,1536]{1,0:T(8,128)(2,1)S(1)} %copy-done.21), channel_id=1, source_target_pairs={{0,1},{1,0},{2,3},{3,2},{4,5},{5,4},{6,7},{7,6},{8,9},{9,8},{10,11... | collective-permute-start | bytes 2359304 | tf_op jit(solution)/shard_map/ppermute | solution.py:58
  416.9 158.8 %collective-permute-start.72 = (bf16[5,3,384,256]{3,2,1,0:T(8,128)(2,1)}, bf16[5,3,384,256]{3,2,1,0:T(8,128)(2,1)}, u32[]{:S(2)}, u32[]{:S(2)}) collective-permute-start(bf16[5,3,384,256]{3,2,1,0:T(8,128)(2,1)} %get-tuple-element.209.refs_2_), channel_id=1, source_target_pairs={{0,8},{8,0},{16,24},{24,16},{1,9},{9,1},{17,25},{25,17},{2,10},{10... | collective-permute-start | bytes 8847368 | tf_op jit(solution)/shard_map/ppermute | solution.py:62
  432.0 61.9 %collective-permute-start.60 = (bf16[2,96,896]{2,1,0:T(8,128)(2,1)}, bf16[2,96,896]{2,1,0:T(8,128)(2,1)}, u32[]{:S(2)}, u32[]{:S(2)}) collective-permute-start(bf16[2,96,896]{2,1,0:T(8,128)(2,1)} %get-tuple-element.293.value_ref), channel_id=1, source_target_pairs={{0,2},{2,0},{4,6},{6,4},{1,3},{3,1},{5,7},{7,5},{8,10},{10,8},{12,... | collective-permute-start | bytes 1032200 | tf_op jit(solution)/shard_map/ppermute | solution.py:62
  474.3 19.6 %collective-permute-start.58 = (bf16[2,96,896]{2,1,0:T(8,128)(2,1)}, bf16[2,96,896]{2,1,0:T(8,128)(2,1)}, u32[]{:S(2)}, u32[]{:S(2)}) collective-permute-start(bf16[2,96,896]{2,1,0:T(8,128)(2,1)} %get-tuple-element.292), channel_id=1, source_target_pairs={{0,4},{2,6},{4,0},{6,2},{1,5},{3,7},{5,1},{7,3},{8,12},{10,14},{12... | collective-permute-start | bytes 1032200 | tf_op jit(solution)/shard_map/ppermute | solution.py:62
  522.4 27.2 %collective-permute-start.57 = (f32[256,1536]{1,0:T(8,128)}, f32[256,1536]{1,0:T(8,128)}, u32[]{:S(2)}, u32[]{:S(2)}) collective-permute-start(f32[256,1536]{1,0:T(8,128)} %subtract_add_fusion), channel_id=1, source_target_pairs={{0,1},{1,0},{2,3},{3,2},{4,5},{5,4},{6,7},{7,6},{8,9},{9,8},{10,11... | collective-permute-start | bytes 4718600 | tf_op jit(solution)/shard_map/ppermute | solution.py:58
  545.6 25.0 %collective-permute-start.66 = (bf16[4,96,1408]{2,1,0:T(8,128)(2,1)}, bf16[4,96,1408]{2,1,0:T(8,128)(2,1)}, u32[]{:S(2)}, u32[]{:S(2)}) collective-permute-start(bf16[4,96,1408]{2,1,0:T(8,128)(2,1)} %pad_maximum_fusion.4.value_ref), channel_id=1, source_target_pairs={{0,2},{2,0},{4,6},{6,4},{1,3},{3,1},{5,7},{7,5},{8,10},{10,8},{12,... | collective-permute-start | bytes 3244040 | tf_op jit(solution)/shard_map/ppermute | solution.py:62
  547.5 24.6 %collective-permute-start.68 = (bf16[4,96,1408]{2,1,0:T(8,128)(2,1)}, bf16[4,96,1408]{2,1,0:T(8,128)(2,1)}, u32[]{:S(2)}, u32[]{:S(2)}) collective-permute-start(bf16[4,96,1408]{2,1,0:T(8,128)(2,1)} %pad_maximum_fusion.5), channel_id=1, source_target_pairs={{0,4},{2,6},{4,0},{6,2},{1,5},{3,7},{5,1},{7,3},{8,12},{10,14},{12... | collective-permute-start | bytes 3244040 | tf_op jit(solution)/shard_map/ppermute | solution.py:62
  (136 other events, 824.5 us)

commit v4 on v3

v4 whole, which is shorter than its diff:
```python
import functools

import jax
import jax.numpy as jnp
from jax import lax
from jax.experimental import pallas as pl
from jax.experimental.pallas import tpu as pltpu
from jax.sharding import PartitionSpec as P

HEAD_DIMENSION = 64
SEQUENCE_LENGTH = 512
ABLK = 256


EPS = 1e-06
VMEM_LIMIT = 56 * 1024 * 1024
HOLDS = True
THETA = 10000.0
bfloat = jnp.bfloat16
single = jnp.float32


def pass_kernel(*refs):
    pass


def after_all(values, *others):
    anywhere = pl.BlockSpec(memory_space=pl.ANY)
    return pl.pallas_call(
        pass_kernel,
        name="after",
        in_specs=[anywhere] * (len(values) + len(others)),
        out_specs=[anywhere] * len(values),
        out_shape=[jax.ShapeDtypeStruct(value.shape, value.dtype) for value in values],
        input_output_aliases={i: i for i in range(len(values))},
        cost_estimate=pl.CostEstimate(flops=0, bytes_accessed=0, transcendentals=0),
    )(*values, *others)


def after(value, *others):
    return after_all([value], *others)[0] if others else value


def hold_kernel(value_ref, out_ref):
    out_ref[...] = jnp.zeros_like(out_ref)


def hold(value):
    if not HOLDS:
        return []
    return [
        pl.pallas_call(
            hold_kernel,
            name="hold",
            in_specs=[pl.BlockSpec(memory_space=pl.ANY)],
            out_shape=jax.ShapeDtypeStruct((8, 128), single),
            cost_estimate=pl.CostEstimate(flops=10**12, bytes_accessed=10**9, transcendentals=0),
        )(value)
    ]


def swap(value):
    return lax.ppermute(value, "tensor", [(0, 1), (1, 0)])


def to_peer(value, axis, step):
    return lax.ppermute(value, axis, [(i, i ^ step) for i in range(lax.axis_size(axis))])


def to_mirror(value):
    count = lax.axis_size("dp")
    return lax.ppermute(value, "dp", [(i, count - 1 - i) for i in range(count)])


def from_peers(value):
    return [to_peer(value, "expert", s) for s in range(1, lax.axis_size("expert"))]


def halves_kernel(low_ref, high_ref, *refs):
    refs[-2][...] = low_ref[...]
    refs[-1][...] = high_ref[...]


def low_and_high(low, high, *others):
    rows, width = low.shape
    half = jax.ShapeDtypeStruct((rows // 2, width), low.dtype)
    return pl.pallas_call(
        halves_kernel,
        name="halves",
        grid=(1,),
        in_specs=[
            pl.BlockSpec((rows // 2, width), lambda i: (0, 0)),
            pl.BlockSpec((rows // 2, width), lambda i: (1, 0)),
        ]
        + [pl.BlockSpec(memory_space=pl.ANY)] * len(others),
        out_specs=[pl.BlockSpec((rows // 2, width), lambda i: (0, 0))] * 2,
        out_shape=[half, half],
        cost_estimate=pl.CostEstimate(flops=0, bytes_accessed=2**20, transcendentals=0),
    )(low, high, *others)


def spread(value, pause=()):
    own_other = swap(value)
    if lax.axis_size("expert") != 4:
        near = from_peers(value)
        near[0] = after(near[0], own_other, *hold(value), *pause)
        return [value, own_other] + [part for mine in near for part in (mine, swap(mine))]
    first, second = to_peer(value, "expert", 1), to_peer(value, "expert", 2)
    for_first, for_second = low_and_high(second, first, own_other, *hold(value), *pause)
    low, high = to_peer(for_first, "expert", 1), to_peer(for_second, "expert", 2)
    first_other, second_other = swap(first), swap(second)
    low = after(low, *hold(for_first), first_other, second_other)
    return [value, own_other, first, first_other, second, second_other, low, high, swap(low), swap(high)]


def farther_kernel(mine_ref, other_ref, low_ref, high_ref):
    cut = low_ref.shape[0]
    total = (mine_ref[0].astype(single) + other_ref[0].astype(single)).astype(bfloat)
    low_ref[...] = total[:cut]
    high_ref[...] = total[cut:]


def nearer_kernel(mine_first, other_first, mine_second, other_second, low_ref, high_ref, first_ref, second_ref):
    step = pl.program_id(0)
    low = jnp.where(step == 0, low_ref[...].astype(single), 0.0)
    high = jnp.where(step == 0, 0.0, high_ref[...].astype(single))
    first = mine_first[0].astype(single) + other_first[0].astype(single) + high
    second = mine_second[0].astype(single) + other_second[0].astype(single) + low
    first_ref[...] = first.astype(bfloat)
    second_ref[...] = second.astype(bfloat)


def send_farthest(mine, other):
    _, span, width = mine.shape
    half = jax.ShapeDtypeStruct((span // 2, width), bfloat)
    low, high = pl.pallas_call(
        farther_kernel,
        name="farther",
        out_shape=[half, half],
        cost_estimate=pl.CostEstimate(flops=0, bytes_accessed=2**21, transcendentals=0),
    )(mine, other)
    return [to_peer(low, "expert", 1), to_peer(high, "expert", 2)], (low, high)


def send_nearer(mine, other, came):
    _, span, width = mine.shape
    half = pl.BlockSpec((span // 2, width), lambda i: (i, 0))
    only = pl.BlockSpec((span // 2, width), lambda i: (0, 0))
    stacked = lambda index: pl.BlockSpec((1, span // 2, width), lambda i: (index, i, 0))
    whole = jax.ShapeDtypeStruct((span, width), bfloat)
    first, second = pl.pallas_call(
        nearer_kernel,
        name="nearer",
        grid=(2,),
        in_specs=[stacked(0), stacked(0), stacked(1), stacked(1), only, only],
        out_specs=[half, half],
        out_shape=[whole, whole],
        cost_estimate=pl.CostEstimate(flops=0, bytes_accessed=2**22, transcendentals=0),
    )(mine, other, mine, other, *came)
    return [to_peer(first, "expert", 1), to_peer(second, "expert", 2)], (first, second)


def start_sum(parts):
    if len(parts) != 4:
        return parts, None
    low, high = parts[3]
    return parts, [to_peer(low, "expert", 1), to_peer(high, "expert", 2)]


def go_on(state, *others):
    parts, came = state
    if came is None:
        sent = [after(part, *others) for part in parts[1:]]
        return [parts[0]] + [to_peer(part, "expert", i) for i, part in enumerate(sent, 1)], sent
    low = after(came[0], *hold(parts[3][0]), *others).astype(single)
    high = came[1].astype(single)
    cut = low.shape[0]
    first, second = parts[1].astype(single), parts[2].astype(single)
    first = jnp.concatenate([first[:cut], first[cut:] + high], axis=0).astype(bfloat)
    second = jnp.concatenate([second[:cut] + low, second[cut:]], axis=0).astype(bfloat)
    return [parts[0], to_peer(first, "expert", 1), to_peer(second, "expert", 2)], [first, second]


def add_up(own, arrived):
    total = own.astype(single)
    for part in arrived:
        total = total + part.astype(single)
    return total


def sum_all(value, axes):
    for axis in axes:
        step = 1
        while step < lax.axis_size(axis):
            value = value + to_peer(value, axis, step)
            step *= 2
    return value


def over_dp(total):
    at_dp, count = lax.axis_index("dp"), lax.axis_size("dp")
    parts = {r: lax.dynamic_index_in_dim(total, at_dp ^ r, 0, keepdims=False) for r in range(count)}
    step = 1
    while step < count:
        leaving = [r for r in parts if r & step]
        sent = jnp.concatenate([parts[r].astype(bfloat) for r in leaving], axis=0)
        came = to_peer(sent, "dp", step).astype(single)
        rows = came.shape[0] // len(leaving)
        for i, r in enumerate(leaving):
            parts[r ^ step] = parts[r ^ step] + came[i * rows : (i + 1) * rows]
            del parts[r]
        step *= 2
    return parts[0]


def dot(left, right):
    return lax.dot_general(left, right, (((1,), (0,)), ((), ())), preferred_element_type=single)


def dot_nt(left, right):
    return lax.dot_general(left, right, (((1,), (1,)), ((), ())), preferred_element_type=single)


def dot_tn(left, right):
    return lax.dot_general(left, right, (((0,), (0,)), ((), ())), preferred_element_type=single)


def picks(slot, capacity):
    return slot == lax.broadcasted_iota(jnp.int32, (capacity, slot.shape[1]), 0)


def group_parts(parts, joined_ref):
    if joined_ref is None:
        return [(parts[i], parts[i + 1]) for i in range(0, len(parts), 2)]
    cut = parts[-1].shape[0]

    @pl.when(pl.program_id(0) == 0)
    def _():
        for i in range(2):
            for j in range(2):
                joined_ref[i, j * cut : (j + 1) * cut, :] = parts[-4 + 2 * i + j][...]

    pairs = [(parts[i], parts[i + 1]) for i in range(0, len(parts) - 4, 2)]
    return pairs + [(joined_ref.at[0], joined_ref.at[1])]


def find_slots(first_ref, top_count, pairs, slots_ref, count_ref):
    groups, experts, tokens = slots_ref.shape
    row = lax.broadcasted_iota(jnp.int32, (tokens, tokens), 0)
    earlier = (row < lax.broadcasted_iota(jnp.int32, (tokens, tokens), 1)).astype(bfloat)
    ids = lax.broadcasted_iota(jnp.int32, (experts, tokens), 0)
    ids = (ids + first_ref[0]).astype(single)
    total = None
    for group, pair in enumerate(pairs):
        tails = [part[:, part.shape[1] - 128 :].astype(single).T for part in pair]
        routes = jnp.concatenate(tails, axis=1)[128 - top_count :]
        valid = routes[:1] >= 64.0
        ahead = jnp.where(valid, 1.0, 0.0)
        total = ahead if total is None else total + ahead
        mask = ids == routes[:1] - 64.0 * ahead
        for k in range(1, top_count):
            mask = mask | (ids == routes[k : k + 1])
        before = dot(mask.astype(single).astype(bfloat), earlier)
        slots_ref[group] = jnp.where(mask, before, -1.0).astype(jnp.int32)
    count_ref[...] = jnp.broadcast_to(jnp.sum(total, axis=1, keepdims=True), count_ref.shape)


def gather_rows(slots_ref, expert, pairs, rows_ref):
    capacity = rows_ref.shape[0] // len(pairs)
    width = rows_ref.shape[1]
    for group, (mine, other) in enumerate(pairs):
        span = mine.shape[0]
        slot = slots_ref[group, pl.ds(expert, 1), :]
        picked = picks(slot, capacity).astype(bfloat)
        rows = dot(picked[:, :span], mine[:, :width]) + dot(picked[:, span:], other[:, :width])
        rows_ref[group * capacity : (group + 1) * capacity, :] = rows.astype(bfloat)


def slot_gates(expert, tails, count):
    lane = lax.broadcasted_iota(jnp.int32, tails.shape, 1)
    chosen = (lane == expert) | (lane == expert + count) | (lane == expert + 2 * count)
    return jnp.sum(jnp.where(chosen, tails.astype(single), 0.0), axis=1, keepdims=True)


def half_columns(place_ref, width):
    return pl.ds(pl.multiple_of(place_ref[1] * width, 128), width)


def return_order(groups):
    rest = list(range(1, groups)) + [0]
    return [[3], [1, 2, 0]] if groups == 4 else [rest]


def forward_kernel(count, top_count, amount, halved, start, with_out, place_ref, gate_w, up_w, *refs):
    if with_out:
        down_w, refs = refs[0], refs[1:]
    parts, refs = refs[:amount], refs[amount:]
    parts, pins = parts[:-1], parts[-1:]
    gate_ref, up_ref, half_ref, tail_ref, slots_ref, count_ref = refs[:6]
    refs = refs[6:]
    step = pl.program_id(0)
    joined_ref = refs[-1] if halved else None
    rows_ref = refs[-2] if halved else refs[-1]
    width = gate_w.shape[1]
    pairs = group_parts(parts, joined_ref)

    @pl.when(step == 0)
    def _():
        find_slots(place_ref, top_count, pairs, slots_ref, count_ref)

    gather_rows(slots_ref, start + step, pairs, rows_ref)
    half_ref[0] = rows_ref[:, half_columns(place_ref, half_ref.shape[2])]
    tails = rows_ref[:, width:]
    tail_ref[0] = tails
    rows = rows_ref[:, :width]
    gate_pre = dot(rows, gate_w[0])
    up_pre = dot(rows, up_w[0])
    gate_ref[0] = gate_pre.astype(bfloat)
    up_ref[0] = up_pre.astype(bfloat)
    if with_out:
        gates = slot_gates(place_ref[0] + start + step, tails, count)
        hidden = (gate_pre * jax.nn.sigmoid(gate_pre) * up_pre * gates).astype(bfloat)
        refs[0][0] = dot(hidden, down_w[0]).astype(bfloat)


def hidden_grads(gate_pre, up_pre, gates, grad_hidden):
    sig = jax.nn.sigmoid(gate_pre)
    silu = gate_pre * sig
    hidden = silu * up_pre
    scaled = grad_hidden * gates
    grad_gate_pre = (scaled * up_pre * sig * (1.0 + gate_pre * (1.0 - sig))).astype(bfloat)
    grad_up_pre = (scaled * silu).astype(bfloat)
    return hidden, (hidden * gates).astype(bfloat), grad_gate_pre, grad_up_pre


def backward_kernel(count, amount, halved, place_ref, slots_ref, gate_w, up_w, down_w, gate_ref, up_ref, tail_ref, *refs):
    parts, refs = refs[:amount], refs[amount:]
    hidden_ref, grad_gate_ref, grad_up_ref, half_ref, refs = refs[0], refs[1], refs[2], refs[3], refs[4:]
    back_ref, rows_ref = refs[:2]
    joined_ref = refs[2] if halved else None
    width = gate_w.shape[1]
    step = pl.program_id(0)
    expert = place_ref[0] + step
    gather_rows(slots_ref, step, group_parts(parts, joined_ref), rows_ref)
    half_ref[0] = rows_ref[:, half_columns(place_ref, half_ref.shape[2])]
    gates = slot_gates(expert, tail_ref[0], count)
    grad_hidden = dot_nt(rows_ref[:, :width], down_w[0])
    hidden, hidden_low, grad_gate_pre, grad_up_pre = hidden_grads(
        gate_ref[0].astype(single), up_ref[0].astype(single), gates, grad_hidden
    )
    hidden_ref[0] = hidden_low
    grad_gate_ref[0] = grad_gate_pre
    grad_up_ref[0] = grad_up_pre
    back = dot_nt(grad_gate_pre, gate_w[0]) + dot_nt(grad_up_pre, up_w[0])
    back_ref[0, :, :width] = back.astype(bfloat)
    tails = rows_ref[:, width:].astype(single)
    lane = lax.broadcasted_iota(jnp.int32, tails.shape, 1)
    inner = jnp.sum(jnp.where(lane < 3, tails, 0.0), axis=1, keepdims=True)
    inner = inner * (place_ref[2] == 0).astype(single)
    grad_logit = gates * (jnp.sum(hidden * grad_hidden, axis=1, keepdims=True) - inner)
    back_ref[0, :, width:] = jnp.where(lane == expert, grad_logit, 0.0).astype(bfloat)


def weights_kernel(count, groups, start, place_ref, slots_ref, down_w, gate_ref, up_ref, tail_ref, *refs):
    hidden_near, gate_near, up_near, near_x, near_g, far_x = refs[:6]
    parts, refs = refs[6 : 6 + 2 * groups], refs[6 + 2 * groups :]
    shards, (rows_ref, full_ref) = refs[:-2], refs[-2:]
    expert = start + pl.program_id(0)
    gather_rows(slots_ref, expert, group_parts(parts, None), rows_ref)
    gates = slot_gates(place_ref[0] + expert, tail_ref[0], count)
    grad_hidden = dot_nt(rows_ref[...], down_w[0])
    _, hidden, grad_gate_pre, grad_up_pre = hidden_grads(
        gate_ref[0].astype(single), up_ref[0].astype(single), gates, grad_hidden
    )
    far_g = rows_ref[:, half_columns(place_ref, full_ref.shape[1])]
    far, near = far_x[0], near_x[0]
    sums = (
        dot_tn(far, grad_gate_pre) + dot_tn(near, gate_near[0]),
        dot_tn(far, grad_up_pre) + dot_tn(near, up_near[0]),
        dot_tn(far_g, hidden) + dot_tn(near_g[0], hidden_near[0]),
    )
    for i, value in enumerate(sums):
        full_ref[i] = value.astype(bfloat)
    size = shards[0].shape[2]
    for step, shard in enumerate(shards):
        at = pl.multiple_of((place_ref[3] ^ step) * size, size)
        for i in range(3):
            shard[0, i] = full_ref[i, pl.ds(at, size), :]


def finish_kernel(scale_ref, own_ref, *refs):
    arrived, (d_gate, d_up, d_down, done_ref) = refs[:-4], refs[-4:]
    scale = scale_ref[:1, :1]

    def total(i):
        value = own_ref[0, i].astype(single)
        for ref in arrived:
            value = value + ref[0, i].astype(single)
        return value * scale

    d_gate[0] = total(0)
    d_up[0] = total(1)
    d_down[0] = total(2).T
    done_ref[...] = scale_ref[...]


def finish_more_kernel(gate_in, up_in, down_in, scale_ref, *refs):
    finish_kernel(scale_ref, *refs)


def return_kernel(first, cycle, slots_ref, rows_ref, mine, other, picked_ref):
    experts, capacity, width = rows_ref.shape
    span = mine.shape[1]
    group = (pl.program_id(0) + first) % cycle

    @pl.when(pl.program_id(1) == 0)
    def _():
        for e in range(experts):
            slot = slots_ref[group, e : e + 1, :]
            picked_ref[e * capacity : (e + 1) * capacity, :] = picks(slot, capacity).astype(bfloat)

    back = dot_tn(picked_ref[...], rows_ref[...].reshape(experts * capacity, width)).astype(bfloat)
    mine[0] = back[:span]
    other[0] = back[span:]


def kernel_call(kernel, name, grid, in_specs, out_specs, out_shape, scratch, flops, moved, args, prefetch=0, aliases=None):
    return pl.pallas_call(
        kernel,
        name=name,
        grid_spec=pltpu.PrefetchScalarGridSpec(
            num_scalar_prefetch=prefetch,
            grid=grid,
            in_specs=in_specs,
            out_specs=out_specs,
            scratch_shapes=scratch,
        ),
        out_shape=out_shape,
        input_output_aliases=aliases or {},
        compiler_params=pltpu.CompilerParams(
            dimension_semantics=("arbitrary",) * len(grid), vmem_limit_bytes=VMEM_LIMIT
        ),
        cost_estimate=pl.CostEstimate(flops=flops, bytes_accessed=moved, transcendentals=0),
    )(*args)


def per_expert(*shape, start=0):
    return pl.BlockSpec((1,) + shape, lambda e, *_: (e + start,) + (0,) * len(shape))


def once(*shape):
    return pl.BlockSpec(
        shape, lambda e, *_: (0,) * len(shape), pipeline_mode=pl.Buffered(buffer_count=1)
    )


def return_rows(slots, rows, order, capacity, span):
    groups, _, tokens = slots.shape
    experts, _, width = rows.shape
    amount, first = len(order), order[0]
    cycle = amount if amount > 1 else groups
    cuts = 2 if width % 256 == 0 else 1
    cut = width // cuts
    part = pl.BlockSpec((1, span, cut), lambda g, n: (g, 0, n))
    return kernel_call(
        functools.partial(return_kernel, first, cycle),
        "return_rows",
        (amount, cuts),
        [
            pl.BlockSpec(slots.shape, lambda g, n: (0, 0, 0)),
            pl.BlockSpec((experts, capacity, cut), lambda g, n: (0, (g + first) % cycle, n)),
        ],
        [part, part],
        [jax.ShapeDtypeStruct((amount, span, width), bfloat)] * 2,
        [pltpu.VMEM((experts * capacity, tokens), bfloat)],
        2 * amount * experts * capacity * tokens * width,
        2 * amount * (experts * capacity + tokens) * width,
        (slots, rows),
    )


def expert_forward(place, count, top_count, pin, weights, parts, groups, capacity, start, experts):
    span, whole = parts[0].shape
    tokens = 2 * span
    width, hidden = weights[0].shape[1:]
    with_out = len(weights) == 3
    total = groups * capacity
    halved = len(parts) > 2 * groups
    specs = [per_expert(width, hidden, start=start)] * 2
    outs = [per_expert(total, hidden)] * 2
    outs += [per_expert(total, width // 2), per_expert(total, whole - width)]
    shapes = [jax.ShapeDtypeStruct((experts, total, hidden), bfloat)] * 2
    shapes += [jax.ShapeDtypeStruct((experts, total, width // 2), bfloat)]
    shapes += [jax.ShapeDtypeStruct((experts, total, whole - width), bfloat)]
    listed = (groups, -(-weights[0].shape[0] // 8) * 8, tokens)
    outs += [pl.BlockSpec(listed, lambda e, *_: (0, 0, 0)), pl.BlockSpec((8, 128), lambda e, *_: (0, 0))]
    shapes += [jax.ShapeDtypeStruct(listed, jnp.int32), jax.ShapeDtypeStruct((8, 128), single)]
    scratch = [pltpu.VMEM((total, whole), bfloat)]
    if halved:
        scratch += [pltpu.VMEM((2, span, whole), bfloat)]
    if with_out:
        specs += [per_expert(hidden, width, start=start)]
        outs += [per_expert(total, width)]
        shapes += [jax.ShapeDtypeStruct((experts, total, width), bfloat)]
    specs += [once(*part.shape) for part in parts] + [pl.BlockSpec(memory_space=pl.ANY)]
    return kernel_call(
        functools.partial(forward_kernel, count, top_count, len(parts) + 1, halved, start, with_out),
        "expert_forward" if with_out else "expert_forward_far",
        (experts,), specs, outs, shapes, scratch,
        2 * experts * total * (width * hidden * len(weights) + tokens * whole),
        2 * experts * (len(weights) * width * hidden + total * width + 4 * total * hidden),
        (place,) + tuple(weights) + tuple(parts) + (pin,),
        prefetch=1,
    )


def expert_backward(place, count, slots, weights, gate_pre, up_pre, tails, parts, capacity):
    groups, _, tokens = slots.shape
    experts = weights[0].shape[0]
    span, whole = parts[0].shape
    width, hidden = weights[0].shape[1:]
    total = groups * capacity
    thin = per_expert(total, hidden)
    specs = [once(*slots.shape)] + [per_expert(width, hidden)] * 2
    specs += [per_expert(hidden, width), thin, thin, per_expert(total, tails.shape[2])]
    outs = [thin] * 3 + [per_expert(total, width // 2), per_expert(total, whole)]
    shapes = [jax.ShapeDtypeStruct((experts, total, hidden), bfloat)] * 3
    shapes += [jax.ShapeDtypeStruct((experts, total, width // 2), bfloat)]
    shapes += [jax.ShapeDtypeStruct((experts, total, whole), bfloat)]
    return kernel_call(
        functools.partial(backward_kernel, count, len(parts), len(parts) > 2 * groups),
        "expert_backward",
        (experts,), specs + [once(*part.shape) for part in parts], outs, shapes,
        [pltpu.VMEM((total, whole), bfloat)]
        + ([pltpu.VMEM((2, span, whole), bfloat)] if len(parts) > 2 * groups else []),
        2 * experts * total * width * (hidden * 3 + tokens),
        2 * experts * (3 * width * hidden + 3 * total * width // 2 + 7 * total * hidden),
        (place, slots) + tuple(weights) + (gate_pre, up_pre, tails) + tuple(parts),
        prefetch=1,
    )


def expert_weights(place, count, slots, down_w, far, near, parts, capacity, start, far_start, experts, shards):
    groups, _, tokens = slots.shape
    hidden, width = down_w.shape[1:]
    total = groups * capacity
    far_pre, (far_tails, far_half) = far[:2], far[2:]
    thin = per_expert(total, hidden, start=far_start)
    wide = per_expert(total, width // 2, start=far_start)
    thin_at = per_expert(total, hidden, start=start)
    wide_at = per_expert(total, width // 2, start=start)
    specs = [once(*slots.shape), per_expert(hidden, width, start=start)]
    specs += [thin, thin, per_expert(total, far_tails.shape[2], start=far_start)] + [thin_at] * 3
    specs += [wide_at, wide_at, wide]
    size = width // (2 * shards)
    return kernel_call(
        functools.partial(weights_kernel, count, groups, start),
        "expert_weights",
        (experts,), specs + [once(*part.shape) for part in parts],
        [per_expert(3, size, hidden)] * shards,
        [jax.ShapeDtypeStruct((experts, 3, size, hidden), bfloat)] * shards,
        [pltpu.VMEM((total, width), bfloat), pltpu.VMEM((3, width // 2, hidden), bfloat)],
        2 * experts * total * width * (hidden * 4 + tokens),
        2 * experts * (5 * width * hidden // 2 + 3 * total * width // 2 + 7 * total * hidden),
        (place, slots, down_w) + tuple(far_pre) + (far_tails,) + tuple(near) + (far_half,) + tuple(parts),
        prefetch=1,
    )


def finish_weights(experts, start, scale, own, arrived, before):
    some, _, size, hidden = own.shape
    ready = [per_expert(3, size, hidden)] * (1 + len(arrived))
    kernel = finish_kernel if before is None else finish_more_kernel
    kept = [] if before is None else [pl.BlockSpec(memory_space=pl.ANY)] * 3
    small = pl.BlockSpec((8, 128), lambda e, *_: (0, 0))
    *grads, done = kernel_call(
        kernel,
        "finish_weights",
        (some,),
        kept + [small] + ready,
        [per_expert(size, hidden, start=start)] * 2 + [per_expert(hidden, size, start=start), small],
        [jax.ShapeDtypeStruct((experts, size, hidden), single)] * 2
        + [jax.ShapeDtypeStruct((experts, hidden, size), single), jax.ShapeDtypeStruct((8, 128), single)],
        [],
        3 * some * size * hidden,
        12 * some * size * hidden,
        tuple(before or ()) + (scale, own) + tuple(arrived),
        aliases={} if before is None else {0: 0, 1: 1, 2: 2},
    )
    return grads, done


def rotate(value, cosines, sines, back):
    pieces = []
    for at in range(0, value.shape[1], 128):
        piece = value[:, at : at + 128]
        lane = lax.broadcasted_iota(jnp.int32, piece.shape, 1)
        later, sooner = pltpu.roll(piece, 96, 1), pltpu.roll(piece, 32, 1)
        if back:
            turned = jnp.where(lane % 64 < 32, later, -sooner)
        else:
            turned = jnp.where(lane % 64 < 32, -later, sooner)
        pieces.append(piece * cosines + turned * sines)
    return pieces[0] if len(pieces) == 1 else jnp.concatenate(pieces, axis=1)


def query_blocks(length):
    return [(at, at + ABLK) for at in range(0, length, ABLK)]


def attend_kernel(place_ref, tokens_ref, gain_ref, query_w, key_w, value_w, out_w, cos_ref, sin_ref,
                  normed_ref, queries_ref, keys_ref, values_ref, mixed_ref, lse_ref, stay_ref, leave_ref, total_ref):
    step = pl.program_id(0)
    length = tokens_ref.shape[0]
    group = query_w.shape[1] // key_w.shape[1]

    @pl.when(step == 0)
    def _():
        inputs = tokens_ref[...].astype(single)
        inverse = lax.rsqrt(jnp.mean(inputs * inputs, axis=1, keepdims=True) + EPS)
        normed_ref[...] = (inputs * inverse * gain_ref[...]).astype(bfloat)

    normed = normed_ref[...]
    cosines, sines = cos_ref[...], sin_ref[...]
    queries = rotate(dot(normed, query_w[...]), cosines, sines, False) * HEAD_DIMENSION ** (-0.5)
    keys = rotate(dot(normed, key_w[...]), cosines, sines, False)
    values = dot(normed, value_w[...])
    size = HEAD_DIMENSION
    mixed = []
    for kv in range(key_w.shape[1] // size):
        key = keys[:, kv * size : (kv + 1) * size].astype(bfloat)
        value = values[:, kv * size : (kv + 1) * size].astype(bfloat)
        keys_ref[kv] = key
        values_ref[kv] = value
        for head in range(kv * group, (kv + 1) * group):
            query = queries[:, head * size : (head + 1) * size].astype(bfloat)
            queries_ref[head] = query
            outs, sums = [], []
            for start, seen in query_blocks(length):
                scores = dot_nt(key[:seen], query[start : start + ABLK])
                peak = jnp.max(scores, axis=0, keepdims=True)
                weights = jnp.exp(scores - peak)
                total = jnp.sum(weights, axis=0, keepdims=True)
                probs = (weights / total).astype(bfloat)
                outs.append(dot_tn(value[:seen], probs))
                sums.append(peak + jnp.log(total))
            mixed.append(jnp.concatenate(outs, axis=1))
            lse_ref[0, head : head + 1, :] = jnp.concatenate(sums, axis=1)
    mixed = jnp.concatenate(mixed, axis=0).T.astype(bfloat)
    mixed_ref[...] = mixed
    part = dot(mixed, out_w[...])

    @pl.when(step == 0)
    def _():
        total_ref[...] = part

    @pl.when(step > 0)
    def _():
        total_ref[...] += part

    @pl.when(step == pl.num_programs(0) - 1)
    def _():
        span = stay_ref.shape[0]
        core = place_ref[2]
        mine = pl.ds(pl.multiple_of(core * span, span), span)
        other = pl.ds(pl.multiple_of((1 - core) * span, span), span)
        stay_ref[...] = total_ref[mine, :] + tokens_ref[mine, :].astype(single)
        leave_ref[...] = total_ref[other, :]


def attend_back_kernel(place_ref, mine_ref, other_ref, tokens_ref, query_w, key_w, value_w, out_w, cos_ref, sin_ref,
                       queries_ref, keys_ref, values_ref, lse_ref,
                       raw_query_ref, raw_key_ref, raw_value_ref, stay_ref, leave_ref, gain_ref, low_ref, total_ref):
    step = pl.program_id(0)
    length = tokens_ref.shape[0]
    span = mine_ref.shape[0]
    core = place_ref[2]
    mine = pl.ds(pl.multiple_of(core * span, span), span)
    other = pl.ds(pl.multiple_of((1 - core) * span, span), span)
    low_ref[mine, :] = dot_nt(mine_ref[...], out_w[...]).astype(bfloat)
    low_ref[other, :] = dot_nt(other_ref[...], out_w[...]).astype(bfloat)
    grads = low_ref[...].astype(single)
    size = HEAD_DIMENSION
    group = query_w.shape[1] // key_w.shape[1]
    grad_queries, grad_keys, grad_values = [], [], []
    for kv in range(key_w.shape[1] // size):
        key, value = keys_ref[kv], values_ref[kv]
        key_parts = [[] for _ in query_blocks(length)]
        value_parts = [[] for _ in query_blocks(length)]
        for head in range(kv * group, (kv + 1) * group):
            query = queries_ref[head]
            grad = grads[:, head * size : (head + 1) * size].astype(bfloat)
            outs = []
            for block, (start, seen) in enumerate(query_blocks(length)):
                rows = slice(start, start + ABLK)
                scores = dot_nt(key[:seen], query[rows])
                probs = jnp.exp(scores - lse_ref[0, head : head + 1, rows])
                grad_probs = dot_nt(value[:seen], grad[rows])
                inner = jnp.sum(probs * grad_probs, axis=0, keepdims=True)
                grad_scores = (probs * (grad_probs - inner)).astype(bfloat)
                outs.append(dot_tn(grad_scores, key[:seen]))
                key_parts[block].append(dot(grad_scores, query[rows]))
                value_parts[block].append(dot(probs.astype(bfloat), grad[rows]))
            grad_queries.append(jnp.concatenate(outs, axis=0))

        def whole(parts):
            rows = []
            for at in range(len(parts)):
                here = slice(at * ABLK, (at + 1) * ABLK)
                rows.append(sum(one[here] for block in parts[at:] for one in block))
            return jnp.concatenate(rows, axis=0)

        grad_keys.append(whole(key_parts))
        grad_values.append(whole(value_parts))
    cosines, sines = cos_ref[...], sin_ref[...]
    grad_query = jnp.concatenate(grad_queries, axis=1) * HEAD_DIMENSION ** (-0.5)
    raw_query = rotate(grad_query, cosines, sines, True).astype(bfloat)
    raw_key = rotate(jnp.concatenate(grad_keys, axis=1), cosines, sines, True).astype(bfloat)
    raw_value = jnp.concatenate(grad_values, axis=1).astype(bfloat)
    raw_query_ref[...] = raw_query
    raw_key_ref[...] = raw_key
    raw_value_ref[...] = raw_value
    part = dot_nt(raw_query, query_w[...]) + dot_nt(raw_key, key_w[...]) + dot_nt(raw_value, value_w[...])

    @pl.when(step == 0)
    def _():
        total_ref[...] = part

    @pl.when(step > 0)
    def _():
        total_ref[...] += part

    @pl.when(step == pl.num_programs(0) - 1)
    def _():
        stay_ref[...] = total_ref[mine, :]
        leave_ref[...] = total_ref[other, :].astype(bfloat)
        inputs = tokens_ref[...].astype(single)
        inverse = lax.rsqrt(jnp.mean(inputs * inputs, axis=1, keepdims=True) + EPS)
        gain = jnp.sum(total_ref[...] * inputs * inverse, axis=0, keepdims=True)
        first = lax.broadcasted_iota(jnp.int32, gain_ref.shape, 0) == 0
        gain_ref[...] = jnp.where(first, gain, 0.0)


def attend(place, tokens, gain, query_w, key_w, value_w, out_w, tables):
    length, width = tokens.shape
    span, size = length // 2, HEAD_DIMENSION
    steps = key_w.shape[1] // 128
    wide, thin = query_w.shape[1] // steps, 128
    heads, kv_heads = query_w.shape[1] // size, key_w.shape[1] // size
    whole = lambda *shape: pl.BlockSpec(shape, lambda i, *_: (0,) * len(shape))
    across = lambda rows, columns: pl.BlockSpec((rows, columns), lambda i, *_: (0, i))
    split = lambda *shape: pl.BlockSpec(shape, lambda i, *_: (i,) + (0,) * (len(shape) - 1))
    low = lambda *shape: jax.ShapeDtypeStruct(shape, bfloat)
    high = lambda *shape: jax.ShapeDtypeStruct(shape, single)
    return kernel_call(
        attend_kernel,
        "attend",
        (steps,),
        [whole(length, width), whole(1, width), across(width, wide), across(width, thin), across(width, thin),
         split(wide, width), whole(length, 128), whole(length, 128)],
        [whole(length, width), split(heads // steps, length, size), split(kv_heads // steps, length, size),
         split(kv_heads // steps, length, size), across(length, wide), split(1, 8, length),
         whole(span, width), whole(span, width)],
        [low(length, width), low(heads, length, size), low(kv_heads, length, size), low(kv_heads, length, size),
         low(length, heads * size), high(steps, 8, length), high(span, width), high(span, width)],
        [pltpu.VMEM((length, width), single)],
        2 * length * width * (2 * heads + 2 * kv_heads) * size,
        2 * (length * width * 6 + 2 * width * (heads + kv_heads) * size),
        (place, tokens, gain, query_w, key_w, value_w, out_w) + tuple(tables),
        prefetch=1,
    )


def attend_back(place, mine, other, tokens, query_w, key_w, value_w, out_w, tables, saved):
    length, width = tokens.shape
    span, size = length // 2, HEAD_DIMENSION
    steps = key_w.shape[1] // 128
    wide, thin = query_w.shape[1] // steps, 128
    heads, kv_heads = query_w.shape[1] // size, key_w.shape[1] // size
    whole = lambda *shape: pl.BlockSpec(shape, lambda i, *_: (0,) * len(shape))
    across = lambda rows, columns: pl.BlockSpec((rows, columns), lambda i, *_: (0, i))
    split = lambda *shape: pl.BlockSpec(shape, lambda i, *_: (i,) + (0,) * (len(shape) - 1))
    low = lambda *shape: jax.ShapeDtypeStruct(shape, bfloat)
    high = lambda *shape: jax.ShapeDtypeStruct(shape, single)
    return kernel_call(
        attend_back_kernel,
        "attend_back",
        (steps,),
        [whole(span, width), whole(span, width), whole(length, width),
         across(width, wide), across(width, thin), across(width, thin), split(wide, width),
         whole(length, 128), whole(length, 128), split(heads // steps, length, size),
         split(kv_heads // steps, length, size), split(kv_heads // steps, length, size), split(1, 8, length)],
        [across(length, wide), across(length, thin), across(length, thin),
         whole(span, width), whole(span, width), whole(8, width)],
        [low(length, heads * size), low(length, kv_heads * size), low(length, kv_heads * size),
         high(span, width), low(span, width), high(8, width)],
        [pltpu.VMEM((length, wide), bfloat), pltpu.VMEM((length, width), single)],
        6 * length * width * (heads + kv_heads) * size,
        2 * (length * width * 6 + 2 * width * (heads + kv_heads) * size),
        (place, mine, other, tokens, query_w, key_w, value_w, out_w) + tuple(tables) + tuple(saved),
        prefetch=1,
    )


def three_lanes(value, starts, lanes):
    total = None
    for start in starts:
        low = value.astype(bfloat).astype(single)
        value = value - low
        moved = pltpu.roll(low, start, 1) if start else low
        total = moved if total is None else total + moved
    return total


def token_kernel(count, place_ref, stay_ref, came_ref, routes_ref, valid_ref, gain_ref, router_ref, hidden_ref, token_ref):
    width = stay_ref.shape[1]
    hidden = stay_ref[...] + came_ref[...]
    hidden_ref[...] = hidden
    inverse = lax.rsqrt(jnp.mean(hidden * hidden, axis=1, keepdims=True) + EPS)
    moe_in = (hidden * inverse * gain_ref[...]).astype(bfloat)
    token_ref[:, :width] = moe_in
    logits = dot(moe_in, router_ref[...])
    logits = jnp.concatenate([logits, jnp.zeros((logits.shape[0], 128 - count), single)], axis=1)
    lane = lax.broadcasted_iota(jnp.int32, logits.shape, 1)
    picked = lane == routes_ref[:, :1]
    for k in range(1, routes_ref.shape[1]):
        picked = picked | (lane == routes_ref[:, k : k + 1])
    peak = jnp.max(jnp.where(picked, logits, -1e30), axis=1, keepdims=True)
    weights = jnp.where(picked, jnp.exp(jnp.where(picked, logits, peak) - peak), 0.0)
    gates = weights / jnp.sum(weights, axis=1, keepdims=True)
    tail = three_lanes(gates, (0, count, 2 * count), 128)
    routes = routes_ref[...].astype(single)
    first = lax.broadcasted_iota(jnp.int32, routes.shape, 1) == 0
    routes = routes + jnp.where(first, 64.0 * valid_ref[...].astype(single), 0.0)
    blank = jnp.zeros((routes.shape[0], 128 - routes.shape[1]), single)
    token_ref[:, width:] = (tail + jnp.concatenate([blank, routes], axis=1)).astype(bfloat)


def layer_kernel(addends, place_ref, hidden_ref, target_ref, valid_ref, *refs):
    parts, (layer_ref, grad_ref, token_ref) = refs[:addends], refs[addends:]
    width = hidden_ref.shape[1]
    moe = sum_of(parts)
    layer = hidden_ref[...] + moe
    layer_ref[...] = layer.astype(bfloat)
    valid = valid_ref[...].astype(single)
    grad = valid * (layer - target_ref[...].astype(single))
    grad_ref[...] = grad
    token_ref[:, :width] = grad.astype(bfloat)
    inner = jnp.sum(grad * moe, axis=1, keepdims=True)
    lane = lax.broadcasted_iota(jnp.int32, (inner.shape[0], 128), 1)
    inner = jnp.where(lane == 0, inner, 0.0)
    token_ref[:, width:] = three_lanes(inner, (0, 1, 2), 128).astype(bfloat)


def sum_of(parts):
    total = None
    for part in parts:
        value = (part[0] if len(part.shape) == 3 else part[...]).astype(single)
        total = value if total is None else total + value
    return total


def norm_kernel(addends, place_ref, hidden_ref, grad_layer_ref, *refs):
    parts, (gain_ref, router_ref, grad_ref, low_ref, logits_ref, sum_ref) = refs[:addends], refs[addends:]
    width = hidden_ref.shape[1]
    wide = sum_of(parts)
    logits = wide[:, width:].astype(bfloat)
    logits_ref[...] = logits
    count = router_ref.shape[1]
    grad_in = wide[:, :width] + dot_nt(logits[:, :count], router_ref[...])
    hidden = hidden_ref[...]
    inverse = lax.rsqrt(jnp.mean(hidden * hidden, axis=1, keepdims=True) + EPS)
    scaled = grad_in * gain_ref[...]
    inner = jnp.mean(scaled * hidden, axis=1, keepdims=True)
    grad = grad_layer_ref[...] + inverse * scaled - hidden * (inverse * inverse * inverse * inner)
    grad_ref[...] = grad
    low_ref[...] = grad.astype(bfloat)
    gain = jnp.sum(grad_in * hidden * inverse, axis=0, keepdims=True)
    first = lax.broadcasted_iota(jnp.int32, sum_ref.shape, 0) == 0
    gain = jnp.where(first, gain, 0.0)

    @pl.when(pl.program_id(0) == 0)
    def _():
        sum_ref[...] = gain

    @pl.when(pl.program_id(0) > 0)
    def _():
        sum_ref[...] += gain


def token_rows(kernel, name, steps, place, rowwise, others, outs, kept=()):
    block = outs[0].shape[0] // steps

    def spec(array):
        if isinstance(array, tuple) and array[1] is None:
            return pl.BlockSpec(
                (block, array[0].shape[1]), lambda i, place: (place[2] * steps + i, 0)
            )
        if isinstance(array, tuple):
            array, index = array
            return pl.BlockSpec((1, block, array.shape[2]), lambda i, place: (index, i, 0))
        return pl.BlockSpec((block, array.shape[1]), lambda i, place: (i, 0))

    bare = [array[0] if isinstance(array, tuple) else array for array in rowwise]
    return kernel_call(
        kernel,
        name,
        (steps,),
        [spec(array) for array in rowwise]
        + [pl.BlockSpec(array.shape, lambda i, place: (0, 0)) for array in others],
        [pl.BlockSpec((block, out.shape[1]), lambda i, place: (i, 0)) for out in outs]
        + [pl.BlockSpec(out.shape, lambda i, place: (0, 0)) for out in kept],
        list(outs) + list(kept),
        [],
        1,
        8 * sum(out.shape[0] * out.shape[1] for out in outs),
        (place,) + tuple(bare) + tuple(others),
        prefetch=1,
    )


def pack_kernel(lane_at, terms, cut, place_ref, sums_ref, *refs):
    lefts, rights, refs = refs[:terms], refs[terms : 2 * terms], refs[2 * terms :]
    outs, full_ref = refs[:-1], refs[-1]
    span = lefts[0].shape[0]
    at = 0
    for term in range(terms):
        left, right = lefts[term], rights[term]
        rows = left.shape[0]
        columns = right.shape[1]
        if right.shape[0] == rows:
            value = dot_tn(left[...], right[...])
        else:
            core = place_ref[2] if term == 0 else 1 - place_ref[2]
            value = dot_tn(left[...], right[pl.ds(pl.multiple_of(core * rows, rows), rows), :])
        if term == 1 and lefts[0].shape[0] != rights[0].shape[0]:
            full_ref[:, :columns] += value
        else:
            full_ref[:, at : at + columns] = value
            at += columns
    sums = sums_ref[...]
    high = sums.astype(bfloat)
    low = (sums - high.astype(single)).astype(bfloat)
    lane = lax.broadcasted_iota(jnp.int32, (sums.shape[0], 128), 1)
    chosen = (lane == lane_at).astype(bfloat)
    column = dot_tn(high, chosen) + dot_tn(low, chosen)
    width = full_ref.shape[1]
    if at < width:
        full_ref[:, width - 128 :] = column
    else:
        full_ref[:, width - 128 :] += column
    some, block = outs[0].shape[:2]

    def blocks(step, i):
        start = (i * cut + (place_ref[4] ^ step)) * block
        return full_ref[pl.ds(pl.multiple_of(start, block), block), :].astype(bfloat)

    for step in range(min(cut, len(outs))):
        if len(outs) > cut and step == cut - 1:
            early = pl.program_id(0) < pl.num_programs(0) // 2

            @pl.when(early)
            def _():
                outs[-2][0] = blocks(step, 0)

            @pl.when(jnp.logical_not(early))
            def _():
                outs[-1][0] = blocks(step, 0)

        else:
            for i in range(some):
                outs[step][i] = blocks(step, i)


def pack_sums(place, lefts, rights, sums, lane_at, columns, count_dp, owners):
    width = sums.shape[1]
    block = width // (count_dp * owners)
    steps = count_dp if (width // count_dp) % 128 == 0 else 1
    tall = lambda array: pl.BlockSpec((array.shape[0], width // steps), lambda i, *_: (0, i))
    whole = lambda array: pl.BlockSpec(array.shape, lambda i, *_: (0, 0))
    some = count_dp // steps
    halved = owners == 4 and steps == count_dp
    specs = [pl.BlockSpec((some, block, columns), lambda i, *_: (i, 0, 0))] * owners
    shapes = [jax.ShapeDtypeStruct((count_dp, block, columns), bfloat)] * owners
    if halved:
        half = count_dp // 2
        specs[3:] = [
            pl.BlockSpec((1, block, columns), lambda i, *_: (jnp.minimum(i, half - 1), 0, 0)),
            pl.BlockSpec((1, block, columns), lambda i, *_: (jnp.maximum(i - half, 0), 0, 0)),
        ]
        shapes[3:] = [jax.ShapeDtypeStruct((half, block, columns), bfloat)] * 2
    outs = kernel_call(
        functools.partial(pack_kernel, lane_at, len(lefts), owners),
        "pack_sums",
        (steps,),
        [tall(sums)] + [tall(left) for left in lefts] + [whole(right) for right in rights],
        specs,
        shapes,
        [pltpu.VMEM((width // steps, columns), single)],
        2 * sum(left.shape[0] * width * columns for left in lefts),
        2 * width * columns,
        (place, sums) + tuple(lefts) + tuple(rights),
        prefetch=1,
    )
    outs = list(outs)
    if halved:
        return outs[:3] + [(outs[3], outs[4])]
    if owners == 4:
        half = count_dp // 2
        return outs[:3] + [(outs[3][:half], outs[3][half:])]
    return outs


def rope_tables(length, head_size):
    half_size = head_size // 2
    frequency = THETA ** (-jnp.arange(half_size, dtype=jnp.float32) * 2.0 / head_size)
    angles = jnp.arange(length, dtype=jnp.float32)[:, None] * frequency[None, :]
    return (jnp.cos(angles), jnp.sin(angles))


def rms_backward(value_matrix, inverse, gain, grad_normed):
    scaled = grad_normed * gain
    grad_gain = jnp.sum(grad_normed * value_matrix * inverse, axis=0)
    grad_values = inverse * scaled - value_matrix * inverse**3 * jnp.mean(
        scaled * value_matrix, axis=-1, keepdims=True
    )
    return (grad_values, grad_gain)


def assemble(mine, other):
    first = lax.axis_index("tensor") == 0
    return jnp.concatenate([jnp.where(first, mine, other), jnp.where(first, other, mine)], axis=0)


def combine_groups(slots, rows, capacity, span, between):
    owners = slots.shape[0]
    orders = return_order(owners)
    if len(orders) == 1:
        mine, other = return_rows(slots, after(rows, *between(())), orders[0], capacity, span)
        other = swap(other)
        sent = [
            (mine[i].astype(single) + other[i].astype(single)).astype(bfloat)
            for i in range(owners - 1)
        ]
        came = [to_peer(part, "expert", i) for i, part in enumerate(sent, 1)]
    else:
        mine, other = return_rows(slots, rows, orders[0], capacity, span)
        other = after(swap(other), *hold(other))
        came, sent = send_farthest(mine, other)
        done = between(sent)
        came[0] = after(came[0], *hold(sent[0]), *done)
        mine, other = return_rows(slots, after(rows, *done), orders[1], capacity, span)
        other = after(swap(other), *hold(other))
        came, sent = send_nearer(mine, other, came)
    own = len(orders[-1]) - 1
    return [(mine, own), (other, own)] + came, sent


def on_device(
    tokens,
    teacher,
    routes,
    valid,
    teacher_rows,
    norm_attn,
    norm_moe,
    w_query,
    key_projection_weight,
    value_projection_weight,
    w_out,
    w_router,
    w_gate,
    w_up,
    w_down,
):
    rows_dev, model_width = tokens.shape
    seq_count = rows_dev // SEQUENCE_LENGTH
    heads_local = w_query.shape[1] // HEAD_DIMENSION
    kv_local = key_projection_weight.shape[1] // HEAD_DIMENSION
    query_width = w_query.shape[1]
    key_width = key_projection_weight.shape[1]
    experts_local = w_gate.shape[0]
    owners = lax.axis_size("expert")
    count_dp = lax.axis_size("dp")
    groups = count_dp * owners
    all_experts = experts_local * owners
    top_count = routes.shape[1]
    capacity = rows_dev * top_count * 5 // (4 * all_experts)
    at_dp, at_ex, core = lax.axis_index("dp"), lax.axis_index("expert"), lax.axis_index("tensor")
    span = rows_dev // 2
    shards = count_dp // 2
    place = [at_ex * experts_local, at_dp // shards, core, at_dp % shards, at_ex]
    place = jnp.stack(place).astype(jnp.int32)

    def mine_of(value, axis=0):
        return lax.dynamic_slice_in_dim(value, core * span, span, axis)

    def other_of(value, axis=0):
        return lax.dynamic_slice_in_dim(value, (1 - core) * span, span, axis)

    tables = [jnp.tile(table, (1, 4)) for table in rope_tables(SEQUENCE_LENGTH, HEAD_DIMENSION)]
    gain_attn, gain_moe = norm_attn.reshape(1, model_width), norm_moe.reshape(1, model_width)

    def tokens_like(columns, kind):
        return jax.ShapeDtypeStruct((span, columns), kind)

    weights = (w_query, key_projection_weight, value_projection_weight, w_out)
    normed, queries, keys, values, mixed, log_sums, staying, leaving = attend(
        place, tokens, gain_attn, *weights, tables
    )
    came = after(swap(leaving), *hold(leaving))
    wide = model_width + 128
    hidden_first, token = token_rows(
        functools.partial(token_kernel, all_experts),
        "token",
        4,
        place,
        [staying, came, (routes, None), (valid[:, None], None)],
        [gain_moe, w_router],
        [tokens_like(model_width, single), tokens_like(wide, bfloat)],
    )

    some = experts_local // 2
    pieces = ((0, some), (some, experts_local - some))
    few = max(1, experts_local // 5)

    def interleave(mine, other):
        return [part for pair in zip(mine, other) for part in pair]

    def far_forward(parts, start, amount, pin):
        return expert_forward(
            place, all_experts, top_count, pin, (w_gate, w_up), parts, owners, capacity, start, amount
        )

    wanted, valid_rows = after_all([teacher_rows, valid[:, None]], token)
    wanted = mine_of(wanted[0])
    chooser = (wanted[:, None] == jnp.arange(rows_dev, dtype=jnp.int32)).astype(bfloat)
    target = jnp.dot(chooser, teacher, preferred_element_type=bfloat)

    mirror = to_mirror(token)
    near_parts = spread(token, (target,))
    mirror = after(mirror, *near_parts)
    peers = from_peers(mirror)
    mirror_other = swap(mirror)
    gate_pre, up_pre, near_half, near_tails, slots, valid_count, results = expert_forward(
        place, all_experts, top_count, mirror, (w_gate, w_up, w_down), near_parts, owners, capacity, 0, experts_local
    )
    results = after(results, mirror_other)
    peers_other = []

    def swap_peers(sent):
        peers[:] = after_all(peers, *sent)
        peers_other.extend(swap(peer) for peer in peers)
        return sent

    addends, sent = combine_groups(slots, results, capacity, span, swap_peers)
    far_tokens = interleave([mirror] + peers, [mirror_other] + peers_other)
    far = [far_forward(far_tokens, *pieces[0], sent[0])]
    addends[-1] = after(addends[-1], far[0][0], *hold(sent[0]))
    layer_low, grad_layer, token_grad = token_rows(
        functools.partial(layer_kernel, len(addends)),
        "layer",
        4,
        place,
        [hidden_first, target, (valid_rows, None)] + addends,
        [],
        [tokens_like(model_width, bfloat), tokens_like(model_width, single), tokens_like(wide, bfloat)],
    )

    far.append(far_forward(far_tokens, *pieces[1], token_grad))
    mirror = to_mirror(token_grad)
    near_parts = spread(token_grad, (far[1][0],))
    mirror = after(mirror, *near_parts)
    peers = from_peers(mirror)
    mirror_other = swap(mirror)
    hidden_low, grad_gate_pre, grad_up_pre, near_grad_half, results = expert_backward(
        place, all_experts, after(slots, mirror), (w_gate, w_up, w_down), gate_pre, up_pre, near_tails, near_parts, capacity
    )
    results = after(results, mirror_other)
    weight_parts, far_grads = [], []

    def weights_of(start, amount, others=()):
        piece = 0 if start < some else 1
        far_gate, far_up, far_half, far_tails, far_slots, _ = far[piece]
        values = expert_weights(
            place,
            all_experts,
            after(far_slots, *others),
            w_down,
            (far_gate, far_up, far_tails, far_half),
            (hidden_low, grad_gate_pre, grad_up_pre, near_half, near_grad_half),
            far_grads,
            capacity,
            start,
            start - pieces[piece][0],
            amount,
            shards,
        )
        came = [to_peer(values[step], "dp", step) for step in range(1, shards)]
        weight_parts.append((start, values[0], came))
        return values

    def first_weights(sent):
        peers[:] = after_all(peers, *sent)
        peers_other = [swap(peer) for peer in peers]
        far_grads.extend(interleave([mirror] + peers, [mirror_other] + peers_other))
        return weights_of(0, few)

    addends, sent = combine_groups(slots, results, capacity, span, first_weights)
    layer_low = after(layer_low, *sent)
    layer_other = swap(layer_low)
    block_out = assemble(layer_low, layer_other)
    done = weights_of(few, some - few, sent)
    addends[-1] = after(addends[-1], *done, layer_other, *hold(sent[0]))
    grad_hidden, grad_attn, grad_logits, gain_sums = token_rows(
        functools.partial(norm_kernel, len(addends)),
        "norm",
        4,
        place,
        [hidden_first, grad_layer] + addends,
        [gain_moe, w_router],
        [tokens_like(model_width, single), tokens_like(model_width, bfloat), tokens_like(128, bfloat)],
        [jax.ShapeDtypeStruct((8, model_width), single)],
    )
    grad_attn_other = after(swap(grad_attn), *hold(grad_attn), *weight_parts[0][2])
    first_parts = pack_sums(
        place,
        [grad_attn, grad_attn_other, token],
        [mixed, mixed, grad_logits],
        gain_sums,
        all_experts,
        query_width + 128,
        count_dp,
        owners,
    )
    first_sum = start_sum(first_parts)
    done = weights_of(some, experts_local - some, first_parts[-1] if owners == 4 else first_parts)
    first_sum, sent = go_on(first_sum, *done)
    grad_attn = after(grad_attn, *sent)
    raw_query, raw_key, raw_value, staying, leaving, gain_sums = attend_back(
        place, grad_attn, grad_attn_other, tokens, *weights, tables, (queries, keys, values, log_sums)
    )
    gain_sums = after(gain_sums, *first_sum[1:], *weight_parts[1][2])
    second_parts = pack_sums(
        place,
        [normed] * 3,
        [raw_query, raw_key, raw_value],
        gain_sums,
        0,
        query_width + 2 * key_width + 128,
        count_dp,
        owners,
    )
    first_total = add_up(first_sum[0], first_sum[1:])
    second_sum = start_sum(second_parts)
    step = 1
    while step < count_dp:
        valid_count = valid_count + to_peer(valid_count, "dp", step)
        step *= 2
    scale = float(rows_dev * groups) / valid_count
    second_sum, sent = go_on(second_sum, scale)
    first_dense = over_dp(after(first_total, *sent))
    weight_grads, done = None, []
    for start, values, came in weight_parts[:2]:
        came = [after(part, sent[0]) for part in came]
        weight_grads, finished = finish_weights(experts_local, start, scale, values, came, weight_grads)
        done.append(finished)
    inputs_mine = mine_of(tokens).astype(single)
    inverse_mine = lax.rsqrt(jnp.mean(inputs_mine * inputs_mine, axis=-1, keepdims=True) + EPS)
    grad_first, _ = rms_backward(
        inputs_mine, inverse_mine, norm_attn, staying + swap(leaving).astype(single)
    )
    grad_tokens_mine = (grad_hidden + grad_first) * scale[0, 0]
    grad_tokens = assemble(grad_tokens_mine, swap(grad_tokens_mine))
    second_total = add_up(second_sum[0], second_sum[1:])
    second_dense = over_dp(after(second_total, grad_tokens, first_dense, *done)) * scale[0, 0]
    first_dense = first_dense * scale[0, 0]
    for start, values, came in weight_parts[2:]:
        came = [after(part, second_total) for part in came]
        weight_grads, _ = finish_weights(experts_local, start, scale, values, came, weight_grads)
    shared = jnp.concatenate([first_dense[:, query_width:], second_dense[:, -128:]], axis=1)
    shared = shared + swap(shared)

    key_at = query_width
    return (
        block_out,
        grad_tokens,
        shared[:, -128],
        shared[:, all_experts],
        second_dense[:, :key_at],
        second_dense[:, key_at : key_at + key_width],
        second_dense[:, key_at + key_width : key_at + 2 * key_width],
        first_dense[:, :query_width].T,
        shared[:, :all_experts],
        weight_grads[0],
        weight_grads[1],
        weight_grads[2],
    )


def solution(mesh):
    placed = (
        P(("dp", "expert"), None),
        P(("dp", "expert"), None),
        P(("dp", "expert"), None),
        P(("dp", "expert")),
        P(("dp", "expert"), None),
        P(),
        P(),
        P(None, "tensor"),
        P(None, "tensor"),
        P(None, "tensor"),
        P("tensor", None),
        P(),
        P("expert", None, "tensor"),
        P("expert", None, "tensor"),
        P("expert", "tensor", None),
    )
    return jax.shard_map(
        on_device,
        mesh=mesh,
        in_specs=placed,
        out_specs=(
            P(("dp", "expert"), None),
            P(("dp", "expert"), None),
            P(("dp", "expert")),
            P(("dp", "expert")),
            P(("dp", "expert"), "tensor"),
            P(("dp", "expert"), "tensor"),
            P(("dp", "expert"), "tensor"),
            P("tensor", ("dp", "expert")),
            P(("dp", "expert"), None),
            P("expert", "dp", "tensor"),
            P("expert", "dp", "tensor"),
            P("expert", "tensor", "dp"),
        ),
        check_vma=False,
    )
```

time: 619 us -> 521 us (0.84)
  Pallas kernels: 233 us -> 310 us
  other arithmetic: 85 us -> 24.3 us
  matrix products: 51.7 us -> 1.54 us
  waiting for transfers between devices: 120 us -> 76.7 us
  local copies, waits for them, and re-layouts: 54.5 us -> 24 us
  starting transfers between devices: 63.1 us -> 72.9 us
    pallas_call x16 -> x21, Pallas kernels: 219 us -> 285 us  [kernel_call(): pl.pallas_call(kernel, name=name, grid_spec=pltpu.PrefetchScalarGridSpec(...]
    dot_general x18 -> x1, matrix products: 51.7 us -> 1.54 us  [on_device(): target = jnp.dot(chooser, teacher, preferred_element_type=bfloat)]
    ppermute x44 -> x39, waiting for transfers between devices: 106 us -> 61.3 us  [to_peer(): lax.ppermute(value, axis, [(i, i ^ step) for i in range(lax.axis_size(axi...]
    convert_element_type x11 -> x0, other arithmetic: 16.6 us -> none  [the longest x1 7.11 us: one_block(): grad_scores = (probs * (grad_probs - row_inner)).astype(jnp.bfloat16)]
    add x11 -> x1, other arithmetic: 12.8 us -> 0.01 us  [on_device(): valid_count = valid_count + to_peer(valid_count, 'dp', step)]
    concatenate x14 -> x4, other arithmetic: 13.5 us -> 1.35 us  [the longest x2 1.17 us: go_on(): jnp.concatenate([second[:cut] + low, second[cut:]], axis=0).astype(bfloat)]
    pallas_call x0 -> x4, Pallas kernels: none -> 11.6 us  [the longest x2 6.77 us: send_nearer(): pl.pallas_call(nearer_kernel, name='nearer', grid=(2,), in_specs=[stacked...]
    unnamed x192 -> x85, local copies, waits for them, and re-layouts: 23.2 us -> 12.9 us
  transfers between devices with their start and end apart: 73 -> 69, of which waited for: 27 -> 23; matrix products, arithmetic and copies ran while one was open for 24% -> 6% of each run, Pallas kernels for 34% -> 54%
where the time goes in v4:
time: 521 us; the launch traced here: 511 us
  Pallas kernels  310 us (60%)
  waiting for transfers between devices  76.7 us (15%)
  starting transfers between devices  72.9 us (14%)
  other arithmetic  24.3 us (5%)
  local copies, waits for them, and re-layouts  24 us (5%)
    pallas_call x21, Pallas kernels, kernel_call(): pl.pallas_call(kernel, name=name, grid_spec=pltpu.PrefetchScalarGridSpec(...  285 us
    ppermute x39, waiting for transfers between devices, to_peer(): lax.ppermute(value, axis, [(i, i ^ step) for i in range(lax.axis_size(axi...  61.3 us
    ppermute x39, starting transfers between devices, to_peer(): lax.ppermute(value, axis, [(i, i ^ step) for i in range(lax.axis_size(axi...  60.3 us
    ppermute x28, waiting for transfers between devices, swap(): return lax.ppermute(value, 'tensor', [(0, 1), (1, 0)])  15.4 us
    unnamed x85, local copies, waits for them, and re-layouts  12.9 us
  transfers between devices with their start and end apart: 69, of which 23 were waited for; matrix products, arithmetic and copies ran while one was open for 6% of the time, Pallas kernels for 54%

profile of v4, /device:TPU:0, one launch (start us, length us, event | category | flops | bytes accessed | tf_op | source)
XLA Modules:
  0.0 511.3 jit_solution(9017990946963800671)
XLA Ops:
  5.4 20.1 %attend.1 = (bf16[512,1536]{1,0:T(8,128)(2,1)}, bf16[12,512,64]{2,1,0:T(8,128)(2,1)}, bf16[4,512,64]{2,1,0:T(8,128)(2,1)}, bf16[4,512,64]{2,1,0:T(8,128)(2,1)}, ...) custom-call(s32[5]{0:T(128)} %stack.23.place_ref, ...), custom_call_target="tpu_custom_call" | custom-call | flops 3221225472 | bytes 15728640 | tf_op jit(solution)/shard_map/attend/pallas_call | solution.py:428
  30.1 5.9 %token_.1 = (f32[256,1536]{1,0:T(8,128)}, bf16[256,1664]{1,0:T(8,128)(2,1)}) custom-call(s32[5]{0:T(128)} %stack.23.place_ref, f32[256,1536]{1,0:T(8,128)} %get-tuple-element.112.stay_ref, f32[256,1536]{1,0:T(8,128)} %after.34.came_ref, s32[512,8]{1,0:T(8,128)} %copy.78.routes_ref, s32[512,1]{1,0:T(8,128)} %copy.79.valid_ref.refs_1_, ...), custom_call_target="tpu_custom_call" | custom-call | flops 1 | bytes 6553600 | tf_op jit(solution)/shard_map/token/pallas_call | solution.py:428
  41.1 3.6 collective-permute-start.10
  47.0 11.5 %collective-permute-done.2.high_ref.refs_3_ = bf16[256,1664]{1,0:T(8,128)(2,1)} collective-permute-done((bf16[256,1664]{1,0:T(8,128)(2,1)}, bf16[256,1664]{1,0:T(8,128)(2,1)}, u32[]{:S(2)}, u32[]{:S(2)}) %collective-permute-start.2) | collective-permute-done | bytes 852000 | tf_op jit(solution)/shard_map/ppermute | solution.py:67
  65.2 8.3 %collective-permute-done.7.refs_8_ = bf16[128,1664]{1,0:T(8,128)(2,1)} collective-permute-done((bf16[128,1664]{1,0:T(8,128)(2,1)}, bf16[128,1664]{1,0:T(8,128)(2,1)}, u32[]{:S(2)}, u32[]{:S(2)}) %collective-permute-start.7) | collective-permute-done | bytes 426016 | tf_op jit(solution)/shard_map/ppermute | solution.py:67
  80.6 30.9 %expert_forward.1 = (bf16[10,512,256]{2,1,0:T(8,128)(2,1)}, bf16[10,512,256]{2,1,0:T(8,128)(2,1)}, bf16[10,512,768]{2,1,0:T(8,128)(2,1)}, bf16[10,512,128]{2,1,0...) custom-call(s32[5]{0:T(128)} %stack.23.place_ref, ...), custom_call_target="tpu_custom_call" | custom-call | flops 20803747840 | bytes 49807360 | tf_op jit(solution)/shard_map/expert_forward/pallas_call | solution.py:428
  112.5 5.3 %return_rows.4 = (bf16[1,256,1536]{2,1,0:T(8,128)(2,1)}, bf16[1,256,1536]{2,1,0:T(8,128)(2,1)}) custom-call(s32[4,16,512]{2,1,0:T(8,128)} %get-tuple-element.120.slots_ref, bf16[10,512,1536]{2,1,0:T(8,128)(2,1)} %after.38.rows_ref.refs_0_), custom_call_target="tpu_custom_call" | custom-call | flops 2013265920 | bytes 5505024 | tf_op jit(solution)/shard_map/return_rows/pallas_call | solution.py:428
  126.1 11.6 %return_rows.5 = (bf16[3,256,1536]{2,1,0:T(8,128)(2,1)}, bf16[3,256,1536]{2,1,0:T(8,128)(2,1)}) custom-call(s32[4,16,512]{2,1,0:T(8,128)} %get-tuple-element.120.slots_ref, bf16[10,512,1536]{2,1,0:T(8,128)(2,1)} %after.40.rows_ref), custom_call_target="tpu_custom_call" | custom-call | flops 6039797760 | bytes 16515072 | tf_op jit(solution)/shard_map/return_rows/pallas_call | solution.py:428
  148.3 15.6 %expert_forward_far.2 = (bf16[5,512,256]{2,1,0:T(8,128)(2,1)}, bf16[5,512,256]{2,1,0:T(8,128)(2,1)}, bf16[5,512,768]{2,1,0:T(8,128)(2,1)}, bf16[5,512,128]{2,1,0...) custom-call(s32[5]{0:T(128)} %stack.23.place_ref, bf16[10,1536,256]{2,1,0:T(8,128)(2,1)} %gate_w.7, ...), custom_call_target="tpu_custom_call" | custom-call | flops 8388608000 | bytes 20971520 | tf_op jit(solution)/shard_map/expert_forward_far/pallas_call | solution.py:428
  167.8 5.8 %layer.1 = (bf16[256,1536]{1,0:T(8,128)(2,1)}, f32[256,1536]{1,0:T(8,128)}, bf16[256,1664]{1,0:T(8,128)(2,1)}) custom-call(s32[5]{0:T(128)} %stack.23.place_ref, f32[256,1536]{1,0:T(8,128)} %get-tuple-element.114.hidden_ref, bf16[256,1536]{1,0:T(8,128)(2,1)} %fusion.9.refs_2_.target_ref, s32[512,1]{1,0:T(8,128)} %get-tuple-element.117.valid_ref, ...), custom_call_target="tpu_custom_call" | custom-call | flops 1 | bytes 9699328 | tf_op jit(solution)/shard_map/layer/pallas_call | solution.py:428
  176.3 3.7 collective-permute-start.24
  180.1 15.6 %expert_forward_far.3 = (bf16[5,512,256]{2,1,0:T(8,128)(2,1)}, bf16[5,512,256]{2,1,0:T(8,128)(2,1)}, bf16[5,512,768]{2,1,0:T(8,128)(2,1)}, bf16[5,512,128]{2,1,0...) custom-call(s32[5]{0:T(128)} %stack.23.place_ref, bf16[10,1536,256]{2,1,0:T(8,128)(2,1)} %gate_w.7, ...), custom_call_target="tpu_custom_call" | custom-call | flops 8388608000 | bytes 20971520 | tf_op jit(solution)/shard_map/expert_forward_far/pallas_call | solution.py:428
  201.7 8.9 %collective-permute-done.31.refs_8_.refs_7_ = bf16[128,1664]{1,0:T(8,128)(2,1)} collective-permute-done((bf16[128,1664]{1,0:T(8,128)(2,1)}, bf16[128,1664]{1,0:T(8,128)(2,1)}, u32[]{:S(2)}, u32[]{:S(2)}) %collective-permute-start.31) | collective-permute-done | bytes 426016 | tf_op jit(solution)/shard_map/ppermute | solution.py:67
  217.7 41.9 %expert_backward.1 = (bf16[10,512,256]{2,1,0:T(8,128)(2,1)}, bf16[10,512,256]{2,1,0:T(8,128)(2,1)}, bf16[10,512,256]{2,1,0:T(8,128)(2,1)}, bf16[10,512,768]{2,1,0:T(8,128)(2,1)}, bf16[10,512,1664]{2,1,0:T(8,128)(2,1)}) custom-call(s32[5]{0:T(128)} %stack.23.place_ref, s32[4,16,512]{2,1,0:T(8,128)} %after.47.slots_ref, bf16[10,1536,256]{2,1,0:T(8,128)(2,1)} %gate_w.7, ...), custom_call_target="tpu_custom_call" | custom-call | flops 20132659200 | bytes 65536000 | tf_op jit(solution)/shard_map/expert_backward/pallas_call | solution.py:428
  260.5 6.0 %return_rows.6 = (bf16[1,256,1664]{2,1,0:T(8,128)(2,1)}, bf16[1,256,1664]{2,1,0:T(8,128)(2,1)}) custom-call(s32[4,16,512]{2,1,0:T(8,128)} %get-tuple-element.120.slots_ref, bf16[10,512,1664]{2,1,0:T(8,128)(2,1)} %after.48.rows_ref.refs_0_), custom_call_target="tpu_custom_call" | custom-call | flops 2181038080 | bytes 5963776 | tf_op jit(solution)/shard_map/return_rows/pallas_call | solution.py:428
  277.5 13.1 %expert_weights.3 = (bf16[2,3,384,256]{3,2,1,0:T(8,128)(2,1)}, bf16[2,3,384,256]{3,2,1,0:T(8,128)(2,1)}) custom-call(s32[5]{0:T(128)} %stack.23.place_ref, s32[4,16,512]{2,1,0:T(8,128)} %get-tuple-element.143.slots_ref.refs_0_, bf16[10,256,1536]{2,1,0:T(8,128)(2,1)} %down_w.7, bf16[5,512,256]{2,1,0:T(8,128)(2,1)} %get-tuple-element.133.refs_1_.gate_ref, ...), custom_call_target="tpu_custom_call" | custom-call | flops 4831838208 | bytes 12320768 | tf_op jit(solution)/shard_map/expert_weights/pallas_call | solution.py:428
  290.6 11.3 %return_rows.7 = (bf16[3,256,1664]{2,1,0:T(8,128)(2,1)}, bf16[3,256,1664]{2,1,0:T(8,128)(2,1)}) custom-call(s32[4,16,512]{2,1,0:T(8,128)} %get-tuple-element.120.slots_ref, bf16[10,512,1664]{2,1,0:T(8,128)(2,1)} %after.51.rows_ref), custom_call_target="tpu_custom_call" | custom-call | flops 6543114240 | bytes 17891328 | tf_op jit(solution)/shard_map/return_rows/pallas_call | solution.py:428
  302.6 6.5 %collective-permute-start.49 = (bf16[2,3,384,256]{3,2,1,0:T(8,128)(2,1)}, bf16[2,3,384,256]{3,2,1,0:T(8,128)(2,1)}, u32[]{:S(2)}, u32[]{:S(2)}) collective-permute-start(bf16[2,3,384,256]{3,2,1,0:T(8,128)(2,1)} %get-tuple-element.160.refs_2_.refs_3_), channel_id=1, source_target_pairs={{0,8},{8,0},{16,24},{24,16},{1,9},{9,1},{17,25},{25,17},{2,10},{10... | collective-permute-start | bytes 3538952 | tf_op jit(solution)/shard_map/ppermute | solution.py:67
  314.4 16.5 %expert_weights.4 = (bf16[3,3,384,256]{3,2,1,0:T(8,128)(2,1)}, bf16[3,3,384,256]{3,2,1,0:T(8,128)(2,1)}) custom-call(s32[5]{0:T(128)} %stack.23.place_ref, s32[4,16,512]{2,1,0:T(8,128)} %after.55.slots_ref, bf16[10,256,1536]{2,1,0:T(8,128)(2,1)} %down_w.7, bf16[5,512,256]{2,1,0:T(8,128)(2,1)} %get-tuple-element.133.refs_1_.gate_ref, ...), custom_call_target="tpu_custom_call" | custom-call | flops 7247757312 | bytes 18481152 | tf_op jit(solution)/shard_map/expert_weights/pallas_call | solution.py:428
  330.9 4.4 collective-permute-start.58
  335.4 6.6 %norm.1 = (f32[256,1536]{1,0:T(8,128)}, bf16[256,1536]{1,0:T(8,128)(2,1)}, bf16[256,128]{1,0:T(8,128)(2,1)}, f32[8,1536]{1,0:T(8,128)}) custom-call(s32[5]{0:T(128)} %stack.23.place_ref, f32[256,1536]{1,0:T(8,128)} %get-tuple-element.114.hidden_ref, f32[256,1536]{1,0:T(8,128)} %get-tuple-element.165.grad_layer_ref, ...), custom_call_target="tpu_custom_call" | custom-call | flops 1 | bytes 6553600 | tf_op jit(solution)/shard_map/norm/pallas_call | solution.py:428
  344.6 6.9 %pack_sums.2 = (bf16[4,96,896]{2,1,0:T(8,128)(2,1)}, bf16[4,96,896]{2,1,0:T(8,128)(2,1)}, bf16[4,96,896]{2,1,0:T(8,128)(2,1)}, bf16[2,96,896]{2,1,0:T(8,128)(2,1)}, bf16[2,96,896]{2,1,0:T(8,128)(2,1)}) custom-call(s32[5]{0:T(128)} %stack.23.place_ref, f32[8,1536]{1,0:T(8,128)} %get-tuple-element.170.sums_ref, ...), custom_call_target="tpu_custom_call" | custom-call | flops 2113929216 | bytes 2752512 | tf_op jit(solution)/shard_map/pack_sums/pallas_call | solution.py:428
  355.1 23.3 %expert_weights.5 = (bf16[5,3,384,256]{3,2,1,0:T(8,128)(2,1)}, bf16[5,3,384,256]{3,2,1,0:T(8,128)(2,1)}) custom-call(s32[5]{0:T(128)} %stack.23.place_ref, s32[4,16,512]{2,1,0:T(8,128)} %after.58.slots_ref, bf16[10,256,1536]{2,1,0:T(8,128)(2,1)} %down_w.7, bf16[5,512,256]{2,1,0:T(8,128)(2,1)} %get-tuple-element.136.refs_2_.gate_ref, ...), custom_call_target="tpu_custom_call" | custom-call | flops 12079595520 | bytes 30801920 | tf_op jit(solution)/shard_map/expert_weights/pallas_call | solution.py:428
  385.8 4.1 collective-permute-start.54
  392.9 25.6 %attend_back.1 = (bf16[512,768]{1,0:T(8,128)(2,1)}, bf16[512,256]{1,0:T(8,128)(2,1)}, bf16[512,256]{1,0:T(8,128)(2,1)}, f32[256,1536]{1,0:T(8,128)}, bf16[256,1536]{1,0:T(8,128)(2,1)}, /*index=5*/f32[8,1536]{1,0:T(8,128)}) custom-call(s32[5]{0:T(128)} %stack.23.place_ref, bf16[256,1536]{1,0:T(8,128)(2,1)} %after.60.mine_ref, ...), custom_call_target="tpu_custom_call" | custom-call | flops 4831838208 | bytes 15728640 | tf_op jit(solution)/shard_map/attend_back/pallas_call | solution.py:428
  419.7 8.3 %pack_sums.3 = (bf16[4,96,1408]{2,1,0:T(8,128)(2,1)}, bf16[4,96,1408]{2,1,0:T(8,128)(2,1)}, bf16[4,96,1408]{2,1,0:T(8,128)(2,1)}, bf16[2,96,1408]{2,1,0:T(8,128)(2,1)}, bf16[2,96,1408]{2,1,0:T(8,128)(2,1)}) custom-call(s32[5]{0:T(128)} %stack.23.place_ref, f32[8,1536]{1,0:T(8,128)} %after.61.sums_ref, ...), custom_call_target="tpu_custom_call" | custom-call | flops 6643777536 | bytes 4325376 | tf_op jit(solution)/shard_map/pack_sums/pallas_call | solution.py:428
  434.9 8.9 %collective-permute-done.59 = bf16[2,96,1408]{2,1,0:T(8,128)(2,1)S(1)} collective-permute-done((bf16[2,96,1408]{2,1,0:T(8,128)(2,1)}, bf16[2,96,1408]{2,1,0:T(8,128)(2,1)S(1)}, u32[]{:S(2)}, u32[]{:S(2)}) %collective-permute-start.59) | collective-permute-done | bytes 540704 | tf_op jit(solution)/shard_map/ppermute | solution.py:67
  451.8 4.7 fusion.4
  456.5 6.2 %collective-permute-done.61 = bf16[192,896]{1,0:T(8,128)(2,1)S(1)} collective-permute-done((bf16[192,896]{1,0:T(8,128)(2,1)S(1)}, bf16[192,896]{1,0:T(8,128)(2,1)S(1)}, u32[]{:S(2)}, u32[]{:S(2)}) %collective-permute-start.61) | collective-permute-done | bytes 344096 | tf_op jit(solution)/shard_map/ppermute | solution.py:67
  469.2 4.8 finish_weights.4
  486.0 9.0 %collective-permute-done.65 = bf16[192,1408]{1,0:T(8,128)(2,1)S(1)} collective-permute-done((bf16[192,1408]{1,0:T(8,128)(2,1)S(1)}, bf16[192,1408]{1,0:T(8,128)(2,1)S(1)}, u32[]{:S(2)}, u32[]{:S(2)}) %collective-permute-start.65) | collective-permute-done | bytes 540704 | tf_op jit(solution)/shard_map/ppermute | solution.py:67
  499.3 7.1 %finish_weights.5 = (f32[10,384,256]{2,1,0:T(8,128)}, f32[10,384,256]{2,1,0:T(8,128)}, f32[10,256,384]{2,1,0:T(8,128)}, f32[8,128]{1,0:T(8,128)}) custom-call(f32[10,384,256]{2,1,0:T(8,128)} %get-tuple-element.206.gate_in, f32[10,384,256]{2,1,0:T(8,128)} %get-tuple-element.207.up_in, ...), custom_call_target="tpu_custom_call", output_to_operand_aliasing={{0}: (0, {}), {1}: (1, {}), {2}: (2, {})} | custom-call | flops 1474560 | bytes 5898240 | tf_op jit(solution)/shard_map/finish_weights/pallas_call | solution.py:428
  (324 shorter events, 147.5 us)
Async XLA Ops:
  36.1 22.4 %collective-permute-start.2 = (bf16[256,1664]{1,0:T(8,128)(2,1)}, bf16[256,1664]{1,0:T(8,128)(2,1)}, u32[]{:S(2)}, u32[]{:S(2)}) collective-permute-start(bf16[256,1664]{1,0:T(8,128)(2,1)} %get-tuple-element.115.refs_2_.value_ref.refs_1_), channel_id=1, source_target_pairs={{0,2},{2,0},{4,6},{6,4},{1,3},{3,1},{5,7},{7,5},{8,10},{10,8},{12,... | collective-permute-start | bytes 2555912 | tf_op jit(solution)/shard_map/ppermute | solution.py:67
  39.0 21.0 %collective-permute-start.4 = (bf16[256,1664]{1,0:T(8,128)(2,1)}, bf16[256,1664]{1,0:T(8,128)(2,1)}, u32[]{:S(2)}, u32[]{:S(2)}) collective-permute-start(bf16[256,1664]{1,0:T(8,128)(2,1)} %get-tuple-element.115.refs_2_.value_ref.refs_1_), channel_id=1, source_target_pairs={{0,4},{2,6},{4,0},{6,2},{1,5},{3,7},{5,1},{7,3},{8,12},{10,14},{12... | collective-permute-start | bytes 2555912 | tf_op jit(solution)/shard_map/ppermute | solution.py:67
  41.1 32.9 %collective-permute-start.10 = (bf16[256,1664]{1,0:T(8,128)(2,1)}, bf16[256,1664]{1,0:T(8,128)(2,1)}, u32[]{:S(2)}, u32[]{:S(2)}) collective-permute-start(bf16[256,1664]{1,0:T(8,128)(2,1)} %get-tuple-element.115.refs_2_.value_ref.refs_1_), channel_id=1, source_target_pairs={{0,24},{8,16},{16,8},{24,0},{1,25},{9,17},{17,9},{25,1},{2,26},{10... | collective-permute-start | bytes 2555912 | tf_op jit(solution)/shard_map/ppermute | solution.py:72
  77.0 34.6 %collective-permute-start.11 = (bf16[256,1664]{1,0:T(8,128)(2,1)}, bf16[256,1664]{1,0:T(8,128)(2,1)S(1)}, u32[]{:S(2)}, u32[]{:S(2)}) collective-permute-start(bf16[256,1664]{1,0:T(8,128)(2,1)} %after.37.refs_11_.refs_0_), channel_id=1, source_target_pairs={{0,1},{1,0},{2,3},{3,2},{4,5},{5,4},{6,7},{7,6},{8,9},{9,8},{10,11... | collective-permute-start | bytes 2555912 | tf_op jit(solution)/shard_map/ppermute | solution.py:63
  77.1 60.6 %collective-permute-start.18 = (bf16[256,1664]{1,0:T(8,128)(2,1)}, bf16[256,1664]{1,0:T(8,128)(2,1)}, u32[]{:S(2)}, u32[]{:S(2)}) collective-permute-start(bf16[256,1664]{1,0:T(8,128)(2,1)} %after.37.refs_11_.refs_0_), channel_id=1, source_target_pairs={{0,2},{2,0},{4,6},{6,4},{1,3},{3,1},{5,7},{7,5},{8,10},{10,8},{12,... | collective-permute-start | bytes 2555912 | tf_op jit(solution)/shard_map/ppermute | solution.py:67
  78.4 59.9 %collective-permute-start.19 = (bf16[256,1664]{1,0:T(8,128)(2,1)}, bf16[256,1664]{1,0:T(8,128)(2,1)}, u32[]{:S(2)}, u32[]{:S(2)}) collective-permute-start(bf16[256,1664]{1,0:T(8,128)(2,1)} %after.37.refs_11_.refs_0_), channel_id=1, source_target_pairs={{0,4},{2,6},{4,0},{6,2},{1,5},{3,7},{5,1},{7,3},{8,12},{10,14},{12... | collective-permute-start | bytes 2555912 | tf_op jit(solution)/shard_map/ppermute | solution.py:67
  79.9 58.4 %collective-permute-start.20 = (bf16[256,1664]{1,0:T(8,128)(2,1)}, bf16[256,1664]{1,0:T(8,128)(2,1)}, u32[]{:S(2)}, u32[]{:S(2)}) collective-permute-start(bf16[256,1664]{1,0:T(8,128)(2,1)} %after.37.refs_11_.refs_0_), channel_id=1, source_target_pairs={{0,6},{2,4},{4,2},{6,0},{1,7},{3,5},{5,3},{7,1},{8,14},{10,12},{12... | collective-permute-start | bytes 2555912 | tf_op jit(solution)/shard_map/ppermute | solution.py:67
  145.9 19.9 %collective-permute-start.17 = (bf16[256,1536]{1,0:T(8,128)(2,1)}, bf16[256,1536]{1,0:T(8,128)(2,1)}, u32[]{:S(2)}, u32[]{:S(2)}) collective-permute-start(bf16[256,1536]{1,0:T(8,128)(2,1)} %get-tuple-element.129), channel_id=1, source_target_pairs={{0,4},{2,6},{4,0},{6,2},{1,5},{3,7},{5,1},{7,3},{8,12},{10,14},{12... | collective-permute-start | bytes 2359304 | tf_op jit(solution)/shard_map/ppermute | solution.py:67
  147.6 19.3 %collective-permute-start.16 = (bf16[256,1536]{1,0:T(8,128)(2,1)S(1)}, bf16[256,1536]{1,0:T(8,128)(2,1)S(1)}, u32[]{:S(2)}, u32[]{:S(2)}) collective-permute-start(bf16[256,1536]{1,0:T(8,128)(2,1)S(1)} %copy-done.39), channel_id=1, source_target_pairs={{0,2},{2,0},{4,6},{6,4},{1,3},{3,1},{5,7},{7,5},{8,10},{10,8},{12,... | collective-permute-start | bytes 2359304 | tf_op jit(solution)/shard_map/ppermute | solution.py:67
  173.5 22.1 %collective-permute-start.25 = (bf16[256,1664]{1,0:T(8,128)(2,1)}, bf16[256,1664]{1,0:T(8,128)(2,1)}, u32[]{:S(2)}, u32[]{:S(2)}) collective-permute-start(bf16[256,1664]{1,0:T(8,128)(2,1)} %get-tuple-element.135.value_ref.refs_8_.refs_1_.refs_0_), channel_id=1, source_target_pairs={{0,1},{1,0},{2,3},{3,2},{4,5},{5,4},{6,7},{7,6},{8,9},{9,8},{10,11... | collective-permute-start | bytes 2555912 | tf_op jit(solution)/shard_map/ppermute | solution.py:63
  173.6 22.1 %collective-permute-start.26 = (bf16[256,1664]{1,0:T(8,128)(2,1)}, bf16[256,1664]{1,0:T(8,128)(2,1)}, u32[]{:S(2)}, u32[]{:S(2)}) collective-permute-start(bf16[256,1664]{1,0:T(8,128)(2,1)} %get-tuple-element.135.value_ref.refs_8_.refs_1_.refs_0_), channel_id=1, source_target_pairs={{0,2},{2,0},{4,6},{6,4},{1,3},{3,1},{5,7},{7,5},{8,10},{10,8},{12,... | collective-permute-start | bytes 2555912 | tf_op jit(solution)/shard_map/ppermute | solution.py:67
  174.4 21.3 %collective-permute-start.28 = (bf16[256,1664]{1,0:T(8,128)(2,1)}, bf16[256,1664]{1,0:T(8,128)(2,1)}, u32[]{:S(2)}, u32[]{:S(2)}) collective-permute-start(bf16[256,1664]{1,0:T(8,128)(2,1)} %get-tuple-element.135.value_ref.refs_8_.refs_1_.refs_0_), channel_id=1, source_target_pairs={{0,4},{2,6},{4,0},{6,2},{1,5},{3,7},{5,1},{7,3},{8,12},{10,14},{12... | collective-permute-start | bytes 2555912 | tf_op jit(solution)/shard_map/ppermute | solution.py:67
  176.3 35.5 %collective-permute-start.24 = (bf16[256,1664]{1,0:T(8,128)(2,1)}, bf16[256,1664]{1,0:T(8,128)(2,1)}, u32[]{:S(2)}, u32[]{:S(2)}) collective-permute-start(bf16[256,1664]{1,0:T(8,128)(2,1)} %get-tuple-element.135.value_ref.refs_8_.refs_1_.refs_0_), channel_id=1, source_target_pairs={{0,24},{8,16},{16,8},{24,0},{1,25},{9,17},{17,9},{25,1},{2,26},{10... | collective-permute-start | bytes 2555912 | tf_op jit(solution)/shard_map/ppermute | solution.py:72
  214.1 45.6 %collective-permute-start.34 = (bf16[256,1664]{1,0:T(8,128)(2,1)}, bf16[256,1664]{1,0:T(8,128)(2,1)S(1)}, u32[]{:S(2)}, u32[]{:S(2)}) collective-permute-start(bf16[256,1664]{1,0:T(8,128)(2,1)} %after.46.refs_1_.refs_6_), channel_id=1, source_target_pairs={{0,1},{1,0},{2,3},{3,2},{4,5},{5,4},{6,7},{7,6},{8,9},{9,8},{10,11... | collective-permute-start | bytes 2555912 | tf_op jit(solution)/shard_map/ppermute | solution.py:63
  214.2 58.1 %collective-permute-start.35 = (bf16[256,1664]{1,0:T(8,128)(2,1)}, bf16[256,1664]{1,0:T(8,128)(2,1)}, u32[]{:S(2)}, u32[]{:S(2)}) collective-permute-start(bf16[256,1664]{1,0:T(8,128)(2,1)} %after.46.refs_1_.refs_6_), channel_id=1, source_target_pairs={{0,2},{2,0},{4,6},{6,4},{1,3},{3,1},{5,7},{7,5},{8,10},{10,8},{12,... | collective-permute-start | bytes 2555912 | tf_op jit(solution)/shard_map/ppermute | solution.py:67
  214.8 57.5 %collective-permute-start.36 = (bf16[256,1664]{1,0:T(8,128)(2,1)}, bf16[256,1664]{1,0:T(8,128)(2,1)}, u32[]{:S(2)}, u32[]{:S(2)}) collective-permute-start(bf16[256,1664]{1,0:T(8,128)(2,1)} %after.46.refs_1_.refs_6_), channel_id=1, source_target_pairs={{0,4},{2,6},{4,0},{6,2},{1,5},{3,7},{5,1},{7,3},{8,12},{10,14},{12... | collective-permute-start | bytes 2555912 | tf_op jit(solution)/shard_map/ppermute | solution.py:67
  216.0 56.3 %collective-permute-start.37 = (bf16[256,1664]{1,0:T(8,128)(2,1)}, bf16[256,1664]{1,0:T(8,128)(2,1)}, u32[]{:S(2)}, u32[]{:S(2)}) collective-permute-start(bf16[256,1664]{1,0:T(8,128)(2,1)} %after.46.refs_1_.refs_6_), channel_id=1, source_target_pairs={{0,6},{2,4},{4,2},{6,0},{1,7},{3,5},{5,3},{7,1},{8,14},{10,12},{12... | collective-permute-start | bytes 2555912 | tf_op jit(solution)/shard_map/ppermute | solution.py:67
  271.7 37.5 %collective-permute-start.43 = (bf16[128,1664]{1,0:T(8,128)(2,1)}, bf16[128,1664]{1,0:T(8,128)(2,1)}, u32[]{:S(2)}, u32[]{:S(2)}) collective-permute-start(bf16[128,1664]{1,0:T(8,128)(2,1)} %get-tuple-element.154.refs_3_.value_ref), channel_id=1, source_target_pairs={{0,2},{2,0},{4,6},{6,4},{1,3},{3,1},{5,7},{7,5},{8,10},{10,8},{12,... | collective-permute-start | bytes 1277960 | tf_op jit(solution)/shard_map/ppermute | solution.py:67
  273.6 35.6 %collective-permute-start.44 = (bf16[128,1664]{1,0:T(8,128)(2,1)}, bf16[128,1664]{1,0:T(8,128)(2,1)}, u32[]{:S(2)}, u32[]{:S(2)}) collective-permute-start(bf16[128,1664]{1,0:T(8,128)(2,1)} %get-tuple-element.155.refs_4_), channel_id=1, source_target_pairs={{0,4},{2,6},{4,0},{6,2},{1,5},{3,7},{5,1},{7,3},{8,12},{10,14},{12... | collective-permute-start | bytes 1277960 | tf_op jit(solution)/shard_map/ppermute | solution.py:67
  302.6 40.2 %collective-permute-start.49 = (bf16[2,3,384,256]{3,2,1,0:T(8,128)(2,1)}, bf16[2,3,384,256]{3,2,1,0:T(8,128)(2,1)}, u32[]{:S(2)}, u32[]{:S(2)}) collective-permute-start(bf16[2,3,384,256]{3,2,1,0:T(8,128)(2,1)} %get-tuple-element.160.refs_2_.refs_3_), channel_id=1, source_target_pairs={{0,8},{8,0},{16,24},{24,16},{1,9},{9,1},{17,25},{25,17},{2,10},{10... | collective-permute-start | bytes 3538952 | tf_op jit(solution)/shard_map/ppermute | solution.py:67
  312.6 22.7 %collective-permute-start.47 = (bf16[256,1664]{1,0:T(8,128)(2,1)}, bf16[256,1664]{1,0:T(8,128)(2,1)}, u32[]{:S(2)}, u32[]{:S(2)}) collective-permute-start(bf16[256,1664]{1,0:T(8,128)(2,1)} %get-tuple-element.164.refs_2_), channel_id=1, source_target_pairs={{0,4},{2,6},{4,0},{6,2},{1,5},{3,7},{5,1},{7,3},{8,12},{10,14},{12... | collective-permute-start | bytes 2555912 | tf_op jit(solution)/shard_map/ppermute | solution.py:67
  313.1 22.2 %collective-permute-start.46 = (bf16[256,1664]{1,0:T(8,128)(2,1)}, bf16[256,1664]{1,0:T(8,128)(2,1)}, u32[]{:S(2)}, u32[]{:S(2)}) collective-permute-start(bf16[256,1664]{1,0:T(8,128)(2,1)} %get-tuple-element.163.refs_1_.value_ref), channel_id=1, source_target_pairs={{0,2},{2,0},{4,6},{6,4},{1,3},{3,1},{5,7},{7,5},{8,10},{10,8},{12,... | collective-permute-start | bytes 2555912 | tf_op jit(solution)/shard_map/ppermute | solution.py:67
  313.8 21.6 %collective-permute-start.45 = (bf16[256,1536]{1,0:T(8,128)(2,1)}, bf16[256,1536]{1,0:T(8,128)(2,1)}, u32[]{:S(2)}, u32[]{:S(2)}) collective-permute-start(bf16[256,1536]{1,0:T(8,128)(2,1)} %after.54), channel_id=1, source_target_pairs={{0,1},{1,0},{2,3},{3,2},{4,5},{5,4},{6,7},{7,6},{8,9},{9,8},{10,11... | collective-permute-start | bytes 2359304 | tf_op jit(solution)/shard_map/ppermute | solution.py:63
  330.9 87.7 %collective-permute-start.58 = (bf16[3,3,384,256]{3,2,1,0:T(8,128)(2,1)}, bf16[3,3,384,256]{3,2,1,0:T(8,128)(2,1)}, u32[]{:S(2)}, u32[]{:S(2)}) collective-permute-start(bf16[3,3,384,256]{3,2,1,0:T(8,128)(2,1)} %get-tuple-element.167.refs_2_), channel_id=1, source_target_pairs={{0,8},{8,0},{16,24},{24,16},{1,9},{9,1},{17,25},{25,17},{2,10},{10... | collective-permute-start | bytes 5308424 | tf_op jit(solution)/shard_map/ppermute | solution.py:67
  351.5 26.9 %collective-permute-start.51 = (bf16[2,96,896]{2,1,0:T(8,128)(2,1)}, bf16[2,96,896]{2,1,0:T(8,128)(2,1)}, u32[]{:S(2)}, u32[]{:S(2)}) collective-permute-start(bf16[2,96,896]{2,1,0:T(8,128)(2,1)} %get-tuple-element.176.value_ref.refs_1_), channel_id=1, source_target_pairs={{0,2},{2,0},{4,6},{6,4},{1,3},{3,1},{5,7},{7,5},{8,10},{10,8},{12,... | collective-permute-start | bytes 1032200 | tf_op jit(solution)/shard_map/ppermute | solution.py:67
  353.6 26.6 %collective-permute-start.50 = (bf16[2,96,896]{2,1,0:T(8,128)(2,1)}, bf16[2,96,896]{2,1,0:T(8,128)(2,1)S(1)}, u32[]{:S(2)}, u32[]{:S(2)}) collective-permute-start(bf16[2,96,896]{2,1,0:T(8,128)(2,1)} %get-tuple-element.174.refs_2_), channel_id=1, source_target_pairs={{0,4},{2,6},{4,0},{6,2},{1,5},{3,7},{5,1},{7,3},{8,12},{10,14},{12... | collective-permute-start | bytes 1032200 | tf_op jit(solution)/shard_map/ppermute | solution.py:67
  379.7 38.9 %collective-permute-start.57 = (bf16[4,96,896]{2,1,0:T(8,128)(2,1)S(1)}, bf16[4,96,896]{2,1,0:T(8,128)(2,1)S(1)}, u32[]{:S(2)}, u32[]{:S(2)}) collective-permute-start(bf16[4,96,896]{2,1,0:T(8,128)(2,1)S(1)} %pad_maximum_fusion.5.refs_2_), channel_id=1, source_target_pairs={{0,4},{2,6},{4,0},{6,2},{1,5},{3,7},{5,1},{7,3},{8,12},{10,14},{12... | collective-permute-start | bytes 2064392 | tf_op jit(solution)/shard_map/ppermute | solution.py:67
  380.4 38.2 %collective-permute-start.56 = (bf16[4,96,896]{2,1,0:T(8,128)(2,1)S(1)}, bf16[4,96,896]{2,1,0:T(8,128)(2,1)S(1)}, u32[]{:S(2)}, u32[]{:S(2)}) collective-permute-start(bf16[4,96,896]{2,1,0:T(8,128)(2,1)S(1)} %pad_maximum_fusion.4.refs_1_), channel_id=1, source_target_pairs={{0,2},{2,0},{4,6},{6,4},{1,3},{3,1},{5,7},{7,5},{8,10},{10,8},{12,... | collective-permute-start | bytes 2064392 | tf_op jit(solution)/shard_map/ppermute | solution.py:67
  392.1 90.8 %collective-permute-start.68 = (bf16[5,3,384,256]{3,2,1,0:T(8,128)(2,1)}, bf16[5,3,384,256]{3,2,1,0:T(8,128)(2,1)}, u32[]{:S(2)}, u32[]{:S(2)}) collective-permute-start(bf16[5,3,384,256]{3,2,1,0:T(8,128)(2,1)} %get-tuple-element.182.refs_3_), channel_id=1, source_target_pairs={{0,8},{8,0},{16,24},{24,16},{1,9},{9,1},{17,25},{25,17},{2,10},{10... | collective-permute-start | bytes 8847368 | tf_op jit(solution)/shard_map/ppermute | solution.py:67
  444.1 31.4 %collective-permute-start.63 = (bf16[4,96,1408]{2,1,0:T(8,128)(2,1)S(1)}, bf16[4,96,1408]{2,1,0:T(8,128)(2,1)}, u32[]{:S(2)}, u32[]{:S(2)}) collective-permute-start(bf16[4,96,1408]{2,1,0:T(8,128)(2,1)S(1)} %pad_maximum_fusion.2.refs_1_), channel_id=1, source_target_pairs={{0,2},{2,0},{4,6},{6,4},{1,3},{3,1},{5,7},{7,5},{8,10},{10,8},{12,... | collective-permute-start | bytes 3244040 | tf_op jit(solution)/shard_map/ppermute | solution.py:67
  447.9 27.7 %collective-permute-start.64 = (bf16[4,96,1408]{2,1,0:T(8,128)(2,1)}, bf16[4,96,1408]{2,1,0:T(8,128)(2,1)}, u32[]{:S(2)}, u32[]{:S(2)}) collective-permute-start(bf16[4,96,1408]{2,1,0:T(8,128)(2,1)} %pad_maximum_fusion.3.refs_2_), channel_id=1, source_target_pairs={{0,4},{2,6},{4,0},{6,2},{1,5},{3,7},{5,1},{7,3},{8,12},{10,14},{12... | collective-permute-start | bytes 3244040 | tf_op jit(solution)/shard_map/ppermute | solution.py:67
  456.5 22.4 %collective-permute-start.55 = (f32[256,1536]{1,0:T(8,128)}, f32[256,1536]{1,0:T(8,128)}, u32[]{:S(2)}, u32[]{:S(2)}) collective-permute-start(f32[256,1536]{1,0:T(8,128)} %fusion.4), channel_id=1, source_target_pairs={{0,1},{1,0},{2,3},{3,2},{4,5},{5,4},{6,7},{7,6},{8,9},{9,8},{10,11... | collective-permute-start | bytes 4718600 | tf_op jit(solution)/shard_map/ppermute | solution.py:63
  (77 other events, 558.9 us)

commit v5 on v4

--- a/solution.py
+++ b/solution.py
@@ -2,6 +2,7 @@
 
 import jax
 import jax.numpy as jnp
+import numpy as np
 from jax import lax
 from jax.experimental import pallas as pl
 from jax.experimental.pallas import tpu as pltpu
@@ -14,7 +15,7 @@
 
 EPS = 1e-06
 VMEM_LIMIT = 56 * 1024 * 1024
-HOLDS = True
+COST = 100
 THETA = 10000.0
 bfloat = jnp.bfloat16
 single = jnp.float32
@@ -41,18 +42,14 @@
     return after_all([value], *others)[0] if others else value
 
 
-def hold_kernel(value_ref, out_ref):
-    out_ref[...] = jnp.zeros_like(out_ref)
-
-
 def hold(value):
-    if not HOLDS:
-        return []
+    anywhere = pl.BlockSpec(memory_space=pl.ANY)
     return [
         pl.pallas_call(
-            hold_kernel,
+            pass_kernel,
             name="hold",
-            in_specs=[pl.BlockSpec(memory_space=pl.ANY)],
+            in_specs=[anywhere],
+            out_specs=anywhere,
             out_shape=jax.ShapeDtypeStruct((8, 128), single),
             cost_estimate=pl.CostEstimate(flops=10**12, bytes_accessed=10**9, transcendentals=0),
         )(value)
@@ -167,18 +164,36 @@
     return parts, [to_peer(low, "expert", 1), to_peer(high, "expert", 2)]
 
 
+def dense_kernel(first_in, second_in, low_ref, high_ref, *refs):
+    first_ref, second_ref = refs[-2:]
+    step = pl.program_id(0)
+    low = jnp.where(step == 0, low_ref[...].astype(single), 0.0)
+    high = jnp.where(step == 0, 0.0, high_ref[...].astype(single))
+    first_ref[...] = (first_in[...].astype(single) + high).astype(bfloat)
+    second_ref[...] = (second_in[...].astype(single) + low).astype(bfloat)
+
+
 def go_on(state, *others):
     parts, came = state
     if came is None:
         sent = [after(part, *others) for part in parts[1:]]
         return [parts[0]] + [to_peer(part, "expert", i) for i, part in enumerate(sent, 1)], sent
-    low = after(came[0], *hold(parts[3][0]), *others).astype(single)
-    high = came[1].astype(single)
-    cut = low.shape[0]
-    first, second = parts[1].astype(single), parts[2].astype(single)
-    first = jnp.concatenate([first[:cut], first[cut:] + high], axis=0).astype(bfloat)
-    second = jnp.concatenate([second[:cut] + low, second[cut:]], axis=0).astype(bfloat)
-    return [parts[0], to_peer(first, "expert", 1), to_peer(second, "expert", 2)], [first, second]
+    low = after(came[0], *hold(parts[3][0]))
+    shape = parts[1].shape
+    half = pl.BlockSpec((shape[0] // 2,) + shape[1:], lambda i: (i, 0, 0))
+    only = pl.BlockSpec((shape[0] // 2,) + shape[1:], lambda i: (0, 0, 0))
+    whole = jax.ShapeDtypeStruct(shape, bfloat)
+    first, second = pl.pallas_call(
+        dense_kernel,
+        name="dense_nearer",
+        grid=(2,),
+        in_specs=[half, half, only, only] + [pl.BlockSpec(memory_space=pl.ANY)] * len(others),
+        out_specs=[half, half],
+        out_shape=[whole, whole],
+        cost_estimate=pl.CostEstimate(flops=0, bytes_accessed=2**22, transcendentals=0),
+    )(parts[1], parts[2], low, came[1], *others)
+    came = to_peer(first, "expert", 1), to_peer(second, "expert", 2)
+    return [parts[0], after(came[0], *hold(first)), came[1]], [first, second]
 
 
 def add_up(own, arrived):
@@ -197,20 +212,67 @@
     return value
 
 
-def over_dp(total):
+def over_dp_start(total):
     at_dp, count = lax.axis_index("dp"), lax.axis_size("dp")
     parts = {r: lax.dynamic_index_in_dim(total, at_dp ^ r, 0, keepdims=False) for r in range(count)}
-    step = 1
-    while step < count:
-        leaving = [r for r in parts if r & step]
-        sent = jnp.concatenate([parts[r].astype(bfloat) for r in leaving], axis=0)
-        came = to_peer(sent, "dp", step).astype(single)
-        rows = came.shape[0] // len(leaving)
-        for i, r in enumerate(leaving):
-            parts[r ^ step] = parts[r ^ step] + came[i * rows : (i + 1) * rows]
-            del parts[r]
-        step *= 2
-    return parts[0]
+    return over_dp_send(parts, 1)
+
+
+def over_dp_send(parts, step):
+    if step >= lax.axis_size("dp"):
+        return parts, None, step
+    return parts, jnp.concatenate([parts[r].astype(bfloat) for r in parts if r & step], axis=0), step
+
+
+def over_dp_step(state, *others):
+    parts, sent, step = state
+    parts = dict(parts)
+    leaving = [r for r in parts if r & step]
+    came = after(to_peer(sent, "dp", step), *hold(sent), *others).astype(single)
+    rows = came.shape[0] // len(leaving)
+    for i, r in enumerate(leaving):
+        parts[r ^ step] = parts[r ^ step] + came[i * rows : (i + 1) * rows]
+        del parts[r]
+    return over_dp_send(parts, 2 * step)
+
+
+def over_dp_end(state, *others):
+    while state[1] is not None:
+        state, others = over_dp_step(state, *others), ()
+    return state[0][0]
+
+
+def over_dp_at_once(total):
+    at_dp = lax.axis_index("dp")
+
+    def row(step):
+        return lax.dynamic_index_in_dim(total, at_dp ^ step, 0, keepdims=False)
+
+    sent = [row(step).astype(bfloat) for step in range(1, lax.axis_size("dp"))]
+    return row(0), [to_peer(part, "dp", step) for step, part in enumerate(sent, 1)], sent
+
+
+def scaled_sum_kernel(amount, widths, scale_ref, *refs):
+    parts, outs = refs[:amount], refs[amount:]
+    total = None
+    for part in parts:
+        value = part[...].astype(single)
+        total = value if total is None else total + value
+    total = total * scale_ref[:1, :1]
+    at = 0
+    for out, width in zip(outs, widths):
+        out[...] = total[:, at : at + width]
+        at += width
+
+
+def scaled_sum(scale, parts, widths):
+    rows = parts[0].shape[0]
+    return pl.pallas_call(
+        functools.partial(scaled_sum_kernel, len(parts), widths),
+        name="scaled_sum",
+        out_shape=[jax.ShapeDtypeStruct((rows, width), single) for width in widths],
+        cost_estimate=pl.CostEstimate(flops=0, bytes_accessed=2**21, transcendentals=0),
+    )(scale, *parts)
 
 
 def dot(left, right):
@@ -244,25 +306,20 @@
     return pairs + [(joined_ref.at[0], joined_ref.at[1])]
 
 
-def find_slots(first_ref, top_count, pairs, slots_ref, count_ref):
+def find_slots(first_ref, top_count, pairs, slots_ref):
     groups, experts, tokens = slots_ref.shape
     row = lax.broadcasted_iota(jnp.int32, (tokens, tokens), 0)
     earlier = (row < lax.broadcasted_iota(jnp.int32, (tokens, tokens), 1)).astype(bfloat)
     ids = lax.broadcasted_iota(jnp.int32, (experts, tokens), 0)
     ids = (ids + first_ref[0]).astype(single)
-    total = None
     for group, pair in enumerate(pairs):
         tails = [part[:, part.shape[1] - 128 :].astype(single).T for part in pair]
         routes = jnp.concatenate(tails, axis=1)[128 - top_count :]
-        valid = routes[:1] >= 64.0
-        ahead = jnp.where(valid, 1.0, 0.0)
-        total = ahead if total is None else total + ahead
-        mask = ids == routes[:1] - 64.0 * ahead
+        mask = ids == routes[:1]
         for k in range(1, top_count):
             mask = mask | (ids == routes[k : k + 1])
         before = dot(mask.astype(single).astype(bfloat), earlier)
         slots_ref[group] = jnp.where(mask, before, -1.0).astype(jnp.int32)
-    count_ref[...] = jnp.broadcast_to(jnp.sum(total, axis=1, keepdims=True), count_ref.shape)
 
 
 def gather_rows(slots_ref, expert, pairs, rows_ref):
@@ -288,7 +345,7 @@
 
 def return_order(groups):
     rest = list(range(1, groups)) + [0]
-    return [[3], [1, 2, 0]] if groups == 4 else [rest]
+    return [[3], [1, 2], [0]] if groups == 4 else [rest]
 
 
 def forward_kernel(count, top_count, amount, halved, start, with_out, place_ref, gate_w, up_w, *refs):
@@ -296,8 +353,8 @@
         down_w, refs = refs[0], refs[1:]
     parts, refs = refs[:amount], refs[amount:]
     parts, pins = parts[:-1], parts[-1:]
-    gate_ref, up_ref, half_ref, tail_ref, slots_ref, count_ref = refs[:6]
-    refs = refs[6:]
+    gate_ref, up_ref, half_ref, tail_ref, slots_ref = refs[:5]
+    refs = refs[5:]
     step = pl.program_id(0)
     joined_ref = refs[-1] if halved else None
     rows_ref = refs[-2] if halved else refs[-1]
@@ -306,7 +363,7 @@
 
     @pl.when(step == 0)
     def _():
-        find_slots(place_ref, top_count, pairs, slots_ref, count_ref)
+        find_slots(place_ref, top_count, pairs, slots_ref)
 
     gather_rows(slots_ref, start + step, pairs, rows_ref)
     half_ref[0] = rows_ref[:, half_columns(place_ref, half_ref.shape[2])]
@@ -333,8 +390,8 @@
     return hidden, (hidden * gates).astype(bfloat), grad_gate_pre, grad_up_pre
 
 
-def backward_kernel(count, amount, halved, place_ref, slots_ref, gate_w, up_w, down_w, gate_ref, up_ref, tail_ref, *refs):
-    parts, refs = refs[:amount], refs[amount:]
+def backward_kernel(count, amount, halved, pins, place_ref, slots_ref, gate_w, up_w, down_w, gate_ref, up_ref, tail_ref, *refs):
+    parts, refs = refs[:amount], refs[amount + pins :]
     hidden_ref, grad_gate_ref, grad_up_ref, half_ref, refs = refs[0], refs[1], refs[2], refs[3], refs[4:]
     back_ref, rows_ref = refs[:2]
     joined_ref = refs[2] if halved else None
@@ -361,9 +418,9 @@
     back_ref[0, :, width:] = jnp.where(lane == expert, grad_logit, 0.0).astype(bfloat)
 
 
-def weights_kernel(count, groups, start, place_ref, slots_ref, down_w, gate_ref, up_ref, tail_ref, *refs):
+def weights_kernel(count, groups, start, pins, place_ref, slots_ref, down_w, gate_ref, up_ref, tail_ref, *refs):
     hidden_near, gate_near, up_near, near_x, near_g, far_x = refs[:6]
-    parts, refs = refs[6 : 6 + 2 * groups], refs[6 + 2 * groups :]
+    parts, refs = refs[6 : 6 + 2 * groups], refs[6 + 2 * groups + pins :]
     shards, (rows_ref, full_ref) = refs[:-2], refs[-2:]
     expert = start + pl.program_id(0)
     gather_rows(slots_ref, expert, group_parts(parts, None), rows_ref)
@@ -440,12 +497,16 @@
         compiler_params=pltpu.CompilerParams(
             dimension_semantics=("arbitrary",) * len(grid), vmem_limit_bytes=VMEM_LIMIT
         ),
-        cost_estimate=pl.CostEstimate(flops=flops, bytes_accessed=moved, transcendentals=0),
+        cost_estimate=pl.CostEstimate(flops=COST * flops, bytes_accessed=moved, transcendentals=0),
     )(*args)
 
 
 def per_expert(*shape, start=0):
     return pl.BlockSpec((1,) + shape, lambda e, *_: (e + start,) + (0,) * len(shape))
+
+
+def anywhere(pins):
+    return [pl.BlockSpec(memory_space=pl.ANY) for _ in pins]
 
 
 def once(*shape):
@@ -458,7 +519,7 @@
     groups, _, tokens = slots.shape
     experts, _, width = rows.shape
     amount, first = len(order), order[0]
-    cycle = amount if amount > 1 else groups
+    cycle = groups
     cuts = 2 if width % 256 == 0 else 1
     cut = width // cuts
     part = pl.BlockSpec((1, span, cut), lambda g, n: (g, 0, n))
@@ -493,8 +554,8 @@
     shapes += [jax.ShapeDtypeStruct((experts, total, width // 2), bfloat)]
     shapes += [jax.ShapeDtypeStruct((experts, total, whole - width), bfloat)]
     listed = (groups, -(-weights[0].shape[0] // 8) * 8, tokens)
-    outs += [pl.BlockSpec(listed, lambda e, *_: (0, 0, 0)), pl.BlockSpec((8, 128), lambda e, *_: (0, 0))]
-    shapes += [jax.ShapeDtypeStruct(listed, jnp.int32), jax.ShapeDtypeStruct((8, 128), single)]
+    outs += [pl.BlockSpec(listed, lambda e, *_: (0, 0, 0))]
+    shapes += [jax.ShapeDtypeStruct(listed, jnp.int32)]
     scratch = [pltpu.VMEM((total, whole), bfloat)]
     if halved:
         scratch += [pltpu.VMEM((2, span, whole), bfloat)]
@@ -514,7 +575,7 @@
     )
 
 
-def expert_backward(place, count, slots, weights, gate_pre, up_pre, tails, parts, capacity):
+def expert_backward(place, count, slots, weights, gate_pre, up_pre, tails, parts, capacity, pins):
     groups, _, tokens = slots.shape
     experts = weights[0].shape[0]
     span, whole = parts[0].shape
@@ -528,19 +589,19 @@
     shapes += [jax.ShapeDtypeStruct((experts, total, width // 2), bfloat)]
     shapes += [jax.ShapeDtypeStruct((experts, total, whole), bfloat)]
     return kernel_call(
-        functools.partial(backward_kernel, count, len(parts), len(parts) > 2 * groups),
+        functools.partial(backward_kernel, count, len(parts), len(parts) > 2 * groups, len(pins)),
         "expert_backward",
-        (experts,), specs + [once(*part.shape) for part in parts], outs, shapes,
+        (experts,), specs + [once(*part.shape) for part in parts] + anywhere(pins), outs, shapes,
         [pltpu.VMEM((total, whole), bfloat)]
         + ([pltpu.VMEM((2, span, whole), bfloat)] if len(parts) > 2 * groups else []),
         2 * experts * total * width * (hidden * 3 + tokens),
         2 * experts * (3 * width * hidden + 3 * total * width // 2 + 7 * total * hidden),
-        (place, slots) + tuple(weights) + (gate_pre, up_pre, tails) + tuple(parts),
+        (place, slots) + tuple(weights) + (gate_pre, up_pre, tails) + tuple(parts) + tuple(pins),
         prefetch=1,
     )
 
 
-def expert_weights(place, count, slots, down_w, far, near, parts, capacity, start, far_start, experts, shards):
+def expert_weights(place, count, slots, down_w, far, near, parts, capacity, start, far_start, experts, shards, pins):
     groups, _, tokens = slots.shape
     hidden, width = down_w.shape[1:]
     total = groups * capacity
@@ -554,15 +615,15 @@
     specs += [wide_at, wide_at, wide]
     size = width // (2 * shards)
     return kernel_call(
-        functools.partial(weights_kernel, count, groups, start),
+        functools.partial(weights_kernel, count, groups, start, len(pins)),
         "expert_weights",
-        (experts,), specs + [once(*part.shape) for part in parts],
+        (experts,), specs + [once(*part.shape) for part in parts] + anywhere(pins),
         [per_expert(3, size, hidden)] * shards,
         [jax.ShapeDtypeStruct((experts, 3, size, hidden), bfloat)] * shards,
         [pltpu.VMEM((total, width), bfloat), pltpu.VMEM((3, width // 2, hidden), bfloat)],
         2 * experts * total * width * (hidden * 4 + tokens),
         2 * experts * (5 * width * hidden // 2 + 3 * total * width // 2 + 7 * total * hidden),
-        (place, slots, down_w) + tuple(far_pre) + (far_tails,) + tuple(near) + (far_half,) + tuple(parts),
+        (place, slots, down_w) + tuple(far_pre) + (far_tails,) + tuple(near) + (far_half,) + tuple(parts) + tuple(pins),
         prefetch=1,
     )
 
@@ -812,14 +873,14 @@
     return total
 
 
-def token_kernel(count, place_ref, stay_ref, came_ref, routes_ref, valid_ref, gain_ref, router_ref, hidden_ref, token_ref):
+def token_kernel(count, place_ref, stay_ref, came_ref, routes_ref, gain_ref, router_ref, hidden_ref, token_ref):
     width = stay_ref.shape[1]
     hidden = stay_ref[...] + came_ref[...]
     hidden_ref[...] = hidden
     inverse = lax.rsqrt(jnp.mean(hidden * hidden, axis=1, keepdims=True) + EPS)
     moe_in = (hidden * inverse * gain_ref[...]).astype(bfloat)
     token_ref[:, :width] = moe_in
-    logits = dot(moe_in, router_ref[...])
+    logits = dot_nt(moe_in, router_ref[...])
     logits = jnp.concatenate([logits, jnp.zeros((logits.shape[0], 128 - count), single)], axis=1)
     lane = lax.broadcasted_iota(jnp.int32, logits.shape, 1)
     picked = lane == routes_ref[:, :1]
@@ -830,21 +891,20 @@
     gates = weights / jnp.sum(weights, axis=1, keepdims=True)
     tail = three_lanes(gates, (0, count, 2 * count), 128)
     routes = routes_ref[...].astype(single)
-    first = lax.broadcasted_iota(jnp.int32, routes.shape, 1) == 0
-    routes = routes + jnp.where(first, 64.0 * valid_ref[...].astype(single), 0.0)
     blank = jnp.zeros((routes.shape[0], 128 - routes.shape[1]), single)
     token_ref[:, width:] = (tail + jnp.concatenate([blank, routes], axis=1)).astype(bfloat)
 
 
 def layer_kernel(addends, place_ref, hidden_ref, target_ref, valid_ref, *refs):
-    parts, (layer_ref, grad_ref, token_ref) = refs[:addends], refs[addends:]
+    parts, (layer_ref, grad_ref, low_ref, token_ref) = refs[:addends], refs[addends:]
     width = hidden_ref.shape[1]
     moe = sum_of(parts)
     layer = hidden_ref[...] + moe
     layer_ref[...] = layer.astype(bfloat)
-    valid = valid_ref[...].astype(single)
+    valid = valid_ref[:, :1].astype(single)
     grad = valid * (layer - target_ref[...].astype(single))
     grad_ref[...] = grad
+    low_ref[...] = grad.astype(bfloat)
     token_ref[:, :width] = grad.astype(bfloat)
     inner = jnp.sum(grad * moe, axis=1, keepdims=True)
     lane = lax.broadcasted_iota(jnp.int32, (inner.shape[0], 128), 1)
@@ -861,13 +921,13 @@
 
 
 def norm_kernel(addends, place_ref, hidden_ref, grad_layer_ref, *refs):
-    parts, (gain_ref, router_ref, grad_ref, low_ref, logits_ref, sum_ref) = refs[:addends], refs[addends:]
+    parts, (gain_ref, router_ref, digits_ref, grad_ref, low_ref, logits_ref, sum_ref) = refs[:addends], refs[addends:]
     width = hidden_ref.shape[1]
     wide = sum_of(parts)
     logits = wide[:, width:].astype(bfloat)
     logits_ref[...] = logits
-    count = router_ref.shape[1]
-    grad_in = wide[:, :width] + dot_nt(logits[:, :count], router_ref[...])
+    count = router_ref.shape[0]
+    grad_in = wide[:, :width] + dot(logits[:, :count], router_ref[...])
     hidden = hidden_ref[...]
     inverse = lax.rsqrt(jnp.mean(hidden * hidden, axis=1, keepdims=True) + EPS)
     scaled = grad_in * gain_ref[...]
@@ -881,7 +941,7 @@
 
     @pl.when(pl.program_id(0) == 0)
     def _():
-        sum_ref[...] = gain
+        sum_ref[...] = gain + digits_ref[:, :1]
 
     @pl.when(pl.program_id(0) > 0)
     def _():
@@ -942,7 +1002,7 @@
     high = sums.astype(bfloat)
     low = (sums - high.astype(single)).astype(bfloat)
     lane = lax.broadcasted_iota(jnp.int32, (sums.shape[0], 128), 1)
-    chosen = (lane == lane_at).astype(bfloat)
+    chosen = (lane == lane_at + lax.broadcasted_iota(jnp.int32, lane.shape, 0)).astype(bfloat)
     column = dot_tn(high, chosen) + dot_tn(low, chosen)
     width = full_ref.shape[1]
     if at < width:
@@ -1013,9 +1073,9 @@
 
 def rope_tables(length, head_size):
     half_size = head_size // 2
-    frequency = THETA ** (-jnp.arange(half_size, dtype=jnp.float32) * 2.0 / head_size)
-    angles = jnp.arange(length, dtype=jnp.float32)[:, None] * frequency[None, :]
-    return (jnp.cos(angles), jnp.sin(angles))
+    frequency = np.float32(THETA) ** (-np.arange(half_size, dtype=np.float32) * np.float32(2.0) / np.float32(head_size))
+    angles = np.arange(length, dtype=np.float32)[:, None] * frequency.astype(np.float32)[None, :]
+    return [jnp.asarray(np.tile(f(angles).astype(np.float32), (1, 128 // half_size))) for f in (np.cos, np.sin)]
 
 
 def rms_backward(value_matrix, inverse, gain, grad_normed):
@@ -1032,7 +1092,7 @@
     return jnp.concatenate([jnp.where(first, mine, other), jnp.where(first, other, mine)], axis=0)
 
 
-def combine_groups(slots, rows, capacity, span, between):
+def combine_groups(slots, rows, capacity, span, between, later=None):
     owners = slots.shape[0]
     orders = return_order(owners)
     if len(orders) == 1:
@@ -1049,9 +1109,14 @@
         came, sent = send_farthest(mine, other)
         done = between(sent)
         came[0] = after(came[0], *hold(sent[0]), *done)
-        mine, other = return_rows(slots, after(rows, *done), orders[1], capacity, span)
+        rows = after(rows, *done, *hold(sent[0]), *hold(sent[1]))
+        mine, other = return_rows(slots, rows, orders[1], capacity, span)
         other = after(swap(other), *hold(other))
         came, sent = send_nearer(mine, other, came)
+        rows = after(rows, *sent, *hold(sent[0]), *hold(sent[1]))
+        done = later(sent) if later else ()
+        mine, other = return_rows(slots, rows, orders[2], capacity, span)
+        other = swap(after(other, *done))
     own = len(orders[-1]) - 1
     return [(mine, own), (other, own)] + came, sent
 
@@ -1098,7 +1163,7 @@
     def other_of(value, axis=0):
         return lax.dynamic_slice_in_dim(value, (1 - core) * span, span, axis)
 
-    tables = [jnp.tile(table, (1, 4)) for table in rope_tables(SEQUENCE_LENGTH, HEAD_DIMENSION)]
+    tables = rope_tables(SEQUENCE_LENGTH, HEAD_DIMENSION)
     gain_attn, gain_moe = norm_attn.reshape(1, model_width), norm_moe.reshape(1, model_width)
 
     def tokens_like(columns, kind):
@@ -1115,14 +1180,14 @@
         "token",
         4,
         place,
-        [staying, came, (routes, None), (valid[:, None], None)],
-        [gain_moe, w_router],
+        [staying, came, (routes, None)],
+        [gain_moe, w_router.T],
         [tokens_like(model_width, single), tokens_like(wide, bfloat)],
     )
 
     some = experts_local // 2
+    few = max(1, some - some // 2)
     pieces = ((0, some), (some, experts_local - some))
-    few = max(1, experts_local // 5)
 
     def interleave(mine, other):
         return [part for pair in zip(mine, other) for part in pair]
@@ -1132,17 +1197,21 @@
             place, all_experts, top_count, pin, (w_gate, w_up), parts, owners, capacity, start, amount
         )
 
-    wanted, valid_rows = after_all([teacher_rows, valid[:, None]], token)
-    wanted = mine_of(wanted[0])
-    chooser = (wanted[:, None] == jnp.arange(rows_dev, dtype=jnp.int32)).astype(bfloat)
+    (wanted,) = after_all([mine_of(teacher_rows, 1)], token)
+    (valid_rows,) = after_all([mine_of(valid)[:, None] + jnp.zeros((span, 128), jnp.int32)], token)
+    chooser = (wanted[0][:, None] == jnp.arange(rows_dev, dtype=jnp.int32)).astype(bfloat)
     target = jnp.dot(chooser, teacher, preferred_element_type=bfloat)
 
     mirror = to_mirror(token)
-    near_parts = spread(token, (target,))
+    (counted,) = after_all([jnp.broadcast_to(valid[None, :], (8, rows_dev))], token)
+    count = jnp.sum(counted[0])
+    digits = jnp.stack([jnp.zeros((), jnp.int32), count // 64, count // 8 % 8, count % 8] + [jnp.zeros((), jnp.int32)] * 4)
+    digits = jnp.broadcast_to(digits.astype(single)[:, None], (8, 128))
+    near_parts = spread(token, (target, digits))
     mirror = after(mirror, *near_parts)
     peers = from_peers(mirror)
     mirror_other = swap(mirror)
-    gate_pre, up_pre, near_half, near_tails, slots, valid_count, results = expert_forward(
+    gate_pre, up_pre, near_half, near_tails, slots, results = expert_forward(
         place, all_experts, top_count, mirror, (w_gate, w_up, w_down), near_parts, owners, capacity, 0, experts_local
     )
     results = after(results, mirror_other)
@@ -1157,35 +1226,35 @@
     far_tokens = interleave([mirror] + peers, [mirror_other] + peers_other)
     far = [far_forward(far_tokens, *pieces[0], sent[0])]
     addends[-1] = after(addends[-1], far[0][0], *hold(sent[0]))
-    layer_low, grad_layer, token_grad = token_rows(
+    layer_low, grad_layer, layer_grad, token_grad = token_rows(
         functools.partial(layer_kernel, len(addends)),
         "layer",
         4,
         place,
-        [hidden_first, target, (valid_rows, None)] + addends,
+        [hidden_first, target, valid_rows] + addends,
         [],
-        [tokens_like(model_width, bfloat), tokens_like(model_width, single), tokens_like(wide, bfloat)],
+        [tokens_like(model_width, bfloat), tokens_like(model_width, single), tokens_like(model_width, bfloat), tokens_like(wide, bfloat)],
     )
 
     far.append(far_forward(far_tokens, *pieces[1], token_grad))
-    mirror = to_mirror(token_grad)
+    mirror = to_mirror(after(layer_grad, *hold(token_grad)))
     near_parts = spread(token_grad, (far[1][0],))
     mirror = after(mirror, *near_parts)
     peers = from_peers(mirror)
     mirror_other = swap(mirror)
     hidden_low, grad_gate_pre, grad_up_pre, near_grad_half, results = expert_backward(
-        place, all_experts, after(slots, mirror), (w_gate, w_up, w_down), gate_pre, up_pre, near_tails, near_parts, capacity
+        place, all_experts, slots, (w_gate, w_up, w_down), gate_pre, up_pre, near_tails, near_parts, capacity, (mirror,)
     )
     results = after(results, mirror_other)
     weight_parts, far_grads = [], []
 
     def weights_of(start, amount, others=()):
         piece = 0 if start < some else 1
-        far_gate, far_up, far_half, far_tails, far_slots, _ = far[piece]
+        far_gate, far_up, far_half, far_tails, far_slots = far[piece]
         values = expert_weights(
             place,
             all_experts,
-            after(far_slots, *others),
+            far_slots,
             w_down,
             (far_gate, far_up, far_tails, far_half),
             (hidden_low, grad_gate_pre, grad_up_pre, near_half, near_grad_half),
@@ -1195,34 +1264,35 @@
             start - pieces[piece][0],
             amount,
             shards,
+            tuple(others),
         )
         came = [to_peer(values[step], "dp", step) for step in range(1, shards)]
         weight_parts.append((start, values[0], came))
-        return values
-
-    def first_weights(sent):
+        return (*values, *[pin for value in values[1:] for pin in hold(value)])
+
+    def swap_far(sent):
         peers[:] = after_all(peers, *sent)
         peers_other = [swap(peer) for peer in peers]
         far_grads.extend(interleave([mirror] + peers, [mirror_other] + peers_other))
-        return weights_of(0, few)
-
-    addends, sent = combine_groups(slots, results, capacity, span, first_weights)
-    layer_low = after(layer_low, *sent)
-    layer_other = swap(layer_low)
-    block_out = assemble(layer_low, layer_other)
-    done = weights_of(few, some - few, sent)
-    addends[-1] = after(addends[-1], *done, layer_other, *hold(sent[0]))
+        return peers_other
+
+    results = after(results, *peers)
+    addends, sent = combine_groups(slots, results, capacity, span, lambda sent: sent, swap_far)
+    if owners != 4:
+        swap_far(sent)
+    done = weights_of(0, few, sent)
+    addends[-1] = after(addends[-1], *done, *hold(sent[0]))
     grad_hidden, grad_attn, grad_logits, gain_sums = token_rows(
         functools.partial(norm_kernel, len(addends)),
         "norm",
         4,
         place,
         [hidden_first, grad_layer] + addends,
-        [gain_moe, w_router],
+        [gain_moe, w_router.T, digits],
         [tokens_like(model_width, single), tokens_like(model_width, bfloat), tokens_like(128, bfloat)],
         [jax.ShapeDtypeStruct((8, model_width), single)],
     )
-    grad_attn_other = after(swap(grad_attn), *hold(grad_attn), *weight_parts[0][2])
+    grad_attn_other = after(swap(grad_attn), *hold(grad_attn))
     first_parts = pack_sums(
         place,
         [grad_attn, grad_attn_other, token],
@@ -1236,62 +1306,70 @@
     first_sum = start_sum(first_parts)
     done = weights_of(some, experts_local - some, first_parts[-1] if owners == 4 else first_parts)
     first_sum, sent = go_on(first_sum, *done)
-    grad_attn = after(grad_attn, *sent)
+    grad_attn, layer_low = after_all([grad_attn, layer_low], *sent, *weight_parts[0][2])
+    layer_other = swap(layer_low)
     raw_query, raw_key, raw_value, staying, leaving, gain_sums = attend_back(
         place, grad_attn, grad_attn_other, tokens, *weights, tables, (queries, keys, values, log_sums)
     )
-    gain_sums = after(gain_sums, *first_sum[1:], *weight_parts[1][2])
     second_parts = pack_sums(
         place,
         [normed] * 3,
         [raw_query, raw_key, raw_value],
-        gain_sums,
+        after(gain_sums, *first_sum[1:], layer_other),
         0,
         query_width + 2 * key_width + 128,
         count_dp,
         owners,
     )
-    first_total = add_up(first_sum[0], first_sum[1:])
     second_sum = start_sum(second_parts)
-    step = 1
-    while step < count_dp:
-        valid_count = valid_count + to_peer(valid_count, "dp", step)
-        step *= 2
-    scale = float(rows_dev * groups) / valid_count
-    second_sum, sent = go_on(second_sum, scale)
-    first_dense = over_dp(after(first_total, *sent))
-    weight_grads, done = None, []
-    for start, values, came in weight_parts[:2]:
-        came = [after(part, sent[0]) for part in came]
-        weight_grads, finished = finish_weights(experts_local, start, scale, values, came, weight_grads)
-        done.append(finished)
+    last = second_parts[-1] if owners == 4 else second_parts
+    leaving = swap(leaving)
+    first_total = add_up(first_sum[0], after_all(first_sum[1:], *last, leaving))
+    first_dense = over_dp_start(first_total)
+    pins = [] if first_dense[1] is None else [first_dense[1], *hold(first_dense[1])]
+    done = weights_of(few, some - few, (*last, *hold(last[0]), *pins))
+    second_sum, sent = go_on(second_sum, *done)
+    first_dense = over_dp_step(first_dense, *sent, *weight_parts[1][2])
+    leaving = after(leaving, *sent)
     inputs_mine = mine_of(tokens).astype(single)
     inverse_mine = lax.rsqrt(jnp.mean(inputs_mine * inputs_mine, axis=-1, keepdims=True) + EPS)
     grad_first, _ = rms_backward(
-        inputs_mine, inverse_mine, norm_attn, staying + swap(leaving).astype(single)
-    )
-    grad_tokens_mine = (grad_hidden + grad_first) * scale[0, 0]
-    grad_tokens = assemble(grad_tokens_mine, swap(grad_tokens_mine))
-    second_total = add_up(second_sum[0], second_sum[1:])
-    second_dense = over_dp(after(second_total, grad_tokens, first_dense, *done)) * scale[0, 0]
-    first_dense = first_dense * scale[0, 0]
-    for start, values, came in weight_parts[2:]:
-        came = [after(part, second_total) for part in came]
-        weight_grads, _ = finish_weights(experts_local, start, scale, values, came, weight_grads)
-    shared = jnp.concatenate([first_dense[:, query_width:], second_dense[:, -128:]], axis=1)
-    shared = shared + swap(shared)
-
-    key_at = query_width
+        inputs_mine, inverse_mine, norm_attn, staying + leaving.astype(single)
+    )
+    grad_tokens_mine = grad_hidden + grad_first
+    pins = [] if first_dense[1] is None else [first_dense[1], *hold(first_dense[1])]
+    second_total = add_up(second_sum[0], after_all(second_sum[1:], grad_tokens_mine, *pins))
+    own, arrived, sent = over_dp_at_once(second_total)
+    first_dense = over_dp_end(first_dense, *sent)
+    tail = first_dense[:, query_width:]
+    tail = tail + after(swap(tail), *hold(tail))
+    counted = tail[:1, all_experts + 1 : all_experts + 4] * jnp.asarray([[32.0, 4.0, 0.5]], single)
+    scale = jnp.broadcast_to(rows_dev * groups / jnp.sum(counted, axis=1, keepdims=True), (8, 128))
+    first_dense, tail = first_dense * scale[0, 0], tail * scale[0, 0]
+    grad_tokens_mine = grad_tokens_mine * scale[0, 0]
+    grad_tokens_other = after(swap(grad_tokens_mine), *hold(grad_tokens_mine))
+    grad_tokens = assemble(grad_tokens_mine, grad_tokens_other)
+    layer_low = after(layer_low, *sent)
+    block_out = assemble(layer_low, layer_other)
+    weight_grads, finished = None, ()
+    for start, values, came in weight_parts:
+        came = [after(part, *sent, grad_tokens_other) for part in came]
+        weight_grads, finished = finish_weights(experts_local, start, scale, values, came, weight_grads)
+    arrived[0] = after(arrived[0], *hold(sent[0]), finished, grad_tokens, tail)
+    grad_query, grad_key, grad_value, second_tail = scaled_sum(
+        scale, [own] + arrived, (query_width, key_width, key_width, 128)
+    )
+    second_tail = second_tail + swap(second_tail)
     return (
         block_out,
         grad_tokens,
-        shared[:, -128],
-        shared[:, all_experts],
-        second_dense[:, :key_at],
-        second_dense[:, key_at : key_at + key_width],
-        second_dense[:, key_at + key_width : key_at + 2 * key_width],
+        second_tail[:, 0],
+        tail[:, all_experts],
+        grad_query,
+        grad_key,
+        grad_value,
         first_dense[:, :query_width].T,
-        shared[:, :all_experts],
+        tail[:, :all_experts],
         weight_grads[0],
         weight_grads[1],
         weight_grads[2],

time: 521 us -> 510 us (0.979)
  waiting for transfers between devices: 76.7 us -> 65.8 us
  starting transfers between devices: 72.9 us -> 67.6 us
    ppermute x39 -> x38, waiting for transfers between devices: 61.3 us -> 45.4 us  [to_peer(): lax.ppermute(value, axis, [(i, i ^ step) for i in range(lax.axis_size(axi...]
    ppermute x39 -> x38, starting transfers between devices: 60.3 us -> 53.3 us  [to_peer(): lax.ppermute(value, axis, [(i, i ^ step) for i in range(lax.axis_size(axi...]
    ppermute x28 -> x31, waiting for transfers between devices: 15.4 us -> 20.4 us  [swap(): return lax.ppermute(value, 'tensor', [(0, 1), (1, 0)])]
    pallas_call x21 -> x23, Pallas kernels: 285 us -> 289 us  [kernel_call(): pl.pallas_call(kernel, name=name, grid_spec=pltpu.PrefetchScalarGridSpec(...]
    unnamed x85 -> x60, local copies, waits for them, and re-layouts: 12.9 us -> 11 us
  transfers between devices with their start and end apart: 69 -> 71, of which waited for: 23 -> 19; matrix products, arithmetic and copies ran while one was open for 6% -> 7% of each run, Pallas kernels for 54% -> 53%
where the time goes in v5:
time: 510 us; the launch traced here: 500 us
  Pallas kernels  313 us (61%)
  starting transfers between devices  67.6 us (13%)
  waiting for transfers between devices  65.8 us (13%)
  other arithmetic  25.8 us (5%)
  local copies, waits for them, and re-layouts  21.3 us (4%)
    pallas_call x23, Pallas kernels, kernel_call(): pl.pallas_call(kernel, name=name, grid_spec=pltpu.PrefetchScalarGridSpec(...  289 us
    ppermute x38, starting transfers between devices, to_peer(): lax.ppermute(value, axis, [(i, i ^ step) for i in range(lax.axis_size(axi...  53.3 us
    ppermute x38, waiting for transfers between devices, to_peer(): lax.ppermute(value, axis, [(i, i ^ step) for i in range(lax.axis_size(axi...  45.4 us
    ppermute x31, waiting for transfers between devices, swap(): return lax.ppermute(value, 'tensor', [(0, 1), (1, 0)])  20.4 us
    unnamed x60, local copies, waits for them, and re-layouts  11 us
  transfers between devices with their start and end apart: 71, of which 19 were waited for; matrix products, arithmetic and copies ran while one was open for 7% of the time, Pallas kernels for 53%

profile of v5, /device:TPU:0, one launch (start us, length us, event | category | flops | bytes accessed | tf_op | source)
XLA Modules:
  0.0 500.5 jit_solution(12550162111384532119)
XLA Ops:
  2.7 20.1 %attend.1 = (bf16[512,1536]{1,0:T(8,128)(2,1)}, bf16[12,512,64]{2,1,0:T(8,128)(2,1)}, bf16[4,512,64]{2,1,0:T(8,128)(2,1)}, bf16[4,512,64]{2,1,0:T(8,128)(2,1)}, ...) custom-call(s32[5]{0:T(128)} %stack.37.place_ref, ...), custom_call_target="tpu_custom_call" | custom-call | flops 322122547200 | bytes 15728640 | tf_op jit(solution)/shard_map/attend/pallas_call | solution.py:485
  26.7 5.8 %token_.1 = (f32[256,1536]{1,0:T(8,128)}, bf16[256,1664]{1,0:T(8,128)(2,1)}) custom-call(s32[5]{0:T(128)} %stack.37.place_ref, f32[256,1536]{1,0:T(8,128)} %get-tuple-element.127.stay_ref, f32[256,1536]{1,0:T(8,128)} %after.46.came_ref, s32[512,8]{1,0:T(8,128)} %copy.91.routes_ref, f32[1,1536]{1,0:T(1,128)} %reshape.98.gain_ref.refs_4_, ...), custom_call_target="tpu_custom_call" | custom-call | flops 100 | bytes 6553600 | tf_op jit(solution)/shard_map/token/pallas_call | solution.py:485
  42.2 3.7 collective-permute-start.10
  48.2 7.0 %collective-permute-done.2.high_ref.refs_3_ = bf16[256,1664]{1,0:T(8,128)(2,1)} collective-permute-done((bf16[256,1664]{1,0:T(8,128)(2,1)}, bf16[256,1664]{1,0:T(8,128)(2,1)}, u32[]{:S(2)}, u32[]{:S(2)}) %collective-permute-start.2) | collective-permute-done | bytes 852000 | tf_op jit(solution)/shard_map/ppermute | solution.py:64
  62.0 9.1 %collective-permute-done.7.refs_8_ = bf16[128,1664]{1,0:T(8,128)(2,1)} collective-permute-done((bf16[128,1664]{1,0:T(8,128)(2,1)}, bf16[128,1664]{1,0:T(8,128)(2,1)}, u32[]{:S(2)}, u32[]{:S(2)}) %collective-permute-start.7) | collective-permute-done | bytes 426016 | tf_op jit(solution)/shard_map/ppermute | solution.py:64
  78.2 30.9 %expert_forward.1 = (bf16[10,512,256]{2,1,0:T(8,128)(2,1)}, bf16[10,512,256]{2,1,0:T(8,128)(2,1)}, bf16[10,512,768]{2,1,0:T(8,128)(2,1)}, bf16[10,512,128]{2,1,0...) custom-call(s32[5]{0:T(128)} %stack.37.place_ref, bf16[10,1536,256]{2,1,0:T(8,128)(2,1)} %gate_w.7, ...), custom_call_target="tpu_custom_call" | custom-call | flops 2080374784000 | bytes 49807360 | tf_op jit(solution)/shard_map/expert_forward/pallas_call | solution.py:485
  109.1 5.3 %return_rows.6 = (bf16[1,256,1536]{2,1,0:T(8,128)(2,1)}, bf16[1,256,1536]{2,1,0:T(8,128)(2,1)}) custom-call(s32[4,16,512]{2,1,0:T(8,128)} %get-tuple-element.133.slots_ref, bf16[10,512,1536]{2,1,0:T(8,128)(2,1)} %after.52.rows_ref.refs_0_), custom_call_target="tpu_custom_call" | custom-call | flops 201326592000 | bytes 5505024 | tf_op jit(solution)/shard_map/return_rows/pallas_call | solution.py:485
  122.3 8.3 %return_rows.7 = (bf16[2,256,1536]{2,1,0:T(8,128)(2,1)}, bf16[2,256,1536]{2,1,0:T(8,128)(2,1)}) custom-call(s32[4,16,512]{2,1,0:T(8,128)} %get-tuple-element.133.slots_ref, bf16[10,512,1536]{2,1,0:T(8,128)(2,1)} %after.54.rows_ref.refs_0_), custom_call_target="tpu_custom_call" | custom-call | flops 402653184000 | bytes 11010048 | tf_op jit(solution)/shard_map/return_rows/pallas_call | solution.py:485
  134.4 3.3 nearer.2
  138.9 5.1 %return_rows.8 = (bf16[1,256,1536]{2,1,0:T(8,128)(2,1)}, bf16[1,256,1536]{2,1,0:T(8,128)(2,1)}) custom-call(s32[4,16,512]{2,1,0:T(8,128)} %get-tuple-element.133.slots_ref, bf16[10,512,1536]{2,1,0:T(8,128)(2,1)} %after.57.rows_ref), custom_call_target="tpu_custom_call" | custom-call | flops 201326592000 | bytes 5505024 | tf_op jit(solution)/shard_map/return_rows/pallas_call | solution.py:485
  144.0 15.6 %expert_forward_far.2 = (bf16[5,512,256]{2,1,0:T(8,128)(2,1)}, bf16[5,512,256]{2,1,0:T(8,128)(2,1)}, bf16[5,512,768]{2,1,0:T(8,128)(2,1)}, bf16[5,512,128]{2,1,0:T(8,128)(2,1)}, s32[4,16,512]{2,1,0:T(8,128)}) custom-call(s32[5]{0:T(128)} %stack.37.place_ref, bf16[10,1536,256]{2,1,0:T(8,128)(2,1)} %gate_w.7, bf16[10,1536,256]{2,1,0:T(8,128)(2,1)} %up_w.7, ...), custom_call_target="tpu_custom_call" | custom-call | flops 838860800000 | bytes 20971520 | tf_op jit(solution)/shard_map/expert_forward_far/pallas_call | solution.py:485
  159.6 6.0 %layer.1 = (bf16[256,1536]{1,0:T(8,128)(2,1)}, f32[256,1536]{1,0:T(8,128)}, bf16[256,1536]{1,0:T(8,128)(2,1)}, bf16[256,1664]{1,0:T(8,128)(2,1)}) custom-call(s32[5]{0:T(128)} %stack.37.place_ref, f32[256,1536]{1,0:T(8,128)} %get-tuple-element.129.hidden_ref, bf16[256,1536]{1,0:T(8,128)(2,1)} %fusion.5.refs_2_.target_ref, s32[256,128]{1,0:T(8,128)} %after.48.valid_ref, ...), custom_call_target="tpu_custom_call" | custom-call | flops 100 | bytes 12845056 | tf_op jit(solution)/shard_map/layer/pallas_call | solution.py:485
  169.0 3.8 collective-permute-start.34
  172.8 15.5 %expert_forward_far.3 = (bf16[5,512,256]{2,1,0:T(8,128)(2,1)}, bf16[5,512,256]{2,1,0:T(8,128)(2,1)}, bf16[5,512,768]{2,1,0:T(8,128)(2,1)}, bf16[5,512,128]{2,1,0:T(8,128)(2,1)}, s32[4,16,512]{2,1,0:T(8,128)}) custom-call(s32[5]{0:T(128)} %stack.37.place_ref, bf16[10,1536,256]{2,1,0:T(8,128)(2,1)} %gate_w.7, bf16[10,1536,256]{2,1,0:T(8,128)(2,1)} %up_w.7, ...), custom_call_target="tpu_custom_call" | custom-call | flops 838860800000 | bytes 20971520 | tf_op jit(solution)/shard_map/expert_forward_far/pallas_call | solution.py:485
  193.2 8.9 %collective-permute-done.31.refs_8_.refs_7_ = bf16[128,1664]{1,0:T(8,128)(2,1)} collective-permute-done((bf16[128,1664]{1,0:T(8,128)(2,1)}, bf16[128,1664]{1,0:T(8,128)(2,1)}, u32[]{:S(2)}, u32[]{:S(2)}) %collective-permute-start.31) | collective-permute-done | bytes 426016 | tf_op jit(solution)/shard_map/ppermute | solution.py:64
  209.2 42.0 %expert_backward.1 = (bf16[10,512,256]{2,1,0:T(8,128)(2,1)}, bf16[10,512,256]{2,1,0:T(8,128)(2,1)}, bf16[10,512,256]{2,1,0:T(8,128)(2,1)}, bf16[10,512,768]{2,1,0:T(8,128)(2,1)}, bf16[10,512,1664]{2,1,0:T(8,128)(2,1)}) custom-call(s32[5]{0:T(128)} %stack.37.place_ref, s32[4,16,512]{2,1,0:T(8,128)} %get-tuple-element.133.slots_ref, ...), custom_call_target="tpu_custom_call" | custom-call | flops 2013265920000 | bytes 65536000 | tf_op jit(solution)/shard_map/expert_backward/pallas_call | solution.py:485
  251.3 6.0 %return_rows.9 = (bf16[1,256,1664]{2,1,0:T(8,128)(2,1)}, bf16[1,256,1664]{2,1,0:T(8,128)(2,1)}) custom-call(s32[4,16,512]{2,1,0:T(8,128)} %get-tuple-element.133.slots_ref, bf16[10,512,1664]{2,1,0:T(8,128)(2,1)} %after.64.rows_ref.refs_0_), custom_call_target="tpu_custom_call" | custom-call | flops 218103808000 | bytes 5963776 | tf_op jit(solution)/shard_map/return_rows/pallas_call | solution.py:485
  265.1 8.5 %return_rows.10 = (bf16[2,256,1664]{2,1,0:T(8,128)(2,1)}, bf16[2,256,1664]{2,1,0:T(8,128)(2,1)}) custom-call(s32[4,16,512]{2,1,0:T(8,128)} %get-tuple-element.133.slots_ref, bf16[10,512,1664]{2,1,0:T(8,128)(2,1)} %after.66.rows_ref.refs_0_), custom_call_target="tpu_custom_call" | custom-call | flops 436207616000 | bytes 11927552 | tf_op jit(solution)/shard_map/return_rows/pallas_call | solution.py:485
  277.6 3.4 nearer.3
  282.9 6.0 %return_rows.11 = (bf16[1,256,1664]{2,1,0:T(8,128)(2,1)}, bf16[1,256,1664]{2,1,0:T(8,128)(2,1)}) custom-call(s32[4,16,512]{2,1,0:T(8,128)} %get-tuple-element.133.slots_ref, bf16[10,512,1664]{2,1,0:T(8,128)(2,1)} %after.69.rows_ref), custom_call_target="tpu_custom_call" | custom-call | flops 218103808000 | bytes 5963776 | tf_op jit(solution)/shard_map/return_rows/pallas_call | solution.py:485
  289.5 16.4 %expert_weights.3 = (bf16[3,3,384,256]{3,2,1,0:T(8,128)(2,1)}, bf16[3,3,384,256]{3,2,1,0:T(8,128)(2,1)}) custom-call(s32[5]{0:T(128)} %stack.37.place_ref, s32[4,16,512]{2,1,0:T(8,128)} %get-tuple-element.172.slots_ref, bf16[10,256,1536]{2,1,0:T(8,128)(2,1)} %down_w.7, bf16[5,512,256]{2,1,0:T(8,128)(2,1)} %get-tuple-element.148.refs_1_.gate_ref, ...), custom_call_target="tpu_custom_call" | custom-call | flops 724775731200 | bytes 18481152 | tf_op jit(solution)/shard_map/expert_weights/pallas_call | solution.py:485
  305.9 9.7 %collective-permute-start.52 = (bf16[3,3,384,256]{3,2,1,0:T(8,128)(2,1)}, bf16[3,3,384,256]{3,2,1,0:T(8,128)(2,1)}, u32[]{:S(2)}, u32[]{:S(2)}) collective-permute-start(bf16[3,3,384,256]{3,2,1,0:T(8,128)(2,1)} %get-tuple-element.182.refs_0_.refs_2_), channel_id=1, source_target_pairs={{0,8},{8,0},{16,24},{24,16},{1,9},{9,1},{17,25},{25,17},{2,10},{10... | collective-permute-start | bytes 5308424 | tf_op jit(solution)/shard_map/ppermute | solution.py:64
  315.6 6.2 %norm.1 = (f32[256,1536]{1,0:T(8,128)}, bf16[256,1536]{1,0:T(8,128)(2,1)}, bf16[256,128]{1,0:T(8,128)(2,1)}, f32[8,1536]{1,0:T(8,128)}) custom-call(s32[5]{0:T(128)} %stack.37.place_ref, f32[256,1536]{1,0:T(8,128)} %get-tuple-element.129.hidden_ref, f32[256,1536]{1,0:T(8,128)} %get-tuple-element.149.grad_layer_ref, ...), custom_call_target="tpu_custom_call" | custom-call | flops 100 | bytes 6553600 | tf_op jit(solution)/shard_map/norm/pallas_call | solution.py:485
  324.5 7.0 %pack_sums.2 = (bf16[4,96,896]{2,1,0:T(8,128)(2,1)}, bf16[4,96,896]{2,1,0:T(8,128)(2,1)}, bf16[4,96,896]{2,1,0:T(8,128)(2,1)}, bf16[2,96,896]{2,1,0:T(8,128)(2,1)}, bf16[2,96,896]{2,1,0:T(8,128)(2,1)}) custom-call(s32[5]{0:T(128)} %stack.37.place_ref, f32[8,1536]{1,0:T(8,128)} %get-tuple-element.185.sums_ref, bf16[256,1536]{1,0:T(8,128)(2,1)} %get-tuple-element.183.refs_0_, ...), custom_call_target="tpu_custom_call" | custom-call | flops 211392921600 | bytes 2752512 | tf_op jit(solution)/shard_map/pack_sums/pallas_call | solution.py:485
  332.6 22.9 %expert_weights.4 = (bf16[5,3,384,256]{3,2,1,0:T(8,128)(2,1)}, bf16[5,3,384,256]{3,2,1,0:T(8,128)(2,1)}) custom-call(s32[5]{0:T(128)} %stack.37.place_ref, s32[4,16,512]{2,1,0:T(8,128)} %get-tuple-element.192.slots_ref, bf16[10,256,1536]{2,1,0:T(8,128)(2,1)} %down_w.7, bf16[5,512,256]{2,1,0:T(8,128)(2,1)} %get-tuple-element.154.refs_2_.gate_ref, ...), custom_call_target="tpu_custom_call" | custom-call | flops 1207959552000 | bytes 30801920 | tf_op jit(solution)/shard_map/expert_weights/pallas_call | solution.py:485
  361.2 25.6 %attend_back.1 = (bf16[512,768]{1,0:T(8,128)(2,1)}, bf16[512,256]{1,0:T(8,128)(2,1)}, bf16[512,256]{1,0:T(8,128)(2,1)}, f32[256,1536]{1,0:T(8,128)}, bf16[256,1536]{1,0:T(8,128)(2,1)}, /*index=5*/f32[8,1536]{1,0:T(8,128)}) custom-call(s32[5]{0:T(128)} %stack.37.place_ref, bf16[256,1536]{1,0:T(8,128)(2,1)} %get-tuple-element.201.mine_ref, ...), custom_call_target="tpu_custom_call" | custom-call | flops 483183820800 | bytes 15728640 | tf_op jit(solution)/shard_map/attend_back/pallas_call | solution.py:485
  387.4 8.1 %pack_sums.3 = (bf16[4,96,1408]{2,1,0:T(8,128)(2,1)}, bf16[4,96,1408]{2,1,0:T(8,128)(2,1)}, bf16[4,96,1408]{2,1,0:T(8,128)(2,1)}, bf16[2,96,1408]{2,1,0:T(8,128)(2,1)}, bf16[2,96,1408]{2,1,0:T(8,128)(2,1)}) custom-call(s32[5]{0:T(128)} %stack.37.place_ref, f32[8,1536]{1,0:T(8,128)} %after.77.sums_ref, ...), custom_call_target="tpu_custom_call" | custom-call | flops 664377753600 | bytes 4325376 | tf_op jit(solution)/shard_map/pack_sums/pallas_call | solution.py:485
  402.6 13.2 %expert_weights.5 = (bf16[2,3,384,256]{3,2,1,0:T(8,128)(2,1)}, bf16[2,3,384,256]{3,2,1,0:T(8,128)(2,1)}) custom-call(s32[5]{0:T(128)} %stack.37.place_ref, s32[4,16,512]{2,1,0:T(8,128)} %get-tuple-element.172.slots_ref, bf16[10,256,1536]{2,1,0:T(8,128)(2,1)} %down_w.7, bf16[5,512,256]{2,1,0:T(8,128)(2,1)} %get-tuple-element.148.refs_1_.gate_ref, ...), custom_call_target="tpu_custom_call" | custom-call | flops 483183820800 | bytes 12320768 | tf_op jit(solution)/shard_map/expert_weights/pallas_call | solution.py:485
  426.7 17.7 %collective-permute-done.59.refs_0_ = bf16[4,96,1408]{2,1,0:T(8,128)(2,1)} collective-permute-done((bf16[4,96,1408]{2,1,0:T(8,128)(2,1)}, bf16[4,96,1408]{2,1,0:T(8,128)(2,1)}, u32[]{:S(2)}, u32[]{:S(2)}) %collective-permute-start.59) | collective-permute-done | bytes 1081376 | tf_op jit(solution)/shard_map/ppermute | solution.py:64
  448.1 3.1 collective-permute-start.63
  476.3 4.7 finish_weights.3
  481.0 7.1 %finish_weights.4 = (f32[10,384,256]{2,1,0:T(8,128)}, f32[10,384,256]{2,1,0:T(8,128)}, f32[10,256,384]{2,1,0:T(8,128)}, f32[8,128]{1,0:T(8,128)}) custom-call(f32[10,384,256]{2,1,0:T(8,128)} %get-tuple-element.228.gate_in, f32[10,384,256]{2,1,0:T(8,128)} %get-tuple-element.229.up_in, ...), custom_call_target="tpu_custom_call", output_to_operand_aliasing={{0}: (0, {}), {1}: (1, {}), {2}: (2, {})} | custom-call | flops 147456000 | bytes 5898240 | tf_op jit(solution)/shard_map/finish_weights/pallas_call | solution.py:485
  (317 shorter events, 139.6 us)
Async XLA Ops:
  32.8 22.4 %collective-permute-start.2 = (bf16[256,1664]{1,0:T(8,128)(2,1)}, bf16[256,1664]{1,0:T(8,128)(2,1)}, u32[]{:S(2)}, u32[]{:S(2)}) collective-permute-start(bf16[256,1664]{1,0:T(8,128)(2,1)} %get-tuple-element.130.refs_1_.refs_0_.refs_2_), channel_id=1, source_target_pairs={{0,2},{2,0},{4,6},{6,4},{1,3},{3,1},{5,7},{7,5},{8,10},{10,8},{12,... | collective-permute-start | bytes 2555912 | tf_op jit(solution)/shard_map/ppermute | solution.py:64
  42.2 30.3 %collective-permute-start.10 = (bf16[256,1664]{1,0:T(8,128)(2,1)}, bf16[256,1664]{1,0:T(8,128)(2,1)}, u32[]{:S(2)}, u32[]{:S(2)}) collective-permute-start(bf16[256,1664]{1,0:T(8,128)(2,1)} %get-tuple-element.130.refs_1_.refs_0_.refs_2_), channel_id=1, source_target_pairs={{0,24},{8,16},{16,8},{24,0},{1,25},{9,17},{17,9},{25,1},{2,26},{10... | collective-permute-start | bytes 2555912 | tf_op jit(solution)/shard_map/ppermute | solution.py:69
  74.6 34.5 %collective-permute-start.11 = (bf16[256,1664]{1,0:T(8,128)(2,1)}, bf16[256,1664]{1,0:T(8,128)(2,1)}, u32[]{:S(2)}, u32[]{:S(2)}) collective-permute-start(bf16[256,1664]{1,0:T(8,128)(2,1)} %after.51.refs_11_.refs_0_), channel_id=1, source_target_pairs={{0,1},{1,0},{2,3},{3,2},{4,5},{5,4},{6,7},{7,6},{8,9},{9,8},{10,11... | collective-permute-start | bytes 2555912 | tf_op jit(solution)/shard_map/ppermute | solution.py:60
  74.7 55.9 %collective-permute-start.19 = (bf16[256,1664]{1,0:T(8,128)(2,1)}, bf16[256,1664]{1,0:T(8,128)(2,1)}, u32[]{:S(2)}, u32[]{:S(2)}) collective-permute-start(bf16[256,1664]{1,0:T(8,128)(2,1)} %after.51.refs_11_.refs_0_), channel_id=1, source_target_pairs={{0,2},{2,0},{4,6},{6,4},{1,3},{3,1},{5,7},{7,5},{8,10},{10,8},{12,... | collective-permute-start | bytes 2555912 | tf_op jit(solution)/shard_map/ppermute | solution.py:64
  76.1 54.6 %collective-permute-start.20 = (bf16[256,1664]{1,0:T(8,128)(2,1)}, bf16[256,1664]{1,0:T(8,128)(2,1)}, u32[]{:S(2)}, u32[]{:S(2)}) collective-permute-start(bf16[256,1664]{1,0:T(8,128)(2,1)} %after.51.refs_11_.refs_0_), channel_id=1, source_target_pairs={{0,4},{2,6},{4,0},{6,2},{1,5},{3,7},{5,1},{7,3},{8,12},{10,14},{12... | collective-permute-start | bytes 2555912 | tf_op jit(solution)/shard_map/ppermute | solution.py:64
  77.6 53.1 %collective-permute-start.21 = (bf16[256,1664]{1,0:T(8,128)(2,1)}, bf16[256,1664]{1,0:T(8,128)(2,1)}, u32[]{:S(2)}, u32[]{:S(2)}) collective-permute-start(bf16[256,1664]{1,0:T(8,128)(2,1)} %after.51.refs_11_.refs_0_), channel_id=1, source_target_pairs={{0,6},{2,4},{4,2},{6,0},{1,7},{3,5},{5,3},{7,1},{8,14},{10,12},{12... | collective-permute-start | bytes 2555912 | tf_op jit(solution)/shard_map/ppermute | solution.py:64
  137.7 21.9 %collective-permute-start.17 = (bf16[256,1536]{1,0:T(8,128)(2,1)}, bf16[256,1536]{1,0:T(8,128)(2,1)}, u32[]{:S(2)}, u32[]{:S(2)}) collective-permute-start(bf16[256,1536]{1,0:T(8,128)(2,1)} %get-tuple-element.141.refs_0_.refs_1_.refs_8_), channel_id=1, source_target_pairs={{0,2},{2,0},{4,6},{6,4},{1,3},{3,1},{5,7},{7,5},{8,10},{10,8},{12,... | collective-permute-start | bytes 2359304 | tf_op jit(solution)/shard_map/ppermute | solution.py:64
  138.3 21.3 %collective-permute-start.18 = (bf16[256,1536]{1,0:T(8,128)(2,1)}, bf16[256,1536]{1,0:T(8,128)(2,1)}, u32[]{:S(2)}, u32[]{:S(2)}) collective-permute-start(bf16[256,1536]{1,0:T(8,128)(2,1)} %get-tuple-element.142.refs_0_.refs_2_), channel_id=1, source_target_pairs={{0,4},{2,6},{4,0},{6,2},{1,5},{3,7},{5,1},{7,3},{8,12},{10,14},{12... | collective-permute-start | bytes 2359304 | tf_op jit(solution)/shard_map/ppermute | solution.py:64
  165.6 22.7 %collective-permute-start.25 = (bf16[256,1664]{1,0:T(8,128)(2,1)}, bf16[256,1664]{1,0:T(8,128)(2,1)}, u32[]{:S(2)}, u32[]{:S(2)}) collective-permute-start(bf16[256,1664]{1,0:T(8,128)(2,1)} %get-tuple-element.153.refs_0_.refs_8_.refs_1_), channel_id=1, source_target_pairs={{0,1},{1,0},{2,3},{3,2},{4,5},{5,4},{6,7},{7,6},{8,9},{9,8},{10,11... | collective-permute-start | bytes 2555912 | tf_op jit(solution)/shard_map/ppermute | solution.py:60
  166.1 22.2 %collective-permute-start.26 = (bf16[256,1664]{1,0:T(8,128)(2,1)}, bf16[256,1664]{1,0:T(8,128)(2,1)}, u32[]{:S(2)}, u32[]{:S(2)}) collective-permute-start(bf16[256,1664]{1,0:T(8,128)(2,1)} %get-tuple-element.153.refs_0_.refs_8_.refs_1_), channel_id=1, source_target_pairs={{0,2},{2,0},{4,6},{6,4},{1,3},{3,1},{5,7},{7,5},{8,10},{10,8},{12,... | collective-permute-start | bytes 2555912 | tf_op jit(solution)/shard_map/ppermute | solution.py:64
  169.0 33.7 %collective-permute-start.34 = (bf16[256,1536]{1,0:T(8,128)(2,1)}, bf16[256,1536]{1,0:T(8,128)(2,1)}, u32[]{:S(2)}, u32[]{:S(2)}) collective-permute-start(bf16[256,1536]{1,0:T(8,128)(2,1)} %after.61), channel_id=1, source_target_pairs={{0,24},{8,16},{16,8},{24,0},{1,25},{9,17},{17,9},{25,1},{2,26},{10... | collective-permute-start | bytes 2359304 | tf_op jit(solution)/shard_map/ppermute | solution.py:69
  205.6 45.7 %collective-permute-start.35 = (bf16[256,1536]{1,0:T(8,128)(2,1)}, bf16[256,1536]{1,0:T(8,128)(2,1)}, u32[]{:S(2)}, u32[]{:S(2)}) collective-permute-start(bf16[256,1536]{1,0:T(8,128)(2,1)} %after.62.refs_10_.refs_6_), channel_id=1, source_target_pairs={{0,1},{1,0},{2,3},{3,2},{4,5},{5,4},{6,7},{7,6},{8,9},{9,8},{10,11... | collective-permute-start | bytes 2359304 | tf_op jit(solution)/shard_map/ppermute | solution.py:60
  205.7 45.6 %collective-permute-start.36 = (bf16[256,1536]{1,0:T(8,128)(2,1)}, bf16[256,1536]{1,0:T(8,128)(2,1)}, u32[]{:S(2)}, u32[]{:S(2)}) collective-permute-start(bf16[256,1536]{1,0:T(8,128)(2,1)} %after.62.refs_10_.refs_6_), channel_id=1, source_target_pairs={{0,2},{2,0},{4,6},{6,4},{1,3},{3,1},{5,7},{7,5},{8,10},{10,8},{12,... | collective-permute-start | bytes 2359304 | tf_op jit(solution)/shard_map/ppermute | solution.py:64
  207.1 44.2 %collective-permute-start.37 = (bf16[256,1536]{1,0:T(8,128)(2,1)}, bf16[256,1536]{1,0:T(8,128)(2,1)}, u32[]{:S(2)}, u32[]{:S(2)}) collective-permute-start(bf16[256,1536]{1,0:T(8,128)(2,1)} %after.62.refs_10_.refs_6_), channel_id=1, source_target_pairs={{0,4},{2,6},{4,0},{6,2},{1,5},{3,7},{5,1},{7,3},{8,12},{10,14},{12... | collective-permute-start | bytes 2359304 | tf_op jit(solution)/shard_map/ppermute | solution.py:64
  208.4 42.9 %collective-permute-start.38 = (bf16[256,1536]{1,0:T(8,128)(2,1)}, bf16[256,1536]{1,0:T(8,128)(2,1)}, u32[]{:S(2)}, u32[]{:S(2)}) collective-permute-start(bf16[256,1536]{1,0:T(8,128)(2,1)} %after.62.refs_10_.refs_6_), channel_id=1, source_target_pairs={{0,6},{2,4},{4,2},{6,0},{1,7},{3,5},{5,3},{7,1},{8,14},{10,12},{12... | collective-permute-start | bytes 2359304 | tf_op jit(solution)/shard_map/ppermute | solution.py:64
  281.0 34.6 %collective-permute-start.47 = (bf16[256,1664]{1,0:T(8,128)(2,1)}, bf16[256,1664]{1,0:T(8,128)(2,1)}, u32[]{:S(2)}, u32[]{:S(2)}) collective-permute-start(bf16[256,1664]{1,0:T(8,128)(2,1)} %get-tuple-element.165.refs_0_.refs_1_.refs_3_.refs_14_), channel_id=1, source_target_pairs={{0,2},{2,0},{4,6},{6,4},{1,3},{3,1},{5,7},{7,5},{8,10},{10,8},{12,... | collective-permute-start | bytes 2555912 | tf_op jit(solution)/shard_map/ppermute | solution.py:64
  281.6 34.0 %collective-permute-start.48 = (bf16[256,1664]{1,0:T(8,128)(2,1)}, bf16[256,1664]{1,0:T(8,128)(2,1)}, u32[]{:S(2)}, u32[]{:S(2)}) collective-permute-start(bf16[256,1664]{1,0:T(8,128)(2,1)} %get-tuple-element.166.refs_0_.refs_2_.refs_4_.refs_15_), channel_id=1, source_target_pairs={{0,4},{2,6},{4,0},{6,2},{1,5},{3,7},{5,1},{7,3},{8,12},{10,14},{12... | collective-permute-start | bytes 2555912 | tf_op jit(solution)/shard_map/ppermute | solution.py:64
  288.9 26.7 %collective-permute-start.46 = (bf16[1,256,1664]{2,1,0:T(8,128)(2,1)}, bf16[1,256,1664]{2,1,0:T(8,128)(2,1)}, u32[]{:S(2)}, u32[]{:S(2)}) collective-permute-start(bf16[1,256,1664]{2,1,0:T(8,128)(2,1)} %after.71), channel_id=1, source_target_pairs={{0,1},{1,0},{2,3},{3,2},{4,5},{5,4},{6,7},{7,6},{8,9},{9,8},{10,11... | collective-permute-start | bytes 2555912 | tf_op jit(solution)/shard_map/ppermute | solution.py:60
  305.9 55.3 %collective-permute-start.52 = (bf16[3,3,384,256]{3,2,1,0:T(8,128)(2,1)}, bf16[3,3,384,256]{3,2,1,0:T(8,128)(2,1)}, u32[]{:S(2)}, u32[]{:S(2)}) collective-permute-start(bf16[3,3,384,256]{3,2,1,0:T(8,128)(2,1)} %get-tuple-element.182.refs_0_.refs_2_), channel_id=1, source_target_pairs={{0,8},{8,0},{16,24},{24,16},{1,9},{9,1},{17,25},{25,17},{2,10},{10... | collective-permute-start | bytes 5308424 | tf_op jit(solution)/shard_map/ppermute | solution.py:64
  331.5 24.2 %collective-permute-start.50 = (bf16[2,96,896]{2,1,0:T(8,128)(2,1)}, bf16[2,96,896]{2,1,0:T(8,128)(2,1)}, u32[]{:S(2)}, u32[]{:S(2)}) collective-permute-start(bf16[2,96,896]{2,1,0:T(8,128)(2,1)} %get-tuple-element.190.refs_0_.refs_14_), channel_id=1, source_target_pairs={{0,2},{2,0},{4,6},{6,4},{1,3},{3,1},{5,7},{7,5},{8,10},{10,8},{12,... | collective-permute-start | bytes 1032200 | tf_op jit(solution)/shard_map/ppermute | solution.py:64
  332.1 23.6 %collective-permute-start.51 = (bf16[2,96,896]{2,1,0:T(8,128)(2,1)}, bf16[2,96,896]{2,1,0:T(8,128)(2,1)}, u32[]{:S(2)}, u32[]{:S(2)}) collective-permute-start(bf16[2,96,896]{2,1,0:T(8,128)(2,1)} %get-tuple-element.191.refs_15_), channel_id=1, source_target_pairs={{0,4},{2,6},{4,0},{6,2},{1,5},{3,7},{5,1},{7,3},{8,12},{10,14},{12... | collective-permute-start | bytes 1032200 | tf_op jit(solution)/shard_map/ppermute | solution.py:64
  355.6 88.9 %collective-permute-start.62 = (bf16[5,3,384,256]{3,2,1,0:T(8,128)(2,1)}, bf16[5,3,384,256]{3,2,1,0:T(8,128)(2,1)}, u32[]{:S(2)}, u32[]{:S(2)}) collective-permute-start(bf16[5,3,384,256]{3,2,1,0:T(8,128)(2,1)} %get-tuple-element.197.refs_0_.refs_1_), channel_id=1, source_target_pairs={{0,8},{8,0},{16,24},{24,16},{1,9},{9,1},{17,25},{25,17},{2,10},{10... | collective-permute-start | bytes 8847368 | tf_op jit(solution)/shard_map/ppermute | solution.py:64
  358.3 29.1 %collective-permute-start.53 = (bf16[4,96,896]{2,1,0:T(8,128)(2,1)}, bf16[4,96,896]{2,1,0:T(8,128)(2,1)}, u32[]{:S(2)}, u32[]{:S(2)}) collective-permute-start(bf16[4,96,896]{2,1,0:T(8,128)(2,1)} %get-tuple-element.198.refs_2_.refs_0_), channel_id=1, source_target_pairs={{0,2},{2,0},{4,6},{6,4},{1,3},{3,1},{5,7},{7,5},{8,10},{10,8},{12,... | collective-permute-start | bytes 2064392 | tf_op jit(solution)/shard_map/ppermute | solution.py:64
  359.7 27.7 %collective-permute-start.54 = (bf16[4,96,896]{2,1,0:T(8,128)(2,1)}, bf16[4,96,896]{2,1,0:T(8,128)(2,1)}, u32[]{:S(2)}, u32[]{:S(2)}) collective-permute-start(bf16[4,96,896]{2,1,0:T(8,128)(2,1)} %get-tuple-element.199.refs_3_), channel_id=1, source_target_pairs={{0,4},{2,6},{4,0},{6,2},{1,5},{3,7},{5,1},{7,3},{8,12},{10,14},{12... | collective-permute-start | bytes 2064392 | tf_op jit(solution)/shard_map/ppermute | solution.py:64
  361.2 26.2 %collective-permute-start.55 = (bf16[256,1536]{1,0:T(8,128)(2,1)}, bf16[256,1536]{1,0:T(8,128)(2,1)}, u32[]{:S(2)}, u32[]{:S(2)}) collective-permute-start(bf16[256,1536]{1,0:T(8,128)(2,1)} %get-tuple-element.200.refs_0_), channel_id=1, source_target_pairs={{0,1},{1,0},{2,3},{3,2},{4,5},{5,4},{6,7},{7,6},{8,9},{9,8},{10,11... | collective-permute-start | bytes 2359304 | tf_op jit(solution)/shard_map/ppermute | solution.py:60
  400.6 43.9 %collective-permute-start.61 = (bf16[192,896]{1,0:T(8,128)(2,1)}, bf16[192,896]{1,0:T(8,128)(2,1)}, u32[]{:S(2)}, u32[]{:S(2)}) collective-permute-start(bf16[192,896]{1,0:T(8,128)(2,1)} %pad_maximum_fusion.2.refs_0_.refs_17_), channel_id=1, source_target_pairs={{0,8},{8,0},{16,24},{24,16},{1,9},{9,1},{17,25},{25,17},{2,10},{10... | collective-permute-start | bytes 1032200 | tf_op jit(solution)/shard_map/ppermute | solution.py:64
  415.8 74.2 %collective-permute-start.67 = (bf16[2,3,384,256]{3,2,1,0:T(8,128)(2,1)}, bf16[2,3,384,256]{3,2,1,0:T(8,128)(2,1)}, u32[]{:S(2)}, u32[]{:S(2)}) collective-permute-start(bf16[2,3,384,256]{3,2,1,0:T(8,128)(2,1)} %get-tuple-element.221.refs_0_.refs_1_), channel_id=1, source_target_pairs={{0,8},{8,0},{16,24},{24,16},{1,9},{9,1},{17,25},{25,17},{2,10},{10... | collective-permute-start | bytes 3538952 | tf_op jit(solution)/shard_map/ppermute | solution.py:64
  418.9 25.6 %collective-permute-start.59 = (bf16[4,96,1408]{2,1,0:T(8,128)(2,1)}, bf16[4,96,1408]{2,1,0:T(8,128)(2,1)}, u32[]{:S(2)}, u32[]{:S(2)}) collective-permute-start(bf16[4,96,1408]{2,1,0:T(8,128)(2,1)} %get-tuple-element.222.refs_0_.refs_1_.refs_2_), channel_id=1, source_target_pairs={{0,2},{2,0},{4,6},{6,4},{1,3},{3,1},{5,7},{7,5},{8,10},{10,8},{12,... | collective-permute-start | bytes 3244040 | tf_op jit(solution)/shard_map/ppermute | solution.py:64
  420.4 30.8 %collective-permute-start.60 = (bf16[4,96,1408]{2,1,0:T(8,128)(2,1)}, bf16[4,96,1408]{2,1,0:T(8,128)(2,1)}, u32[]{:S(2)}, u32[]{:S(2)}) collective-permute-start(bf16[4,96,1408]{2,1,0:T(8,128)(2,1)} %get-tuple-element.223.refs_2_.refs_3_), channel_id=1, source_target_pairs={{0,4},{2,6},{4,0},{6,2},{1,5},{3,7},{5,1},{7,3},{8,12},{10,14},{12... | collective-permute-start | bytes 3244040 | tf_op jit(solution)/shard_map/ppermute | solution.py:64
  455.3 39.4 %collective-permute-start.66 = (bf16[96,1408]{1,0:T(8,128)(2,1)}, bf16[96,1408]{1,0:T(8,128)(2,1)}, u32[]{:S(2)}, u32[]{:S(2)}) collective-permute-start(bf16[96,1408]{1,0:T(8,128)(2,1)} %get-tuple-element.272.refs_1_.refs_2_.refs_0_), channel_id=1, source_target_pairs={{0,8},{8,0},{16,24},{24,16},{1,9},{9,1},{17,25},{25,17},{2,10},{10... | collective-permute-start | bytes 811016 | tf_op jit(solution)/shard_map/ppermute | solution.py:64
  455.6 39.0 %collective-permute-start.68 = (bf16[96,1408]{1,0:T(8,128)(2,1)}, bf16[96,1408]{1,0:T(8,128)(2,1)}, u32[]{:S(2)}, u32[]{:S(2)}) collective-permute-start(bf16[96,1408]{1,0:T(8,128)(2,1)} %get-tuple-element.271.refs_2_.refs_3_), channel_id=1, source_target_pairs={{0,16},{8,24},{16,0},{24,8},{1,17},{9,25},{17,1},{25,9},{2,18},{10... | collective-permute-start | bytes 811016 | tf_op jit(solution)/shard_map/ppermute | solution.py:64
  456.9 37.8 %collective-permute-start.69 = (bf16[96,1408]{1,0:T(8,128)(2,1)}, bf16[96,1408]{1,0:T(8,128)(2,1)}, u32[]{:S(2)}, u32[]{:S(2)}) collective-permute-start(bf16[96,1408]{1,0:T(8,128)(2,1)} %get-tuple-element.270.refs_3_.refs_4_), channel_id=1, source_target_pairs={{0,24},{8,16},{16,8},{24,0},{1,25},{9,17},{17,9},{25,1},{2,26},{10... | collective-permute-start | bytes 811016 | tf_op jit(solution)/shard_map/ppermute | solution.py:64
  (68 other events, 474.7 us)
